TPU v7x, 32 devices: a whole 2x2x4 slice. The times are simulated.
32 devices in a mesh: section: 2 (over core), fsdp: 4 (over z), ctx: 4 (over y, x).
Axes of the slice: x: 2, y: 2, z: 4, core: 2. Of those that a mesh axis runs over, the one named last changes fastest.
Arguments:
- boundary: bfloat16 [2, 2, 4, 1024, 640], P('section', None, 'fsdp', 'ctx'), may hold values from -6 to 6
- positions: int32 [2, 4, 1024], P(None, 'fsdp'), may hold values from 0 to 1023, each once within a row
- w_query: bfloat16 [2, 640, 1024], P('section', ('fsdp', 'ctx')), may hold values from -0.25 to 0.25
- w_key_value: bfloat16 [2, 640, 512], P('section', ('fsdp', 'ctx')), may hold values from -0.25 to 0.25
- w_out: bfloat16 [2, 1024, 640], P('section', ('fsdp', 'ctx')), may hold values from -0.1875 to 0.1875
- w_gate_up: bfloat16 [2, 640, 4096], P('section', ('fsdp', 'ctx')), may hold values from -0.25 to 0.25
- w_down: bfloat16 [2, 2048, 640], P('section', ('fsdp', 'ctx')), may hold values from -0.125 to 0.125
- norm_gains: bfloat16 [2, 4, 640], P('section', None, ('fsdp', 'ctx')), may hold values from 0.25 to 1.75
- head_gains: bfloat16 [2, 2, 256], P('section', None, ('fsdp', 'ctx')), may hold values from 0.25 to 1.75
Outputs:
- boundary_out: float32 [2, 2, 4, 1024, 640], P('section', None, 'fsdp', 'ctx')
- grad_query: float32 [2, 640, 1024], P('section', ('fsdp', 'ctx'))
- grad_key_value: float32 [2, 640, 512], P('section', ('fsdp', 'ctx'))
- grad_out: float32 [2, 1024, 640], P('section', ('fsdp', 'ctx'))
- grad_gate_up: float32 [2, 640, 4096], P('section', ('fsdp', 'ctx'))
- grad_down: float32 [2, 2048, 640], P('section', ('fsdp', 'ctx'))
- grad_norm_gains: float32 [2, 4, 640], P('section', None, ('fsdp', 'ctx'))
- grad_head_gains: float32 [2, 2, 256], P('section', None, ('fsdp', 'ctx'))
Inputs may be any that keep to these rules, and one draw needn't show every extreme that they name: `positions`: each row of 1024 holds every place 0 to 1023 once.
All inputs are finite; a program needn't handle non-finite values.
Results may differ from a plain program's by a relative error of at most 0.025.
Values may be sent and summed in bfloat16 or wider, within the bound.
No kernel may reach another device: no remote copies, remote signals or barrier semaphores. Data moves between devices by JAX's collectives and lax.ppermute only.
A program may use at most 320 MiB of HBM per device.

v0:
```python
import math

import jax
import jax.numpy as jnp
from jax import lax
from jax.sharding import PartitionSpec as P

D = 640
FF = 2048
HEADS = 4
HD = 256
WIN = 512
MB = 2


EPS = 1e-06
LOG_LOCAL = math.log(10000.0)
LOG_GLOBAL = math.log(1000000.0)


def shifted(shard, axis, by):
    count = lax.axis_size(axis)
    pairs = [(i, i + by) for i in range(count) if 0 <= i + by < count]
    return lax.ppermute(shard, axis, pairs)


def rms_norm(values_in, gain):
    return (
        values_in * lax.rsqrt(jnp.mean(values_in * values_in, axis=-1, keepdims=True) + EPS) * gain
    )


def rotate(values_in, cosine, sine_table):
    half_width = values_in.shape[-1] // 2
    lower_half = values_in[..., :half_width]
    upper_half = values_in[..., half_width:]
    return jnp.concatenate(
        [
            lower_half * cosine - upper_half * sine_table,
            upper_half * cosine + lower_half * sine_table,
        ],
        axis=-1,
    )


def rope_tables(places, log_base):
    half_width = HD // 2
    inverse = jnp.exp(-log_base * (jnp.arange(half_width, dtype=jnp.float32) * (2.0 / HD)))
    angles = places.astype(jnp.float32)[:, None] * inverse[None, :]
    return (jnp.cos(angles), jnp.sin(angles))


def head_prepare(query_product, key_product, query_gain, key_gain, cosine, sine_table):
    token_count = query_product.shape[0]
    queries = rms_norm(query_product.reshape(token_count, HEADS, HD), query_gain)
    keys_normed = rms_norm(key_product, key_gain)
    return (
        rotate(queries, cosine[:, None, :], sine_table[:, None, :]),
        rotate(keys_normed, cosine, sine_table),
    )


def gated(gate_up):
    return jax.nn.gelu(gate_up[:, :FF], approximate=True) * gate_up[:, FF:]


def attention_weights(flat_queries, all_keys, places, all_places, window):
    score_scale = 1.0 / math.sqrt(HD)
    query_places = jnp.repeat(places, HEADS)
    allowed = (all_places[None, :] <= query_places[:, None]) & (
        query_places[:, None] - all_places[None, :] < window
    )
    scores = (
        jnp.einsum("qd,kd->qk", flat_queries, all_keys, preferred_element_type=jnp.float32)
        * score_scale
    )
    scores = jnp.where(allowed, scores, -1e30)
    maximum = jnp.max(scores, axis=-1, keepdims=True)
    weights = jnp.exp(scores - maximum)
    return weights / jnp.sum(weights, axis=-1, keepdims=True)


def layer_forward(full, hidden_in, places, all_places, window, log_base):
    w_query, w_key_value, w_out, w_gate_up, w_down, norm_gains, head_gains = full
    gain_rows = norm_gains.astype(jnp.float32)
    head_rows = head_gains.astype(jnp.float32)
    token_count = hidden_in.shape[0]
    normed = rms_norm(hidden_in, gain_rows[0]).astype(jnp.bfloat16)
    query_product = jnp.dot(normed, w_query, preferred_element_type=jnp.float32)
    pair_product = jnp.dot(normed, w_key_value, preferred_element_type=jnp.float32)
    cosine, sine_table = rope_tables(places, log_base)
    queries, keys_rot = head_prepare(
        query_product, pair_product[:, :HD], head_rows[0], head_rows[1], cosine, sine_table
    )
    flat_queries = queries.astype(jnp.bfloat16).reshape(token_count * HEADS, HD)
    keys_low = keys_rot.astype(jnp.bfloat16)
    values_low = pair_product[:, HD:].astype(jnp.bfloat16)
    all_keys, all_values = (
        lax.all_gather(keys_low, "ctx", axis=0, tiled=True),
        lax.all_gather(values_low, "ctx", axis=0, tiled=True),
    )
    probabilities = attention_weights(flat_queries, all_keys, places, all_places, window)
    prob_low = probabilities.astype(jnp.bfloat16)
    mixed = jnp.dot(prob_low, all_values, preferred_element_type=jnp.float32)
    mixed = mixed.reshape(token_count, HEADS * HD).astype(jnp.bfloat16)
    branch = jnp.dot(mixed, w_out, preferred_element_type=jnp.float32)
    middle = hidden_in + rms_norm(branch, gain_rows[1])
    normed_two = rms_norm(middle, gain_rows[2]).astype(jnp.bfloat16)
    gate_up = jnp.dot(normed_two, w_gate_up, preferred_element_type=jnp.float32)
    hidden = gated(gate_up).astype(jnp.bfloat16)
    down_out = jnp.dot(hidden, w_down, preferred_element_type=jnp.float32)
    result = middle + rms_norm(down_out, gain_rows[3])
    kept = {
        "normed": normed,
        "query_product": query_product,
        "pair_product": pair_product,
        "flat_queries": flat_queries,
        "all_keys": all_keys,
        "all_values": all_values,
        "mixed": mixed,
        "branch": branch,
        "middle": middle,
        "normed_two": normed_two,
        "gate_up": gate_up,
        "hidden": hidden,
        "down_out": down_out,
    }
    return (result, kept)


def layer_backward_input(full, kept, hidden_in, grad_result, places, all_places, window, log_base):
    w_query, w_key_value, w_out, w_gate_up, w_down, norm_gains, head_gains = full
    gain_rows = norm_gains.astype(jnp.float32)
    head_rows = head_gains.astype(jnp.float32)
    token_count = hidden_in.shape[0]
    score_scale = 1.0 / math.sqrt(HD)
    _, back_last = jax.vjp(rms_norm, kept["down_out"], gain_rows[3])
    grad_down, grad_gain_three = back_last(grad_result)
    grad_down_low = grad_down.astype(jnp.bfloat16)
    grad_hidden = jnp.einsum("td,fd->tf", grad_down_low, w_down, preferred_element_type=jnp.float32)
    _, back_gated = jax.vjp(gated, kept["gate_up"])
    (grad_gate_up,) = back_gated(grad_hidden)
    grad_gate_low = grad_gate_up.astype(jnp.bfloat16)
    grad_normed_two = jnp.einsum(
        "tc,dc->td", grad_gate_low, w_gate_up, preferred_element_type=jnp.float32
    )
    _, back_norm_two = jax.vjp(rms_norm, kept["middle"], gain_rows[2])
    grad_middle_part, grad_gain_two = back_norm_two(grad_normed_two)
    grad_middle = grad_result + grad_middle_part
    _, back_norm_one = jax.vjp(rms_norm, kept["branch"], gain_rows[1])
    grad_branch, grad_gain_one = back_norm_one(grad_middle)
    grad_branch_low = grad_branch.astype(jnp.bfloat16)
    grad_mixed = jnp.einsum("td,ed->te", grad_branch_low, w_out, preferred_element_type=jnp.float32)
    grad_mixed = grad_mixed.astype(jnp.bfloat16).reshape(token_count * HEADS, HD)
    flat_queries = kept["flat_queries"]
    all_keys = kept["all_keys"]
    all_values = kept["all_values"]
    probabilities = attention_weights(flat_queries, all_keys, places, all_places, window)
    prob_low = probabilities.astype(jnp.bfloat16)
    grad_probs = jnp.einsum("qd,kd->qk", grad_mixed, all_values, preferred_element_type=jnp.float32)
    inner_sum = jnp.sum(probabilities * grad_probs, axis=-1, keepdims=True)
    grad_scores = (probabilities * (grad_probs - inner_sum)).astype(jnp.bfloat16)
    grad_queries = jnp.dot(grad_scores, all_keys, preferred_element_type=jnp.float32) * score_scale
    grad_keys_all = (
        jnp.einsum("qk,qd->kd", grad_scores, flat_queries, preferred_element_type=jnp.float32)
        * score_scale
    )
    grad_values_all = jnp.einsum(
        "qk,qd->kd", prob_low, grad_mixed, preferred_element_type=jnp.float32
    )
    grad_keys, grad_values = (
        lax.psum_scatter(
            grad_keys_all.astype(jnp.bfloat16), "ctx", scatter_dimension=0, tiled=True
        ).astype(jnp.float32),
        lax.psum_scatter(
            grad_values_all.astype(jnp.bfloat16), "ctx", scatter_dimension=0, tiled=True
        ).astype(jnp.float32),
    )
    cosine, sine_table = rope_tables(places, log_base)

    def prepare(query_in, key_in, query_gain, key_gain):
        return head_prepare(query_in, key_in, query_gain, key_gain, cosine, sine_table)

    _, back_heads = jax.vjp(
        prepare, kept["query_product"], kept["pair_product"][:, :HD], head_rows[0], head_rows[1]
    )
    grad_query_product, grad_key_product, grad_query_gain, grad_key_gain = back_heads(
        (grad_queries.reshape(token_count, HEADS, HD), grad_keys)
    )
    grad_pair_low = jnp.concatenate([grad_key_product, grad_values], axis=1).astype(jnp.bfloat16)
    grad_query_low = grad_query_product.astype(jnp.bfloat16)
    grad_normed = jnp.einsum(
        "te,de->td", grad_query_low, w_query, preferred_element_type=jnp.float32
    )
    grad_normed = grad_normed + jnp.einsum(
        "tc,dc->td", grad_pair_low, w_key_value, preferred_element_type=jnp.float32
    )
    _, back_norm_zero = jax.vjp(rms_norm, hidden_in, gain_rows[0])
    grad_input_part, grad_gain_zero = back_norm_zero(grad_normed)
    grad_input = grad_middle + grad_input_part
    gain_grads = (
        jnp.stack([grad_gain_zero, grad_gain_one, grad_gain_two, grad_gain_three]),
        jnp.stack([grad_query_gain, grad_key_gain]),
    )
    saved = (grad_down_low, grad_gate_low, grad_branch_low, grad_query_low, grad_pair_low)
    return (grad_input, saved, gain_grads)


def layer_weight_grads(kept, saved):
    grad_down_low, grad_gate_low, grad_branch_low, grad_query_low, grad_pair_low = saved
    grad_w_down = jnp.einsum(
        "tf,td->fd", kept["hidden"], grad_down_low, preferred_element_type=jnp.float32
    )
    grad_w_gate_up = jnp.einsum(
        "td,tc->dc", kept["normed_two"], grad_gate_low, preferred_element_type=jnp.float32
    )
    grad_w_out = jnp.einsum(
        "te,td->ed", kept["mixed"], grad_branch_low, preferred_element_type=jnp.float32
    )
    grad_w_query = jnp.einsum(
        "td,te->de", kept["normed"], grad_query_low, preferred_element_type=jnp.float32
    )
    grad_w_key_value = jnp.einsum(
        "td,tc->dc", kept["normed"], grad_pair_low, preferred_element_type=jnp.float32
    )
    return (grad_w_query, grad_w_key_value, grad_w_out, grad_w_gate_up, grad_w_down)


def send_gradient(grad_input):
    return shifted(grad_input.astype(jnp.bfloat16), "section", -1).astype(jnp.float32)


def local(
    boundary, positions, w_query, w_key_value, w_out, w_gate_up, w_down, norm_gains, head_gains
):
    section_index = lax.axis_index("section")
    first_section = section_index == 0
    ctx_index = lax.axis_index("ctx")
    shard_rows = boundary.shape[3]
    seq_length = positions.shape[-1]
    window = jnp.where(first_section, WIN, seq_length).astype(jnp.int32)
    log_base = jnp.where(first_section, LOG_LOCAL, LOG_GLOBAL).astype(jnp.float32)
    seq_places = [positions[batch_index, 0] for batch_index in range(MB)]
    own_places = [
        lax.dynamic_slice_in_dim(seq_places[batch_index], ctx_index * shard_rows, shard_rows)
        for batch_index in range(MB)
    ]
    gathered = (
        lax.all_gather(w_query, ("fsdp", "ctx"), axis=1, tiled=True),
        lax.all_gather(w_key_value, ("fsdp", "ctx"), axis=1, tiled=True),
        lax.all_gather(w_out, ("fsdp", "ctx"), axis=1, tiled=True),
        lax.all_gather(w_gate_up, ("fsdp", "ctx"), axis=1, tiled=True),
        lax.all_gather(w_down, ("fsdp", "ctx"), axis=1, tiled=True),
        lax.all_gather(norm_gains, ("fsdp", "ctx"), axis=2, tiled=True),
        lax.all_gather(head_gains, ("fsdp", "ctx"), axis=2, tiled=True),
    )
    full = tuple((weight[0] for weight in gathered))
    received = jnp.zeros((shard_rows, D), jnp.bfloat16)
    kept_ticks = []
    last_outputs = []
    for tick_index in range(MB + 1):
        first_batch = min(tick_index, MB - 1)
        second_batch = max(tick_index - 1, 0)
        if tick_index < MB:
            entering = jnp.where(first_section, boundary[0, tick_index, 0], received)
        else:
            entering = received
        places = jnp.where(first_section, own_places[first_batch], own_places[second_batch])
        all_places = jnp.where(first_section, seq_places[first_batch], seq_places[second_batch])
        hidden_in = entering.astype(jnp.float32)
        result, kept = layer_forward(full, hidden_in, places, all_places, window, log_base)
        kept_ticks.append((hidden_in, places, all_places, kept))
        if tick_index >= 1:
            last_outputs.append(result)
        if tick_index < MB:
            received = shifted(result.astype(jnp.bfloat16), "section", 1)
    incoming = jnp.zeros((shard_rows, D), jnp.float32)
    first_grads = [incoming for batch_index in range(MB)]
    summed = None
    for tick_back in range(MB + 1):
        hidden_in, places, all_places, kept = kept_ticks[MB - tick_back]
        if tick_back < MB:
            grad_result = jnp.where(
                first_section, incoming, boundary[0, MB - 1 - tick_back, 0].astype(jnp.float32)
            )
        else:
            grad_result = jnp.where(first_section, incoming, jnp.zeros_like(incoming))
        grad_input, saved, gain_grads = layer_backward_input(
            full, kept, hidden_in, grad_result, places, all_places, window, log_base
        )
        matrix_grads = layer_weight_grads(kept, saved)
        if tick_back < MB:
            incoming = send_gradient(grad_input)
        grads = matrix_grads + gain_grads
        if tick_back >= 1:
            first_grads[MB - tick_back] = grad_input
        stacked = tuple((grad[None] for grad in grads))
        if summed is None:
            summed = stacked
        else:
            summed = tuple((total_grad + grad for total_grad, grad in zip(summed, stacked)))
    summed = (
        lax.psum_scatter(summed[0], ("fsdp", "ctx"), scatter_dimension=1, tiled=True),
        lax.psum_scatter(summed[1], ("fsdp", "ctx"), scatter_dimension=1, tiled=True),
        lax.psum_scatter(summed[2], ("fsdp", "ctx"), scatter_dimension=1, tiled=True),
        lax.psum_scatter(summed[3], ("fsdp", "ctx"), scatter_dimension=1, tiled=True),
        lax.psum_scatter(summed[4], ("fsdp", "ctx"), scatter_dimension=1, tiled=True),
        lax.psum_scatter(summed[5], ("fsdp", "ctx"), scatter_dimension=2, tiled=True),
        lax.psum_scatter(summed[6], ("fsdp", "ctx"), scatter_dimension=2, tiled=True),
    )
    boundary_out = jnp.where(first_section, jnp.stack(first_grads), jnp.stack(last_outputs))[
        None, :, None
    ]
    return (
        boundary_out,
        summed[0],
        summed[1],
        summed[2],
        summed[3],
        summed[4],
        summed[5],
        summed[6],
    )


def solution(mesh):
    in_specs = (
        P("section", None, "fsdp", "ctx", None),
        P(None, "fsdp", None),
        P("section", ("fsdp", "ctx"), None),
        P("section", ("fsdp", "ctx"), None),
        P("section", ("fsdp", "ctx"), None),
        P("section", ("fsdp", "ctx"), None),
        P("section", ("fsdp", "ctx"), None),
        P("section", None, ("fsdp", "ctx")),
        P("section", None, ("fsdp", "ctx")),
    )
    out_specs = (
        P("section", None, "fsdp", "ctx", None),
        P("section", ("fsdp", "ctx"), None),
        P("section", ("fsdp", "ctx"), None),
        P("section", ("fsdp", "ctx"), None),
        P("section", ("fsdp", "ctx"), None),
        P("section", ("fsdp", "ctx"), None),
        P("section", None, ("fsdp", "ctx")),
        P("section", None, ("fsdp", "ctx")),
    )
    return jax.shard_map(local, mesh=mesh, in_specs=in_specs, out_specs=out_specs, check_vma=False)
```

profile of v0, /device:TPU:0, one launch (start us, length us, event | category | flops | bytes accessed | tf_op | source)
XLA Modules:
  0.0 1292.3 jit_solution(13975335043276014258)
XLA Ops:
  10.0 47.7 %all_gather.42 = bf16[1,640,512]{2,1,0:T(8,128)(2,1)S(1)} all-gather(bf16[1,40,512]{2,1,0:T(8,128)(2,1)} %param.12), channel_id=1, replica_groups=mesh['section'=2,'fsdp'=4,'ctx'=4] {'fsdp','ctx'}, dimensions={1}, use_global_device_ids=true | all-gather | bytes 696320 | tf_op jit(solution)/shard_map/all_gather | solution.py:250
  58.5 37.8 %all_gather.39 = bf16[1,4,640]{1,0,2:T(2,128)(2,1)S(1)} all-gather(bf16[1,4,40]{1,0,2:T(2,128)(2,1)S(1)} %copy.52), channel_id=1, replica_groups=mesh['section'=2,'fsdp'=4,'ctx'=4] {'fsdp','ctx'}, dimensions={2}, use_global_device_ids=true | all-gather | bytes 5440 | tf_op jit(solution)/shard_map/all_gather | solution.py:254
  96.7 8.9 slice_reduce_fusion
  106.6 38.6 %all_gather.41 = bf16[1,2,256]{1,0,2:T(2,128)(2,1)S(1)} all-gather(bf16[1,2,16]{1,0,2:T(2,128)(2,1)S(1)} %copy.54), channel_id=1, replica_groups=mesh['section'=2,'fsdp'=4,'ctx'=4] {'fsdp','ctx'}, dimensions={2}, use_global_device_ids=true | all-gather | bytes 1088 | tf_op jit(solution)/shard_map/all_gather | solution.py:255
  145.3 3.6 slice_reduce_fusion.5
  149.1 9.8 all_gather.44
  159.7 13.3 %all_gather.43 = bf16[1024,256]{1,0:T(8,128)(2,1)S(1)} all-gather(bf16[256,256]{1,0:T(8,128)(2,1)S(1)} %pad_maximum_fusion.18), channel_id=1, replica_groups=mesh['section'=2,'fsdp'=4,'ctx'=4] {'ctx'}, dimensions={0}, use_global_device_ids=true | all-gather | bytes 655360 | tf_op jit(solution)/shard_map/all_gather | solution.py:99
  184.9 33.9 %all-gather.9.cloned.1.call-done = bf16[1,640,4096]{2,1,0:T(8,128)(2,1)} async-done(((bf16[1,40,4096]{2,1,0:T(8,128)(2,1)}), bf16[1,640,4096]{2,1,0:T(8,128)(2,1)}) %all-gather.9.cloned.1.call-update) | async-done | bytes 5242896 | tf_op jit(solution)/shard_map/all_gather | solution.py:252
  218.8 4.3 fusion.10
  225.9 58.0 %all-gather.11.cloned.1.call-done = bf16[1,2048,640]{2,1,0:T(8,128)(2,1)} async-done(((bf16[1,128,640]{2,1,0:T(8,128)(2,1)}), bf16[1,2048,640]{2,1,0:T(8,128)(2,1)}) %all-gather.11.cloned.1.call-update) | async-done | bytes 2621456 | tf_op jit(solution)/shard_map/all_gather | solution.py:253
  283.9 2.8 multiply_reduce_fusion.36
  292.3 10.4 all_gather.49
  303.9 9.5 all_gather.48
  325.7 4.3 fusion.8
  340.7 11.3 all_gather.51
  353.4 8.7 all_gather.50
  374.2 4.6 fusion.6
  386.1 2.6 multiply_reduce_fusion.19
  394.9 3.6 multiply_reduce_fusion.2
  402.7 3.4 convolution_multiply_fusion.5
  414.9 2.7 fusion.91
  419.6 11.4 reduce-scatter.16.cloned.1.call-done
  437.3 21.5 %reduce-scatter.18.cloned.1.call-done = bf16[256,256]{1,0:T(8,128)(2,1)} async-done(((bf16[1024,256]{1,0:T(8,128)(2,1)}), bf16[256,256]{1,0:T(8,128)(2,1)}) %reduce-scatter.18.cloned.1.call-update) | async-done | bytes 131088 | tf_op jit(solution)/shard_map/reduce_scatter | solution.py:175
  460.1 2.9 fusion.115
  479.5 3.6 multiply_reduce_fusion.1
  487.3 3.4 convolution_multiply_fusion.3
  499.1 2.7 fusion.92
  503.9 11.8 reduce-scatter.20.cloned.1.call-done
  520.0 24.1 %reduce-scatter.22.cloned.1.call-done = bf16[256,256]{1,0:T(8,128)(2,1)} async-done(((bf16[1024,256]{1,0:T(8,128)(2,1)}), bf16[256,256]{1,0:T(8,128)(2,1)}) %reduce-scatter.22.cloned.1.call-update) | async-done | bytes 131088 | tf_op jit(solution)/shard_map/reduce_scatter | solution.py:175
  545.4 2.9 fusion.117
  556.4 2.6 multiply_reduce_fusion.13
  564.4 3.5 multiply_reduce_fusion
  572.1 3.4 convolution_multiply_fusion.1
  578.2 3.9 convolution_convert_fusion
  586.3 11.5 reduce-scatter.24.cloned.1.call-done
  607.7 18.4 %reduce-scatter.26.cloned.1.call-done = bf16[256,256]{1,0:T(8,128)(2,1)} async-done(((bf16[1024,256]{1,0:T(8,128)(2,1)}), bf16[256,256]{1,0:T(8,128)(2,1)}) %reduce-scatter.26.cloned.1.call-update) | async-done | bytes 131088 | tf_op jit(solution)/shard_map/reduce_scatter | solution.py:175
  626.1 3.0 fusion.51
  629.2 3.2 fusion.260
  648.6 3.4 add_bitcast_fusion.1
  653.1 4.0 fusion.168
  657.2 5.6 fusion.169
  662.8 10.6 add_bitcast_fusion
  677.5 76.1 %all-reduce.18 = f32[1,4,640]{2,1,0:T(4,128)S(1)} all-reduce(f32[1,4,640]{2,1,0:T(4,128)S(1)} %fusion.218), channel_id=13, replica_groups=mesh['section'=2,'fsdp'=4,'ctx'=4] {'fsdp','ctx'}, use_global_device_ids=true, to_apply=%region_68.69.clone | all-reduce | flops 2560 | bytes 20480
  759.3 22.5 %reduce-scatter.30.cloned.1.call-done = f32[1,40,512]{2,1,0:T(8,128)} async-done(((f32[1,640,512]{2,1,0:T(8,128)}), f32[1,40,512]{2,1,0:T(8,128)}) %reduce-scatter.30.cloned.1.call-update) | async-done | bytes 81936 | tf_op jit(solution)/shard_map/reduce_scatter | solution.py:304
  781.9 82.0 %reduce-scatter.28.cloned.1.call-done = f32[1,40,1024]{2,1,0:T(8,128)} async-done(((f32[1,640,1024]{2,1,0:T(8,128)}), f32[1,40,1024]{2,1,0:T(8,128)}) %reduce-scatter.28.cloned.1.call-update) | async-done | bytes 163856 | tf_op jit(solution)/shard_map/reduce_scatter | solution.py:303
  863.8 81.9 %reduce-scatter.32.cloned.1.call-done = f32[1,64,640]{2,1,0:T(8,128)} async-done(((f32[1,1024,640]{2,1,0:T(8,128)}), f32[1,64,640]{2,1,0:T(8,128)}) %reduce-scatter.32.cloned.1.call-update) | async-done | bytes 163856 | tf_op jit(solution)/shard_map/reduce_scatter | solution.py:305
  945.8 115.9 %reduce-scatter.36.cloned.1.call-done = f32[1,128,640]{2,1,0:T(8,128)} async-done(((f32[1,2048,640]{2,1,0:T(8,128)}), f32[1,128,640]{2,1,0:T(8,128)}) %reduce-scatter.36.cloned.1.call-update) | async-done | bytes 327696 | tf_op jit(solution)/shard_map/reduce_scatter | solution.py:307
  1061.7 223.7 %reduce-scatter.34.cloned.1.call-done = f32[1,40,4096]{2,1,0:T(8,128)} async-done(((f32[1,640,4096]{2,1,0:T(8,128)}), f32[1,40,4096]{2,1,0:T(8,128)}) %reduce-scatter.34.cloned.1.call-update) | async-done | bytes 655376 | tf_op jit(solution)/shard_map/reduce_scatter | solution.py:306
  (773 shorter events, 194.5 us)
Async XLA Ops:
  7.2 98.4 %copy-start.1 = (bf16[1,2,1,256,640]{4,3,2,1,0:T(8,128)(2,1)S(1)}, bf16[1,2,1,256,640]{4,3,2,1,0:T(8,128)(2,1)}, u32[]{:S(2)}) copy-start(bf16[1,2,1,256,640]{4,3,2,1,0:T(8,128)(2,1)} %param.9) | copy-start | bytes 1966084
  7.2 165.9 %all-gather.5.cloned.1.call-start = ((), (), s32[]{:S(2)}) async-start(), calls=%async_computation.12 | async-start | bytes 1392640 | tf_op jit(solution)/shard_map/all_gather | solution.py:249
  7.9 173.6 %all-gather.7.cloned.1.call-start = ((), (), s32[]{:S(2)}) async-start(), calls=%async_computation.13 | async-start | bytes 1392640 | tf_op jit(solution)/shard_map/all_gather | solution.py:251
  8.7 210.1 %all-gather.9.cloned.1.call-start = ((), (), s32[]{:S(2)}) async-start(), calls=%async_computation.14 | async-start | bytes 5570560 | tf_op jit(solution)/shard_map/all_gather | solution.py:252
  9.4 274.5 %all-gather.11.cloned.1.call-start = ((), (), s32[]{:S(2)}) async-start(), calls=%async_computation.15 | async-start | bytes 2785280 | tf_op jit(solution)/shard_map/all_gather | solution.py:253
  10.0 421.0 %reduce-scatter.16.cloned.1.call-start = ((), (), s32[]{:S(2)}) async-start(), calls=%async_computation.16 | async-start | bytes 655360 | tf_op jit(solution)/shard_map/reduce_scatter | solution.py:172
  105.8 39.5 %copy-start.218 = (f32[256]{0:T(256)}, f32[256]{0:T(256)S(1)}, u32[]{:S(2)}) copy-start(f32[256]{0:T(256)S(1)} %fusion.120) | copy-start | bytes 3076
  105.8 69.2 %copy-start.168 = (f32[256]{0:T(256)}, f32[256]{0:T(256)S(1)}, u32[]{:S(2)}) copy-start(f32[256]{0:T(256)S(1)} %fusion.223) | copy-start | bytes 3076
  106.2 66.8 %copy-start.74 = (f32[256,512]{1,0:T(8,128)}, f32[256,512]{1,0:T(8,128)S(1)}, u32[]{:S(2)}) copy-start(f32[256,512]{1,0:T(8,128)S(1)} %fusion.152) | copy-start | bytes 1572868
  106.4 42.7 %copy-start.220 = (f32[256]{0:T(256)}, f32[256]{0:T(256)S(1)}, u32[]{:S(2)}) copy-start(f32[256]{0:T(256)S(1)} %multiply_reduce_fusion.47) | copy-start | bytes 3076
  106.4 68.5 %copy-start.164 = (f32[128]{0:T(128)}, f32[128]{0:T(128)S(1)}, u32[]{:S(2)}) copy-start(f32[128]{0:T(128)S(1)} %multiply_exponential_fusion) | copy-start | bytes 1540
  106.4 184.1 %copy-start.162 = (s32[1,1,1024]{2,1,0:T(1,128)}, s32[1,1,1024]{2,1,0:T(1,128)S(1)}, u32[]{:S(2)}) copy-start(s32[1,1,1024]{2,1,0:T(1,128)S(1)} %get-tuple-element.105) | copy-start | bytes 12292
  148.9 26.9 %copy-start.127 = (f32[256]{0:T(256)}, f32[256]{0:T(256)S(1)}, u32[]{:S(2)}) copy-start(f32[256]{0:T(256)S(1)} %get-tuple-element.48) | copy-start | bytes 3076
  148.9 153.8 %copy-start.134 = (f32[256]{0:T(256)}, f32[256]{0:T(256)S(1)}, u32[]{:S(2)}) copy-start(f32[256]{0:T(256)S(1)} %get-tuple-element.49) | copy-start | bytes 3076
  148.9 26.0 %copy-start.173 = (f32[256]{0:T(256)}, f32[256]{0:T(256)S(1)}, u32[]{:S(2)}) copy-start(f32[256]{0:T(256)S(1)} %fusion.224) | copy-start | bytes 3076
  149.1 140.1 %copy-start.190 = (s32[1,1,256]{2,1,0:T(1,128)}, s32[1,1,256]{2,1,0:T(1,128)S(1)}, u32[]{:S(2)}) copy-start(s32[1,1,256]{2,1,0:T(1,128)S(1)} %get-tuple-element.155) | copy-start | bytes 3076
  183.7 39.5 %copy-start.221 = (f32[256]{0:T(256)}, f32[256]{0:T(256)S(1)}, u32[]{:S(2)}) copy-start(f32[256]{0:T(256)S(1)} %get-tuple-element.123) | copy-start | bytes 3076
  184.8 38.3 %copy-start.223 = (f32[256]{0:T(256)}, f32[256]{0:T(256)S(1)}, u32[]{:S(2)}) copy-start(f32[256]{0:T(256)S(1)} %get-tuple-element.61) | copy-start | bytes 3076
  184.8 101.9 %copy-start.7 = (f32[256,640]{1,0:T(8,128)}, f32[256,640]{1,0:T(8,128)S(1)}, u32[]{:S(2)}) copy-start(f32[256,640]{1,0:T(8,128)S(1)} %get-tuple-element.62) | copy-start | bytes 1966084
  184.8 38.3 %copy-start.159 = (f32[256]{0:T(256)}, f32[256]{0:T(256)S(1)}, u32[]{:S(2)}) copy-start(f32[256]{0:T(256)S(1)} %fusion.226) | copy-start | bytes 3076
  225.9 60.8 %copy-start.64 = (bf16[256,2048]{1,0:T(8,128)(2,1)}, bf16[256,2048]{1,0:T(8,128)(2,1)S(1)}, u32[]{:S(2)}) copy-start(bf16[256,2048]{1,0:T(8,128)(2,1)S(1)} %multiply_convert_fusion.5) | copy-start | bytes 3145732
  287.7 2.9 collective-permute-start
  291.5 21.9 %copy-start.128 = (f32[256]{0:T(256)S(1)}, f32[256]{0:T(256)}, u32[]{:S(2)}) copy-start(f32[256]{0:T(256)} %copy-done.127) | copy-start | bytes 3076
  292.3 21.4 %copy-start.10 = (f32[256,4,256]{2,0,1:T(8,128)}, f32[256,4,256]{2,0,1:T(8,128)S(1)}, u32[]{:S(2)}) copy-start(f32[256,4,256]{2,0,1:T(8,128)S(1)} %get-tuple-element.128) | copy-start | bytes 3145732
  292.3 21.4 %copy-start.155 = (f32[256,4]{0,1:T(4,128)}, f32[256,4]{0,1:T(4,128)S(1)}, u32[]{:S(2)}) copy-start(f32[256,4]{0,1:T(4,128)S(1)} %get-tuple-element.127) | copy-start | bytes 12292
  335.6 4.3 collective-permute-start.1
  340.1 22.1 %copy-start.148 = (f32[256]{0:T(256)}, f32[256]{0:T(256)S(1)}, u32[]{:S(2)}) copy-start(f32[256]{0:T(256)S(1)} %fusion.233) | copy-start | bytes 3076
  340.1 22.1 %copy-start.29 = (bf16[1024,640]{1,0:T(8,128)(2,1)S(1)}, bf16[1024,640]{1,0:T(8,128)(2,1)}, u32[]{:S(2)}) copy-start(bf16[1024,640]{1,0:T(8,128)(2,1)} %copy-done.27) | copy-start | bytes 3932164
  406.1 52.6 %reduce-scatter.18.cloned.1.call-start = ((), (), s32[]{:S(2)}) async-start(), calls=%async_computation.17 | async-start | bytes 655360 | tf_op jit(solution)/shard_map/reduce_scatter | solution.py:175
  414.4 101.2 %reduce-scatter.20.cloned.1.call-start = ((), (), s32[]{:S(2)}) async-start(), calls=%async_computation.18 | async-start | bytes 655360 | tf_op jit(solution)/shard_map/reduce_scatter | solution.py:172
  463.4 3.8 collective-permute-start.2
  490.7 53.4 %reduce-scatter.22.cloned.1.call-start = ((), (), s32[]{:S(2)}) async-start(), calls=%async_computation.19 | async-start | bytes 655360 | tf_op jit(solution)/shard_map/reduce_scatter | solution.py:175
  499.0 18.2 %copy-start.136 = (f32[256]{0:T(256)S(1)}, f32[256]{0:T(256)}, u32[]{:S(2)}) copy-start(f32[256]{0:T(256)} %copy-done.134) | copy-start | bytes 3076
  499.0 18.2 %copy-start.175 = (f32[256]{0:T(256)S(1)}, f32[256]{0:T(256)}, u32[]{:S(2)}) copy-start(f32[256]{0:T(256)} %copy-done.174) | copy-start | bytes 3076
  499.0 19.8 %copy-start.226 = (f32[256]{0:T(256)S(1)}, f32[256]{0:T(256)}, u32[]{:S(2)}) copy-start(f32[256]{0:T(256)} %copy-done.225) | copy-start | bytes 3076
  499.0 98.7 %reduce-scatter.24.cloned.1.call-start = ((), (), s32[]{:S(2)}) async-start(), calls=%async_computation.20 | async-start | bytes 655360 | tf_op jit(solution)/shard_map/reduce_scatter | solution.py:172
  549.5 3.8 collective-permute-start.3
  572.1 54.0 %reduce-scatter.26.cloned.1.call-start = ((), (), s32[]{:S(2)}) async-start(), calls=%async_computation.21 | async-start | bytes 655360 | tf_op jit(solution)/shard_map/reduce_scatter | solution.py:175
  582.1 175.9 %reduce-scatter.38.cloned.1.call-start = ((), (), s32[]{:S(2)}) async-start(), calls=%async_computation.27 | async-start | bytes 139264
  607.6 174.2 %reduce-scatter.30.cloned.1.call-start = ((), (), s32[]{:S(2)}) async-start(), calls=%async_computation.23 | async-start | bytes 1392640 | tf_op jit(solution)/shard_map/reduce_scatter | solution.py:304
  629.1 234.7 %reduce-scatter.28.cloned.1.call-start = ((), (), s32[]{:S(2)}) async-start(), calls=%async_computation.22 | async-start | bytes 2785280 | tf_op jit(solution)/shard_map/reduce_scatter | solution.py:303
  638.9 306.9 %reduce-scatter.32.cloned.1.call-start = ((), (), s32[]{:S(2)}) async-start(), calls=%async_computation.24 | async-start | bytes 2785280 | tf_op jit(solution)/shard_map/reduce_scatter | solution.py:305
  643.9 417.7 %reduce-scatter.36.cloned.1.call-start = ((), (), s32[]{:S(2)}) async-start(), calls=%async_computation.26 | async-start | bytes 5570560 | tf_op jit(solution)/shard_map/reduce_scatter | solution.py:307
  652.1 633.2 %reduce-scatter.34.cloned.1.call-start = ((), (), s32[]{:S(2)}) async-start(), calls=%async_computation.25 | async-start | bytes 11141120 | tf_op jit(solution)/shard_map/reduce_scatter | solution.py:306
  675.9 78.3 %copy-start.219 = (f32[256]{0:T(256)S(1)}, f32[256]{0:T(256)}, u32[]{:S(2)}) copy-start(f32[256]{0:T(256)} %copy-done.218) | copy-start | bytes 3076
  676.0 78.3 %copy-start.46 = (f32[256,640]{1,0:T(8,128)S(1)}, f32[256,640]{1,0:T(8,128)}, u32[]{:S(2)}) copy-start(f32[256,640]{1,0:T(8,128)} %copy-done.45) | copy-start | bytes 1966084
  677.5 78.1 %copy-start.75 = (f32[1,1,1,256,640]{4,3,2,1,0:T(8,128)S(1)}, f32[1,1,1,256,640]{4,3,2,1,0:T(8,128)}, u32[]{:S(2)}) copy-start(f32[1,1,1,256,640]{4,3,2,1,0:T(8,128)} %get-tuple-element.71) | copy-start | bytes 1966084
  677.5 78.2 %copy-start.76 = (f32[1,1,1,256,640]{4,3,2,1,0:T(8,128)S(1)}, f32[1,1,1,256,640]{4,3,2,1,0:T(8,128)}, u32[]{:S(2)}) copy-start(f32[1,1,1,256,640]{4,3,2,1,0:T(8,128)} %get-tuple-element.91) | copy-start | bytes 1966084
  (232 other events, 805.8 us)
Sparse Core Ops, SparseCore 0:
  10.8 61.8 all-gather.4
  75.4 55.1 all-gather.6
  133.4 85.3 all-gather.8
  221.4 62.5 all-gather.10
  406.2 24.7 reduce-scatter.15
  433.9 24.7 reduce-scatter.17
  490.8 24.7 reduce-scatter.19
  519.3 24.7 reduce-scatter.21
  572.2 25.5 reduce-scatter.23
  601.3 24.7 reduce-scatter.25
  628.3 75.8 reduce-scatter.37
  707.0 74.8 reduce-scatter.29
  784.8 78.9 reduce-scatter.27
  866.6 79.0 reduce-scatter.31
  948.6 113.0 reduce-scatter.35
  1064.5 220.7 reduce-scatter.33
where the time goes:
time: 1300 us; the launch traced here: 1290 us
  waiting for transfers between devices  722 us (56%)
  blocking collectives  263 us (20%)
  matrix products  138 us (11%)
  local copies, waits for them, and re-layouts  84.3 us (6%)
  other arithmetic  59.3 us (5%)
  between operations  18.6 us (1%)
    reduce_scatter x1, waiting for transfers between devices, local(): lax.psum_scatter(summed[3], ('fsdp', 'ctx'), scatter_dimension=1, tiled=T...  224 us
    reduce_scatter x1, waiting for transfers between devices, local(): lax.psum_scatter(summed[4], ('fsdp', 'ctx'), scatter_dimension=1, tiled=T...  116 us
    reduce_scatter x1, waiting for transfers between devices, local(): lax.psum_scatter(summed[0], ('fsdp', 'ctx'), scatter_dimension=1, tiled=T...  82 us
    reduce_scatter x1, waiting for transfers between devices, local(): lax.psum_scatter(summed[2], ('fsdp', 'ctx'), scatter_dimension=1, tiled=T...  81.9 us
    unnamed x1, blocking collectives  76.1 us
    reduce_scatter x3, waiting for transfers between devices, layer_backward_input(): lax.psum_scatter(grad_values_all.astype(jnp.bfloat16), 'ctx', scatter_dim...  63.9 us
    all_gather x1, waiting for transfers between devices, local(): lax.all_gather(w_down, ('fsdp', 'ctx'), axis=1, tiled=True)  58 us
    all_gather x1, blocking collectives, local(): lax.all_gather(w_key_value, ('fsdp', 'ctx'), axis=1, tiled=True)  47.7 us
  transfers between devices with their start and end apart: 20, of which 14 were waited for; matrix products, arithmetic and copies ran while one was open for 11% of the time, Pallas kernels for 0%

commit v1 on v0

v1 whole, which is shorter than its diff:
```python
import math

import jax
import jax.numpy as jnp
from jax import lax
from jax.sharding import PartitionSpec as P

D = 640
FF = 2048
HEADS = 4
HD = 256
WIN = 512
MB = 2
QH = 2 * HD
QW = QH + HD
QP = QW + 128

EPS = 1e-06
BASES = (math.log(10000.0), math.log(1000000.0))
SCALE = 1.0 / math.sqrt(HD)
BF = jnp.bfloat16
F32 = jnp.float32


def bits_of(axis):
    return (lax.axis_size(axis) - 1).bit_length()


def exchange(shard, axis, flip):
    pairs = [(i, i ^ flip) for i in range(lax.axis_size(axis))]
    return lax.ppermute(shard, axis, pairs)


def my_bit(axis, bit):
    return (lax.axis_index(axis) >> bit) & 1


def grid_steps(order):
    steps = []
    fb, cb = bits_of("fsdp"), bits_of("ctx")
    fsteps = [("fsdp", b, fb - 1 - b) for b in range(fb)]
    csteps = [("ctx", b, fb + cb - 1 - b) for b in range(cb)]
    if order == "yx":
        csteps = csteps[::-1]
    return fsteps + csteps


def gather_blocks(block, order):
    nb = bits_of("fsdp") + bits_of("ctx")
    buf = block.reshape((1,) * nb + block.shape)
    for axis, bit, dim in grid_steps(order):
        recv = exchange(buf, axis, 1 << bit)
        low = my_bit(axis, bit) == 0
        buf = jnp.concatenate([jnp.where(low, buf, recv), jnp.where(low, recv, buf)], axis=dim)
    return buf.reshape((-1,) + block.shape)


def scatter_blocks(blocks, order, last=F32):
    nb = bits_of("fsdp") + bits_of("ctx")
    buf = blocks.reshape((2,) * nb + blocks.shape[1:])
    steps = grid_steps(order)[::-1]
    for at, (axis, bit, dim) in enumerate(steps):
        mine = my_bit(axis, bit)
        send = lax.dynamic_index_in_dim(buf, 1 - mine, dim, keepdims=True)
        keep = lax.dynamic_index_in_dim(buf, mine, dim, keepdims=True)
        recv = exchange(send, axis, 1 << bit)
        kind = last if at == len(steps) - 1 else BF
        buf = (keep.astype(F32) + recv.astype(F32)).astype(kind)
    return buf.reshape(blocks.shape[1:])


def rms_norm(values_in, gain):
    return (
        values_in * lax.rsqrt(jnp.mean(values_in * values_in, axis=-1, keepdims=True) + EPS) * gain
    )


def rotate(values_in, cosine, sine_table):
    half_width = values_in.shape[-1] // 2
    lower_half = values_in[..., :half_width]
    upper_half = values_in[..., half_width:]
    return jnp.concatenate(
        [
            lower_half * cosine - upper_half * sine_table,
            upper_half * cosine + lower_half * sine_table,
        ],
        axis=-1,
    )


def rope_tables(places, log_base):
    half_width = HD // 2
    inverse = jnp.exp(-log_base * (jnp.arange(half_width, dtype=F32) * (2.0 / HD)))
    angles = places.astype(F32)[:, None] * inverse[None, :]
    return (jnp.cos(angles), jnp.sin(angles))


def head_prepare(query_product, key_product, query_gain, key_gain, cosine, sine_table):
    token_count = query_product.shape[0]
    queries = rms_norm(query_product.reshape(token_count, HEADS, HD), query_gain)
    keys_normed = rms_norm(key_product, key_gain)
    return (
        rotate(queries, cosine[:, None, :], sine_table[:, None, :]),
        rotate(keys_normed, cosine, sine_table),
    )


def gated(gate, up):
    return jax.nn.gelu(gate, approximate=True) * up


def dot(a, b):
    return jnp.dot(a, b, preferred_element_type=F32)


def dot_t(a, b):
    return jnp.einsum("tc,dc->td", a, b, preferred_element_type=F32)


def t_dot(a, b):
    return jnp.einsum("ta,tb->ab", a, b, preferred_element_type=F32)


def attention_weights(flat_queries, all_keys, places, all_places, window):
    query_places = jnp.repeat(places, HEADS)
    allowed = (all_places[None, :] <= query_places[:, None]) & (
        query_places[:, None] - all_places[None, :] < window
    )
    scores = dot_t(flat_queries, all_keys) * SCALE
    scores = jnp.where(allowed, scores, -1e30)
    maximum = jnp.max(scores, axis=-1, keepdims=True)
    weights = jnp.exp(scores - maximum)
    return weights / jnp.sum(weights, axis=-1, keepdims=True)


def pick(first, own, other):
    return jnp.where(first, own, other), jnp.where(first, other, own)


def key_exchange(keys_values):
    count = lax.axis_size("ctx")
    return [keys_values] + [exchange(keys_values, "ctx", j) for j in range(1, count)]


def key_return(blocks):
    count = lax.axis_size("ctx")
    total = blocks[0]
    for j in range(1, count):
        total = total + exchange(blocks[j].astype(BF), "ctx", j).astype(F32)
    return total


def layer_forward(full, x, places, all_places, window, cosine, sine_table, first):
    q_own, q_oth, g_own, g_oth, w_out, w_down, gains, heads = full
    tokens = x.shape[0]
    normed = rms_norm(x, gains[0]).astype(BF)
    lo, hi = pick(first, dot(normed, q_own), dot(normed, q_oth))
    query_product = jnp.concatenate([lo[:, :QH], hi[:, :QH]], axis=1)
    key_product = lo[:, QH:]
    queries, keys_rot = head_prepare(
        query_product, key_product, heads[0], heads[1], cosine, sine_table
    )
    flat_queries = queries.astype(BF).reshape(tokens * HEADS, HD)
    keys_values = jnp.concatenate([keys_rot, hi[:, QH:]], axis=1).astype(BF)
    all_kv = jnp.concatenate(key_exchange(keys_values), axis=0)
    all_keys, all_values = all_kv[:, :HD], all_kv[:, HD:]
    prob_low = attention_weights(flat_queries, all_keys, places, all_places, window).astype(BF)
    mixed = dot(prob_low, all_values).reshape(tokens, HEADS * HD).astype(BF)
    branch = dot(mixed, w_out)
    middle = x + rms_norm(branch, gains[1])
    normed_two = rms_norm(middle, gains[2]).astype(BF)
    gate, up = pick(first, dot(normed_two, g_own), dot(normed_two, g_oth))
    hidden = gated(gate, up).astype(BF)
    down_out = dot(hidden, w_down)
    result = middle + rms_norm(down_out, gains[3])
    kept = dict(
        normed=normed, query_product=query_product, key_product=key_product,
        flat_queries=flat_queries, all_keys=all_keys, all_values=all_values, mixed=mixed,
        branch=branch, middle=middle, normed_two=normed_two, gate=gate, up=up, hidden=hidden,
        down_out=down_out, x=x,
    )
    return result, kept


def halves(grad, count):
    return grad.reshape(count, 2, -1, grad.shape[-1])


def layer_backward(full, kept, grad_result, places, all_places, window, cosine, sine_table, first):
    q_own, q_oth, g_own, g_oth, w_out, w_down, gains, heads = full
    x = kept["x"]
    tokens = x.shape[0]
    _, back_last = jax.vjp(rms_norm, kept["down_out"], gains[3])
    grad_down, gain_three = back_last(grad_result)
    grad_down_low = grad_down.astype(BF)
    grad_hidden = dot_t(grad_down_low, w_down)
    _, back_gated = jax.vjp(gated, kept["gate"], kept["up"])
    grad_gate, grad_up = back_gated(grad_hidden)
    gu_own, gu_oth = pick(first, grad_gate.astype(BF), grad_up.astype(BF))
    grad_normed_two = dot_t(gu_own, g_own) + dot_t(gu_oth, g_oth)
    _, back_norm_two = jax.vjp(rms_norm, kept["middle"], gains[2])
    grad_middle_part, gain_two = back_norm_two(grad_normed_two)
    grad_middle = grad_result + grad_middle_part
    _, back_norm_one = jax.vjp(rms_norm, kept["branch"], gains[1])
    grad_branch, gain_one = back_norm_one(grad_middle)
    grad_branch_low = grad_branch.astype(BF)
    grad_mixed = dot_t(grad_branch_low, w_out).astype(BF).reshape(tokens * HEADS, HD)
    wg_g = (
        t_dot(kept["normed_two"], gu_own).astype(BF),
        t_dot(kept["normed_two"], gu_oth).astype(BF),
    )
    wg_out = t_dot(kept["mixed"], grad_branch_low).astype(BF)
    wg_down = t_dot(kept["hidden"], grad_down_low).astype(BF)
    flat_queries, all_keys, all_values = kept["flat_queries"], kept["all_keys"], kept["all_values"]
    probabilities = attention_weights(flat_queries, all_keys, places, all_places, window)
    prob_low = probabilities.astype(BF)
    grad_probs = dot_t(grad_mixed, all_values)
    inner_sum = jnp.sum(probabilities * grad_probs, axis=-1, keepdims=True)
    grad_scores = (probabilities * (grad_probs - inner_sum)).astype(BF)
    grad_keys_all = t_dot(grad_scores, flat_queries) * SCALE
    grad_values_all = t_dot(prob_low, grad_mixed)
    blocks = jnp.concatenate([grad_keys_all, grad_values_all], axis=1)
    grad_kv = key_return(jnp.split(blocks, lax.axis_size("ctx"), axis=0))
    grad_queries = dot(grad_scores, all_keys) * SCALE

    def prepare(query_in, key_in, query_gain, key_gain):
        return head_prepare(query_in, key_in, query_gain, key_gain, cosine, sine_table)

    _, back_heads = jax.vjp(
        prepare, kept["query_product"], kept["key_product"], heads[0], heads[1]
    )
    grad_qp, grad_kp, query_gain, key_gain = back_heads(
        (grad_queries.reshape(tokens, HEADS, HD), grad_kv[:, :HD])
    )
    lo = jnp.concatenate([grad_qp[:, :QH], grad_kp], axis=1).astype(BF)
    hi = jnp.concatenate([grad_qp[:, QH:], grad_kv[:, HD:]], axis=1).astype(BF)
    q_grad_own, q_grad_oth = pick(first, lo, hi)
    grad_normed = dot_t(q_grad_own, q_own) + dot_t(q_grad_oth, q_oth)
    _, back_norm_zero = jax.vjp(rms_norm, x, gains[0])
    grad_part, gain_zero = back_norm_zero(grad_normed)
    grad_x = grad_middle + grad_part
    wg_q = (
        t_dot(kept["normed"], q_grad_own).astype(BF),
        t_dot(kept["normed"], q_grad_oth).astype(BF),
    )
    gain_grads = (
        jnp.stack([gain_zero, gain_one, gain_two, gain_three]),
        jnp.stack([query_gain, key_gain]),
    )
    return grad_x, wg_q, wg_g, wg_out, wg_down, gain_grads


def local(
    boundary, positions, w_query, w_key_value, w_out, w_gate_up, w_down, norm_gains, head_gains
):
    section = lax.axis_index("section")
    first = section == 0
    ctx_index = lax.axis_index("ctx")
    tokens = boundary.shape[3]
    seq_length = positions.shape[-1]
    nr = w_query.shape[1]
    hr = head_gains.shape[2]
    ro, rd = w_out.shape[1], w_down.shape[1]
    blocks = lax.axis_size("fsdp") * lax.axis_size("ctx")

    moved = exchange(lax.dynamic_index_in_dim(boundary[0, :, 0], 1 - section, 0, False), "section", 1)
    kept_in = lax.dynamic_index_in_dim(boundary[0, :, 0], section, 0, False)
    x0, cotangent = pick(first, kept_in, moved)
    x0, cotangent = x0.astype(F32), cotangent.astype(F32)
    seq_places = lax.dynamic_index_in_dim(positions[:, 0], section, 0, False)
    near = [
        lax.dynamic_slice_in_dim(seq_places, (ctx_index ^ j) * tokens, tokens)
        for j in range(lax.axis_size("ctx"))
    ]
    places, all_places = near[0], jnp.concatenate(near)

    gain_cols = jnp.concatenate(
        [
            norm_gains[0].T,
            jnp.pad(head_gains[0].T, ((0, nr - hr), (0, 0))),
            jnp.zeros((nr, 128 - 6), BF),
        ],
        axis=1,
    )
    cols = [
        jnp.concatenate(
            [
                w_query[0, :, h * QH : (h + 1) * QH],
                w_key_value[0, :, h * HD : (h + 1) * HD],
                gain_cols,
                w_gate_up[0, :, h * FF : (h + 1) * FF],
            ],
            axis=1,
        )
        for h in range(2)
    ]
    rows = [
        jnp.concatenate(
            [
                w_out[0, h * ro // 2 : (h + 1) * ro // 2],
                w_down[0, h * rd // 2 : (h + 1) * rd // 2],
            ],
            axis=0,
        )
        for h in range(2)
    ]
    col_keep, col_send = pick(first, cols[0], cols[1])
    row_keep, row_send = pick(first, rows[0], rows[1])
    col_recv = exchange(col_send, "section", 1)
    row_recv = exchange(row_send, "section", 1)
    layer_cols = pick(first, col_keep, col_recv)
    layer_rows = pick(first, row_keep, row_recv)

    def swap(own):
        return own, exchange(own, "section", 1)

    def assemble(q_pair, g_pair, b_pair):
        q_own, q_oth = [v.reshape(blocks * nr, -1) for v in q_pair]
        g_own, g_oth = [v.reshape(blocks * nr, -1) for v in g_pair]
        b_own, b_oth = b_pair
        b_lo, b_hi = pick(first, b_own, b_oth)
        full_out = jnp.concatenate([b_lo[:, : ro // 2], b_hi[:, : ro // 2]], axis=1)
        full_down = jnp.concatenate([b_lo[:, ro // 2 :], b_hi[:, ro // 2 :]], axis=1)
        gain_part = q_own[:, QW:].astype(F32)
        gains = gain_part[:, :4].T
        heads = gain_part[:, 4:6].reshape(blocks, nr, 2)[:, :hr].reshape(blocks * hr, 2).T
        return (
            q_own[:, :QW], q_oth[:, :QW], g_own, g_oth,
            full_out.reshape(-1, D), full_down.reshape(-1, D), gains, heads,
        )

    full0 = assemble(
        swap(gather_blocks(layer_cols[0][:, :QP], "yx")),
        swap(gather_blocks(layer_cols[0][:, QP:], "xy")),
        swap(gather_blocks(layer_rows[0], "yx")),
    )
    col_pair = swap(gather_blocks(layer_cols[1], "xy"))
    full1 = assemble(
        [v[..., :QP] for v in col_pair],
        [v[..., QP:] for v in col_pair],
        swap(gather_blocks(layer_rows[1], "yx")),
    )

    tables = [rope_tables(places, base) for base in BASES]
    windows = (WIN, seq_length)

    y0, kept0 = layer_forward(full0, x0, places, all_places, windows[0], *tables[0], first)
    y1, kept1 = layer_forward(
        full1, y0.astype(BF).astype(F32), places, all_places, windows[1], *tables[1], first
    )

    def reduce_g(wg_g):
        return wg_g[0].astype(F32) + exchange(wg_g[1], "section", 1).astype(F32)

    def reduce_b(wg_out, wg_down):
        out_half, down_half = halves(wg_out, blocks), halves(wg_down, blocks)

        def part(index):
            return jnp.concatenate(
                [
                    lax.dynamic_index_in_dim(out_half, index, 1, False),
                    lax.dynamic_index_in_dim(down_half, index, 1, False),
                ],
                axis=1,
            )

        recv = exchange(part(1 - section), "section", 1)
        summed = (part(section).astype(F32) + recv.astype(F32)).astype(BF)
        return scatter_blocks(summed, "yx")

    def gain_columns(gain_grads):
        norm_part = gain_grads[0].T
        head_part = gain_grads[1].T.reshape(blocks, hr, 2)
        head_part = jnp.pad(head_part, ((0, 0), (0, nr - hr), (0, 0))).reshape(blocks * nr, 2)
        return jnp.concatenate(
            [norm_part, head_part, jnp.zeros((blocks * nr, 128 - 6), F32)], axis=1
        ).astype(BF)

    def reduce_q(wg_q, gain_grads):
        cols = gain_columns(gain_grads)
        own = jnp.concatenate([wg_q[0], cols], axis=1)
        oth = jnp.concatenate([wg_q[1], cols], axis=1)
        return own.astype(F32) + exchange(oth, "section", 1).astype(F32)

    def in_blocks(v):
        return v.astype(BF).reshape(blocks, nr, -1)

    grad1, wg_q, wg_g, wg_out, wg_down, gain_grads = layer_backward(
        full1, kept1, cotangent, places, all_places, windows[1], *tables[1], first
    )
    red_b1 = reduce_b(wg_out, wg_down)
    col_sum = jnp.concatenate([reduce_q(wg_q, gain_grads), reduce_g(wg_g)], axis=1)
    red_c1 = scatter_blocks(in_blocks(col_sum), "xy")
    grad0, wg_q, wg_g, wg_out, wg_down, gain_grads = layer_backward(
        full0, kept0, grad1.astype(BF).astype(F32), places, all_places, windows[0], *tables[0], first
    )
    red_b0 = reduce_b(wg_out, wg_down)
    red_g0 = scatter_blocks(in_blocks(reduce_g(wg_g)), "xy")
    red_q0 = scatter_blocks(in_blocks(reduce_q(wg_q, gain_grads)), "yx")
    red_c0 = jnp.concatenate([red_q0, red_g0], axis=1)

    out_moved = exchange(jnp.where(first, y1, grad0), "section", 1)
    c_keep, c_send = pick(first, red_c0, red_c1)
    b_keep, b_send = pick(first, red_b0, red_b1)
    c_lo, c_hi = pick(first, c_keep, exchange(c_send, "section", 1))
    b_lo, b_hi = pick(first, b_keep, exchange(b_send, "section", 1))
    boundary_out = jnp.where(
        first, jnp.stack([grad0, out_moved]), jnp.stack([out_moved, y1])
    )[None, :, None]
    return (
        boundary_out,
        jnp.concatenate([c_lo[:, :QH], c_hi[:, :QH]], axis=1)[None],
        jnp.concatenate([c_lo[:, QH:QW], c_hi[:, QH:QW]], axis=1)[None],
        jnp.concatenate([b_lo[: ro // 2], b_hi[: ro // 2]], axis=0)[None],
        jnp.concatenate([c_lo[:, QP:], c_hi[:, QP:]], axis=1)[None],
        jnp.concatenate([b_lo[ro // 2 :], b_hi[ro // 2 :]], axis=0)[None],
        c_lo[:, QW : QW + 4].T[None],
        c_lo[:hr, QW + 4 : QW + 6].T[None],
    )


def solution(mesh):
    in_specs = (
        P("section", None, "fsdp", "ctx", None),
        P(None, "fsdp", None),
        P("section", ("fsdp", "ctx"), None),
        P("section", ("fsdp", "ctx"), None),
        P("section", ("fsdp", "ctx"), None),
        P("section", ("fsdp", "ctx"), None),
        P("section", ("fsdp", "ctx"), None),
        P("section", None, ("fsdp", "ctx")),
        P("section", None, ("fsdp", "ctx")),
    )
    out_specs = (
        P("section", None, "fsdp", "ctx", None),
        P("section", ("fsdp", "ctx"), None),
        P("section", ("fsdp", "ctx"), None),
        P("section", ("fsdp", "ctx"), None),
        P("section", ("fsdp", "ctx"), None),
        P("section", ("fsdp", "ctx"), None),
        P("section", None, ("fsdp", "ctx")),
        P("section", None, ("fsdp", "ctx")),
    )
    return jax.shard_map(local, mesh=mesh, in_specs=in_specs, out_specs=out_specs, check_vma=False)
```

time: 1300 us -> 617 us (0.47)
  waiting for transfers between devices: 722 us -> 277 us
  blocking collectives: 263 us -> 0 us
  starting transfers between devices: 7.52 us -> 70.7 us
  matrix products: 138 us -> 84.6 us
  other arithmetic: 59.3 us -> 92.6 us
  between operations: 18.6 us -> 4.94 us
    reduce_scatter x11 -> x0, waiting for transfers between devices: 625 us -> none  [the longest x1 224 us: local(): lax.psum_scatter(summed[3], ('fsdp', 'ctx'), scatter_dimension=1, tiled=T...]
    ppermute x4 -> x69, waiting for transfers between devices: 2.27 us -> 277 us  [exchange(): return lax.ppermute(shard, axis, pairs)]
    all_gather x9 -> x0, blocking collectives: 187 us -> none  [the longest x1 47.7 us: local(): lax.all_gather(w_key_value, ('fsdp', 'ctx'), axis=1, tiled=True)]
    all_gather x4 -> x0, waiting for transfers between devices: 92 us -> none  [the longest x1 58 us: local(): lax.all_gather(w_down, ('fsdp', 'ctx'), axis=1, tiled=True)]
    unnamed x1 -> x0, blocking collectives: 76.1 us -> none
    ppermute x4 -> x69, starting transfers between devices: 6 us -> 70.7 us  [exchange(): return lax.ppermute(shard, axis, pairs)]
    dot_general x63 -> x48, matrix products: 138 us -> 84.6 us  [the longest x16 29.6 us: t_dot(): return jnp.einsum('ta,tb->ab', a, b, preferred_element_type=F32)]
    concatenate x3 -> x35, other arithmetic: 0.05 us -> 28.4 us  [the longest x20 15.6 us: gather_blocks(): jnp.concatenate([jnp.where(low, buf, recv), jnp.where(low, recv, buf)], a...]
  transfers between devices with their start and end apart: 20 -> 69, of which waited for: 14 -> 27; matrix products, arithmetic and copies ran while one was open for 11% -> 31% of each run, Pallas kernels for 0% -> 0%
where the time goes in v1:
time: 617 us; the launch traced here: 606 us
  waiting for transfers between devices  277 us (45%)
  other arithmetic  92.6 us (15%)
  matrix products  84.6 us (14%)
  local copies, waits for them, and re-layouts  76.7 us (12%)
  starting transfers between devices  70.7 us (11%)
    ppermute x69, waiting for transfers between devices, exchange(): return lax.ppermute(shard, axis, pairs)  277 us
    ppermute x69, starting transfers between devices, exchange(): return lax.ppermute(shard, axis, pairs)  70.7 us
    dot_general x16, matrix products, t_dot(): return jnp.einsum('ta,tb->ab', a, b, preferred_element_type=F32)  29.6 us
    dot_general x16, matrix products, dot(): return jnp.dot(a, b, preferred_element_type=F32)  28 us
    dot_general x16, matrix products, dot_t(): return jnp.einsum('tc,dc->td', a, b, preferred_element_type=F32)  27 us
    unnamed x493, local copies, waits for them, and re-layouts  21 us
    concatenate x20, other arithmetic, gather_blocks(): jnp.concatenate([jnp.where(low, buf, recv), jnp.where(low, recv, buf)], a...  15.6 us
  transfers between devices with their start and end apart: 69, of which 27 were waited for; matrix products, arithmetic and copies ran while one was open for 31% of the time, Pallas kernels for 0%

profile of v1, /device:TPU:0, one launch (start us, length us, event | category | flops | bytes accessed | tf_op | source)
XLA Modules:
  0.0 606.2 jit_solution(12876405557218551722)
XLA Ops:
  10.3 2.7 collective-permute-start.29
  19.8 3.0 collective-permute-start.30
  22.8 8.8 %collective-permute-done.6 = bf16[1,1,1,1,40,896]{5,4,3,2,1,0:T(8,128)(2,1)S(1)} collective-permute-done((bf16[1,1,1,1,40,896]{5,4,3,2,1,0:T(8,128)(2,1)S(1)}, bf16[1,1,1,1,40,896]{5,4,3,2,1,0:T(8,128)(2,1)S(1)}, u32[]{:S(2)}, u32[]{:S(2)}) %collective-permute-start.6) | collective-permute-done | bytes 71712 | tf_op jit(solution)/shard_map/ppermute | solution.py:31
  37.2 23.7 %collective-permute-done.7 = bf16[1,2,1,1,40,896]{5,4,3,2,1,0:T(8,128)(2,1)S(1)} collective-permute-done((bf16[1,2,1,1,40,896]{5,4,3,2,1,0:T(8,128)(2,1)S(1)}, bf16[1,2,1,1,40,896]{5,4,3,2,1,0:T(8,128)(2,1)S(1)}, u32[]{:S(2)}, u32[]{:S(2)}) %collective-permute-start.7) | collective-permute-done | bytes 143392 | tf_op jit(solution)/shard_map/ppermute | solution.py:31
  65.3 12.8 %collective-permute-done.21 = bf16[1,2,1,1,40,2048]{5,4,3,2,1,0:T(8,128)(2,1)S(1)} collective-permute-done((bf16[1,2,1,1,40,2048]{5,4,3,2,1,0:T(8,128)(2,1)S(1)}, bf16[1,2,1,1,40,2048]{5,4,3,2,1,0:T(8,128)(2,1)S(1)}, u32[]{:S(2)}, u32[]{:S(2)}) %collective-permute-start.21) | collective-permute-done | bytes 327712 | tf_op jit(solution)/shard_map/ppermute | solution.py:31
  81.2 6.8 %collective-permute-done.3 = bf16[1,2,1,1,40,2944]{5,4,3,2,1,0:T(8,128)(2,1)S(1)} collective-permute-done((bf16[1,2,1,1,40,2944]{5,4,3,2,1,0:T(8,128)(2,1)S(1)}, bf16[1,2,1,1,40,2944]{5,4,3,2,1,0:T(8,128)(2,1)S(1)}, u32[]{:S(2)}, u32[]{:S(2)}) %collective-permute-start.3) | collective-permute-done | bytes 471072 | tf_op jit(solution)/shard_map/ppermute | solution.py:31
  95.4 13.7 %collective-permute-done.9 = bf16[2,2,2,1,40,896]{5,4,3,2,1,0:T(8,128)(2,1)S(1)} collective-permute-done((bf16[2,2,2,1,40,896]{5,4,3,2,1,0:T(8,128)(2,1)S(1)}, bf16[2,2,2,1,40,896]{5,4,3,2,1,0:T(8,128)(2,1)S(1)}, u32[]{:S(2)}, u32[]{:S(2)}) %collective-permute-start.9) | collective-permute-done | bytes 573472 | tf_op jit(solution)/shard_map/ppermute | solution.py:31
  116.9 12.5 %collective-permute-done.4 = bf16[2,2,1,1,40,2944]{5,4,3,2,1,0:T(8,128)(2,1)} collective-permute-done((bf16[2,2,1,1,40,2944]{5,4,3,2,1,0:T(8,128)(2,1)}, bf16[2,2,1,1,40,2944]{5,4,3,2,1,0:T(8,128)(2,1)}, u32[]{:S(2)}, u32[]{:S(2)}) %collective-permute-start.4) | collective-permute-done | bytes 942112 | tf_op jit(solution)/shard_map/ppermute | solution.py:31
  133.8 16.7 %collective-permute-done.32 = bf16[2,2,2,1,96,640]{5,4,3,2,1,0:T(8,128)(2,1)} collective-permute-done((bf16[2,2,2,1,96,640]{5,4,3,2,1,0:T(8,128)(2,1)}, bf16[2,2,2,1,96,640]{5,4,3,2,1,0:T(8,128)(2,1)}, u32[]{:S(2)}, u32[]{:S(2)}) %collective-permute-start.32) | collective-permute-done | bytes 983072 | tf_op jit(solution)/shard_map/ppermute | solution.py:31
  153.4 17.1 %collective-permute-done.18 = bf16[2,2,2,1,96,640]{5,4,3,2,1,0:T(8,128)(2,1)} collective-permute-done((bf16[2,2,2,1,96,640]{5,4,3,2,1,0:T(8,128)(2,1)}, bf16[2,2,2,1,96,640]{5,4,3,2,1,0:T(8,128)(2,1)}, u32[]{:S(2)}, u32[]{:S(2)}) %collective-permute-start.18) | collective-permute-done | bytes 983072 | tf_op jit(solution)/shard_map/ppermute | solution.py:31
  192.0 6.5 %collective-permute-done.12 = bf16[256,512]{1,0:T(8,128)(2,1)} collective-permute-done((bf16[256,512]{1,0:T(8,128)(2,1)}, bf16[256,512]{1,0:T(8,128)(2,1)}, u32[]{:S(2)}, u32[]{:S(2)}) %collective-permute-start.12) | collective-permute-done | bytes 262176 | tf_op jit(solution)/shard_map/ppermute | solution.py:31
  213.0 4.0 slice.424
  218.9 2.5 broadcast_select_fusion.1
  223.6 2.5 broadcast_select_fusion.3
  231.1 2.9 fusion.165
  234.1 6.0 multiply_convert_fusion.5
  260.3 3.7 slice.425
  282.4 2.6 multiply_convert_fusion.3
  294.2 3.3 fusion.28
  302.9 2.6 convolution_convert_fusion
  305.5 2.5 convolution_convert_fusion.2
  312.4 2.5 reshape.648
  318.1 2.6 multiply_reduce_fusion.2
  339.8 2.6 convolution_convert_fusion.1
  346.3 3.2 fusion.94
  349.6 3.6 multiply_reduce_fusion.10
  360.2 3.3 fusion.31
  388.4 2.7 convolution_convert_fusion.8
  396.9 3.2 fusion.59
  408.3 5.0 collective-permute-done.51
  418.4 11.9 %collective-permute-done.42 = bf16[2,2,2,1,40,896]{5,4,3,2,1,0:T(8,128)(2,1)S(1)} collective-permute-done((bf16[2,2,2,1,40,896]{5,4,3,2,1,0:T(8,128)(2,1)S(1)}, bf16[2,2,2,1,40,896]{5,4,3,2,1,0:T(8,128)(2,1)S(1)}, u32[]{:S(2)}, u32[]{:S(2)}) %collective-permute-start.42) | collective-permute-done | bytes 573472 | tf_op jit(solution)/shard_map/ppermute | solution.py:31
  434.4 4.0 collective-permute-done.43
  438.6 2.6 add_convert_fusion
  441.2 3.7 collective-permute-done.44
  447.1 2.6 collective-permute-done.45
  453.3 18.6 %collective-permute-done.59 = bf16[2,2,2,1,96,640]{5,4,3,2,1,0:T(8,128)(2,1)S(1)} collective-permute-done((bf16[2,2,2,1,96,640]{5,4,3,2,1,0:T(8,128)(2,1)S(1)}, bf16[2,2,2,1,96,640]{5,4,3,2,1,0:T(8,128)(2,1)S(1)}, u32[]{:S(2)}, u32[]{:S(2)}) %collective-permute-start.59) | collective-permute-done | bytes 983072 | tf_op jit(solution)/shard_map/ppermute | solution.py:31
  474.5 25.5 %collective-permute-done.65 = bf16[2,2,1,1,96,640]{5,4,3,2,1,0:T(8,128)(2,1)S(1)} collective-permute-done((bf16[2,2,1,1,96,640]{5,4,3,2,1,0:T(8,128)(2,1)S(1)}, bf16[2,2,1,1,96,640]{5,4,3,2,1,0:T(8,128)(2,1)S(1)}, u32[]{:S(2)}, u32[]{:S(2)}) %collective-permute-start.65) | collective-permute-done | bytes 491552 | tf_op jit(solution)/shard_map/ppermute | solution.py:31
  500.2 3.1 collective-permute-start.66
  503.3 7.3 %collective-permute-done.60 = bf16[2,2,1,1,96,640]{5,4,3,2,1,0:T(8,128)(2,1)S(1)} collective-permute-done((bf16[2,2,1,1,96,640]{5,4,3,2,1,0:T(8,128)(2,1)S(1)}, bf16[2,2,1,1,96,640]{5,4,3,2,1,0:T(8,128)(2,1)S(1)}, u32[]{:S(2)}, u32[]{:S(2)}) %collective-permute-start.60) | collective-permute-done | bytes 491552 | tf_op jit(solution)/shard_map/ppermute | solution.py:31
  510.8 3.1 collective-permute-start.61
  514.1 6.7 %collective-permute-done.61 = bf16[1,2,1,1,96,640]{5,4,3,2,1,0:T(8,128)(2,1)S(1)} collective-permute-done((bf16[1,2,1,1,96,640]{5,4,3,2,1,0:T(8,128)(2,1)S(1)}, bf16[1,2,1,1,96,640]{5,4,3,2,1,0:T(8,128)(2,1)S(1)}, u32[]{:S(2)}, u32[]{:S(2)}) %collective-permute-start.61) | collective-permute-done | bytes 245792 | tf_op jit(solution)/shard_map/ppermute | solution.py:31
  521.0 15.6 %collective-permute-done.47 = bf16[2,2,1,2,40,2048]{5,4,3,2,1,0:T(8,128)(2,1)S(1)} collective-permute-done((bf16[2,2,1,2,40,2048]{5,4,3,2,1,0:T(8,128)(2,1)S(1)}, bf16[2,2,1,2,40,2048]{5,4,3,2,1,0:T(8,128)(2,1)S(1)}, u32[]{:S(2)}, u32[]{:S(2)}) %collective-permute-start.47) | collective-permute-done | bytes 1310752 | tf_op jit(solution)/shard_map/ppermute | solution.py:31
  539.9 14.9 %collective-permute-done.48 = bf16[2,2,1,1,40,2048]{5,4,3,2,1,0:T(8,128)(2,1)S(1)} collective-permute-done((bf16[2,2,1,1,40,2048]{5,4,3,2,1,0:T(8,128)(2,1)S(1)}, bf16[2,2,1,1,40,2048]{5,4,3,2,1,0:T(8,128)(2,1)S(1)}, u32[]{:S(2)}, u32[]{:S(2)}) %collective-permute-start.48) | collective-permute-done | bytes 655392 | tf_op jit(solution)/shard_map/ppermute | solution.py:31
  555.0 2.8 collective-permute-start.49
  557.9 14.1 %collective-permute-done.54 = bf16[2,2,1,1,40,2944]{5,4,3,2,1,0:T(8,128)(2,1)S(1)} collective-permute-done((bf16[2,2,1,1,40,2944]{5,4,3,2,1,0:T(8,128)(2,1)S(1)}, bf16[2,2,1,1,40,2944]{5,4,3,2,1,0:T(8,128)(2,1)S(1)}, u32[]{:S(2)}, u32[]{:S(2)}) %collective-permute-start.54) | collective-permute-done | bytes 942112 | tf_op jit(solution)/shard_map/ppermute | solution.py:31
  572.2 2.5 collective-permute-start.55
  575.5 17.5 %collective-permute-done.55 = bf16[1,2,1,1,40,2944]{5,4,3,2,1,0:T(8,128)(2,1)S(1)} collective-permute-done((bf16[1,2,1,1,40,2944]{5,4,3,2,1,0:T(8,128)(2,1)S(1)}, bf16[1,2,1,1,40,2944]{5,4,3,2,1,0:T(8,128)(2,1)S(1)}, u32[]{:S(2)}, u32[]{:S(2)}) %collective-permute-start.55) | collective-permute-done | bytes 471072 | tf_op jit(solution)/shard_map/ppermute | solution.py:31
  593.3 6.9 %collective-permute-done.56 = bf16[1,1,1,1,40,2944]{5,4,3,2,1,0:T(8,128)(2,1)S(1)} collective-permute-done((bf16[1,1,1,1,40,2944]{5,4,3,2,1,0:T(8,128)(2,1)S(1)}, bf16[1,1,1,1,40,2944]{5,4,3,2,1,0:T(8,128)(2,1)S(1)}, u32[]{:S(2)}, u32[]{:S(2)}) %collective-permute-start.56) | collective-permute-done | bytes 235552 | tf_op jit(solution)/shard_map/ppermute | solution.py:31
  (924 shorter events, 252.5 us)
Async XLA Ops:
  7.5 26.3 %collective-permute-start = (bf16[256,640]{1,0:T(8,128)(2,1)S(1)}, bf16[256,640]{1,0:T(8,128)(2,1)S(1)}, u32[]{:S(2)}, u32[]{:S(2)}) collective-permute-start(bf16[256,640]{1,0:T(8,128)(2,1)S(1)} %dynamic-slice_bitcast_fusion.8), channel_id=1, source_target_pairs={{0,16},{16,0},{1,17},{17,1},{2,18},{18,2},{3,19},{19,3},{4,20},{20... | collective-permute-start | bytes 983048 | tf_op jit(solution)/shard_map/ppermute | solution.py:31
  13.2 49.4 %collective-permute-start.2 = (bf16[1,1,1,1,40,2944]{5,4,3,2,1,0:T(8,128)(2,1)S(1)}, bf16[1,1,1,1,40,2944]{5,4,3,2,1,0:T(8,128)(2,1)S(1)}, u32[]{:S(2)}, u32[]{:S(2)}) collective-permute-start(bf16[1,1,1,1,40,2944]{5,4,3,2,1,0:T(8,128)(2,1)S(1)} %get-tuple-element.150), channel_id=1, source_target_pairs={{0,4},{4,0},{8,12},{12,8},{1,5},{5,1},{9,13},{13,9},{2,6},{6,2},{1... | collective-permute-start | bytes 706568 | tf_op jit(solution)/shard_map/ppermute | solution.py:31
  17.2 17.8 %collective-permute-start.20 = (bf16[1,1,1,1,40,2048]{5,4,3,2,1,0:T(8,128)(2,1)S(1)}, bf16[1,1,1,1,40,2048]{5,4,3,2,1,0:T(8,128)(2,1)S(1)}, u32[]{:S(2)}, u32[]{:S(2)}) collective-permute-start(bf16[1,1,1,1,40,2048]{5,4,3,2,1,0:T(8,128)(2,1)S(1)} %slice_bitcast_fusion.2), channel_id=1, source_target_pairs={{0,4},{4,0},{8,12},{12,8},{1,5},{5,1},{9,13},{13,9},{2,6},{6,2},{1... | collective-permute-start | bytes 491528 | tf_op jit(solution)/shard_map/ppermute | solution.py:31
  19.8 43.0 %collective-permute-start.30 = (bf16[1,2,1,1,96,640]{5,4,3,2,1,0:T(8,128)(2,1)S(1)}, bf16[1,2,1,1,96,640]{5,4,3,2,1,0:T(8,128)(2,1)S(1)}, u32[]{:S(2)}, u32[]{:S(2)}) collective-permute-start(bf16[1,2,1,1,96,640]{5,4,3,2,1,0:T(8,128)(2,1)S(1)} %pad_maximum_fusion.51), channel_id=1, source_target_pairs={{0,8},{4,12},{8,0},{12,4},{1,9},{5,13},{9,1},{13,5},{2,10},{6,14},... | collective-permute-start | bytes 737288 | tf_op jit(solution)/shard_map/ppermute | solution.py:31
  31.7 31.9 %collective-permute-start.16 = (bf16[1,2,1,1,96,640]{5,4,3,2,1,0:T(8,128)(2,1)S(1)}, bf16[1,2,1,1,96,640]{5,4,3,2,1,0:T(8,128)(2,1)S(1)}, u32[]{:S(2)}, u32[]{:S(2)}) collective-permute-start(bf16[1,2,1,1,96,640]{5,4,3,2,1,0:T(8,128)(2,1)S(1)} %pad_maximum_fusion.50), channel_id=1, source_target_pairs={{0,8},{4,12},{8,0},{12,4},{1,9},{5,13},{9,1},{13,5},{2,10},{6,14},... | collective-permute-start | bytes 737288 | tf_op jit(solution)/shard_map/ppermute | solution.py:31
  33.8 27.1 %collective-permute-start.7 = (bf16[1,2,1,1,40,896]{5,4,3,2,1,0:T(8,128)(2,1)S(1)}, bf16[1,2,1,1,40,896]{5,4,3,2,1,0:T(8,128)(2,1)S(1)}, u32[]{:S(2)}, u32[]{:S(2)}) collective-permute-start(bf16[1,2,1,1,40,896]{5,4,3,2,1,0:T(8,128)(2,1)S(1)} %pad_maximum_fusion.52), channel_id=1, source_target_pairs={{0,8},{4,12},{8,0},{12,4},{1,9},{5,13},{9,1},{13,5},{2,10},{6,14},... | collective-permute-start | bytes 430088 | tf_op jit(solution)/shard_map/ppermute | solution.py:31
  35.0 43.0 %collective-permute-start.21 = (bf16[1,2,1,1,40,2048]{5,4,3,2,1,0:T(8,128)(2,1)S(1)}, bf16[1,2,1,1,40,2048]{5,4,3,2,1,0:T(8,128)(2,1)S(1)}, u32[]{:S(2)}, u32[]{:S(2)}) collective-permute-start(bf16[1,2,1,1,40,2048]{5,4,3,2,1,0:T(8,128)(2,1)S(1)} %pad_maximum_fusion.46), channel_id=1, source_target_pairs={{0,8},{4,12},{8,0},{12,4},{1,9},{5,13},{9,1},{13,5},{2,10},{6,14},... | collective-permute-start | bytes 983048 | tf_op jit(solution)/shard_map/ppermute | solution.py:31
  61.0 19.5 %collective-permute-start.8 = (bf16[2,2,1,1,40,896]{5,4,3,2,1,0:T(8,128)(2,1)S(1)}, bf16[2,2,1,1,40,896]{5,4,3,2,1,0:T(8,128)(2,1)S(1)}, u32[]{:S(2)}, u32[]{:S(2)}) collective-permute-start(bf16[2,2,1,1,40,896]{5,4,3,2,1,0:T(8,128)(2,1)S(1)} %pad_maximum_fusion.47), channel_id=1, source_target_pairs={{0,2},{1,3},{2,0},{3,1},{4,6},{5,7},{6,4},{7,5},{8,10},{9,11},{10,... | collective-permute-start | bytes 860168 | tf_op jit(solution)/shard_map/ppermute | solution.py:31
  62.7 25.3 %collective-permute-start.3 = (bf16[1,2,1,1,40,2944]{5,4,3,2,1,0:T(8,128)(2,1)S(1)}, bf16[1,2,1,1,40,2944]{5,4,3,2,1,0:T(8,128)(2,1)S(1)}, u32[]{:S(2)}, u32[]{:S(2)}) collective-permute-start(bf16[1,2,1,1,40,2944]{5,4,3,2,1,0:T(8,128)(2,1)S(1)} %pad_maximum_fusion.36), channel_id=1, source_target_pairs={{0,8},{4,12},{8,0},{12,4},{1,9},{5,13},{9,1},{13,5},{2,10},{6,14},... | collective-permute-start | bytes 1413128 | tf_op jit(solution)/shard_map/ppermute | solution.py:31
  63.0 27.9 %collective-permute-start.31 = (bf16[2,2,1,1,96,640]{5,4,3,2,1,0:T(8,128)(2,1)S(1)}, bf16[2,2,1,1,96,640]{5,4,3,2,1,0:T(8,128)(2,1)S(1)}, u32[]{:S(2)}, u32[]{:S(2)}) collective-permute-start(bf16[2,2,1,1,96,640]{5,4,3,2,1,0:T(8,128)(2,1)S(1)} %pad_maximum_fusion.35), channel_id=1, source_target_pairs={{0,2},{1,3},{2,0},{3,1},{4,6},{5,7},{6,4},{7,5},{8,10},{9,11},{10,... | collective-permute-start | bytes 1474568 | tf_op jit(solution)/shard_map/ppermute | solution.py:31
  63.7 29.1 %collective-permute-start.17 = (bf16[2,2,1,1,96,640]{5,4,3,2,1,0:T(8,128)(2,1)S(1)}, bf16[2,2,1,1,96,640]{5,4,3,2,1,0:T(8,128)(2,1)S(1)}, u32[]{:S(2)}, u32[]{:S(2)}) collective-permute-start(bf16[2,2,1,1,96,640]{5,4,3,2,1,0:T(8,128)(2,1)S(1)} %pad_maximum_fusion.34), channel_id=1, source_target_pairs={{0,2},{1,3},{2,0},{3,1},{4,6},{5,7},{6,4},{7,5},{8,10},{9,11},{10,... | collective-permute-start | bytes 1474568 | tf_op jit(solution)/shard_map/ppermute | solution.py:31
  79.0 33.8 %collective-permute-start.22 = (bf16[2,2,1,1,40,2048]{5,4,3,2,1,0:T(8,128)(2,1)}, bf16[2,2,1,1,40,2048]{5,4,3,2,1,0:T(8,128)(2,1)}, u32[]{:S(2)}, u32[]{:S(2)}) collective-permute-start(bf16[2,2,1,1,40,2048]{5,4,3,2,1,0:T(8,128)(2,1)} %pad_maximum_fusion.30), channel_id=1, source_target_pairs={{0,1},{1,0},{2,3},{3,2},{4,5},{5,4},{6,7},{7,6},{8,9},{9,8},{10,11... | collective-permute-start | bytes 1966088 | tf_op jit(solution)/shard_map/ppermute | solution.py:31
  80.7 28.4 %collective-permute-start.9 = (bf16[2,2,2,1,40,896]{5,4,3,2,1,0:T(8,128)(2,1)S(1)}, bf16[2,2,2,1,40,896]{5,4,3,2,1,0:T(8,128)(2,1)S(1)}, u32[]{:S(2)}, u32[]{:S(2)}) collective-permute-start(bf16[2,2,2,1,40,896]{5,4,3,2,1,0:T(8,128)(2,1)S(1)} %pad_maximum_fusion.31), channel_id=1, source_target_pairs={{0,1},{1,0},{2,3},{3,2},{4,5},{5,4},{6,7},{7,6},{8,9},{9,8},{10,11... | collective-permute-start | bytes 1720328 | tf_op jit(solution)/shard_map/ppermute | solution.py:31
  89.4 40.0 %collective-permute-start.4 = (bf16[2,2,1,1,40,2944]{5,4,3,2,1,0:T(8,128)(2,1)}, bf16[2,2,1,1,40,2944]{5,4,3,2,1,0:T(8,128)(2,1)}, u32[]{:S(2)}, u32[]{:S(2)}) collective-permute-start(bf16[2,2,1,1,40,2944]{5,4,3,2,1,0:T(8,128)(2,1)} %pad_maximum_fusion.29), channel_id=1, source_target_pairs={{0,1},{1,0},{2,3},{3,2},{4,5},{5,4},{6,7},{7,6},{8,9},{9,8},{10,11... | collective-permute-start | bytes 2826248 | tf_op jit(solution)/shard_map/ppermute | solution.py:31
  92.2 58.3 %collective-permute-start.32 = (bf16[2,2,2,1,96,640]{5,4,3,2,1,0:T(8,128)(2,1)}, bf16[2,2,2,1,96,640]{5,4,3,2,1,0:T(8,128)(2,1)}, u32[]{:S(2)}, u32[]{:S(2)}) collective-permute-start(bf16[2,2,2,1,96,640]{5,4,3,2,1,0:T(8,128)(2,1)} %pad_maximum_fusion.28), channel_id=1, source_target_pairs={{0,1},{1,0},{2,3},{3,2},{4,5},{5,4},{6,7},{7,6},{8,9},{9,8},{10,11... | collective-permute-start | bytes 2949128 | tf_op jit(solution)/shard_map/ppermute | solution.py:31
  93.9 76.6 %collective-permute-start.18 = (bf16[2,2,2,1,96,640]{5,4,3,2,1,0:T(8,128)(2,1)}, bf16[2,2,2,1,96,640]{5,4,3,2,1,0:T(8,128)(2,1)}, u32[]{:S(2)}, u32[]{:S(2)}) collective-permute-start(bf16[2,2,2,1,96,640]{5,4,3,2,1,0:T(8,128)(2,1)} %pad_maximum_fusion.27), channel_id=1, source_target_pairs={{0,1},{1,0},{2,3},{3,2},{4,5},{5,4},{6,7},{7,6},{8,9},{9,8},{10,11... | collective-permute-start | bytes 2949128 | tf_op jit(solution)/shard_map/ppermute | solution.py:31
  110.4 63.1 %collective-permute-start.10 = (bf16[16,40,896]{2,1,0:T(8,128)(2,1)}, bf16[16,40,896]{2,1,0:T(8,128)(2,1)}, u32[]{:S(2)}, u32[]{:S(2)}) collective-permute-start(bf16[16,40,896]{2,1,0:T(8,128)(2,1)} %bitcast.24), channel_id=1, source_target_pairs={{0,16},{16,0},{1,17},{17,1},{2,18},{18,2},{3,19},{19,3},{4,20},{20... | collective-permute-start | bytes 3440648 | tf_op jit(solution)/shard_map/ppermute | solution.py:31
  115.3 72.8 %collective-permute-start.23 = (bf16[2,2,1,2,40,2048]{5,4,3,2,1,0:T(8,128)(2,1)}, bf16[2,2,1,2,40,2048]{5,4,3,2,1,0:T(8,128)(2,1)}, u32[]{:S(2)}, u32[]{:S(2)}) collective-permute-start(bf16[2,2,1,2,40,2048]{5,4,3,2,1,0:T(8,128)(2,1)} %pad_maximum_fusion.20), channel_id=1, source_target_pairs={{0,2},{1,3},{2,0},{3,1},{4,6},{5,7},{6,4},{7,5},{8,10},{9,11},{10,... | collective-permute-start | bytes 3932168 | tf_op jit(solution)/shard_map/ppermute | solution.py:31
  132.3 74.6 %collective-permute-start.5 = (bf16[2,2,1,2,40,2944]{5,4,3,2,1,0:T(8,128)(2,1)}, bf16[2,2,1,2,40,2944]{5,4,3,2,1,0:T(8,128)(2,1)}, u32[]{:S(2)}, u32[]{:S(2)}) collective-permute-start(bf16[2,2,1,2,40,2944]{5,4,3,2,1,0:T(8,128)(2,1)} %pad_maximum_fusion.10), channel_id=1, source_target_pairs={{0,2},{1,3},{2,0},{3,1},{4,6},{5,7},{6,4},{7,5},{8,10},{9,11},{10,... | collective-permute-start | bytes 5652488 | tf_op jit(solution)/shard_map/ppermute | solution.py:31
  153.4 65.5 %collective-permute-start.33 = (bf16[16,96,640]{2,1,0:T(8,128)(2,1)}, bf16[16,96,640]{2,1,0:T(8,128)(2,1)}, u32[]{:S(2)}, u32[]{:S(2)}) collective-permute-start(bf16[16,96,640]{2,1,0:T(8,128)(2,1)} %bitcast.54), channel_id=1, source_target_pairs={{0,16},{16,0},{1,17},{17,1},{2,18},{18,2},{3,19},{19,3},{4,20},{20... | collective-permute-start | bytes 5898248 | tf_op jit(solution)/shard_map/ppermute | solution.py:31
  181.4 17.0 %collective-permute-start.12 = (bf16[256,512]{1,0:T(8,128)(2,1)}, bf16[256,512]{1,0:T(8,128)(2,1)}, u32[]{:S(2)}, u32[]{:S(2)}) collective-permute-start(bf16[256,512]{1,0:T(8,128)(2,1)} %pad_maximum_fusion.48), channel_id=1, source_target_pairs={{0,2},{1,3},{2,0},{3,1},{4,6},{5,7},{6,4},{7,5},{8,10},{9,11},{10,... | collective-permute-start | bytes 786440 | tf_op jit(solution)/shard_map/ppermute | solution.py:31
  192.0 31.7 %collective-permute-start.19 = (bf16[16,96,640]{2,1,0:T(8,128)(2,1)}, bf16[16,96,640]{2,1,0:T(8,128)(2,1)}, u32[]{:S(2)}, u32[]{:S(2)}) collective-permute-start(bf16[16,96,640]{2,1,0:T(8,128)(2,1)} %bitcast.38), channel_id=1, source_target_pairs={{0,16},{16,0},{1,17},{17,1},{2,18},{18,2},{3,19},{19,3},{4,20},{20... | collective-permute-start | bytes 5898248 | tf_op jit(solution)/shard_map/ppermute | solution.py:31
  198.5 35.6 %collective-permute-start.24 = (bf16[16,40,2048]{2,1,0:T(8,128)(2,1)}, bf16[16,40,2048]{2,1,0:T(8,128)(2,1)}, u32[]{:S(2)}, u32[]{:S(2)}) collective-permute-start(bf16[16,40,2048]{2,1,0:T(8,128)(2,1)} %bitcast.42), channel_id=1, source_target_pairs={{0,16},{16,0},{1,17},{17,1},{2,18},{18,2},{3,19},{19,3},{4,20},{20... | collective-permute-start | bytes 7864328 | tf_op jit(solution)/shard_map/ppermute | solution.py:31
  211.1 31.5 %collective-permute-start.25 = (bf16[16,40,2944]{2,1,0:T(8,128)(2,1)}, bf16[16,40,2944]{2,1,0:T(8,128)(2,1)}, u32[]{:S(2)}, u32[]{:S(2)}) collective-permute-start(bf16[16,40,2944]{2,1,0:T(8,128)(2,1)} %bitcast.14), channel_id=1, source_target_pairs={{0,16},{16,0},{1,17},{17,1},{2,18},{18,2},{3,19},{19,3},{4,20},{20... | collective-permute-start | bytes 11304968 | tf_op jit(solution)/shard_map/ppermute | solution.py:31
  247.4 16.9 %collective-permute-start.26 = (bf16[256,512]{1,0:T(8,128)(2,1)}, bf16[256,512]{1,0:T(8,128)(2,1)}, u32[]{:S(2)}, u32[]{:S(2)}) collective-permute-start(bf16[256,512]{1,0:T(8,128)(2,1)} %pad_maximum_fusion.49), channel_id=1, source_target_pairs={{0,1},{1,0},{2,3},{3,2},{4,5},{5,4},{6,7},{7,6},{8,9},{9,8},{10,11... | collective-permute-start | bytes 786440 | tf_op jit(solution)/shard_map/ppermute | solution.py:31
  309.0 22.5 %collective-permute-start.34 = (bf16[256,512]{1,0:T(8,128)(2,1)}, bf16[256,512]{1,0:T(8,128)(2,1)}, u32[]{:S(2)}, u32[]{:S(2)}) collective-permute-start(bf16[256,512]{1,0:T(8,128)(2,1)} %get-tuple-element.138), channel_id=1, source_target_pairs={{0,1},{1,0},{2,3},{3,2},{4,5},{5,4},{6,7},{7,6},{8,9},{9,8},{10,11... | collective-permute-start | bytes 786440 | tf_op jit(solution)/shard_map/ppermute | solution.py:31
  310.5 21.0 %collective-permute-start.35 = (bf16[256,512]{1,0:T(8,128)(2,1)}, bf16[256,512]{1,0:T(8,128)(2,1)}, u32[]{:S(2)}, u32[]{:S(2)}) collective-permute-start(bf16[256,512]{1,0:T(8,128)(2,1)} %get-tuple-element.140), channel_id=1, source_target_pairs={{0,2},{1,3},{2,0},{3,1},{4,6},{5,7},{6,4},{7,5},{8,10},{9,11},{10,... | collective-permute-start | bytes 786440 | tf_op jit(solution)/shard_map/ppermute | solution.py:31
  312.0 19.5 %collective-permute-start.36 = (bf16[256,512]{1,0:T(8,128)(2,1)}, bf16[256,512]{1,0:T(8,128)(2,1)}, u32[]{:S(2)}, u32[]{:S(2)}) collective-permute-start(bf16[256,512]{1,0:T(8,128)(2,1)} %get-tuple-element.139), channel_id=1, source_target_pairs={{0,3},{1,2},{2,1},{3,0},{4,7},{5,6},{6,5},{7,4},{8,11},{9,10},{10,... | collective-permute-start | bytes 786440 | tf_op jit(solution)/shard_map/ppermute | solution.py:31
  329.7 108.8 %collective-permute-start.52 = (bf16[640,2048]{1,0:T(8,128)(2,1)}, bf16[640,2048]{1,0:T(8,128)(2,1)}, u32[]{:S(2)}, u32[]{:S(2)}) collective-permute-start(bf16[640,2048]{1,0:T(8,128)(2,1)} %convolution_convert_fusion.2), channel_id=1, source_target_pairs={{0,16},{16,0},{1,17},{17,1},{2,18},{18,2},{3,19},{19,3},{4,20},{20... | collective-permute-start | bytes 7864328 | tf_op jit(solution)/shard_map/ppermute | solution.py:31
  370.0 21.2 %collective-permute-start.37 = (bf16[256,512]{1,0:T(8,128)(2,1)}, bf16[256,512]{1,0:T(8,128)(2,1)}, u32[]{:S(2)}, u32[]{:S(2)}) collective-permute-start(bf16[256,512]{1,0:T(8,128)(2,1)} %get-tuple-element.135), channel_id=1, source_target_pairs={{0,1},{1,0},{2,3},{3,2},{4,5},{5,4},{6,7},{7,6},{8,9},{9,8},{10,11... | collective-permute-start | bytes 786440 | tf_op jit(solution)/shard_map/ppermute | solution.py:31
  371.5 19.7 %collective-permute-start.38 = (bf16[256,512]{1,0:T(8,128)(2,1)}, bf16[256,512]{1,0:T(8,128)(2,1)}, u32[]{:S(2)}, u32[]{:S(2)}) collective-permute-start(bf16[256,512]{1,0:T(8,128)(2,1)} %get-tuple-element.137), channel_id=1, source_target_pairs={{0,2},{1,3},{2,0},{3,1},{4,6},{5,7},{6,4},{7,5},{8,10},{9,11},{10,... | collective-permute-start | bytes 786440 | tf_op jit(solution)/shard_map/ppermute | solution.py:31
  373.0 18.2 %collective-permute-start.39 = (bf16[256,512]{1,0:T(8,128)(2,1)}, bf16[256,512]{1,0:T(8,128)(2,1)}, u32[]{:S(2)}, u32[]{:S(2)}) collective-permute-start(bf16[256,512]{1,0:T(8,128)(2,1)} %get-tuple-element.136), channel_id=1, source_target_pairs={{0,3},{1,2},{2,1},{3,0},{4,7},{5,6},{6,5},{7,4},{8,11},{9,10},{10,... | collective-permute-start | bytes 786440 | tf_op jit(solution)/shard_map/ppermute | solution.py:31
  404.9 27.3 %collective-permute-start.58 = (bf16[16,96,640]{2,1,0:T(8,128)(2,1)S(1)}, bf16[16,96,640]{2,1,0:T(8,128)(2,1)S(1)}, u32[]{:S(2)}, u32[]{:S(2)}) collective-permute-start(bf16[16,96,640]{2,1,0:T(8,128)(2,1)S(1)} %pad_maximum_fusion.8), channel_id=1, source_target_pairs={{0,16},{16,0},{1,17},{17,1},{2,18},{18,2},{3,19},{19,3},{4,20},{20... | collective-permute-start | bytes 5898248 | tf_op jit(solution)/shard_map/ppermute | solution.py:31
  413.4 36.3 %collective-permute-start.46 = (bf16[640,2048]{1,0:T(8,128)(2,1)S(1)}, bf16[640,2048]{1,0:T(8,128)(2,1)S(1)}, u32[]{:S(2)}, u32[]{:S(2)}) collective-permute-start(bf16[640,2048]{1,0:T(8,128)(2,1)S(1)} %convolution_convert_fusion.4), channel_id=1, source_target_pairs={{0,16},{16,0},{1,17},{17,1},{2,18},{18,2},{3,19},{19,3},{4,20},{20... | collective-permute-start | bytes 7864328 | tf_op jit(solution)/shard_map/ppermute | solution.py:31
  417.9 33.6 %collective-permute-start.64 = (bf16[2,2,2,1,96,640]{5,4,3,2,1,0:T(8,128)(2,1)S(1)}, bf16[2,2,2,1,96,640]{5,4,3,2,1,0:T(8,128)(2,1)S(1)}, u32[]{:S(2)}, u32[]{:S(2)}) collective-permute-start(bf16[2,2,2,1,96,640]{5,4,3,2,1,0:T(8,128)(2,1)S(1)} %constant_dynamic-slice_fusion.3), channel_id=1, source_target_pairs={{0,1},{1,0},{2,3},{3,2},{4,5},{5,4},{6,7},{7,6},{8,9},{9,8},{10,11... | collective-permute-start | bytes 2949128 | tf_op jit(solution)/shard_map/ppermute | solution.py:31
  432.7 39.2 %collective-permute-start.59 = (bf16[2,2,2,1,96,640]{5,4,3,2,1,0:T(8,128)(2,1)S(1)}, bf16[2,2,2,1,96,640]{5,4,3,2,1,0:T(8,128)(2,1)S(1)}, u32[]{:S(2)}, u32[]{:S(2)}) collective-permute-start(bf16[2,2,2,1,96,640]{5,4,3,2,1,0:T(8,128)(2,1)S(1)} %constant_dynamic-slice_fusion.7), channel_id=1, source_target_pairs={{0,1},{1,0},{2,3},{3,2},{4,5},{5,4},{6,7},{7,6},{8,9},{9,8},{10,11... | collective-permute-start | bytes 2949128 | tf_op jit(solution)/shard_map/ppermute | solution.py:31
  445.5 93.2 %collective-permute-start.53 = (bf16[2,2,1,2,40,2944]{5,4,3,2,1,0:T(8,128)(2,1)S(1)}, bf16[2,2,1,2,40,2944]{5,4,3,2,1,0:T(8,128)(2,1)S(1)}, u32[]{:S(2)}, u32[]{:S(2)}) collective-permute-start(bf16[2,2,1,2,40,2944]{5,4,3,2,1,0:T(8,128)(2,1)S(1)} %fusion.20), channel_id=1, source_target_pairs={{0,2},{1,3},{2,0},{3,1},{4,6},{5,7},{6,4},{7,5},{8,10},{9,11},{10,... | collective-permute-start | bytes 5652488 | tf_op jit(solution)/shard_map/ppermute | solution.py:31
  451.7 48.3 %collective-permute-start.65 = (bf16[2,2,1,1,96,640]{5,4,3,2,1,0:T(8,128)(2,1)S(1)}, bf16[2,2,1,1,96,640]{5,4,3,2,1,0:T(8,128)(2,1)S(1)}, u32[]{:S(2)}, u32[]{:S(2)}) collective-permute-start(bf16[2,2,1,1,96,640]{5,4,3,2,1,0:T(8,128)(2,1)S(1)} %constant_dynamic-slice_fusion.2), channel_id=1, source_target_pairs={{0,2},{1,3},{2,0},{3,1},{4,6},{5,7},{6,4},{7,5},{8,10},{9,11},{10,... | collective-permute-start | bytes 1474568 | tf_op jit(solution)/shard_map/ppermute | solution.py:31
  472.2 38.4 %collective-permute-start.60 = (bf16[2,2,1,1,96,640]{5,4,3,2,1,0:T(8,128)(2,1)S(1)}, bf16[2,2,1,1,96,640]{5,4,3,2,1,0:T(8,128)(2,1)S(1)}, u32[]{:S(2)}, u32[]{:S(2)}) collective-permute-start(bf16[2,2,1,1,96,640]{5,4,3,2,1,0:T(8,128)(2,1)S(1)} %constant_dynamic-slice_fusion.6), channel_id=1, source_target_pairs={{0,2},{1,3},{2,0},{3,1},{4,6},{5,7},{6,4},{7,5},{8,10},{9,11},{10,... | collective-permute-start | bytes 1474568 | tf_op jit(solution)/shard_map/ppermute | solution.py:31
  474.0 62.6 %collective-permute-start.47 = (bf16[2,2,1,2,40,2048]{5,4,3,2,1,0:T(8,128)(2,1)S(1)}, bf16[2,2,1,2,40,2048]{5,4,3,2,1,0:T(8,128)(2,1)S(1)}, u32[]{:S(2)}, u32[]{:S(2)}) collective-permute-start(bf16[2,2,1,2,40,2048]{5,4,3,2,1,0:T(8,128)(2,1)S(1)} %constant_dynamic-slice_fusion.14), channel_id=1, source_target_pairs={{0,2},{1,3},{2,0},{3,1},{4,6},{5,7},{6,4},{7,5},{8,10},{9,11},{10,... | collective-permute-start | bytes 3932168 | tf_op jit(solution)/shard_map/ppermute | solution.py:31
  514.0 25.8 %collective-permute-start.67 = (bf16[1,1,1,1,96,640]{5,4,3,2,1,0:T(8,128)(2,1)S(1)}, bf16[1,1,1,1,96,640]{5,4,3,2,1,0:T(8,128)(2,1)S(1)}, u32[]{:S(2)}, u32[]{:S(2)}) collective-permute-start(bf16[1,1,1,1,96,640]{5,4,3,2,1,0:T(8,128)(2,1)S(1)} %constant_dynamic-slice_fusion), channel_id=1, source_target_pairs={{0,4},{4,0},{8,12},{12,8},{1,5},{5,1},{9,13},{13,9},{2,6},{6,2},{1... | collective-permute-start | bytes 368648 | tf_op jit(solution)/shard_map/ppermute | solution.py:31
  520.9 18.9 %collective-permute-start.62 = (bf16[1,1,1,1,96,640]{5,4,3,2,1,0:T(8,128)(2,1)S(1)}, bf16[1,1,1,1,96,640]{5,4,3,2,1,0:T(8,128)(2,1)S(1)}, u32[]{:S(2)}, u32[]{:S(2)}) collective-permute-start(bf16[1,1,1,1,96,640]{5,4,3,2,1,0:T(8,128)(2,1)S(1)} %constant_dynamic-slice_fusion.4), channel_id=1, source_target_pairs={{0,4},{4,0},{8,12},{12,8},{1,5},{5,1},{9,13},{13,9},{2,6},{6,2},{1... | collective-permute-start | bytes 368648 | tf_op jit(solution)/shard_map/ppermute | solution.py:31
  537.1 17.7 %collective-permute-start.48 = (bf16[2,2,1,1,40,2048]{5,4,3,2,1,0:T(8,128)(2,1)S(1)}, bf16[2,2,1,1,40,2048]{5,4,3,2,1,0:T(8,128)(2,1)S(1)}, u32[]{:S(2)}, u32[]{:S(2)}) collective-permute-start(bf16[2,2,1,1,40,2048]{5,4,3,2,1,0:T(8,128)(2,1)S(1)} %constant_dynamic-slice_fusion.13), channel_id=1, source_target_pairs={{0,1},{1,0},{2,3},{3,2},{4,5},{5,4},{6,7},{7,6},{8,9},{9,8},{10,11... | collective-permute-start | bytes 1966088 | tf_op jit(solution)/shard_map/ppermute | solution.py:31
  539.2 32.7 %collective-permute-start.54 = (bf16[2,2,1,1,40,2944]{5,4,3,2,1,0:T(8,128)(2,1)S(1)}, bf16[2,2,1,1,40,2944]{5,4,3,2,1,0:T(8,128)(2,1)S(1)}, u32[]{:S(2)}, u32[]{:S(2)}) collective-permute-start(bf16[2,2,1,1,40,2944]{5,4,3,2,1,0:T(8,128)(2,1)S(1)} %constant_dynamic-slice_fusion.10), channel_id=1, source_target_pairs={{0,1},{1,0},{2,3},{3,2},{4,5},{5,4},{6,7},{7,6},{8,9},{9,8},{10,11... | collective-permute-start | bytes 2826248 | tf_op jit(solution)/shard_map/ppermute | solution.py:31
  539.8 60.5 %collective-permute-start.68 = (f32[96,640]{1,0:T(8,128)S(1)}, f32[96,640]{1,0:T(8,128)S(1)}, u32[]{:S(2)}, u32[]{:S(2)}) collective-permute-start(f32[96,640]{1,0:T(8,128)S(1)} %select_bitcast_fusion), channel_id=1, source_target_pairs={{0,16},{16,0},{1,17},{17,1},{2,18},{18,2},{3,19},{19,3},{4,20},{20... | collective-permute-start | bytes 737288 | tf_op jit(solution)/shard_map/ppermute | solution.py:31
  555.0 19.7 %collective-permute-start.49 = (bf16[1,2,1,1,40,2048]{5,4,3,2,1,0:T(8,128)(2,1)S(1)}, bf16[1,2,1,1,40,2048]{5,4,3,2,1,0:T(8,128)(2,1)S(1)}, u32[]{:S(2)}, u32[]{:S(2)}) collective-permute-start(bf16[1,2,1,1,40,2048]{5,4,3,2,1,0:T(8,128)(2,1)S(1)} %constant_dynamic-slice_fusion.12), channel_id=1, source_target_pairs={{0,8},{4,12},{8,0},{12,4},{1,9},{5,13},{9,1},{13,5},{2,10},{6,14},... | collective-permute-start | bytes 983048 | tf_op jit(solution)/shard_map/ppermute | solution.py:31
  572.2 20.8 %collective-permute-start.55 = (bf16[1,2,1,1,40,2944]{5,4,3,2,1,0:T(8,128)(2,1)S(1)}, bf16[1,2,1,1,40,2944]{5,4,3,2,1,0:T(8,128)(2,1)S(1)}, u32[]{:S(2)}, u32[]{:S(2)}) collective-permute-start(bf16[1,2,1,1,40,2944]{5,4,3,2,1,0:T(8,128)(2,1)S(1)} %constant_dynamic-slice_fusion.9), channel_id=1, source_target_pairs={{0,8},{4,12},{8,0},{12,4},{1,9},{5,13},{9,1},{13,5},{2,10},{6,14},... | collective-permute-start | bytes 1413128 | tf_op jit(solution)/shard_map/ppermute | solution.py:31
  574.8 18.4 %collective-permute-start.50 = (bf16[1,1,1,1,40,2048]{5,4,3,2,1,0:T(8,128)(2,1)S(1)}, bf16[1,1,1,1,40,2048]{5,4,3,2,1,0:T(8,128)(2,1)S(1)}, u32[]{:S(2)}, u32[]{:S(2)}) collective-permute-start(bf16[1,1,1,1,40,2048]{5,4,3,2,1,0:T(8,128)(2,1)S(1)} %constant_dynamic-slice_fusion.11), channel_id=1, source_target_pairs={{0,4},{4,0},{8,12},{12,8},{1,5},{5,1},{9,13},{13,9},{2,6},{6,2},{1... | collective-permute-start | bytes 491528 | tf_op jit(solution)/shard_map/ppermute | solution.py:31
  (265 other events, 2205.2 us)

commit v2 on v1

--- a/solution.py
+++ b/solution.py
@@ -35,38 +35,114 @@
     return (lax.axis_index(axis) >> bit) & 1
 
 
-def grid_steps(order):
-    steps = []
-    fb, cb = bits_of("fsdp"), bits_of("ctx")
-    fsteps = [("fsdp", b, fb - 1 - b) for b in range(fb)]
-    csteps = [("ctx", b, fb + cb - 1 - b) for b in range(cb)]
-    if order == "yx":
-        csteps = csteps[::-1]
-    return fsteps + csteps
-
-
-def gather_blocks(block, order):
-    nb = bits_of("fsdp") + bits_of("ctx")
-    buf = block.reshape((1,) * nb + block.shape)
-    for axis, bit, dim in grid_steps(order):
-        recv = exchange(buf, axis, 1 << bit)
-        low = my_bit(axis, bit) == 0
+def tie(*values):
+    return lax.optimization_barrier(values)
+
+
+def ctx_steps(order):
+    count = bits_of("ctx")
+    steps = [(bit, count - bit) for bit in range(count)]
+    return steps if order == "xy" else steps[::-1]
+
+
+def z_gather(block):
+    count = lax.axis_size("fsdp")
+    pieces = [block] + [exchange(block, "fsdp", j) for j in range(1, count)]
+    me = lax.axis_index("fsdp")
+    return jnp.stack([lax.select_n(me ^ at, *pieces) for at in range(count)])
+
+
+def ctx_open(buf):
+    return buf.reshape((buf.shape[0],) + (1,) * bits_of("ctx") + buf.shape[1:])
+
+
+def ctx_gather(buf, steps):
+    for bit, dim in steps:
+        recv = exchange(buf, "ctx", 1 << bit)
+        low = my_bit("ctx", bit) == 0
         buf = jnp.concatenate([jnp.where(low, buf, recv), jnp.where(low, recv, buf)], axis=dim)
-    return buf.reshape((-1,) + block.shape)
-
-
-def scatter_blocks(blocks, order, last=F32):
-    nb = bits_of("fsdp") + bits_of("ctx")
-    buf = blocks.reshape((2,) * nb + blocks.shape[1:])
-    steps = grid_steps(order)[::-1]
-    for at, (axis, bit, dim) in enumerate(steps):
-        mine = my_bit(axis, bit)
+    return buf
+
+
+def ctx_close(buf, tail):
+    return buf.reshape((-1,) + tail)
+
+
+def ctx_scatter(buf, steps):
+    for bit, dim in steps:
+        mine = my_bit("ctx", bit)
         send = lax.dynamic_index_in_dim(buf, 1 - mine, dim, keepdims=True)
         keep = lax.dynamic_index_in_dim(buf, mine, dim, keepdims=True)
-        recv = exchange(send, axis, 1 << bit)
-        kind = last if at == len(steps) - 1 else BF
-        buf = (keep.astype(F32) + recv.astype(F32)).astype(kind)
-    return buf.reshape(blocks.shape[1:])
+        recv = exchange(send, "ctx", 1 << bit)
+        buf = (keep.astype(F32) + recv.astype(F32)).astype(BF)
+    return buf
+
+
+def z_scatter(buf):
+    me = lax.axis_index("fsdp")
+    total = lax.dynamic_index_in_dim(buf, me, 0, False).astype(F32)
+    for j in range(1, lax.axis_size("fsdp")):
+        part = lax.dynamic_index_in_dim(buf, me ^ j, 0, False)
+        total = total + exchange(part, "fsdp", j).astype(F32)
+    return total
+
+
+class Gather:
+    ORDERS = ("yx", "xy", "yx", "xy")
+
+    def __init__(self, cols, rows):
+        self.q, self.g, self.b = cols[:, :QP], cols[:, QP:], rows
+
+    def after(self, *others):
+        self.q, self.g, self.b = tie(self.q, self.g, self.b, *others)[:3]
+
+    def along_z(self):
+        q, g, b = z_gather(self.q), z_gather(self.g), z_gather(self.b)
+        half = g.shape[0] // 2
+        self.parts = [ctx_open(v) for v in (q, g[:half], g[half:], b)]
+
+    def parts_after(self, *others):
+        self.parts = list(tie(*self.parts, *others)[:4])
+
+    def plane(self, stage):
+        done = []
+        for v, order in zip(self.parts, self.ORDERS):
+            steps = ctx_steps(order)
+            done.append(ctx_gather(v, steps[:1] if stage == 0 else steps[1:]))
+        self.parts = done
+
+    def pairs(self):
+        q, g1, g2, b = self.parts
+        q = ctx_close(q, self.q.shape)
+        b = ctx_close(b, self.b.shape)
+        g = jnp.concatenate([ctx_close(g1, self.g.shape), ctx_close(g2, self.g.shape)], axis=0)
+        return [(v, exchange(v, "section", 1)) for v in (q, g, b)]
+
+
+class Scatter:
+    def __init__(self, blocks, split):
+        fs, cb = lax.axis_size("fsdp"), bits_of("ctx")
+        self.tail = blocks.shape[1:]
+        buf = blocks.reshape((fs,) + (2,) * cb + self.tail)
+        self.parts = [(buf[: fs // 2], "xy"), (buf[fs // 2 :], "yx")] if split else [(buf, "xy")]
+
+    def after(self, *others):
+        values = tie(*[p[0] for p in self.parts], *others)
+        self.parts = [(v, p[1]) for v, p in zip(values, self.parts)]
+
+    def values(self):
+        return [p[0] for p in self.parts]
+
+    def plane(self, stage):
+        done = []
+        for v, order in self.parts:
+            steps = ctx_steps(order)
+            done.append((ctx_scatter(v, steps[:1] if stage == 0 else steps[1:]), order))
+        self.parts = done
+
+    def along_z(self):
+        buf = jnp.concatenate([v.reshape((-1,) + self.tail) for v in self.values()], axis=0)
+        return z_scatter(buf)
 
 
 def rms_norm(values_in, gain):
@@ -150,8 +226,8 @@
     return total
 
 
-def layer_forward(full, x, places, all_places, window, cosine, sine_table, first):
-    q_own, q_oth, g_own, g_oth, w_out, w_down, gains, heads = full
+def forward_keys(full, x, cosine, sine_table, first):
+    q_own, q_oth, gains, heads = full
     tokens = x.shape[0]
     normed = rms_norm(x, gains[0]).astype(BF)
     lo, hi = pick(first, dot(normed, q_own), dot(normed, q_oth))
@@ -163,33 +239,41 @@
     flat_queries = queries.astype(BF).reshape(tokens * HEADS, HD)
     keys_values = jnp.concatenate([keys_rot, hi[:, QH:]], axis=1).astype(BF)
     all_kv = jnp.concatenate(key_exchange(keys_values), axis=0)
-    all_keys, all_values = all_kv[:, :HD], all_kv[:, HD:]
-    prob_low = attention_weights(flat_queries, all_keys, places, all_places, window).astype(BF)
-    mixed = dot(prob_low, all_values).reshape(tokens, HEADS * HD).astype(BF)
+    return dict(
+        x=x, normed=normed, query_product=query_product, key_product=key_product,
+        flat_queries=flat_queries, all_keys=all_kv[:, :HD], all_values=all_kv[:, HD:],
+    )
+
+
+def forward_attend(kept, places, all_places, window):
+    tokens = kept["x"].shape[0]
+    prob_low = attention_weights(
+        kept["flat_queries"], kept["all_keys"], places, all_places, window
+    ).astype(BF)
+    return dot(prob_low, kept["all_values"]).reshape(tokens, HEADS * HD).astype(BF)
+
+
+def forward_rest(full, kept, mixed, first):
+    g_own, g_oth, w_out, w_down, gains = full
     branch = dot(mixed, w_out)
-    middle = x + rms_norm(branch, gains[1])
+    middle = kept["x"] + rms_norm(branch, gains[1])
     normed_two = rms_norm(middle, gains[2]).astype(BF)
     gate, up = pick(first, dot(normed_two, g_own), dot(normed_two, g_oth))
     hidden = gated(gate, up).astype(BF)
     down_out = dot(hidden, w_down)
-    result = middle + rms_norm(down_out, gains[3])
-    kept = dict(
-        normed=normed, query_product=query_product, key_product=key_product,
-        flat_queries=flat_queries, all_keys=all_keys, all_values=all_values, mixed=mixed,
-        branch=branch, middle=middle, normed_two=normed_two, gate=gate, up=up, hidden=hidden,
-        down_out=down_out, x=x,
-    )
-    return result, kept
+    kept.update(
+        mixed=mixed, branch=branch, middle=middle, normed_two=normed_two, gate=gate, up=up,
+        hidden=hidden, down_out=down_out,
+    )
+    return middle + rms_norm(down_out, gains[3])
 
 
 def halves(grad, count):
     return grad.reshape(count, 2, -1, grad.shape[-1])
 
 
-def layer_backward(full, kept, grad_result, places, all_places, window, cosine, sine_table, first):
-    q_own, q_oth, g_own, g_oth, w_out, w_down, gains, heads = full
-    x = kept["x"]
-    tokens = x.shape[0]
+def backward_feed(full, kept, grad_result, first):
+    g_own, g_oth, w_out, w_down, gains = full
     _, back_last = jax.vjp(rms_norm, kept["down_out"], gains[3])
     grad_down, gain_three = back_last(grad_result)
     grad_down_low = grad_down.astype(BF)
@@ -204,13 +288,15 @@
     _, back_norm_one = jax.vjp(rms_norm, kept["branch"], gains[1])
     grad_branch, gain_one = back_norm_one(grad_middle)
     grad_branch_low = grad_branch.astype(BF)
-    grad_mixed = dot_t(grad_branch_low, w_out).astype(BF).reshape(tokens * HEADS, HD)
-    wg_g = (
-        t_dot(kept["normed_two"], gu_own).astype(BF),
-        t_dot(kept["normed_two"], gu_oth).astype(BF),
-    )
+    wg_g = (t_dot(kept["normed_two"], gu_own), t_dot(kept["normed_two"], gu_oth).astype(BF))
     wg_out = t_dot(kept["mixed"], grad_branch_low).astype(BF)
     wg_down = t_dot(kept["hidden"], grad_down_low).astype(BF)
+    return grad_middle, grad_branch_low, wg_g, wg_out, wg_down, [gain_one, gain_two, gain_three]
+
+
+def backward_attend(w_out, kept, grad_branch_low, places, all_places, window):
+    tokens = kept["x"].shape[0]
+    grad_mixed = dot_t(grad_branch_low, w_out).astype(BF).reshape(tokens * HEADS, HD)
     flat_queries, all_keys, all_values = kept["flat_queries"], kept["all_keys"], kept["all_values"]
     probabilities = attention_weights(flat_queries, all_keys, places, all_places, window)
     prob_low = probabilities.astype(BF)
@@ -222,6 +308,11 @@
     blocks = jnp.concatenate([grad_keys_all, grad_values_all], axis=1)
     grad_kv = key_return(jnp.split(blocks, lax.axis_size("ctx"), axis=0))
     grad_queries = dot(grad_scores, all_keys) * SCALE
+    return grad_queries.reshape(tokens, HEADS, HD), grad_kv
+
+
+def backward_keys(full, kept, grad_middle, grad_queries, grad_kv, cosine, sine_table, first):
+    q_own, q_oth, gains, heads = full
 
     def prepare(query_in, key_in, query_gain, key_gain):
         return head_prepare(query_in, key_in, query_gain, key_gain, cosine, sine_table)
@@ -229,25 +320,18 @@
     _, back_heads = jax.vjp(
         prepare, kept["query_product"], kept["key_product"], heads[0], heads[1]
     )
-    grad_qp, grad_kp, query_gain, key_gain = back_heads(
-        (grad_queries.reshape(tokens, HEADS, HD), grad_kv[:, :HD])
-    )
+    grad_qp, grad_kp, query_gain, key_gain = back_heads((grad_queries, grad_kv[:, :HD]))
     lo = jnp.concatenate([grad_qp[:, :QH], grad_kp], axis=1).astype(BF)
     hi = jnp.concatenate([grad_qp[:, QH:], grad_kv[:, HD:]], axis=1).astype(BF)
     q_grad_own, q_grad_oth = pick(first, lo, hi)
     grad_normed = dot_t(q_grad_own, q_own) + dot_t(q_grad_oth, q_oth)
-    _, back_norm_zero = jax.vjp(rms_norm, x, gains[0])
+    _, back_norm_zero = jax.vjp(rms_norm, kept["x"], gains[0])
     grad_part, gain_zero = back_norm_zero(grad_normed)
-    grad_x = grad_middle + grad_part
     wg_q = (
         t_dot(kept["normed"], q_grad_own).astype(BF),
         t_dot(kept["normed"], q_grad_oth).astype(BF),
     )
-    gain_grads = (
-        jnp.stack([gain_zero, gain_one, gain_two, gain_three]),
-        jnp.stack([query_gain, key_gain]),
-    )
-    return grad_x, wg_q, wg_g, wg_out, wg_down, gain_grads
+    return grad_middle + grad_part, wg_q, gain_zero, [query_gain, key_gain]
 
 
 def local(
@@ -311,48 +395,25 @@
     layer_cols = pick(first, col_keep, col_recv)
     layer_rows = pick(first, row_keep, row_recv)
 
-    def swap(own):
-        return own, exchange(own, "section", 1)
-
-    def assemble(q_pair, g_pair, b_pair):
-        q_own, q_oth = [v.reshape(blocks * nr, -1) for v in q_pair]
-        g_own, g_oth = [v.reshape(blocks * nr, -1) for v in g_pair]
-        b_own, b_oth = b_pair
-        b_lo, b_hi = pick(first, b_own, b_oth)
-        full_out = jnp.concatenate([b_lo[:, : ro // 2], b_hi[:, : ro // 2]], axis=1)
-        full_down = jnp.concatenate([b_lo[:, ro // 2 :], b_hi[:, ro // 2 :]], axis=1)
+    def query_side(pair):
+        q_own, q_oth = [v.reshape(blocks * nr, -1) for v in pair]
         gain_part = q_own[:, QW:].astype(F32)
         gains = gain_part[:, :4].T
         heads = gain_part[:, 4:6].reshape(blocks, nr, 2)[:, :hr].reshape(blocks * hr, 2).T
-        return (
-            q_own[:, :QW], q_oth[:, :QW], g_own, g_oth,
-            full_out.reshape(-1, D), full_down.reshape(-1, D), gains, heads,
-        )
-
-    full0 = assemble(
-        swap(gather_blocks(layer_cols[0][:, :QP], "yx")),
-        swap(gather_blocks(layer_cols[0][:, QP:], "xy")),
-        swap(gather_blocks(layer_rows[0], "yx")),
-    )
-    col_pair = swap(gather_blocks(layer_cols[1], "xy"))
-    full1 = assemble(
-        [v[..., :QP] for v in col_pair],
-        [v[..., QP:] for v in col_pair],
-        swap(gather_blocks(layer_rows[1], "yx")),
-    )
-
-    tables = [rope_tables(places, base) for base in BASES]
-    windows = (WIN, seq_length)
-
-    y0, kept0 = layer_forward(full0, x0, places, all_places, windows[0], *tables[0], first)
-    y1, kept1 = layer_forward(
-        full1, y0.astype(BF).astype(F32), places, all_places, windows[1], *tables[1], first
-    )
-
-    def reduce_g(wg_g):
-        return wg_g[0].astype(F32) + exchange(wg_g[1], "section", 1).astype(F32)
-
-    def reduce_b(wg_out, wg_down):
+        return q_own[:, :QW], q_oth[:, :QW], gains, heads
+
+    def feed_side(g_pair, b_pair, gains):
+        g_own, g_oth = [v.reshape(blocks * nr, -1) for v in g_pair]
+        b_lo, b_hi = pick(first, *b_pair)
+        full_out = jnp.concatenate([b_lo[:, : ro // 2], b_hi[:, : ro // 2]], axis=1)
+        full_down = jnp.concatenate([b_lo[:, ro // 2 :], b_hi[:, ro // 2 :]], axis=1)
+        return g_own, g_oth, full_out.reshape(-1, D), full_down.reshape(-1, D), gains
+
+    def reduce_cols(own, other):
+        summed = own.astype(F32) + exchange(other, "section", 1).astype(F32)
+        return summed.astype(BF).reshape(blocks, nr, -1)
+
+    def reduce_rows(wg_out, wg_down):
         out_half, down_half = halves(wg_out, blocks), halves(wg_down, blocks)
 
         def part(index):
@@ -365,39 +426,107 @@
             )
 
         recv = exchange(part(1 - section), "section", 1)
-        summed = (part(section).astype(F32) + recv.astype(F32)).astype(BF)
-        return scatter_blocks(summed, "yx")
-
-    def gain_columns(gain_grads):
-        norm_part = gain_grads[0].T
-        head_part = gain_grads[1].T.reshape(blocks, hr, 2)
+        return (part(section).astype(F32) + recv.astype(F32)).astype(BF)
+
+    def reduce_query(wg_q, norm_grads, head_grads):
+        norm_part = jnp.stack(norm_grads).T
+        head_part = jnp.stack(head_grads).T.reshape(blocks, hr, 2)
         head_part = jnp.pad(head_part, ((0, 0), (0, nr - hr), (0, 0))).reshape(blocks * nr, 2)
-        return jnp.concatenate(
-            [norm_part, head_part, jnp.zeros((blocks * nr, 128 - 6), F32)], axis=1
-        ).astype(BF)
-
-    def reduce_q(wg_q, gain_grads):
-        cols = gain_columns(gain_grads)
+        fill = jnp.zeros((blocks * nr, 128 - 6), F32)
+        cols = jnp.concatenate([norm_part, head_part, fill], axis=1).astype(BF)
         own = jnp.concatenate([wg_q[0], cols], axis=1)
         oth = jnp.concatenate([wg_q[1], cols], axis=1)
-        return own.astype(F32) + exchange(oth, "section", 1).astype(F32)
-
-    def in_blocks(v):
-        return v.astype(BF).reshape(blocks, nr, -1)
-
-    grad1, wg_q, wg_g, wg_out, wg_down, gain_grads = layer_backward(
-        full1, kept1, cotangent, places, all_places, windows[1], *tables[1], first
-    )
-    red_b1 = reduce_b(wg_out, wg_down)
-    col_sum = jnp.concatenate([reduce_q(wg_q, gain_grads), reduce_g(wg_g)], axis=1)
-    red_c1 = scatter_blocks(in_blocks(col_sum), "xy")
-    grad0, wg_q, wg_g, wg_out, wg_down, gain_grads = layer_backward(
-        full0, kept0, grad1.astype(BF).astype(F32), places, all_places, windows[0], *tables[0], first
-    )
-    red_b0 = reduce_b(wg_out, wg_down)
-    red_g0 = scatter_blocks(in_blocks(reduce_g(wg_g)), "xy")
-    red_q0 = scatter_blocks(in_blocks(reduce_q(wg_q, gain_grads)), "yx")
+        return reduce_cols(own, oth)
+
+    tables = [rope_tables(places, base) for base in BASES]
+    windows = (WIN, seq_length)
+
+    gather0 = Gather(layer_cols[0], layer_rows[0])
+    gather1 = Gather(layer_cols[1], layer_rows[1])
+    gather0.along_z()
+    gather1.after(*gather0.parts)
+    gather0.plane(0)
+    gather0.plane(1)
+    pairs0 = gather0.pairs()
+    query0 = query_side(pairs0[0])
+    kept0 = forward_keys(query0, x0, *tables[0], first)
+    gather1.along_z()
+    kept0["all_keys"], *gather1.parts = tie(kept0["all_keys"], *gather1.parts, *gather0.parts)[:5]
+    mixed = forward_attend(kept0, places, all_places, windows[0])
+    gather1.plane(0)
+    mixed, *gather1.parts = tie(mixed, *gather1.parts)
+    feed0 = feed_side(*pairs0[1:], query0[2])
+    y0 = forward_rest(feed0, kept0, mixed, first).astype(BF)
+    gather1.plane(1)
+    y0, *gather1.parts = tie(y0, *gather1.parts)
+    pairs1 = gather1.pairs()
+    query1 = query_side(pairs1[0])
+    kept1 = forward_keys(query1, y0.astype(F32), *tables[1], first)
+    mixed = forward_attend(kept1, places, all_places, windows[1])
+    feed1 = feed_side(*pairs1[1:], query1[2])
+    y1 = forward_rest(feed1, kept1, mixed, first)
+
+    middle1, branch1, wg_g, wg_out, wg_down, norm_grads = backward_feed(
+        feed1, kept1, cotangent, first
+    )
+    wg_own, wg_oth, wg_out, wg_down = tie(wg_g[0], wg_g[1], wg_out, wg_down)
+    scat_g1 = Scatter(reduce_cols(wg_own, wg_oth), True)
+    scat_b1 = Scatter(reduce_rows(wg_out, wg_down), False)
+    grad_q, grad_kv = backward_attend(feed1[2], kept1, branch1, places, all_places, windows[1])
+    grad_q, grad_kv, *held = tie(grad_q, grad_kv, *scat_g1.values(), *scat_b1.values())
+    scat_g1.after(*held)
+    scat_b1.after(*held)
+    scat_g1.plane(0)
+    scat_b1.plane(0)
+    grad1, wg_q, gain_zero, head_grads = backward_keys(
+        query1, kept1, middle1, grad_q, grad_kv, *tables[1], first
+    )
+    grad1 = grad1.astype(BF)
+    wg_q0, wg_q1, grad1, *held = tie(wg_q[0], wg_q[1], grad1, *scat_g1.values(), *scat_b1.values())
+    scat_g1.after(*held)
+    scat_b1.after(*held)
+    scat_g1.plane(1)
+    scat_b1.plane(1)
+    scat_q1 = Scatter(reduce_query((wg_q0, wg_q1), [gain_zero] + norm_grads, head_grads), False)
+
+    middle0, branch0, wg_g, wg_out, wg_down, norm_grads = backward_feed(
+        feed0, kept0, grad1.astype(F32), first
+    )
+    branch0, wg_own, wg_oth, wg_out, wg_down, *held = tie(
+        branch0, wg_g[0], wg_g[1], wg_out, wg_down,
+        *scat_g1.values(), *scat_b1.values(), *scat_q1.values()
+    )
+    scat_g1.after(*held)
+    scat_b1.after(*held)
+    scat_q1.after(*held)
+    red_g1, red_b1 = scat_g1.along_z(), scat_b1.along_z()
+    scat_g0 = Scatter(reduce_cols(wg_own, wg_oth), True)
+    scat_b0 = Scatter(reduce_rows(wg_out, wg_down), False)
+    scat_q1.plane(0)
+    grad_q, grad_kv = backward_attend(feed0[2], kept0, branch0, places, all_places, windows[0])
+    grad_q, grad_kv, red_g1, red_b1, *held = tie(
+        grad_q, grad_kv, red_g1, red_b1,
+        *scat_g0.values(), *scat_b0.values(), *scat_q1.values()
+    )
+    scat_g0.after(*held)
+    scat_b0.after(*held)
+    scat_q1.after(*held)
+    scat_q1.plane(1)
+    scat_g0.plane(0)
+    scat_b0.plane(0)
+    grad0, wg_q, gain_zero, head_grads = backward_keys(
+        query0, kept0, middle0, grad_q, grad_kv, *tables[0], first
+    )
+    red_q1 = scat_q1.along_z()
+    scat_q0 = Scatter(reduce_query(wg_q, [gain_zero] + norm_grads, head_grads), False)
+    scat_g0.plane(1)
+    scat_b0.plane(1)
+    scat_q0.plane(0)
+    scat_q0.plane(1)
+    red_g0, red_b0 = scat_g0.along_z(), scat_b0.along_z()
+    red_q0 = scat_q0.along_z()
     red_c0 = jnp.concatenate([red_q0, red_g0], axis=1)
+    red_c1 = jnp.concatenate([red_q1, red_g1], axis=1)
 
     out_moved = exchange(jnp.where(first, y1, grad0), "section", 1)
     c_keep, c_send = pick(first, red_c0, red_c1)

time: 617 us -> 630 us (1.021)
  waiting for transfers between devices: 277 us -> 200 us
  starting transfers between devices: 70.7 us -> 127 us
  other arithmetic: 92.6 us -> 115 us
  matrix products: 84.6 us -> 94.4 us
    ppermute x69 -> x98, waiting for transfers between devices: 277 us -> 200 us  [exchange(): return lax.ppermute(shard, axis, pairs)]
    ppermute x69 -> x98, starting transfers between devices: 70.7 us -> 127 us  [exchange(): return lax.ppermute(shard, axis, pairs)]
    convert_element_type x29 -> x33, other arithmetic: 10.9 us -> 31.5 us  [the longest x14 9.34 us: ctx_scatter(): buf = (keep.astype(F32) + recv.astype(F32)).astype(BF)]
    dot_general x16, matrix products: 28 us -> 36.1 us  [dot(): return jnp.dot(a, b, preferred_element_type=F32)]
    slice x30 -> x33, local copies, waits for them, and re-layouts: 15.9 us -> 10.2 us  [the longest x2 3.61 us: __init__(): buf[fs // 2:]]
    unnamed x493 -> x447, local copies, waits for them, and re-layouts: 21 us -> 17.6 us
    concatenate x32 -> x29, other arithmetic: 27.5 us -> 24.7 us  [the longest x15 13.9 us: ctx_gather(): jnp.concatenate([jnp.where(low, buf, recv), jnp.where(low, recv, buf)], a...]
  transfers between devices with their start and end apart: 69 -> 98, of which waited for: 27 -> 48; matrix products, arithmetic and copies ran while one was open for 31% -> 27% of each run, Pallas kernels for 0% -> 0%
where the time goes in v2:
time: 630 us; the launch traced here: 619 us
  waiting for transfers between devices  200 us (32%)
  starting transfers between devices  127 us (20%)
  other arithmetic  115 us (18%)
  matrix products  94.4 us (15%)
  local copies, waits for them, and re-layouts  77.6 us (12%)
    ppermute x98, waiting for transfers between devices, exchange(): return lax.ppermute(shard, axis, pairs)  200 us
    ppermute x98, starting transfers between devices, exchange(): return lax.ppermute(shard, axis, pairs)  127 us
    dot_general x16, matrix products, dot(): return jnp.dot(a, b, preferred_element_type=F32)  36.1 us
    dot_general x16, matrix products, dot_t(): return jnp.einsum('tc,dc->td', a, b, preferred_element_type=F32)  31.2 us
    dot_general x16, matrix products, t_dot(): return jnp.einsum('ta,tb->ab', a, b, preferred_element_type=F32)  27.1 us
    unnamed x447, local copies, waits for them, and re-layouts  17.6 us
    concatenate x15, other arithmetic, ctx_gather(): jnp.concatenate([jnp.where(low, buf, recv), jnp.where(low, recv, buf)], a...  13.9 us
  transfers between devices with their start and end apart: 98, of which 48 were waited for; matrix products, arithmetic and copies ran while one was open for 27% of the time, Pallas kernels for 0%

profile of v2, /device:TPU:0, one launch (start us, length us, event | category | flops | bytes accessed | tf_op | source)
XLA Modules:
  0.0 618.9 jit_solution(5612782638416806972)
XLA Ops:
  9.0 3.7 collective-permute-start.16
  14.4 2.9 collective-permute-start.3
  17.3 4.9 collective-permute-done.16
  22.2 3.8 collective-permute-start.4
  29.5 3.3 collective-permute-start.14
  32.7 5.8 collective-permute-start.12
  49.1 4.2 collective-permute-done.19
  54.3 4.0 collective-permute-start.26
  61.6 4.0 collective-permute-done.25
  67.1 8.3 %collective-permute-start.21 = (bf16[40,2048]{1,0:T(8,128)(2,1)S(1)}, bf16[40,2048]{1,0:T(8,128)(2,1)S(1)}, u32[]{:S(2)}, u32[]{:S(2)}) collective-permute-start(bf16[40,2048]{1,0:T(8,128)(2,1)S(1)} %slice.422), channel_id=1, source_target_pairs={{0,4},{4,0},{8,12},{12,8},{1,5},{5,1},{9,13},{13,9},{2,6},{6,2},{1... | collective-permute-start | bytes 491528 | tf_op jit(solution)/shard_map/ppermute | solution.py:31
  83.6 5.7 collective-permute-done.27
  96.1 5.5 collective-permute-done.6
  105.2 3.0 collective-permute-done.28
  109.4 3.0 collective-permute-done.30
  115.4 7.1 %collective-permute-done.32 = bf16[4,1,2,96,640]{4,3,2,1,0:T(8,128)(2,1)} collective-permute-done((bf16[4,1,2,96,640]{4,3,2,1,0:T(8,128)(2,1)}, bf16[4,1,2,96,640]{4,3,2,1,0:T(8,128)(2,1)}, u32[]{:S(2)}, u32[]{:S(2)}) %collective-permute-start.32) | collective-permute-done | bytes 983072 | tf_op jit(solution)/shard_map/ppermute | solution.py:31
  138.6 5.2 collective-permute-done.9
  158.6 5.6 collective-permute-done.34
  166.1 6.8 %collective-permute-done.36 = bf16[4,1,1,96,640]{4,3,2,1,0:T(8,128)(2,1)S(1)} collective-permute-done((bf16[4,1,1,96,640]{4,3,2,1,0:T(8,128)(2,1)S(1)}, bf16[4,1,1,96,640]{4,3,2,1,0:T(8,128)(2,1)S(1)}, u32[]{:S(2)}, u32[]{:S(2)}) %collective-permute-start.36) | collective-permute-done | bytes 491552 | tf_op jit(solution)/shard_map/ppermute | solution.py:31
  181.1 9.3 %collective-permute-done.39 = bf16[4,2,1,40,896]{4,3,2,1,0:T(8,128)(2,1)} collective-permute-done((bf16[4,2,1,40,896]{4,3,2,1,0:T(8,128)(2,1)}, bf16[4,2,1,40,896]{4,3,2,1,0:T(8,128)(2,1)}, u32[]{:S(2)}, u32[]{:S(2)}) %collective-permute-start.39) | collective-permute-done | bytes 573472 | tf_op jit(solution)/shard_map/ppermute | solution.py:31
  203.5 3.6 multiply_convert_fusion.5
  208.8 7.9 %collective-permute-done.42 = bf16[4,1,2,96,640]{4,3,2,1,0:T(8,128)(2,1)S(1)} collective-permute-done((bf16[4,1,2,96,640]{4,3,2,1,0:T(8,128)(2,1)S(1)}, bf16[4,1,2,96,640]{4,3,2,1,0:T(8,128)(2,1)S(1)}, u32[]{:S(2)}, u32[]{:S(2)}) %collective-permute-start.42) | collective-permute-done | bytes 983072 | tf_op jit(solution)/shard_map/ppermute | solution.py:31
  225.6 11.2 %fusion.37 = f32[256,768]{1,0:T(8,128)S(1)} fusion(bf16[640,896]{1,0:T(8,128)(2,1)} %bitcast.71, bf16[256,640]{1,0:T(8,128)(2,1)S(1)} %add_convert_fusion.20, f32[640]{0:T(1024)S(1)} %get-tuple-element.195, f32[256]{0:T(256)S(1)} %fusion.163), kind=kOutput, calls=%fused_computation.206 | convolution fusion | flops 252313600 | bytes 2100736 | tf_op jit(solution)/shard_map/dot_general | solution.py:189
  252.6 4.3 collective-permute-done.45
  273.3 3.3 multiply_convert_fusion.4
  284.3 3.2 fusion.89
  289.9 2.9 multiply_reduce_fusion.10
  301.2 3.7 multiply_reduce_fusion.1
  319.4 2.9 reshape.716
  324.5 5.2 collective-permute-done.50
  331.1 3.3 add_convert_fusion.3
  334.5 4.3 add_convert_fusion.1
  365.2 9.6 %collective-permute-done.54 = bf16[2,2,1,40,2048]{4,3,0,2,1:T(8,128)(2,1)} collective-permute-done((bf16[2,2,1,40,2048]{4,3,0,2,1:T(8,128)(2,1)}, bf16[2,2,1,40,2048]{4,3,0,2,1:T(8,128)(2,1)}, u32[]{:S(2)}, u32[]{:S(2)}) %collective-permute-start.54) | collective-permute-done | bytes 655392 | tf_op jit(solution)/shard_map/ppermute | solution.py:31
  377.5 17.4 %collective-permute-done.56 = bf16[4,2,1,96,640]{4,3,2,1,0:T(8,128)(2,1)} collective-permute-done((bf16[4,2,1,96,640]{4,3,2,1,0:T(8,128)(2,1)}, bf16[4,2,1,96,640]{4,3,2,1,0:T(8,128)(2,1)}, u32[]{:S(2)}, u32[]{:S(2)}) %collective-permute-start.56) | collective-permute-done | bytes 983072 | tf_op jit(solution)/shard_map/ppermute | solution.py:31
  402.6 3.2 fusion.91
  418.6 3.4 collective-permute-done.57
  422.2 8.5 %collective-permute-done.59 = bf16[4,1,1,96,640]{4,3,2,1,0:T(8,128)(2,1)S(1)} collective-permute-done((bf16[4,1,1,96,640]{4,3,2,1,0:T(8,128)(2,1)S(1)}, bf16[4,1,1,96,640]{4,3,2,1,0:T(8,128)(2,1)S(1)}, u32[]{:S(2)}, u32[]{:S(2)}) %collective-permute-start.59) | collective-permute-done | bytes 491552 | tf_op jit(solution)/shard_map/ppermute | solution.py:31
  435.9 3.5 multiply_reduce_fusion
  441.3 3.1 collective-permute-start.66
  472.5 4.0 collective-permute-done.65
  483.9 3.2 collective-permute-done.61
  488.2 8.9 %collective-permute-done.72 = bf16[4,2,1,40,896]{4,3,2,1,0:T(8,128)(2,1)S(1)} collective-permute-done((bf16[4,2,1,40,896]{4,3,2,1,0:T(8,128)(2,1)}, bf16[4,2,1,40,896]{4,3,2,1,0:T(8,128)(2,1)S(1)}, u32[]{:S(2)}, u32[]{:S(2)}) %collective-permute-start.72) | collective-permute-done | bytes 573472 | tf_op jit(solution)/shard_map/ppermute | solution.py:31
  533.3 4.4 collective-permute-start.90
  547.1 11.3 %collective-permute-done.82 = bf16[2,1,2,40,2048]{4,3,0,2,1:T(8,128)(2,1)S(1)} collective-permute-done((bf16[2,1,2,40,2048]{4,3,0,2,1:T(8,128)(2,1)S(1)}, bf16[2,1,2,40,2048]{4,3,0,2,1:T(8,128)(2,1)S(1)}, u32[]{:S(2)}, u32[]{:S(2)}) %collective-permute-start.82) | collective-permute-done | bytes 655392 | tf_op jit(solution)/shard_map/ppermute | solution.py:31
  562.7 12.0 %collective-permute-done.83 = bf16[2,1,1,40,2048]{4,3,0,2,1:T(8,128)(2,1)S(1)} collective-permute-done((bf16[2,1,1,40,2048]{4,3,0,2,1:T(8,128)(2,1)S(1)}, bf16[2,1,1,40,2048]{4,3,0,2,1:T(8,128)(2,1)S(1)}, u32[]{:S(2)}, u32[]{:S(2)}) %collective-permute-start.83) | collective-permute-done | bytes 327712 | tf_op jit(solution)/shard_map/ppermute | solution.py:31
  584.0 6.6 %collective-permute-done.85 = bf16[40,2048]{1,0:T(8,128)(2,1)S(1)} collective-permute-done((bf16[40,2048]{1,0:T(8,128)(2,1)S(1)}, bf16[40,2048]{1,0:T(8,128)(2,1)S(1)}, u32[]{:S(2)}, u32[]{:S(2)}) %collective-permute-start.85) | collective-permute-done | bytes 163872 | tf_op jit(solution)/shard_map/ppermute | solution.py:31
  590.8 3.2 collective-permute-done.75
  603.1 4.2 collective-permute-start.77
  607.3 3.7 collective-permute-done.95
  (962 shorter events, 351.7 us)
Async XLA Ops:
  5.7 34.5 %collective-permute-start = (bf16[256,640]{1,0:T(8,128)(2,1)S(1)}, bf16[256,640]{1,0:T(8,128)(2,1)S(1)}, u32[]{:S(2)}, u32[]{:S(2)}) collective-permute-start(bf16[256,640]{1,0:T(8,128)(2,1)S(1)} %dynamic-slice_bitcast_fusion.8), channel_id=1, source_target_pairs={{0,16},{16,0},{1,17},{17,1},{2,18},{18,2},{3,19},{19,3},{4,20},{20... | collective-permute-start | bytes 983048 | tf_op jit(solution)/shard_map/ppermute | solution.py:31
  14.4 15.0 %collective-permute-start.3 = (bf16[40,896]{1,0:T(8,128)(2,1)S(1)}, bf16[40,896]{1,0:T(8,128)(2,1)S(1)}, u32[]{:S(2)}, u32[]{:S(2)}) collective-permute-start(bf16[40,896]{1,0:T(8,128)(2,1)S(1)} %slice.402), channel_id=1, source_target_pairs={{0,8},{4,12},{8,0},{12,4},{1,9},{5,13},{9,1},{13,5},{2,10},{6,14},... | collective-permute-start | bytes 215048 | tf_op jit(solution)/shard_map/ppermute | solution.py:31
  27.0 15.1 %collective-permute-start.13 = (bf16[40,2048]{1,0:T(8,128)(2,1)S(1)}, bf16[40,2048]{1,0:T(8,128)(2,1)S(1)}, u32[]{:S(2)}, u32[]{:S(2)}) collective-permute-start(bf16[40,2048]{1,0:T(8,128)(2,1)S(1)} %slice.423), channel_id=1, source_target_pairs={{0,8},{4,12},{8,0},{12,4},{1,9},{5,13},{9,1},{13,5},{2,10},{6,14},... | collective-permute-start | bytes 491528 | tf_op jit(solution)/shard_map/ppermute | solution.py:31
  38.5 55.8 %collective-permute-start.31 = (bf16[4,1,1,96,640]{4,3,2,1,0:T(8,128)(2,1)S(1)}, bf16[4,1,1,96,640]{4,3,2,1,0:T(8,128)(2,1)S(1)}, u32[]{:S(2)}, u32[]{:S(2)}) collective-permute-start(bf16[4,1,1,96,640]{4,3,2,1,0:T(8,128)(2,1)S(1)} %maximum_bitcast_fusion.1), channel_id=1, source_target_pairs={{0,1},{1,0},{2,3},{3,2},{4,5},{5,4},{6,7},{7,6},{8,9},{9,8},{10,11... | collective-permute-start | bytes 1474568 | tf_op jit(solution)/shard_map/ppermute | solution.py:31
  40.2 42.6 %collective-permute-start.5 = (bf16[4,1,1,40,896]{4,3,2,1,0:T(8,128)(2,1)S(1)}, bf16[4,1,1,40,896]{4,3,2,1,0:T(8,128)(2,1)S(1)}, u32[]{:S(2)}, u32[]{:S(2)}) collective-permute-start(bf16[4,1,1,40,896]{4,3,2,1,0:T(8,128)(2,1)S(1)} %maximum_bitcast_fusion.8), channel_id=1, source_target_pairs={{0,2},{1,3},{2,0},{3,1},{4,6},{5,7},{6,4},{7,5},{8,10},{9,11},{10,... | collective-permute-start | bytes 860168 | tf_op jit(solution)/shard_map/ppermute | solution.py:31
  65.6 14.7 %collective-permute-start.23 = (bf16[40,2048]{1,0:T(8,128)(2,1)S(1)}, bf16[40,2048]{1,0:T(8,128)(2,1)S(1)}, u32[]{:S(2)}, u32[]{:S(2)}) collective-permute-start(bf16[40,2048]{1,0:T(8,128)(2,1)S(1)} %slice.422), channel_id=1, source_target_pairs={{0,12},{4,8},{8,4},{12,0},{1,13},{5,9},{9,5},{13,1},{2,14},{6,10},... | collective-permute-start | bytes 491528 | tf_op jit(solution)/shard_map/ppermute | solution.py:31
  67.1 14.6 %collective-permute-start.21 = (bf16[40,2048]{1,0:T(8,128)(2,1)S(1)}, bf16[40,2048]{1,0:T(8,128)(2,1)S(1)}, u32[]{:S(2)}, u32[]{:S(2)}) collective-permute-start(bf16[40,2048]{1,0:T(8,128)(2,1)S(1)} %slice.422), channel_id=1, source_target_pairs={{0,4},{4,0},{8,12},{12,8},{1,5},{5,1},{9,13},{13,9},{2,6},{6,2},{1... | collective-permute-start | bytes 491528 | tf_op jit(solution)/shard_map/ppermute | solution.py:31
  82.9 18.6 %collective-permute-start.6 = (bf16[4,2,1,40,896]{4,3,2,1,0:T(8,128)(2,1)S(1)}, bf16[4,2,1,40,896]{4,3,2,1,0:T(8,128)(2,1)S(1)}, u32[]{:S(2)}, u32[]{:S(2)}) collective-permute-start(bf16[4,2,1,40,896]{4,3,2,1,0:T(8,128)(2,1)S(1)} %pad_maximum_fusion.36), channel_id=1, source_target_pairs={{0,1},{1,0},{2,3},{3,2},{4,5},{5,4},{6,7},{7,6},{8,9},{9,8},{10,11... | collective-permute-start | bytes 1720328 | tf_op jit(solution)/shard_map/ppermute | solution.py:31
  90.2 18.0 %collective-permute-start.28 = (bf16[2,1,2,40,2048]{4,3,0,2,1:T(8,128)(2,1)}, bf16[2,1,2,40,2048]{4,3,0,2,1:T(8,128)(2,1)}, u32[]{:S(2)}, u32[]{:S(2)}) collective-permute-start(bf16[2,1,2,40,2048]{4,3,0,2,1:T(8,128)(2,1)} %pad_maximum_fusion.32), channel_id=1, source_target_pairs={{0,2},{1,3},{2,0},{3,1},{4,6},{5,7},{6,4},{7,5},{8,10},{9,11},{10,... | collective-permute-start | bytes 1966088 | tf_op jit(solution)/shard_map/ppermute | solution.py:31
  92.9 19.5 %collective-permute-start.30 = (bf16[2,2,1,40,2048]{4,3,0,2,1:T(8,128)(2,1)}, bf16[2,2,1,40,2048]{4,3,0,2,1:T(8,128)(2,1)}, u32[]{:S(2)}, u32[]{:S(2)}) collective-permute-start(bf16[2,2,1,40,2048]{4,3,0,2,1:T(8,128)(2,1)} %pad_maximum_fusion.33), channel_id=1, source_target_pairs={{0,1},{1,0},{2,3},{3,2},{4,5},{5,4},{6,7},{7,6},{8,9},{9,8},{10,11... | collective-permute-start | bytes 1966088 | tf_op jit(solution)/shard_map/ppermute | solution.py:31
  95.6 26.9 %collective-permute-start.32 = (bf16[4,1,2,96,640]{4,3,2,1,0:T(8,128)(2,1)}, bf16[4,1,2,96,640]{4,3,2,1,0:T(8,128)(2,1)}, u32[]{:S(2)}, u32[]{:S(2)}) collective-permute-start(bf16[4,1,2,96,640]{4,3,2,1,0:T(8,128)(2,1)} %pad_maximum_fusion.30), channel_id=1, source_target_pairs={{0,2},{1,3},{2,0},{3,1},{4,6},{5,7},{6,4},{7,5},{8,10},{9,11},{10,... | collective-permute-start | bytes 2949128 | tf_op jit(solution)/shard_map/ppermute | solution.py:31
  101.9 22.3 %collective-permute-start.7 = (bf16[16,40,896]{2,1,0:T(8,128)(2,1)S(1)}, bf16[16,40,896]{2,1,0:T(8,128)(2,1)}, u32[]{:S(2)}, u32[]{:S(2)}) collective-permute-start(bf16[16,40,896]{2,1,0:T(8,128)(2,1)S(1)} %bitcast.370), channel_id=1, source_target_pairs={{0,16},{16,0},{1,17},{17,1},{2,18},{18,2},{3,19},{19,3},{4,20},{20... | collective-permute-start | bytes 3440648 | tf_op jit(solution)/shard_map/ppermute | solution.py:31
  124.1 70.2 %collective-permute-start.37 = (bf16[16,96,640]{2,1,0:T(8,128)(2,1)S(1)}, bf16[16,96,640]{2,1,0:T(8,128)(2,1)}, u32[]{:S(2)}, u32[]{:S(2)}) collective-permute-start(bf16[16,96,640]{2,1,0:T(8,128)(2,1)S(1)} %bitcast.354), channel_id=1, source_target_pairs={{0,16},{16,0},{1,17},{17,1},{2,18},{18,2},{3,19},{19,3},{4,20},{20... | collective-permute-start | bytes 5898248 | tf_op jit(solution)/shard_map/ppermute | solution.py:31
  130.0 13.9 %collective-permute-start.9 = (bf16[256,512]{1,0:T(8,128)(2,1)}, bf16[256,512]{1,0:T(8,128)(2,1)}, u32[]{:S(2)}, u32[]{:S(2)}) collective-permute-start(bf16[256,512]{1,0:T(8,128)(2,1)} %pad_maximum_fusion.50), channel_id=1, source_target_pairs={{0,2},{1,3},{2,0},{3,1},{4,6},{5,7},{6,4},{7,5},{8,10},{9,11},{10,... | collective-permute-start | bytes 786440 | tf_op jit(solution)/shard_map/ppermute | solution.py:31
  155.4 17.6 %collective-permute-start.36 = (bf16[4,1,1,96,640]{4,3,2,1,0:T(8,128)(2,1)S(1)}, bf16[4,1,1,96,640]{4,3,2,1,0:T(8,128)(2,1)S(1)}, u32[]{:S(2)}, u32[]{:S(2)}) collective-permute-start(bf16[4,1,1,96,640]{4,3,2,1,0:T(8,128)(2,1)S(1)} %copy-done.87), channel_id=1, source_target_pairs={{0,1},{1,0},{2,3},{3,2},{4,5},{5,4},{6,7},{7,6},{8,9},{9,8},{10,11... | collective-permute-start | bytes 1474568 | tf_op jit(solution)/shard_map/ppermute | solution.py:31
  174.2 16.2 %collective-permute-start.39 = (bf16[4,2,1,40,896]{4,3,2,1,0:T(8,128)(2,1)}, bf16[4,2,1,40,896]{4,3,2,1,0:T(8,128)(2,1)}, u32[]{:S(2)}, u32[]{:S(2)}) collective-permute-start(bf16[4,2,1,40,896]{4,3,2,1,0:T(8,128)(2,1)} %pad_maximum_fusion.37), channel_id=1, source_target_pairs={{0,1},{1,0},{2,3},{3,2},{4,5},{5,4},{6,7},{7,6},{8,9},{9,8},{10,11... | collective-permute-start | bytes 1720328 | tf_op jit(solution)/shard_map/ppermute | solution.py:31
  178.5 25.0 %collective-permute-start.38 = (bf16[16,40,2048]{2,1,0:T(8,128)(2,1)S(1)}, bf16[16,40,2048]{2,1,0:T(8,128)(2,1)S(1)}, u32[]{:S(2)}, u32[]{:S(2)}) collective-permute-start(bf16[16,40,2048]{2,1,0:T(8,128)(2,1)S(1)} %pad_maximum_fusion), channel_id=1, source_target_pairs={{0,16},{16,0},{1,17},{17,1},{2,18},{18,2},{3,19},{19,3},{4,20},{20... | collective-permute-start | bytes 7864328 | tf_op jit(solution)/shard_map/ppermute | solution.py:31
  179.3 21.3 %collective-permute-start.40 = (bf16[2,1,2,40,2048]{4,3,0,2,1:T(8,128)(2,1)S(1)}, bf16[2,1,2,40,2048]{4,3,0,2,1:T(8,128)(2,1)S(1)}, u32[]{:S(2)}, u32[]{:S(2)}) collective-permute-start(bf16[2,1,2,40,2048]{4,3,0,2,1:T(8,128)(2,1)S(1)} %copy-done.74), channel_id=1, source_target_pairs={{0,2},{1,3},{2,0},{3,1},{4,6},{5,7},{6,4},{7,5},{8,10},{9,11},{10,... | collective-permute-start | bytes 1966088 | tf_op jit(solution)/shard_map/ppermute | solution.py:31
  179.8 22.4 %collective-permute-start.41 = (bf16[2,2,1,40,2048]{4,3,0,2,1:T(8,128)(2,1)S(1)}, bf16[2,2,1,40,2048]{4,3,0,2,1:T(8,128)(2,1)S(1)}, u32[]{:S(2)}, u32[]{:S(2)}) collective-permute-start(bf16[2,2,1,40,2048]{4,3,0,2,1:T(8,128)(2,1)S(1)} %copy-done.73), channel_id=1, source_target_pairs={{0,1},{1,0},{2,3},{3,2},{4,5},{5,4},{6,7},{7,6},{8,9},{9,8},{10,11... | collective-permute-start | bytes 1966088 | tf_op jit(solution)/shard_map/ppermute | solution.py:31
  190.4 26.4 %collective-permute-start.42 = (bf16[4,1,2,96,640]{4,3,2,1,0:T(8,128)(2,1)S(1)}, bf16[4,1,2,96,640]{4,3,2,1,0:T(8,128)(2,1)S(1)}, u32[]{:S(2)}, u32[]{:S(2)}) collective-permute-start(bf16[4,1,2,96,640]{4,3,2,1,0:T(8,128)(2,1)S(1)} %copy-done.65), channel_id=1, source_target_pairs={{0,2},{1,3},{2,0},{3,1},{4,6},{5,7},{6,4},{7,5},{8,10},{9,11},{10,... | collective-permute-start | bytes 2949128 | tf_op jit(solution)/shard_map/ppermute | solution.py:31
  219.6 17.3 %collective-permute-start.43 = (bf16[16,40,896]{2,1,0:T(8,128)(2,1)}, bf16[16,40,896]{2,1,0:T(8,128)(2,1)}, u32[]{:S(2)}, u32[]{:S(2)}) collective-permute-start(bf16[16,40,896]{2,1,0:T(8,128)(2,1)} %bitcast.73), channel_id=1, source_target_pairs={{0,16},{16,0},{1,17},{17,1},{2,18},{18,2},{3,19},{19,3},{4,20},{20... | collective-permute-start | bytes 3440648 | tf_op jit(solution)/shard_map/ppermute | solution.py:31
  219.9 45.3 %collective-permute-start.47 = (bf16[16,96,640]{2,1,0:T(8,128)(2,1)}, bf16[16,96,640]{2,1,0:T(8,128)(2,1)}, u32[]{:S(2)}, u32[]{:S(2)}) collective-permute-start(bf16[16,96,640]{2,1,0:T(8,128)(2,1)} %bitcast.355), channel_id=1, source_target_pairs={{0,16},{16,0},{1,17},{17,1},{2,18},{18,2},{3,19},{19,3},{4,20},{20... | collective-permute-start | bytes 5898248 | tf_op jit(solution)/shard_map/ppermute | solution.py:31
  223.8 49.6 %collective-permute-start.48 = (bf16[16,40,2048]{2,1,0:T(8,128)(2,1)}, bf16[16,40,2048]{2,1,0:T(8,128)(2,1)}, u32[]{:S(2)}, u32[]{:S(2)}) collective-permute-start(bf16[16,40,2048]{2,1,0:T(8,128)(2,1)} %pad_maximum_fusion.2), channel_id=1, source_target_pairs={{0,16},{16,0},{1,17},{17,1},{2,18},{18,2},{3,19},{19,3},{4,20},{20... | collective-permute-start | bytes 7864328 | tf_op jit(solution)/shard_map/ppermute | solution.py:31
  242.9 14.1 %collective-permute-start.45 = (bf16[256,512]{1,0:T(8,128)(2,1)}, bf16[256,512]{1,0:T(8,128)(2,1)}, u32[]{:S(2)}, u32[]{:S(2)}) collective-permute-start(bf16[256,512]{1,0:T(8,128)(2,1)} %pad_maximum_fusion.51), channel_id=1, source_target_pairs={{0,2},{1,3},{2,0},{3,1},{4,6},{5,7},{6,4},{7,5},{8,10},{9,11},{10,... | collective-permute-start | bytes 786440 | tf_op jit(solution)/shard_map/ppermute | solution.py:31
  304.9 29.6 %collective-permute-start.52 = (bf16[640,2048]{1,0:T(8,128)(2,1)}, bf16[640,2048]{1,0:T(8,128)(2,1)}, u32[]{:S(2)}, u32[]{:S(2)}) collective-permute-start(bf16[640,2048]{1,0:T(8,128)(2,1)} %convolution_convert_fusion.3), channel_id=1, source_target_pairs={{0,16},{16,0},{1,17},{17,1},{2,18},{18,2},{3,19},{19,3},{4,20},{20... | collective-permute-start | bytes 7864328 | tf_op jit(solution)/shard_map/ppermute | solution.py:31
  309.0 22.1 %collective-permute-start.53 = (bf16[16,96,640]{2,1,0:T(8,128)(2,1)}, bf16[16,96,640]{2,1,0:T(8,128)(2,1)}, u32[]{:S(2)}, u32[]{:S(2)}) collective-permute-start(bf16[16,96,640]{2,1,0:T(8,128)(2,1)} %pad_maximum_fusion.8), channel_id=1, source_target_pairs={{0,16},{16,0},{1,17},{17,1},{2,18},{18,2},{3,19},{19,3},{4,20},{20... | collective-permute-start | bytes 5898248 | tf_op jit(solution)/shard_map/ppermute | solution.py:31
  315.4 14.3 %collective-permute-start.50 = (bf16[256,512]{1,0:T(8,128)(2,1)}, bf16[256,512]{1,0:T(8,128)(2,1)}, u32[]{:S(2)}, u32[]{:S(2)}) collective-permute-start(bf16[256,512]{1,0:T(8,128)(2,1)} %get-tuple-element.273), channel_id=1, source_target_pairs={{0,2},{1,3},{2,0},{3,1},{4,6},{5,7},{6,4},{7,5},{8,10},{9,11},{10,... | collective-permute-start | bytes 786440 | tf_op jit(solution)/shard_map/ppermute | solution.py:31
  316.0 13.7 %collective-permute-start.49 = (bf16[256,512]{1,0:T(8,128)(2,1)}, bf16[256,512]{1,0:T(8,128)(2,1)}, u32[]{:S(2)}, u32[]{:S(2)}) collective-permute-start(bf16[256,512]{1,0:T(8,128)(2,1)} %get-tuple-element.271), channel_id=1, source_target_pairs={{0,1},{1,0},{2,3},{3,2},{4,5},{5,4},{6,7},{7,6},{8,9},{9,8},{10,11... | collective-permute-start | bytes 786440 | tf_op jit(solution)/shard_map/ppermute | solution.py:31
  356.9 17.9 %collective-permute-start.54 = (bf16[2,2,1,40,2048]{4,3,0,2,1:T(8,128)(2,1)}, bf16[2,2,1,40,2048]{4,3,0,2,1:T(8,128)(2,1)}, u32[]{:S(2)}, u32[]{:S(2)}) collective-permute-start(bf16[2,2,1,40,2048]{4,3,0,2,1:T(8,128)(2,1)} %constant_dynamic-slice_fusion.15), channel_id=1, source_target_pairs={{0,1},{1,0},{2,3},{3,2},{4,5},{5,4},{6,7},{7,6},{8,9},{9,8},{10,11... | collective-permute-start | bytes 1966088 | tf_op jit(solution)/shard_map/ppermute | solution.py:31
  358.2 17.9 %collective-permute-start.55 = (bf16[2,1,2,40,2048]{4,3,0,2,1:T(8,128)(2,1)}, bf16[2,1,2,40,2048]{4,3,0,2,1:T(8,128)(2,1)}, u32[]{:S(2)}, u32[]{:S(2)}) collective-permute-start(bf16[2,1,2,40,2048]{4,3,0,2,1:T(8,128)(2,1)} %constant_dynamic-slice_fusion.14), channel_id=1, source_target_pairs={{0,2},{1,3},{2,0},{3,1},{4,6},{5,7},{6,4},{7,5},{8,10},{9,11},{10,... | collective-permute-start | bytes 1966088 | tf_op jit(solution)/shard_map/ppermute | solution.py:31
  360.7 34.3 %collective-permute-start.56 = (bf16[4,2,1,96,640]{4,3,2,1,0:T(8,128)(2,1)}, bf16[4,2,1,96,640]{4,3,2,1,0:T(8,128)(2,1)}, u32[]{:S(2)}, u32[]{:S(2)}) collective-permute-start(bf16[4,2,1,96,640]{4,3,2,1,0:T(8,128)(2,1)} %constant_dynamic-slice_fusion.13), channel_id=1, source_target_pairs={{0,1},{1,0},{2,3},{3,2},{4,5},{5,4},{6,7},{7,6},{8,9},{9,8},{10,11... | collective-permute-start | bytes 2949128 | tf_op jit(solution)/shard_map/ppermute | solution.py:31
  413.3 17.4 %collective-permute-start.59 = (bf16[4,1,1,96,640]{4,3,2,1,0:T(8,128)(2,1)S(1)}, bf16[4,1,1,96,640]{4,3,2,1,0:T(8,128)(2,1)S(1)}, u32[]{:S(2)}, u32[]{:S(2)}) collective-permute-start(bf16[4,1,1,96,640]{4,3,2,1,0:T(8,128)(2,1)S(1)} %constant_dynamic-slice_fusion.10), channel_id=1, source_target_pairs={{0,2},{1,3},{2,0},{3,1},{4,6},{5,7},{6,4},{7,5},{8,10},{9,11},{10,... | collective-permute-start | bytes 1474568 | tf_op jit(solution)/shard_map/ppermute | solution.py:31
  414.3 17.4 %collective-permute-start.60 = (bf16[640,896]{1,0:T(8,128)(2,1)S(1)}, bf16[640,896]{1,0:T(8,128)(2,1)S(1)}, u32[]{:S(2)}, u32[]{:S(2)}) collective-permute-start(bf16[640,896]{1,0:T(8,128)(2,1)S(1)} %fusion.23), channel_id=1, source_target_pairs={{0,16},{16,0},{1,17},{17,1},{2,18},{18,2},{3,19},{19,3},{4,20},{20... | collective-permute-start | bytes 3440648 | tf_op jit(solution)/shard_map/ppermute | solution.py:31
  441.3 27.7 %collective-permute-start.66 = (bf16[40,2048]{1,0:T(8,128)(2,1)}, bf16[40,2048]{1,0:T(8,128)(2,1)}, u32[]{:S(2)}, u32[]{:S(2)}) collective-permute-start(bf16[40,2048]{1,0:T(8,128)(2,1)} %get-tuple-element.291), channel_id=1, source_target_pairs={{0,12},{4,8},{8,4},{12,0},{1,13},{5,9},{9,5},{13,1},{2,14},{6,10},... | collective-permute-start | bytes 491528 | tf_op jit(solution)/shard_map/ppermute | solution.py:31
  445.8 15.9 %collective-permute-start.68 = (bf16[96,640]{1,0:T(8,128)(2,1)S(1)}, bf16[96,640]{1,0:T(8,128)(2,1)S(1)}, u32[]{:S(2)}, u32[]{:S(2)}) collective-permute-start(bf16[96,640]{1,0:T(8,128)(2,1)S(1)} %get-tuple-element.321), channel_id=1, source_target_pairs={{0,8},{4,12},{8,0},{12,4},{1,9},{5,13},{9,1},{13,5},{2,10},{6,14},... | collective-permute-start | bytes 368648 | tf_op jit(solution)/shard_map/ppermute | solution.py:31
  447.8 52.3 %collective-permute-start.70 = (bf16[640,2048]{1,0:T(8,128)(2,1)}, bf16[640,2048]{1,0:T(8,128)(2,1)}, u32[]{:S(2)}, u32[]{:S(2)}) collective-permute-start(bf16[640,2048]{1,0:T(8,128)(2,1)} %convolution_convert_fusion.1), channel_id=1, source_target_pairs={{0,16},{16,0},{1,17},{17,1},{2,18},{18,2},{3,19},{19,3},{4,20},{20... | collective-permute-start | bytes 7864328 | tf_op jit(solution)/shard_map/ppermute | solution.py:31
  451.5 46.6 %collective-permute-start.71 = (bf16[16,96,640]{2,1,0:T(8,128)(2,1)}, bf16[16,96,640]{2,1,0:T(8,128)(2,1)}, u32[]{:S(2)}, u32[]{:S(2)}) collective-permute-start(bf16[16,96,640]{2,1,0:T(8,128)(2,1)} %pad_maximum_fusion.9), channel_id=1, source_target_pairs={{0,16},{16,0},{1,17},{17,1},{2,18},{18,2},{3,19},{19,3},{4,20},{20... | collective-permute-start | bytes 5898248 | tf_op jit(solution)/shard_map/ppermute | solution.py:31
  457.8 20.7 %collective-permute-start.63 = (bf16[256,512]{1,0:T(8,128)(2,1)}, bf16[256,512]{1,0:T(8,128)(2,1)}, u32[]{:S(2)}, u32[]{:S(2)}) collective-permute-start(bf16[256,512]{1,0:T(8,128)(2,1)} %get-tuple-element.269), channel_id=1, source_target_pairs={{0,3},{1,2},{2,1},{3,0},{4,7},{5,6},{6,5},{7,4},{8,11},{9,10},{10,... | collective-permute-start | bytes 786440 | tf_op jit(solution)/shard_map/ppermute | solution.py:31
  478.5 18.6 %collective-permute-start.72 = (bf16[4,2,1,40,896]{4,3,2,1,0:T(8,128)(2,1)}, bf16[4,2,1,40,896]{4,3,2,1,0:T(8,128)(2,1)S(1)}, u32[]{:S(2)}, u32[]{:S(2)}) collective-permute-start(bf16[4,2,1,40,896]{4,3,2,1,0:T(8,128)(2,1)} %constant_dynamic-slice_fusion.9), channel_id=1, source_target_pairs={{0,1},{1,0},{2,3},{3,2},{4,5},{5,4},{6,7},{7,6},{8,9},{9,8},{10,11... | collective-permute-start | bytes 1720328 | tf_op jit(solution)/shard_map/ppermute | solution.py:31
  521.9 37.5 %collective-permute-start.73 = (f32[256,640]{1,0:T(8,128)}, f32[256,640]{1,0:T(8,128)}, u32[]{:S(2)}, u32[]{:S(2)}) collective-permute-start(f32[256,640]{1,0:T(8,128)} %get-tuple-element.236), channel_id=1, source_target_pairs={{0,16},{16,0},{1,17},{17,1},{2,18},{18,2},{3,19},{19,3},{4,20},{20... | collective-permute-start | bytes 1966088 | tf_op jit(solution)/shard_map/ppermute | solution.py:31
  524.2 20.0 %collective-permute-start.80 = (bf16[2,2,1,40,2048]{4,3,0,2,1:T(8,128)(2,1)}, bf16[2,2,1,40,2048]{4,3,0,2,1:T(8,128)(2,1)}, u32[]{:S(2)}, u32[]{:S(2)}) collective-permute-start(bf16[2,2,1,40,2048]{4,3,0,2,1:T(8,128)(2,1)} %constant_dynamic-slice_fusion.6), channel_id=1, source_target_pairs={{0,1},{1,0},{2,3},{3,2},{4,5},{5,4},{6,7},{7,6},{8,9},{9,8},{10,11... | collective-permute-start | bytes 1966088 | tf_op jit(solution)/shard_map/ppermute | solution.py:31
  540.7 17.7 %collective-permute-start.82 = (bf16[2,1,2,40,2048]{4,3,0,2,1:T(8,128)(2,1)S(1)}, bf16[2,1,2,40,2048]{4,3,0,2,1:T(8,128)(2,1)S(1)}, u32[]{:S(2)}, u32[]{:S(2)}) collective-permute-start(bf16[2,1,2,40,2048]{4,3,0,2,1:T(8,128)(2,1)S(1)} %copy-done.117), channel_id=1, source_target_pairs={{0,2},{1,3},{2,0},{3,1},{4,6},{5,7},{6,4},{7,5},{8,10},{9,11},{10,... | collective-permute-start | bytes 1966088 | tf_op jit(solution)/shard_map/ppermute | solution.py:31
  543.5 36.3 %collective-permute-start.74 = (bf16[640,896]{1,0:T(8,128)(2,1)S(1)}, bf16[640,896]{1,0:T(8,128)(2,1)S(1)}, u32[]{:S(2)}, u32[]{:S(2)}) collective-permute-start(bf16[640,896]{1,0:T(8,128)(2,1)S(1)} %fusion.21), channel_id=1, source_target_pairs={{0,16},{16,0},{1,17},{17,1},{2,18},{18,2},{3,19},{19,3},{4,20},{20... | collective-permute-start | bytes 3440648 | tf_op jit(solution)/shard_map/ppermute | solution.py:31
  543.5 35.9 %collective-permute-start.92 = (bf16[4,2,1,96,640]{4,3,2,1,0:T(8,128)(2,1)S(1)}, bf16[4,2,1,96,640]{4,3,2,1,0:T(8,128)(2,1)S(1)}, u32[]{:S(2)}, u32[]{:S(2)}) collective-permute-start(bf16[4,2,1,96,640]{4,3,2,1,0:T(8,128)(2,1)S(1)} %constant_dynamic-slice_fusion.1), channel_id=1, source_target_pairs={{0,1},{1,0},{2,3},{3,2},{4,5},{5,4},{6,7},{7,6},{8,9},{9,8},{10,11... | collective-permute-start | bytes 2949128 | tf_op jit(solution)/shard_map/ppermute | solution.py:31
  545.6 17.0 %collective-permute-start.81 = (bf16[2,1,1,40,2048]{4,3,0,2,1:T(8,128)(2,1)S(1)}, bf16[2,1,1,40,2048]{4,3,0,2,1:T(8,128)(2,1)S(1)}, u32[]{:S(2)}, u32[]{:S(2)}) collective-permute-start(bf16[2,1,1,40,2048]{4,3,0,2,1:T(8,128)(2,1)S(1)} %constant_dynamic-slice_fusion.5), channel_id=1, source_target_pairs={{0,2},{1,3},{2,0},{3,1},{4,6},{5,7},{6,4},{7,5},{8,10},{9,11},{10,... | collective-permute-start | bytes 983048 | tf_op jit(solution)/shard_map/ppermute | solution.py:31
  558.6 16.0 %collective-permute-start.83 = (bf16[2,1,1,40,2048]{4,3,0,2,1:T(8,128)(2,1)S(1)}, bf16[2,1,1,40,2048]{4,3,0,2,1:T(8,128)(2,1)S(1)}, u32[]{:S(2)}, u32[]{:S(2)}) collective-permute-start(bf16[2,1,1,40,2048]{4,3,0,2,1:T(8,128)(2,1)S(1)} %constant_dynamic-slice_fusion.3), channel_id=1, source_target_pairs={{0,1},{1,0},{2,3},{3,2},{4,5},{5,4},{6,7},{7,6},{8,9},{9,8},{10,11... | collective-permute-start | bytes 983048 | tf_op jit(solution)/shard_map/ppermute | solution.py:31
  580.2 13.7 %collective-permute-start.75 = (bf16[4,2,1,40,896]{4,3,2,1,0:T(8,128)(2,1)S(1)}, bf16[4,2,1,40,896]{4,3,2,1,0:T(8,128)(2,1)S(1)}, u32[]{:S(2)}, u32[]{:S(2)}) collective-permute-start(bf16[4,2,1,40,896]{4,3,2,1,0:T(8,128)(2,1)S(1)} %constant_dynamic-slice_fusion.8), channel_id=1, source_target_pairs={{0,1},{1,0},{2,3},{3,2},{4,5},{5,4},{6,7},{7,6},{8,9},{9,8},{10,11... | collective-permute-start | bytes 1720328 | tf_op jit(solution)/shard_map/ppermute | solution.py:31
  581.0 14.0 %collective-permute-start.93 = (bf16[4,1,1,96,640]{4,3,2,1,0:T(8,128)(2,1)S(1)}, bf16[4,1,1,96,640]{4,3,2,1,0:T(8,128)(2,1)S(1)}, u32[]{:S(2)}, u32[]{:S(2)}) collective-permute-start(bf16[4,1,1,96,640]{4,3,2,1,0:T(8,128)(2,1)S(1)} %constant_dynamic-slice_fusion), channel_id=1, source_target_pairs={{0,2},{1,3},{2,0},{3,1},{4,6},{5,7},{6,4},{7,5},{8,10},{9,11},{10,... | collective-permute-start | bytes 1474568 | tf_op jit(solution)/shard_map/ppermute | solution.py:31
  (271 other events, 2086.9 us)

commit v3 on v2

--- a/solution.py
+++ b/solution.py
@@ -19,6 +19,7 @@
 BASES = (math.log(10000.0), math.log(1000000.0))
 SCALE = 1.0 / math.sqrt(HD)
 BF = jnp.bfloat16
+GRID = ("fsdp", "ctx")
 F32 = jnp.float32
 
 
@@ -47,9 +48,12 @@
 
 def z_gather(block):
     count = lax.axis_size("fsdp")
-    pieces = [block] + [exchange(block, "fsdp", j) for j in range(1, count)]
+    pairs = [(i, (i + 1) % count) for i in range(count)]
+    pieces = [block]
+    for _ in range(count - 1):
+        pieces.append(lax.ppermute(pieces[-1], "fsdp", pairs))
     me = lax.axis_index("fsdp")
-    return jnp.stack([lax.select_n(me ^ at, *pieces) for at in range(count)])
+    return jnp.stack([lax.select_n((me - at) % count, *pieces) for at in range(count)])
 
 
 def ctx_open(buf):
@@ -220,6 +224,7 @@
 
 def key_return(blocks):
     count = lax.axis_size("ctx")
+    blocks = jnp.split(blocks, count, axis=0)
     total = blocks[0]
     for j in range(1, count):
         total = total + exchange(blocks[j].astype(BF), "ctx", j).astype(F32)
@@ -306,9 +311,12 @@
     grad_keys_all = t_dot(grad_scores, flat_queries) * SCALE
     grad_values_all = t_dot(prob_low, grad_mixed)
     blocks = jnp.concatenate([grad_keys_all, grad_values_all], axis=1)
-    grad_kv = key_return(jnp.split(blocks, lax.axis_size("ctx"), axis=0))
-    grad_queries = dot(grad_scores, all_keys) * SCALE
-    return grad_queries.reshape(tokens, HEADS, HD), grad_kv
+    return grad_scores, blocks
+
+
+def backward_queries(kept, grad_scores):
+    grad_queries = dot(grad_scores, kept["all_keys"]) * SCALE
+    return grad_queries.reshape(-1, HEADS, HD)
 
 
 def backward_keys(full, kept, grad_middle, grad_queries, grad_kv, cosine, sine_table, first):
@@ -442,83 +450,64 @@
     windows = (WIN, seq_length)
 
     gather0 = Gather(layer_cols[0], layer_rows[0])
-    gather1 = Gather(layer_cols[1], layer_rows[1])
     gather0.along_z()
-    gather1.after(*gather0.parts)
+    cols1, rows1, *gather0.parts = tie(layer_cols[1], layer_rows[1], *gather0.parts)
+    cols1 = lax.all_gather(cols1, GRID, axis=0)
+    rows1 = lax.all_gather(rows1, GRID, axis=0)
     gather0.plane(0)
     gather0.plane(1)
     pairs0 = gather0.pairs()
     query0 = query_side(pairs0[0])
     kept0 = forward_keys(query0, x0, *tables[0], first)
-    gather1.along_z()
-    kept0["all_keys"], *gather1.parts = tie(kept0["all_keys"], *gather1.parts, *gather0.parts)[:5]
     mixed = forward_attend(kept0, places, all_places, windows[0])
-    gather1.plane(0)
-    mixed, *gather1.parts = tie(mixed, *gather1.parts)
     feed0 = feed_side(*pairs0[1:], query0[2])
     y0 = forward_rest(feed0, kept0, mixed, first).astype(BF)
-    gather1.plane(1)
-    y0, *gather1.parts = tie(y0, *gather1.parts)
-    pairs1 = gather1.pairs()
-    query1 = query_side(pairs1[0])
+    cols1 = (cols1, exchange(cols1, "section", 1))
+    rows1 = (rows1, exchange(rows1, "section", 1))
+    query1 = query_side([v[..., :QP] for v in cols1])
     kept1 = forward_keys(query1, y0.astype(F32), *tables[1], first)
     mixed = forward_attend(kept1, places, all_places, windows[1])
-    feed1 = feed_side(*pairs1[1:], query1[2])
+    feed1 = feed_side([v[..., QP:] for v in cols1], rows1, query1[2])
     y1 = forward_rest(feed1, kept1, mixed, first)
 
     middle1, branch1, wg_g, wg_out, wg_down, norm_grads = backward_feed(
         feed1, kept1, cotangent, first
     )
-    wg_own, wg_oth, wg_out, wg_down = tie(wg_g[0], wg_g[1], wg_out, wg_down)
-    scat_g1 = Scatter(reduce_cols(wg_own, wg_oth), True)
-    scat_b1 = Scatter(reduce_rows(wg_out, wg_down), False)
-    grad_q, grad_kv = backward_attend(feed1[2], kept1, branch1, places, all_places, windows[1])
-    grad_q, grad_kv, *held = tie(grad_q, grad_kv, *scat_g1.values(), *scat_b1.values())
-    scat_g1.after(*held)
-    scat_b1.after(*held)
-    scat_g1.plane(0)
-    scat_b1.plane(0)
+    sum_g1 = reduce_cols(*wg_g)
+    sum_b1 = reduce_rows(wg_out, wg_down)
+    red_b1 = lax.psum_scatter(sum_b1, GRID, scatter_dimension=0).astype(F32)
+    scores1, kv_blocks = backward_attend(feed1[2], kept1, branch1, places, all_places, windows[1])
+    scores1, kv_blocks, sum_g1 = tie(scores1, kv_blocks, sum_g1)
+    grad_kv = key_return(kv_blocks)
+    grad_q = backward_queries(kept1, scores1)
     grad1, wg_q, gain_zero, head_grads = backward_keys(
         query1, kept1, middle1, grad_q, grad_kv, *tables[1], first
     )
+    sum_q1 = reduce_query(wg_q, [gain_zero] + norm_grads, head_grads)
+    sum_c1 = jnp.concatenate([sum_q1, sum_g1], axis=-1)
+    red_c1 = lax.psum_scatter(sum_c1, GRID, scatter_dimension=0).astype(F32)
     grad1 = grad1.astype(BF)
-    wg_q0, wg_q1, grad1, *held = tie(wg_q[0], wg_q[1], grad1, *scat_g1.values(), *scat_b1.values())
-    scat_g1.after(*held)
-    scat_b1.after(*held)
-    scat_g1.plane(1)
-    scat_b1.plane(1)
-    scat_q1 = Scatter(reduce_query((wg_q0, wg_q1), [gain_zero] + norm_grads, head_grads), False)
 
     middle0, branch0, wg_g, wg_out, wg_down, norm_grads = backward_feed(
         feed0, kept0, grad1.astype(F32), first
     )
-    branch0, wg_own, wg_oth, wg_out, wg_down, *held = tie(
-        branch0, wg_g[0], wg_g[1], wg_out, wg_down,
-        *scat_g1.values(), *scat_b1.values(), *scat_q1.values()
-    )
-    scat_g1.after(*held)
-    scat_b1.after(*held)
-    scat_q1.after(*held)
-    red_g1, red_b1 = scat_g1.along_z(), scat_b1.along_z()
-    scat_g0 = Scatter(reduce_cols(wg_own, wg_oth), True)
+    scat_g0 = Scatter(reduce_cols(*wg_g), True)
     scat_b0 = Scatter(reduce_rows(wg_out, wg_down), False)
-    scat_q1.plane(0)
-    grad_q, grad_kv = backward_attend(feed0[2], kept0, branch0, places, all_places, windows[0])
-    grad_q, grad_kv, red_g1, red_b1, *held = tie(
-        grad_q, grad_kv, red_g1, red_b1,
-        *scat_g0.values(), *scat_b0.values(), *scat_q1.values()
-    )
+    scores0, kv_blocks = backward_attend(feed0[2], kept0, branch0, places, all_places, windows[0])
+    scores0, kv_blocks, *held = tie(scores0, kv_blocks, *scat_g0.values(), *scat_b0.values())
     scat_g0.after(*held)
     scat_b0.after(*held)
-    scat_q1.after(*held)
-    scat_q1.plane(1)
+    grad_kv = key_return(kv_blocks)
     scat_g0.plane(0)
     scat_b0.plane(0)
+    grad_q = backward_queries(kept0, scores0)
     grad0, wg_q, gain_zero, head_grads = backward_keys(
         query0, kept0, middle0, grad_q, grad_kv, *tables[0], first
     )
-    red_q1 = scat_q1.along_z()
-    scat_q0 = Scatter(reduce_query(wg_q, [gain_zero] + norm_grads, head_grads), False)
+    wg_q0, wg_q1, *held = tie(wg_q[0], wg_q[1], *scat_g0.values(), *scat_b0.values())
+    scat_g0.after(*held)
+    scat_b0.after(*held)
+    scat_q0 = Scatter(reduce_query((wg_q0, wg_q1), [gain_zero] + norm_grads, head_grads), False)
     scat_g0.plane(1)
     scat_b0.plane(1)
     scat_q0.plane(0)
@@ -526,7 +515,6 @@
     red_g0, red_b0 = scat_g0.along_z(), scat_b0.along_z()
     red_q0 = scat_q0.along_z()
     red_c0 = jnp.concatenate([red_q0, red_g0], axis=1)
-    red_c1 = jnp.concatenate([red_q1, red_g1], axis=1)
 
     out_moved = exchange(jnp.where(first, y1, grad0), "section", 1)
     c_keep, c_send = pick(first, red_c0, red_c1)

time: 630 us -> 556 us (0.88)
  starting transfers between devices: 127 us -> 79.2 us
  other arithmetic: 115 us -> 97.5 us
  between operations: 4.98 us -> 17.4 us
  matrix products: 94.4 us -> 83.7 us
  waiting for transfers between devices: 200 us -> 190 us
    ppermute x98 -> x54, waiting for transfers between devices: 200 us -> 126 us  [exchange(): return lax.ppermute(shard, axis, pairs)]
    ppermute x98 -> x54, starting transfers between devices: 127 us -> 69.2 us  [exchange(): return lax.ppermute(shard, axis, pairs)]
    all_gather x0 -> x2, waiting for transfers between devices: none -> 27.4 us  [the longest x1 27.4 us: local(): cols1 = lax.all_gather(cols1, GRID, axis=0)]
    ppermute x0 -> x9, waiting for transfers between devices: none -> 24 us  [z_gather(): pieces.append(lax.ppermute(pieces[-1], 'fsdp', pairs))]
    unnamed x0 -> x5, waiting for transfers between devices: none -> 13.5 us
    concatenate x15 -> x8, other arithmetic: 13.9 us -> 3.47 us  [ctx_gather(): jnp.concatenate([jnp.where(low, buf, recv), jnp.where(low, recv, buf)], a...]
    ppermute x0 -> x9, starting transfers between devices: none -> 9.26 us  [z_gather(): pieces.append(lax.ppermute(pieces[-1], 'fsdp', pairs))]
    convert_element_type x4 -> x1, other arithmetic: 8.9 us -> 0.86 us  [reduce_cols(): return summed.astype(BF).reshape(blocks, nr, -1)]
  transfers between devices with their start and end apart: 98 -> 67, of which waited for: 48 -> 31; matrix products, arithmetic and copies ran while one was open for 27% -> 37% of each run, Pallas kernels for 0% -> 0%
where the time goes in v3:
time: 556 us; the launch traced here: 549 us
  waiting for transfers between devices  190 us (34%)
  other arithmetic  97.5 us (18%)
  matrix products  83.7 us (15%)
  local copies, waits for them, and re-layouts  80.4 us (14%)
  starting transfers between devices  79.2 us (14%)
  between operations  17.4 us (3%)
    ppermute x54, waiting for transfers between devices, exchange(): return lax.ppermute(shard, axis, pairs)  126 us
    ppermute x54, starting transfers between devices, exchange(): return lax.ppermute(shard, axis, pairs)  69.2 us
    dot_general x16, matrix products, dot_t(): return jnp.einsum('tc,dc->td', a, b, preferred_element_type=F32)  29.2 us
    dot_general x16, matrix products, dot(): return jnp.dot(a, b, preferred_element_type=F32)  28.2 us
    all_gather x1, waiting for transfers between devices, local(): cols1 = lax.all_gather(cols1, GRID, axis=0)  27.4 us
    dot_general x16, matrix products, t_dot(): return jnp.einsum('ta,tb->ab', a, b, preferred_element_type=F32)  26.3 us
    ppermute x9, waiting for transfers between devices, z_gather(): pieces.append(lax.ppermute(pieces[-1], 'fsdp', pairs))  24 us
    unnamed x417, local copies, waits for them, and re-layouts  22.7 us
  transfers between devices with their start and end apart: 67, of which 31 were waited for; matrix products, arithmetic and copies ran while one was open for 37% of the time, Pallas kernels for 0%

profile of v3, /device:TPU:0, one launch (start us, length us, event | category | flops | bytes accessed | tf_op | source)
XLA Modules:
  0.0 548.7 jit_solution(10556219997173651954)
XLA Ops:
  14.7 3.0 collective-permute-start.9
  21.7 3.7 collective-permute-done.3
  26.8 4.8 collective-permute-done.4
  34.6 4.0 collective-permute-done.5
  38.6 3.3 collective-permute-done.7
  42.2 6.9 %collective-permute-done.8 = bf16[40,2048]{1,0:T(8,128)(2,1)S(1)} collective-permute-done((bf16[40,2048]{1,0:T(8,128)(2,1)S(1)}, bf16[40,2048]{1,0:T(8,128)(2,1)S(1)}, u32[]{:S(2)}, u32[]{:S(2)}) %collective-permute-start.8) | collective-permute-done | bytes 163872 | tf_op jit(solution)/shard_map/ppermute | solution.py:54
  57.4 5.9 %collective-permute-done.12 = bf16[4,1,1,40,896]{4,3,0,2,1:T(8,128)(2,1)S(1)} collective-permute-done((bf16[4,1,1,40,896]{4,3,0,2,1:T(8,128)(2,1)S(1)}, bf16[4,1,1,40,896]{4,3,0,2,1:T(8,128)(2,1)S(1)}, u32[]{:S(2)}, u32[]{:S(2)}) %collective-permute-start.12) | collective-permute-done | bytes 286752 | tf_op jit(solution)/shard_map/ppermute | solution.py:32
  64.9 13.1 %collective-permute-done.21 = bf16[2,1,1,40,2048]{4,3,0,2,1:T(8,128)(2,1)} collective-permute-done((bf16[2,1,1,40,2048]{4,3,0,2,1:T(8,128)(2,1)S(1)}, bf16[2,1,1,40,2048]{4,3,0,2,1:T(8,128)(2,1)}, u32[]{:S(2)}, u32[]{:S(2)}) %collective-permute-start.21) | collective-permute-done | bytes 327712 | tf_op jit(solution)/shard_map/ppermute | solution.py:32
  88.0 4.3 collective-permute-done.13
  96.2 4.3 collective-permute-done.22
  101.6 11.1 %collective-permute-done.24 = bf16[2,2,1,40,2048]{4,3,0,2,1:T(8,128)(2,1)} collective-permute-done((bf16[2,2,1,40,2048]{4,3,0,2,1:T(8,128)(2,1)}, bf16[2,2,1,40,2048]{4,3,0,2,1:T(8,128)(2,1)}, u32[]{:S(2)}, u32[]{:S(2)}) %collective-permute-start.24) | collective-permute-done | bytes 655392 | tf_op jit(solution)/shard_map/ppermute | solution.py:32
  116.1 6.7 %collective-permute-done.19 = bf16[4,1,2,96,640]{4,3,2,1,0:T(8,128)(2,1)} collective-permute-done((bf16[4,1,2,96,640]{4,3,2,1,0:T(8,128)(2,1)}, bf16[4,1,2,96,640]{4,3,2,1,0:T(8,128)(2,1)}, u32[]{:S(2)}, u32[]{:S(2)}) %collective-permute-start.19) | collective-permute-done | bytes 983072 | tf_op jit(solution)/shard_map/ppermute | solution.py:32
  131.2 2.6 collective-permute-start.15
  143.6 4.9 collective-permute-done.16
  155.0 3.5 broadcast_select_fusion.1
  165.1 27.4 %all-gather.5.cloned.1.call-done = bf16[640,2944]{1,0:T(8,128)(2,1)} async-done(((bf16[40,2944]{1,0:T(8,128)(2,1)}), bf16[640,2944]{1,0:T(8,128)(2,1)}) %all-gather.5.cloned.1.call-update) | async-done | bytes 3768336 | tf_op jit(solution)/shard_map/all_gather | solution.py:455
  195.2 2.7 fusion.176
  198.0 6.0 %multiply_convert_fusion.5 = (bf16[256,2048]{1,0:T(8,128)(2,1)S(1)}, f32[256,2048]{1,0:T(8,128)}, f32[256,2048]{1,0:T(8,128)}) fusion(f32[256,2048]{1,0:T(8,128)S(1)} %fusion.176, pred[]{:T(512)S(6)} %eq.28, bf16[256,640]{1,0:T(8,128)(2,1)S(1)} %multiply_convert_fusion.7, bf16[640,2048]{1,0:T(8,128)(2,1)} %bitcast.56), kind=kOutput, calls=%fused_computation.53 | convolution fusion | flops 677380096 | bytes 10289153 | tf_op jit(solution)/shard_map/dot_general | solution.py:193
  228.4 3.7 slice.445
  249.6 2.4 multiply_convert_fusion.3
  252.1 2.5 convolution_convert_fusion.3
  255.5 2.6 convolution_convert_fusion
  279.1 4.8 add_convert_fusion.1
  290.2 2.5 reshape.665
  312.6 3.2 fusion.84
  315.8 2.4 convolution_convert_fusion.2
  318.2 3.0 multiply_reduce_fusion.10
  329.0 5.2 multiply_reduce_fusion
  337.7 4.7 multiply_convert_fusion
  350.4 3.3 add_convert_fusion
  364.1 2.6 reshape.671
  375.7 13.4 %collective-permute-done.37 = bf16[256,512]{1,0:T(8,128)(2,1)} collective-permute-done((bf16[256,512]{1,0:T(8,128)(2,1)}, bf16[256,512]{1,0:T(8,128)(2,1)}, u32[]{:S(2)}, u32[]{:S(2)}) %collective-permute-start.37) | collective-permute-done | bytes 262176 | tf_op jit(solution)/shard_map/ppermute | solution.py:32
  390.1 5.3 collective-permute-done.39
  399.5 3.2 fusion.55
  410.9 2.4 add_convert_fusion.6
  423.1 2.7 fusion.160
  428.1 2.4 maximum_select_fusion
  431.9 12.3 %collective-permute-done.51 = bf16[2,1,1,40,2048]{4,3,0,2,1:T(8,128)(2,1)S(1)} collective-permute-done((bf16[2,1,1,40,2048]{4,3,0,2,1:T(8,128)(2,1)S(1)}, bf16[2,1,1,40,2048]{4,3,0,2,1:T(8,128)(2,1)S(1)}, u32[]{:S(2)}, u32[]{:S(2)}) %collective-permute-start.51) | collective-permute-done | bytes 327712 | tf_op jit(solution)/shard_map/ppermute | solution.py:32
  446.4 2.6 collective-permute-start.53
  451.7 6.3 %collective-permute-start.57 = (bf16[4,1,1,96,640]{4,3,2,1,0:T(8,128)(2,1)S(1)}, bf16[4,1,1,96,640]{4,3,2,1,0:T(8,128)(2,1)S(1)}, u32[]{:S(2)}, u32[]{:S(2)}) collective-permute-start(bf16[4,1,1,96,640]{4,3,2,1,0:T(8,128)(2,1)S(1)} %constant_dynamic-slice_fusion), channel_id=1, source_target_pairs={{0,2},{1,3},{2,0},{3,1},{4,6},{5,7},{6,4},{7,5},{8,10},{9,11},{10,... | collective-permute-start | bytes 1474568 | tf_op jit(solution)/shard_map/ppermute | solution.py:32
  459.7 6.2 %collective-permute-done.54 = bf16[40,2048]{1,0:T(8,128)(2,1)S(1)} collective-permute-done((bf16[40,2048]{1,0:T(8,128)(2,1)S(1)}, bf16[40,2048]{1,0:T(8,128)(2,1)S(1)}, u32[]{:S(2)}, u32[]{:S(2)}) %collective-permute-start.54) | collective-permute-done | bytes 163872 | tf_op jit(solution)/shard_map/ppermute | solution.py:32
  466.0 15.6 %collective-permute-done.45 = bf16[4,2,1,40,896]{4,3,2,1,0:T(8,128)(2,1)S(1)} collective-permute-done((bf16[4,2,1,40,896]{4,3,2,1,0:T(8,128)(2,1)S(1)}, bf16[4,2,1,40,896]{4,3,2,1,0:T(8,128)(2,1)S(1)}, u32[]{:S(2)}, u32[]{:S(2)}) %collective-permute-start.45) | collective-permute-done | bytes 573472 | tf_op jit(solution)/shard_map/ppermute | solution.py:32
  481.8 14.7 %collective-permute-start.46 = (bf16[4,1,1,40,896]{4,3,2,1,0:T(8,128)(2,1)S(1)}, bf16[4,1,1,40,896]{4,3,2,1,0:T(8,128)(2,1)S(1)}, u32[]{:S(2)}, u32[]{:S(2)}) collective-permute-start(bf16[4,1,1,40,896]{4,3,2,1,0:T(8,128)(2,1)S(1)} %constant_dynamic-slice_fusion.3), channel_id=1, source_target_pairs={{0,2},{1,3},{2,0},{3,1},{4,6},{5,7},{6,4},{7,5},{8,10},{9,11},{10,... | collective-permute-start | bytes 860168 | tf_op jit(solution)/shard_map/ppermute | solution.py:32
  498.1 3.0 collective-permute-start.60
  501.1 6.2 %collective-permute-done.46 = bf16[4,1,1,40,896]{4,3,2,1,0:T(8,128)(2,1)S(1)} collective-permute-done((bf16[4,1,1,40,896]{4,3,2,1,0:T(8,128)(2,1)S(1)}, bf16[4,1,1,40,896]{4,3,2,1,0:T(8,128)(2,1)S(1)}, u32[]{:S(2)}, u32[]{:S(2)}) %collective-permute-start.46) | collective-permute-done | bytes 286752 | tf_op jit(solution)/shard_map/ppermute | solution.py:32
  507.6 4.3 collective-permute-start.49
  514.8 6.9 %collective-permute-done.48 = bf16[40,896]{1,0:T(8,128)(2,1)S(1)} collective-permute-done((bf16[40,896]{1,0:T(8,128)(2,1)S(1)}, bf16[40,896]{1,0:T(8,128)(2,1)S(1)}, u32[]{:S(2)}, u32[]{:S(2)}) %collective-permute-start.48) | collective-permute-done | bytes 71712 | tf_op jit(solution)/shard_map/ppermute | solution.py:32
  521.7 13.5 %reduce-scatter.8.cloned.1.call-done = bf16[1,40,2944]{2,1,0:T(8,128)(2,1)} async-done(((bf16[16,40,2944]{2,1,0:T(8,128)(2,1)}), bf16[1,40,2944]{2,1,0:T(8,128)(2,1)}) %reduce-scatter.8.cloned.1.call-update) | async-done | bytes 235536
  (824 shorter events, 249.4 us)
Async XLA Ops:
  7.2 135.1 %all-gather.7.cloned.1.call-start = ((), (), s32[]{:S(2)}) async-start(), calls=%async_computation.4 | async-start | bytes 2088960 | tf_op jit(solution)/shard_map/all_gather | solution.py:456
  20.1 12.8 %collective-permute-start.6 = (bf16[40,2048]{1,0:T(8,128)(2,1)S(1)}, bf16[40,2048]{1,0:T(8,128)(2,1)S(1)}, u32[]{:S(2)}, u32[]{:S(2)}) collective-permute-start(bf16[40,2048]{1,0:T(8,128)(2,1)S(1)} %slice.391), channel_id=1, source_target_pairs={{0,4},{4,8},{8,12},{12,0},{1,5},{5,9},{9,13},{13,1},{2,6},{6,10},{... | collective-permute-start | bytes 491528 | tf_op jit(solution)/shard_map/ppermute | solution.py:54
  49.3 143.2 %all-gather.5.cloned.1.call-start = ((), (), s32[]{:S(2)}) async-start(), calls=%async_computation.3 | async-start | bytes 4003840 | tf_op jit(solution)/shard_map/all_gather | solution.py:455
  54.5 29.4 %collective-permute-start.18 = (bf16[4,1,1,96,640]{4,3,2,1,0:T(8,128)(2,1)S(1)}, bf16[4,1,1,96,640]{4,3,2,1,0:T(8,128)(2,1)}, u32[]{:S(2)}, u32[]{:S(2)}) collective-permute-start(bf16[4,1,1,96,640]{4,3,2,1,0:T(8,128)(2,1)S(1)} %maximum_bitcast_fusion.1), channel_id=1, source_target_pairs={{0,1},{1,0},{2,3},{3,2},{4,5},{5,4},{6,7},{7,6},{8,9},{9,8},{10,11... | collective-permute-start | bytes 1474568 | tf_op jit(solution)/shard_map/ppermute | solution.py:32
  56.0 22.0 %collective-permute-start.21 = (bf16[2,1,1,40,2048]{4,3,0,2,1:T(8,128)(2,1)S(1)}, bf16[2,1,1,40,2048]{4,3,0,2,1:T(8,128)(2,1)}, u32[]{:S(2)}, u32[]{:S(2)}) collective-permute-start(bf16[2,1,1,40,2048]{4,3,0,2,1:T(8,128)(2,1)S(1)} %maximum_bitcast_fusion.2), channel_id=1, source_target_pairs={{0,1},{1,0},{2,3},{3,2},{4,5},{5,4},{6,7},{7,6},{8,9},{9,8},{10,11... | collective-permute-start | bytes 983048 | tf_op jit(solution)/shard_map/ppermute | solution.py:32
  56.6 23.4 %collective-permute-start.23 = (bf16[2,1,1,40,2048]{4,3,0,2,1:T(8,128)(2,1)S(1)}, bf16[2,1,1,40,2048]{4,3,0,2,1:T(8,128)(2,1)}, u32[]{:S(2)}, u32[]{:S(2)}) collective-permute-start(bf16[2,1,1,40,2048]{4,3,0,2,1:T(8,128)(2,1)S(1)} %maximum_bitcast_fusion.3), channel_id=1, source_target_pairs={{0,2},{1,3},{2,0},{3,1},{4,6},{5,7},{6,4},{7,5},{8,10},{9,11},{10,... | collective-permute-start | bytes 983048 | tf_op jit(solution)/shard_map/ppermute | solution.py:32
  57.1 454.8 %reduce-scatter.6.cloned.1.call-start = ((), (), s32[]{:S(2)}) async-start(), calls=%async_computation.2 | async-start | bytes 2088960 | tf_op jit(solution)/shard_map/reduce_scatter | solution.py:478
  63.4 28.9 %collective-permute-start.13 = (bf16[4,2,1,40,896]{4,3,0,2,1:T(8,128)(2,1)S(1)}, bf16[4,2,1,40,896]{4,3,0,2,1:T(8,128)(2,1)S(1)}, u32[]{:S(2)}, u32[]{:S(2)}) collective-permute-start(bf16[4,2,1,40,896]{4,3,0,2,1:T(8,128)(2,1)S(1)} %pad_maximum_fusion.29), channel_id=1, source_target_pairs={{0,1},{1,0},{2,3},{3,2},{4,5},{5,4},{6,7},{7,6},{8,9},{9,8},{10,11... | collective-permute-start | bytes 1720328 | tf_op jit(solution)/shard_map/ppermute | solution.py:32
  80.0 20.5 %collective-permute-start.22 = (bf16[2,1,2,40,2048]{4,3,0,2,1:T(8,128)(2,1)}, bf16[2,1,2,40,2048]{4,3,0,2,1:T(8,128)(2,1)}, u32[]{:S(2)}, u32[]{:S(2)}) collective-permute-start(bf16[2,1,2,40,2048]{4,3,0,2,1:T(8,128)(2,1)} %pad_maximum_fusion.27), channel_id=1, source_target_pairs={{0,2},{1,3},{2,0},{3,1},{4,6},{5,7},{6,4},{7,5},{8,10},{9,11},{10,... | collective-permute-start | bytes 1966088 | tf_op jit(solution)/shard_map/ppermute | solution.py:32
  81.9 30.8 %collective-permute-start.24 = (bf16[2,2,1,40,2048]{4,3,0,2,1:T(8,128)(2,1)}, bf16[2,2,1,40,2048]{4,3,0,2,1:T(8,128)(2,1)}, u32[]{:S(2)}, u32[]{:S(2)}) collective-permute-start(bf16[2,2,1,40,2048]{4,3,0,2,1:T(8,128)(2,1)} %pad_maximum_fusion.28), channel_id=1, source_target_pairs={{0,1},{1,0},{2,3},{3,2},{4,5},{5,4},{6,7},{7,6},{8,9},{9,8},{10,11... | collective-permute-start | bytes 1966088 | tf_op jit(solution)/shard_map/ppermute | solution.py:32
  86.1 36.8 %collective-permute-start.19 = (bf16[4,1,2,96,640]{4,3,2,1,0:T(8,128)(2,1)}, bf16[4,1,2,96,640]{4,3,2,1,0:T(8,128)(2,1)}, u32[]{:S(2)}, u32[]{:S(2)}) collective-permute-start(bf16[4,1,2,96,640]{4,3,2,1,0:T(8,128)(2,1)} %pad_maximum_fusion.26), channel_id=1, source_target_pairs={{0,2},{1,3},{2,0},{3,1},{4,6},{5,7},{6,4},{7,5},{8,10},{9,11},{10,... | collective-permute-start | bytes 2949128 | tf_op jit(solution)/shard_map/ppermute | solution.py:32
  93.7 30.9 %collective-permute-start.14 = (bf16[16,40,896]{2,1,0:T(8,128)(2,1)}, bf16[16,40,896]{2,1,0:T(8,128)(2,1)}, u32[]{:S(2)}, u32[]{:S(2)}) collective-permute-start(bf16[16,40,896]{2,1,0:T(8,128)(2,1)} %bitcast.42), channel_id=1, source_target_pairs={{0,16},{16,0},{1,17},{17,1},{2,18},{18,2},{3,19},{19,3},{4,20},{20... | collective-permute-start | bytes 3440648 | tf_op jit(solution)/shard_map/ppermute | solution.py:32
  124.5 30.5 %collective-permute-start.20 = (bf16[16,96,640]{2,1,0:T(8,128)(2,1)S(1)}, bf16[16,96,640]{2,1,0:T(8,128)(2,1)}, u32[]{:S(2)}, u32[]{:S(2)}) collective-permute-start(bf16[16,96,640]{2,1,0:T(8,128)(2,1)S(1)} %bitcast.275), channel_id=1, source_target_pairs={{0,16},{16,0},{1,17},{17,1},{2,18},{18,2},{3,19},{19,3},{4,20},{20... | collective-permute-start | bytes 5898248 | tf_op jit(solution)/shard_map/ppermute | solution.py:32
  131.2 12.4 %collective-permute-start.15 = (bf16[256,512]{1,0:T(8,128)(2,1)}, bf16[256,512]{1,0:T(8,128)(2,1)}, u32[]{:S(2)}, u32[]{:S(2)}) collective-permute-start(bf16[256,512]{1,0:T(8,128)(2,1)} %pad_maximum_fusion.41), channel_id=1, source_target_pairs={{0,1},{1,0},{2,3},{3,2},{4,5},{5,4},{6,7},{7,6},{8,9},{9,8},{10,11... | collective-permute-start | bytes 786440 | tf_op jit(solution)/shard_map/ppermute | solution.py:32
  133.8 14.7 %collective-permute-start.16 = (bf16[256,512]{1,0:T(8,128)(2,1)}, bf16[256,512]{1,0:T(8,128)(2,1)}, u32[]{:S(2)}, u32[]{:S(2)}) collective-permute-start(bf16[256,512]{1,0:T(8,128)(2,1)} %pad_maximum_fusion.41), channel_id=1, source_target_pairs={{0,2},{1,3},{2,0},{3,1},{4,6},{5,7},{6,4},{7,5},{8,10},{9,11},{10,... | collective-permute-start | bytes 786440 | tf_op jit(solution)/shard_map/ppermute | solution.py:32
  134.1 14.5 %collective-permute-start.17 = (bf16[256,512]{1,0:T(8,128)(2,1)}, bf16[256,512]{1,0:T(8,128)(2,1)}, u32[]{:S(2)}, u32[]{:S(2)}) collective-permute-start(bf16[256,512]{1,0:T(8,128)(2,1)} %pad_maximum_fusion.41), channel_id=1, source_target_pairs={{0,3},{1,2},{2,1},{3,0},{4,7},{5,6},{6,5},{7,4},{8,11},{9,10},{10,... | collective-permute-start | bytes 786440 | tf_op jit(solution)/shard_map/ppermute | solution.py:32
  142.3 12.7 %collective-permute-start.30 = (bf16[16,96,640]{2,1,0:T(8,128)(2,1)}, bf16[16,96,640]{2,1,0:T(8,128)(2,1)}, u32[]{:S(2)}, u32[]{:S(2)}) collective-permute-start(bf16[16,96,640]{2,1,0:T(8,128)(2,1)} %bitcast.300), channel_id=1, source_target_pairs={{0,16},{16,0},{1,17},{17,1},{2,18},{18,2},{3,19},{19,3},{4,20},{20... | collective-permute-start | bytes 5898248 | tf_op jit(solution)/shard_map/ppermute | solution.py:32
  143.5 54.4 %collective-permute-start.25 = (bf16[16,40,2048]{2,1,0:T(8,128)(2,1)}, bf16[16,40,2048]{2,1,0:T(8,128)(2,1)}, u32[]{:S(2)}, u32[]{:S(2)}) collective-permute-start(bf16[16,40,2048]{2,1,0:T(8,128)(2,1)} %pad_maximum_fusion.1), channel_id=1, source_target_pairs={{0,16},{16,0},{1,17},{17,1},{2,18},{18,2},{3,19},{19,3},{4,20},{20... | collective-permute-start | bytes 7864328 | tf_op jit(solution)/shard_map/ppermute | solution.py:32
  192.5 20.0 %collective-permute-start.26 = (bf16[16,40,2944]{2,1,0:T(8,128)(2,1)}, bf16[16,40,2944]{2,1,0:T(8,128)(2,1)}, u32[]{:S(2)}, u32[]{:S(2)}) collective-permute-start(bf16[16,40,2944]{2,1,0:T(8,128)(2,1)} %bitcast.289), channel_id=1, source_target_pairs={{0,16},{16,0},{1,17},{17,1},{2,18},{18,2},{3,19},{19,3},{4,20},{20... | collective-permute-start | bytes 11304968 | tf_op jit(solution)/shard_map/ppermute | solution.py:32
  217.1 15.4 %collective-permute-start.27 = (bf16[256,512]{1,0:T(8,128)(2,1)}, bf16[256,512]{1,0:T(8,128)(2,1)}, u32[]{:S(2)}, u32[]{:S(2)}) collective-permute-start(bf16[256,512]{1,0:T(8,128)(2,1)} %pad_maximum_fusion.42), channel_id=1, source_target_pairs={{0,1},{1,0},{2,3},{3,2},{4,5},{5,4},{6,7},{7,6},{8,9},{9,8},{10,11... | collective-permute-start | bytes 786440 | tf_op jit(solution)/shard_map/ppermute | solution.py:32
  218.4 14.1 %collective-permute-start.28 = (bf16[256,512]{1,0:T(8,128)(2,1)}, bf16[256,512]{1,0:T(8,128)(2,1)}, u32[]{:S(2)}, u32[]{:S(2)}) collective-permute-start(bf16[256,512]{1,0:T(8,128)(2,1)} %pad_maximum_fusion.42), channel_id=1, source_target_pairs={{0,2},{1,3},{2,0},{3,1},{4,6},{5,7},{6,4},{7,5},{8,10},{9,11},{10,... | collective-permute-start | bytes 786440 | tf_op jit(solution)/shard_map/ppermute | solution.py:32
  219.1 13.6 %collective-permute-start.29 = (bf16[256,512]{1,0:T(8,128)(2,1)}, bf16[256,512]{1,0:T(8,128)(2,1)}, u32[]{:S(2)}, u32[]{:S(2)}) collective-permute-start(bf16[256,512]{1,0:T(8,128)(2,1)} %pad_maximum_fusion.42), channel_id=1, source_target_pairs={{0,3},{1,2},{2,1},{3,0},{4,7},{5,6},{6,5},{7,4},{8,11},{9,10},{10,... | collective-permute-start | bytes 786440 | tf_op jit(solution)/shard_map/ppermute | solution.py:32
  263.7 15.4 %collective-permute-start.31 = (bf16[640,2048]{1,0:T(8,128)(2,1)}, bf16[640,2048]{1,0:T(8,128)(2,1)}, u32[]{:S(2)}, u32[]{:S(2)}) collective-permute-start(bf16[640,2048]{1,0:T(8,128)(2,1)} %convolution_convert_fusion.3), channel_id=1, source_target_pairs={{0,16},{16,0},{1,17},{17,1},{2,18},{18,2},{3,19},{19,3},{4,20},{20... | collective-permute-start | bytes 7864328 | tf_op jit(solution)/shard_map/ppermute | solution.py:32
  278.6 256.5 %reduce-scatter.8.cloned.1.call-start = ((), (), s32[]{:S(2)}) async-start(), calls=%async_computation.5 | async-start | bytes 4003840
  285.0 15.5 %collective-permute-start.32 = (bf16[256,512]{1,0:T(8,128)(2,1)}, bf16[256,512]{1,0:T(8,128)(2,1)}, u32[]{:S(2)}, u32[]{:S(2)}) collective-permute-start(bf16[256,512]{1,0:T(8,128)(2,1)} %get-tuple-element.194), channel_id=1, source_target_pairs={{0,1},{1,0},{2,3},{3,2},{4,5},{5,4},{6,7},{7,6},{8,9},{9,8},{10,11... | collective-permute-start | bytes 786440 | tf_op jit(solution)/shard_map/ppermute | solution.py:32
  286.1 14.3 %collective-permute-start.33 = (bf16[256,512]{1,0:T(8,128)(2,1)}, bf16[256,512]{1,0:T(8,128)(2,1)}, u32[]{:S(2)}, u32[]{:S(2)}) collective-permute-start(bf16[256,512]{1,0:T(8,128)(2,1)} %get-tuple-element.196), channel_id=1, source_target_pairs={{0,2},{1,3},{2,0},{3,1},{4,6},{5,7},{6,4},{7,5},{8,10},{9,11},{10,... | collective-permute-start | bytes 786440 | tf_op jit(solution)/shard_map/ppermute | solution.py:32
  287.2 14.0 %collective-permute-start.34 = (bf16[256,512]{1,0:T(8,128)(2,1)}, bf16[256,512]{1,0:T(8,128)(2,1)}, u32[]{:S(2)}, u32[]{:S(2)}) collective-permute-start(bf16[256,512]{1,0:T(8,128)(2,1)} %get-tuple-element.195), channel_id=1, source_target_pairs={{0,3},{1,2},{2,1},{3,0},{4,7},{5,6},{6,5},{7,4},{8,11},{9,10},{10,... | collective-permute-start | bytes 786440 | tf_op jit(solution)/shard_map/ppermute | solution.py:32
  328.1 20.1 %collective-permute-start.36 = (bf16[16,96,640]{2,1,0:T(8,128)(2,1)}, bf16[16,96,640]{2,1,0:T(8,128)(2,1)}, u32[]{:S(2)}, u32[]{:S(2)}) collective-permute-start(bf16[16,96,640]{2,1,0:T(8,128)(2,1)} %pad_maximum_fusion.7), channel_id=1, source_target_pairs={{0,16},{16,0},{1,17},{17,1},{2,18},{18,2},{3,19},{19,3},{4,20},{20... | collective-permute-start | bytes 5898248 | tf_op jit(solution)/shard_map/ppermute | solution.py:32
  328.1 22.3 %collective-permute-start.35 = (bf16[640,2048]{1,0:T(8,128)(2,1)}, bf16[640,2048]{1,0:T(8,128)(2,1)}, u32[]{:S(2)}, u32[]{:S(2)}) collective-permute-start(bf16[640,2048]{1,0:T(8,128)(2,1)} %convolution_convert_fusion.2), channel_id=1, source_target_pairs={{0,16},{16,0},{1,17},{17,1},{2,18},{18,2},{3,19},{19,3},{4,20},{20... | collective-permute-start | bytes 7864328 | tf_op jit(solution)/shard_map/ppermute | solution.py:32
  356.5 54.4 %collective-permute-start.43 = (bf16[4,2,1,96,640]{4,3,2,1,0:T(8,128)(2,1)}, bf16[4,2,1,96,640]{4,3,2,1,0:T(8,128)(2,1)}, u32[]{:S(2)}, u32[]{:S(2)}) collective-permute-start(bf16[4,2,1,96,640]{4,3,2,1,0:T(8,128)(2,1)} %constant_dynamic-slice_fusion.5), channel_id=1, source_target_pairs={{0,1},{1,0},{2,3},{3,2},{4,5},{5,4},{6,7},{7,6},{8,9},{9,8},{10,11... | collective-permute-start | bytes 2949128 | tf_op jit(solution)/shard_map/ppermute | solution.py:32
  358.6 30.5 %collective-permute-start.37 = (bf16[256,512]{1,0:T(8,128)(2,1)}, bf16[256,512]{1,0:T(8,128)(2,1)}, u32[]{:S(2)}, u32[]{:S(2)}) collective-permute-start(bf16[256,512]{1,0:T(8,128)(2,1)} %get-tuple-element.191), channel_id=1, source_target_pairs={{0,1},{1,0},{2,3},{3,2},{4,5},{5,4},{6,7},{7,6},{8,9},{9,8},{10,11... | collective-permute-start | bytes 786440 | tf_op jit(solution)/shard_map/ppermute | solution.py:32
  359.6 30.5 %collective-permute-start.38 = (bf16[256,512]{1,0:T(8,128)(2,1)}, bf16[256,512]{1,0:T(8,128)(2,1)}, u32[]{:S(2)}, u32[]{:S(2)}) collective-permute-start(bf16[256,512]{1,0:T(8,128)(2,1)} %get-tuple-element.193), channel_id=1, source_target_pairs={{0,2},{1,3},{2,0},{3,1},{4,6},{5,7},{6,4},{7,5},{8,10},{9,11},{10,... | collective-permute-start | bytes 786440 | tf_op jit(solution)/shard_map/ppermute | solution.py:32
  361.1 34.3 %collective-permute-start.39 = (bf16[256,512]{1,0:T(8,128)(2,1)}, bf16[256,512]{1,0:T(8,128)(2,1)}, u32[]{:S(2)}, u32[]{:S(2)}) collective-permute-start(bf16[256,512]{1,0:T(8,128)(2,1)} %get-tuple-element.192), channel_id=1, source_target_pairs={{0,3},{1,2},{2,1},{3,0},{4,7},{5,6},{6,5},{7,4},{8,11},{9,10},{10,... | collective-permute-start | bytes 786440 | tf_op jit(solution)/shard_map/ppermute | solution.py:32
  373.2 32.3 %collective-permute-start.42 = (bf16[2,1,2,40,2048]{4,3,0,2,1:T(8,128)(2,1)}, bf16[2,1,2,40,2048]{4,3,0,2,1:T(8,128)(2,1)}, u32[]{:S(2)}, u32[]{:S(2)}) collective-permute-start(bf16[2,1,2,40,2048]{4,3,0,2,1:T(8,128)(2,1)} %constant_dynamic-slice_fusion.6), channel_id=1, source_target_pairs={{0,2},{1,3},{2,0},{3,1},{4,6},{5,7},{6,4},{7,5},{8,10},{9,11},{10,... | collective-permute-start | bytes 1966088 | tf_op jit(solution)/shard_map/ppermute | solution.py:32
  389.1 19.7 %collective-permute-start.41 = (bf16[2,2,1,40,2048]{4,3,0,2,1:T(8,128)(2,1)}, bf16[2,2,1,40,2048]{4,3,0,2,1:T(8,128)(2,1)}, u32[]{:S(2)}, u32[]{:S(2)}) collective-permute-start(bf16[2,2,1,40,2048]{4,3,0,2,1:T(8,128)(2,1)} %constant_dynamic-slice_fusion.7), channel_id=1, source_target_pairs={{0,1},{1,0},{2,3},{3,2},{4,5},{5,4},{6,7},{7,6},{8,9},{9,8},{10,11... | collective-permute-start | bytes 1966088 | tf_op jit(solution)/shard_map/ppermute | solution.py:32
  427.0 17.2 %collective-permute-start.51 = (bf16[2,1,1,40,2048]{4,3,0,2,1:T(8,128)(2,1)S(1)}, bf16[2,1,1,40,2048]{4,3,0,2,1:T(8,128)(2,1)S(1)}, u32[]{:S(2)}, u32[]{:S(2)}) collective-permute-start(bf16[2,1,1,40,2048]{4,3,0,2,1:T(8,128)(2,1)S(1)} %constant_dynamic-slice_fusion.1), channel_id=1, source_target_pairs={{0,1},{1,0},{2,3},{3,2},{4,5},{5,4},{6,7},{7,6},{8,9},{9,8},{10,11... | collective-permute-start | bytes 983048 | tf_op jit(solution)/shard_map/ppermute | solution.py:32
  430.6 14.3 %collective-permute-start.50 = (bf16[2,1,1,40,2048]{4,3,0,2,1:T(8,128)(2,1)S(1)}, bf16[2,1,1,40,2048]{4,3,0,2,1:T(8,128)(2,1)S(1)}, u32[]{:S(2)}, u32[]{:S(2)}) collective-permute-start(bf16[2,1,1,40,2048]{4,3,0,2,1:T(8,128)(2,1)S(1)} %constant_dynamic-slice_fusion.2), channel_id=1, source_target_pairs={{0,2},{1,3},{2,0},{3,1},{4,6},{5,7},{6,4},{7,5},{8,10},{9,11},{10,... | collective-permute-start | bytes 983048 | tf_op jit(solution)/shard_map/ppermute | solution.py:32
  445.2 12.9 %collective-permute-start.52 = (bf16[40,2048]{1,0:T(8,128)(2,1)S(1)}, bf16[40,2048]{1,0:T(8,128)(2,1)S(1)}, u32[]{:S(2)}, u32[]{:S(2)}) collective-permute-start(bf16[40,2048]{1,0:T(8,128)(2,1)S(1)} %get-tuple-element.205), channel_id=1, source_target_pairs={{0,4},{4,0},{8,12},{12,8},{1,5},{5,1},{9,13},{13,9},{2,6},{6,2},{1... | collective-permute-start | bytes 491528 | tf_op jit(solution)/shard_map/ppermute | solution.py:32
  446.4 13.2 %collective-permute-start.53 = (bf16[40,2048]{1,0:T(8,128)(2,1)S(1)}, bf16[40,2048]{1,0:T(8,128)(2,1)S(1)}, u32[]{:S(2)}, u32[]{:S(2)}) collective-permute-start(bf16[40,2048]{1,0:T(8,128)(2,1)S(1)} %get-tuple-element.206), channel_id=1, source_target_pairs={{0,8},{4,12},{8,0},{12,4},{1,9},{5,13},{9,1},{13,5},{2,10},{6,14},... | collective-permute-start | bytes 491528 | tf_op jit(solution)/shard_map/ppermute | solution.py:32
  449.0 16.8 %collective-permute-start.54 = (bf16[40,2048]{1,0:T(8,128)(2,1)S(1)}, bf16[40,2048]{1,0:T(8,128)(2,1)S(1)}, u32[]{:S(2)}, u32[]{:S(2)}) collective-permute-start(bf16[40,2048]{1,0:T(8,128)(2,1)S(1)} %get-tuple-element.207), channel_id=1, source_target_pairs={{0,12},{4,8},{8,4},{12,0},{1,13},{5,9},{9,5},{13,1},{2,14},{6,10},... | collective-permute-start | bytes 491528 | tf_op jit(solution)/shard_map/ppermute | solution.py:32
  449.7 32.0 %collective-permute-start.45 = (bf16[4,2,1,40,896]{4,3,2,1,0:T(8,128)(2,1)S(1)}, bf16[4,2,1,40,896]{4,3,2,1,0:T(8,128)(2,1)S(1)}, u32[]{:S(2)}, u32[]{:S(2)}) collective-permute-start(bf16[4,2,1,40,896]{4,3,2,1,0:T(8,128)(2,1)S(1)} %constant_dynamic-slice_fusion.4), channel_id=1, source_target_pairs={{0,1},{1,0},{2,3},{3,2},{4,5},{5,4},{6,7},{7,6},{8,9},{9,8},{10,11... | collective-permute-start | bytes 1720328 | tf_op jit(solution)/shard_map/ppermute | solution.py:32
  451.7 44.8 %collective-permute-start.57 = (bf16[4,1,1,96,640]{4,3,2,1,0:T(8,128)(2,1)S(1)}, bf16[4,1,1,96,640]{4,3,2,1,0:T(8,128)(2,1)S(1)}, u32[]{:S(2)}, u32[]{:S(2)}) collective-permute-start(bf16[4,1,1,96,640]{4,3,2,1,0:T(8,128)(2,1)S(1)} %constant_dynamic-slice_fusion), channel_id=1, source_target_pairs={{0,2},{1,3},{2,0},{3,1},{4,6},{5,7},{6,4},{7,5},{8,10},{9,11},{10,... | collective-permute-start | bytes 1474568 | tf_op jit(solution)/shard_map/ppermute | solution.py:32
  481.8 25.5 %collective-permute-start.46 = (bf16[4,1,1,40,896]{4,3,2,1,0:T(8,128)(2,1)S(1)}, bf16[4,1,1,40,896]{4,3,2,1,0:T(8,128)(2,1)S(1)}, u32[]{:S(2)}, u32[]{:S(2)}) collective-permute-start(bf16[4,1,1,40,896]{4,3,2,1,0:T(8,128)(2,1)S(1)} %constant_dynamic-slice_fusion.3), channel_id=1, source_target_pairs={{0,2},{1,3},{2,0},{3,1},{4,6},{5,7},{6,4},{7,5},{8,10},{9,11},{10,... | collective-permute-start | bytes 860168 | tf_op jit(solution)/shard_map/ppermute | solution.py:32
  498.1 13.8 %collective-permute-start.59 = (bf16[96,640]{1,0:T(8,128)(2,1)S(1)}, bf16[96,640]{1,0:T(8,128)(2,1)S(1)}, u32[]{:S(2)}, u32[]{:S(2)}) collective-permute-start(bf16[96,640]{1,0:T(8,128)(2,1)S(1)} %get-tuple-element.226), channel_id=1, source_target_pairs={{0,8},{4,12},{8,0},{12,4},{1,9},{5,13},{9,1},{13,5},{2,10},{6,14},... | collective-permute-start | bytes 368648 | tf_op jit(solution)/shard_map/ppermute | solution.py:32
  498.1 13.8 %collective-permute-start.60 = (bf16[96,640]{1,0:T(8,128)(2,1)S(1)}, bf16[96,640]{1,0:T(8,128)(2,1)S(1)}, u32[]{:S(2)}, u32[]{:S(2)}) collective-permute-start(bf16[96,640]{1,0:T(8,128)(2,1)S(1)} %get-tuple-element.225), channel_id=1, source_target_pairs={{0,12},{4,8},{8,4},{12,0},{1,13},{5,9},{9,5},{13,1},{2,14},{6,10},... | collective-permute-start | bytes 368648 | tf_op jit(solution)/shard_map/ppermute | solution.py:32
  507.5 14.2 %collective-permute-start.48 = (bf16[40,896]{1,0:T(8,128)(2,1)S(1)}, bf16[40,896]{1,0:T(8,128)(2,1)S(1)}, u32[]{:S(2)}, u32[]{:S(2)}) collective-permute-start(bf16[40,896]{1,0:T(8,128)(2,1)S(1)} %get-tuple-element.241), channel_id=1, source_target_pairs={{0,8},{4,12},{8,0},{12,4},{1,9},{5,13},{9,1},{13,5},{2,10},{6,14},... | collective-permute-start | bytes 215048 | tf_op jit(solution)/shard_map/ppermute | solution.py:32
  507.6 14.1 %collective-permute-start.49 = (bf16[40,896]{1,0:T(8,128)(2,1)S(1)}, bf16[40,896]{1,0:T(8,128)(2,1)S(1)}, u32[]{:S(2)}, u32[]{:S(2)}) collective-permute-start(bf16[40,896]{1,0:T(8,128)(2,1)S(1)} %get-tuple-element.240), channel_id=1, source_target_pairs={{0,12},{4,8},{8,4},{12,0},{1,13},{5,9},{9,5},{13,1},{2,14},{6,10},... | collective-permute-start | bytes 215048 | tf_op jit(solution)/shard_map/ppermute | solution.py:32
  512.9 23.4 %collective-permute-start.62 = (f32[96,640]{1,0:T(8,128)S(1)}, f32[96,640]{1,0:T(8,128)S(1)}, u32[]{:S(2)}, u32[]{:S(2)}) collective-permute-start(f32[96,640]{1,0:T(8,128)S(1)} %get-tuple-element.130), channel_id=1, source_target_pairs={{0,16},{16,0},{1,17},{17,1},{2,18},{18,2},{3,19},{19,3},{4,20},{20... | collective-permute-start | bytes 737288 | tf_op jit(solution)/shard_map/ppermute | solution.py:32
  (225 other events, 1511.2 us)
Sparse Core Ops, SparseCore 0:
  49.4 67.3 all-gather.6
  119.4 72.9 all-gather.4
  278.8 129.0 reduce-scatter.5
  421.8 113.3 reduce-scatter.7

commit v4 on v3

--- a/solution.py
+++ b/solution.py
@@ -1,8 +1,11 @@
+import functools
 import math
 
 import jax
 import jax.numpy as jnp
 from jax import lax
+from jax.experimental import pallas as pl
+from jax.experimental.pallas import tpu as pltpu
 from jax.sharding import PartitionSpec as P
 
 D = 640
@@ -149,25 +152,6 @@
         return z_scatter(buf)
 
 
-def rms_norm(values_in, gain):
-    return (
-        values_in * lax.rsqrt(jnp.mean(values_in * values_in, axis=-1, keepdims=True) + EPS) * gain
-    )
-
-
-def rotate(values_in, cosine, sine_table):
-    half_width = values_in.shape[-1] // 2
-    lower_half = values_in[..., :half_width]
-    upper_half = values_in[..., half_width:]
-    return jnp.concatenate(
-        [
-            lower_half * cosine - upper_half * sine_table,
-            upper_half * cosine + lower_half * sine_table,
-        ],
-        axis=-1,
-    )
-
-
 def rope_tables(places, log_base):
     half_width = HD // 2
     inverse = jnp.exp(-log_base * (jnp.arange(half_width, dtype=F32) * (2.0 / HD)))
@@ -175,20 +159,6 @@
     return (jnp.cos(angles), jnp.sin(angles))
 
 
-def head_prepare(query_product, key_product, query_gain, key_gain, cosine, sine_table):
-    token_count = query_product.shape[0]
-    queries = rms_norm(query_product.reshape(token_count, HEADS, HD), query_gain)
-    keys_normed = rms_norm(key_product, key_gain)
-    return (
-        rotate(queries, cosine[:, None, :], sine_table[:, None, :]),
-        rotate(keys_normed, cosine, sine_table),
-    )
-
-
-def gated(gate, up):
-    return jax.nn.gelu(gate, approximate=True) * up
-
-
 def dot(a, b):
     return jnp.dot(a, b, preferred_element_type=F32)
 
@@ -199,18 +169,6 @@
 
 def t_dot(a, b):
     return jnp.einsum("ta,tb->ab", a, b, preferred_element_type=F32)
-
-
-def attention_weights(flat_queries, all_keys, places, all_places, window):
-    query_places = jnp.repeat(places, HEADS)
-    allowed = (all_places[None, :] <= query_places[:, None]) & (
-        query_places[:, None] - all_places[None, :] < window
-    )
-    scores = dot_t(flat_queries, all_keys) * SCALE
-    scores = jnp.where(allowed, scores, -1e30)
-    maximum = jnp.max(scores, axis=-1, keepdims=True)
-    weights = jnp.exp(scores - maximum)
-    return weights / jnp.sum(weights, axis=-1, keepdims=True)
 
 
 def pick(first, own, other):
@@ -231,115 +189,278 @@
     return total
 
 
-def forward_keys(full, x, cosine, sine_table, first):
+def whole_call(body, outs, args, flops, window=None):
+    vmem = pl.BlockSpec(memory_space=pltpu.VMEM)
+    moved = sum(math.prod(v.shape) * v.dtype.itemsize for v in args)
+    moved += sum(math.prod(s) * jnp.dtype(t).itemsize for s, t in outs)
+    return pl.pallas_call(
+        body,
+        out_shape=[jax.ShapeDtypeStruct(s, t) for s, t in outs],
+        in_specs=[pl.BlockSpec(memory_space=pltpu.SMEM)] + [vmem] * (len(args) - 1),
+        out_specs=[vmem] * len(outs),
+        compiler_params=pltpu.CompilerParams(vmem_limit_bytes=52 * 2**20),
+        cost_estimate=pl.CostEstimate(
+            flops=int(flops), bytes_accessed=int(moved), transcendentals=0
+        ),
+    )(*args)
+
+
+def inverse_rms(u):
+    return lax.rsqrt(jnp.mean(u * u, axis=-1, keepdims=True) + EPS)
+
+
+def rms_back(u, gain, dz):
+    r = inverse_rms(u)
+    scaled = dz * gain
+    mean = jnp.mean(u * scaled, axis=-1, keepdims=True)
+    du = r * (scaled - u * (r * r * mean))
+    return du, jnp.sum(dz * u * r, axis=0, keepdims=True)
+
+
+def last_dot(a, b):
+    return lax.dot_general(a, b, (((1,), (1,)), ((), ())), preferred_element_type=F32)
+
+
+def first_dot(a, b):
+    return lax.dot_general(a, b, (((0,), (0,)), ((), ())), preferred_element_type=F32)
+
+
+def chosen(flag, own, other):
+    return jnp.where(flag, own, other), jnp.where(flag, other, own)
+
+
+def keys_body(flag, x, q_own, q_oth, gains, heads, cosine, sine, normed, qp, kp, q, kv):
+    first = flag[0] == 0
+    u = x[...]
+    h = (u * inverse_rms(u) * gains[0:1, :]).astype(BF)
+    normed[...] = h
+    lo, hi = chosen(first, dot(h, q_own[:, :QW]), dot(h, q_oth[:, :QW]))
+    cos, sin = cosine[...], sine[...]
+    half = HD // 2
+
+    def turned(v, gain, out, at):
+        n = v * inverse_rms(v) * gain
+        a, b = n[:, :half], n[:, half:]
+        out[:, at : at + half] = (a * cos - b * sin).astype(BF)
+        out[:, at + half : at + HD] = (b * cos + a * sin).astype(BF)
+
+    for head in range(HEADS):
+        part = (lo if head < 2 else hi)[:, (head % 2) * HD : (head % 2 + 1) * HD]
+        qp[:, head * HD : (head + 1) * HD] = part
+        turned(part, heads[0:1, :], q, head * HD)
+    k_part = lo[:, QH:]
+    kp[...] = k_part
+    turned(k_part, heads[1:2, :], kv, 0)
+    kv[:, HD:] = hi[:, QH:].astype(BF)
+
+
+def forward_keys(full, x, cosine, sine_table, flag):
     q_own, q_oth, gains, heads = full
-    tokens = x.shape[0]
-    normed = rms_norm(x, gains[0]).astype(BF)
-    lo, hi = pick(first, dot(normed, q_own), dot(normed, q_oth))
-    query_product = jnp.concatenate([lo[:, :QH], hi[:, :QH]], axis=1)
-    key_product = lo[:, QH:]
-    queries, keys_rot = head_prepare(
-        query_product, key_product, heads[0], heads[1], cosine, sine_table
-    )
-    flat_queries = queries.astype(BF).reshape(tokens * HEADS, HD)
-    keys_values = jnp.concatenate([keys_rot, hi[:, QH:]], axis=1).astype(BF)
-    all_kv = jnp.concatenate(key_exchange(keys_values), axis=0)
-    return dict(
-        x=x, normed=normed, query_product=query_product, key_product=key_product,
-        flat_queries=flat_queries, all_keys=all_kv[:, :HD], all_values=all_kv[:, HD:],
-    )
-
-
-def forward_attend(kept, places, all_places, window):
-    tokens = kept["x"].shape[0]
-    prob_low = attention_weights(
-        kept["flat_queries"], kept["all_keys"], places, all_places, window
-    ).astype(BF)
-    return dot(prob_low, kept["all_values"]).reshape(tokens, HEADS * HD).astype(BF)
-
-
-def forward_rest(full, kept, mixed, first):
+    t = x.shape[0]
+    normed, qp, kp, q, kv = whole_call(
+        keys_body,
+        [((t, D), BF), ((t, HEADS * HD), F32), ((t, HD), F32), ((t, HEADS * HD), BF), ((t, 2 * HD), BF)],
+        (flag, x, q_own, q_oth, gains, heads, cosine, sine_table),
+        2 * t * D * 2 * QW,
+    )
+    all_kv = jnp.concatenate(key_exchange(kv), axis=0)
+    return dict(x=x, normed=normed, qp=qp, kp=kp, q=q, kv=all_kv)
+
+
+CHUNK = 512
+GELU_A = math.sqrt(2.0 / math.pi)
+GELU_B = 0.044715
+
+
+def rest_body(
+    window, flag, x, q, kv, pos_q, pos_k, w_out, g_own, g_oth, w_down, gains,
+    mixed, branch, middle, normed, gate_out, up_out, hidden, down, result,
+):
+    first = flag[0] == 0
+    reach = pos_q[...] - pos_k[...]
+    allowed = (reach >= 0) & (reach < window)
+    k, v = kv[:, :HD], kv[:, HD:]
+    for head in range(HEADS):
+        cols = slice(head * HD, (head + 1) * HD)
+        s = jnp.where(allowed, last_dot(q[:, cols], k) * SCALE, -1e30)
+        e = jnp.exp(s - jnp.max(s, axis=-1, keepdims=True))
+        total = jnp.sum(e, axis=-1, keepdims=True)
+        mixed[:, cols] = (dot(e.astype(BF), v) * (1.0 / total)).astype(BF)
+    b = dot(mixed[...], w_out[...])
+    branch[...] = b
+    m = x[...] + b * inverse_rms(b) * gains[1:2, :]
+    middle[...] = m
+    h = (m * inverse_rms(m) * gains[2:3, :]).astype(BF)
+    normed[...] = h
+    total = jnp.zeros(m.shape, F32)
+    for at in range(0, FF, CHUNK):
+        cols = slice(at, at + CHUNK)
+        gate, up = chosen(first, dot(h, g_own[:, cols]), dot(h, g_oth[:, cols]))
+        gate_out[:, cols] = gate
+        up_out[:, cols] = up
+        th = jnp.tanh(GELU_A * (gate + GELU_B * gate * gate * gate))
+        hid = (0.5 * gate * (1.0 + th) * up).astype(BF)
+        hidden[:, cols] = hid
+        total = total + dot(hid, w_down[cols, :])
+    down[...] = total
+    result[...] = m + total * inverse_rms(total) * gains[3:4, :]
+
+
+def forward_rest(full, kept, pos, window, flag):
     g_own, g_oth, w_out, w_down, gains = full
-    branch = dot(mixed, w_out)
-    middle = kept["x"] + rms_norm(branch, gains[1])
-    normed_two = rms_norm(middle, gains[2]).astype(BF)
-    gate, up = pick(first, dot(normed_two, g_own), dot(normed_two, g_oth))
-    hidden = gated(gate, up).astype(BF)
-    down_out = dot(hidden, w_down)
-    kept.update(
-        mixed=mixed, branch=branch, middle=middle, normed_two=normed_two, gate=gate, up=up,
-        hidden=hidden, down_out=down_out,
-    )
-    return middle + rms_norm(down_out, gains[3])
+    t = kept["x"].shape[0]
+    keys = kept["kv"].shape[0]
+    names = ("mixed", "branch", "middle", "normed_two", "gate", "up", "hidden", "down", "result")
+    outs = whole_call(
+        functools.partial(rest_body, window),
+        [
+            ((t, HEADS * HD), BF), ((t, D), F32), ((t, D), F32), ((t, D), BF), ((t, FF), F32),
+            ((t, FF), F32), ((t, FF), BF), ((t, D), F32), ((t, D), F32),
+        ],
+        (
+            flag, kept["x"], kept["q"], kept["kv"], pos[0][:, None], pos[1][None, :], w_out,
+            g_own, g_oth, w_down, gains,
+        ),
+        2 * t * HEADS * HD * (2 * keys + D) + 6 * t * D * FF,
+    )
+    kept.update(zip(names, outs))
+    return kept["result"]
+
+
+def feed_body(
+    flag, dy, down, gate, up, middle, branch, gains, w_down, g_own, g_oth,
+    grad_middle, grad_down, gu_own, gu_oth, grad_branch, gain_grads,
+):
+    first = flag[0] == 0
+    dz = dy[...].astype(F32)
+    df, gain_three = rms_back(down[...], gains[3:4, :], dz)
+    df = df.astype(BF)
+    grad_down[...] = df
+    total = jnp.zeros(dz.shape, F32)
+    for at in range(0, FF, CHUNK):
+        cols = slice(at, at + CHUNK)
+        dm = last_dot(df, w_down[cols, :])
+        u = gate[:, cols]
+        th = jnp.tanh(GELU_A * (u + GELU_B * u * u * u))
+        plus = 0.5 * (1.0 + th)
+        slope = plus + 0.5 * u * (1.0 - th * th) * (GELU_A * (1.0 + 3.0 * GELU_B * u * u))
+        d_gate = (dm * up[:, cols] * slope).astype(BF)
+        d_up = (dm * (u * plus)).astype(BF)
+        own, oth = chosen(first, d_gate, d_up)
+        gu_own[:, cols] = own
+        gu_oth[:, cols] = oth
+        total = total + last_dot(own, g_own[:, cols]) + last_dot(oth, g_oth[:, cols])
+    part, gain_two = rms_back(middle[...], gains[2:3, :], total)
+    dx = dz + part
+    grad_middle[...] = dx
+    da, gain_one = rms_back(branch[...], gains[1:2, :], dx)
+    grad_branch[...] = da.astype(BF)
+    gain_grads[...] = jnp.concatenate([gain_one, gain_two, gain_three], axis=0)
+
+
+def backward_feed(full, kept, grad_result, flag):
+    g_own, g_oth, w_out, w_down, gains = full
+    t = kept["x"].shape[0]
+    middle, down_low, gu_own, gu_oth, branch_low, gain_grads = whole_call(
+        feed_body,
+        [((t, D), F32), ((t, D), BF), ((t, FF), BF), ((t, FF), BF), ((t, D), BF), ((3, D), F32)],
+        (
+            flag, grad_result, kept["down"], kept["gate"], kept["up"], kept["middle"],
+            kept["branch"], gains, w_down, g_own, g_oth,
+        ),
+        6 * t * D * FF,
+    )
+    wg_g = (t_dot(kept["normed_two"], gu_own), t_dot(kept["normed_two"], gu_oth).astype(BF))
+    wg_out = t_dot(kept["mixed"], branch_low).astype(BF)
+    wg_down = t_dot(kept["hidden"], down_low).astype(BF)
+    return middle, branch_low, wg_g, wg_out, wg_down, gain_grads
+
+
+def attend_body(window, flag, da, w_out, q, kv, pos_q, pos_k, grad_q, grad_kv):
+    reach = pos_q[...] - pos_k[...]
+    allowed = (reach >= 0) & (reach < window)
+    k, v = kv[:, :HD], kv[:, HD:]
+    for head in range(HEADS):
+        cols = slice(head * HD, (head + 1) * HD)
+        do = last_dot(da[...], w_out[cols, :]).astype(BF)
+        s = jnp.where(allowed, last_dot(k, q[:, cols]) * SCALE, -1e30)
+        e = jnp.exp(s - jnp.max(s, axis=0, keepdims=True))
+        p = e * (1.0 / jnp.sum(e, axis=0, keepdims=True))
+        dp = last_dot(v, do)
+        inner = jnp.sum(p * dp, axis=0, keepdims=True)
+        ds = (p * (dp - inner)).astype(BF)
+        grad_q[:, cols] = first_dot(ds, k) * SCALE
+        dk = dot(ds, q[:, cols]) * SCALE
+        dv = dot(p.astype(BF), do)
+        if head == 0:
+            total_k, total_v = dk, dv
+        else:
+            total_k, total_v = total_k + dk, total_v + dv
+    grad_kv[:, :HD] = total_k.astype(BF)
+    grad_kv[:, HD:] = total_v.astype(BF)
+
+
+def backward_attend(w_out, kept, branch_low, pos, window, flag):
+    t, keys = kept["x"].shape[0], kept["kv"].shape[0]
+    return whole_call(
+        functools.partial(attend_body, window),
+        [((t, HEADS * HD), F32), ((keys, 2 * HD), BF)],
+        (flag, branch_low, w_out, kept["q"], kept["kv"], pos[0][None, :], pos[1][:, None]),
+        2 * t * HEADS * HD * (5 * keys + D),
+    )
+
+
+def back_body(
+    flag, grad_q, grad_kv, qp, kp, heads, cosine, sine, x, dx, q_own, q_oth, gains,
+    grad_x, gq_own, gq_oth, gain_zero, head_grads,
+):
+    first = flag[0] == 0
+    cos, sin = cosine[...], sine[...]
+    half = HD // 2
+
+    def turned_back(d, u, gain):
+        a, b = d[:, :half], d[:, half:]
+        n = jnp.concatenate([a * cos + b * sin, b * cos - a * sin], axis=1)
+        return rms_back(u, gain, n)
+
+    parts = []
+    query_gain = jnp.zeros((1, HD), F32)
+    for head in range(HEADS):
+        cols = slice(head * HD, (head + 1) * HD)
+        du, dg = turned_back(grad_q[:, cols], qp[:, cols], heads[0:1, :])
+        parts.append(du.astype(BF))
+        query_gain = query_gain + dg
+    dk, key_gain = turned_back(grad_kv[:, :HD], kp[...], heads[1:2, :])
+    lo = jnp.concatenate(parts[:2] + [dk.astype(BF)], axis=1)
+    hi = jnp.concatenate(parts[2:] + [grad_kv[:, HD:].astype(BF)], axis=1)
+    own, oth = chosen(first, lo, hi)
+    gq_own[...] = own
+    gq_oth[...] = oth
+    dz = last_dot(own, q_own[:, :QW]) + last_dot(oth, q_oth[:, :QW])
+    part, gain = rms_back(x[...], gains[0:1, :], dz)
+    grad_x[...] = dx[...] + part
+    gain_zero[...] = gain
+    head_grads[...] = jnp.concatenate([query_gain, key_gain], axis=0)
+
+
+def backward_keys(full, kept, middle, grad_q, grad_kv, cosine, sine_table, flag):
+    q_own, q_oth, gains, heads = full
+    t = kept["x"].shape[0]
+    grad_x, gq_own, gq_oth, gain_zero, head_grads = whole_call(
+        back_body,
+        [((t, D), F32), ((t, QW), BF), ((t, QW), BF), ((1, D), F32), ((2, HD), F32)],
+        (
+            flag, grad_q, grad_kv, kept["qp"], kept["kp"], heads, cosine, sine_table, kept["x"],
+            middle, q_own, q_oth, gains,
+        ),
+        4 * t * D * QW,
+    )
+    wg_q = (t_dot(kept["normed"], gq_own).astype(BF), t_dot(kept["normed"], gq_oth).astype(BF))
+    return grad_x, wg_q, gain_zero, head_grads
 
 
 def halves(grad, count):
     return grad.reshape(count, 2, -1, grad.shape[-1])
-
-
-def backward_feed(full, kept, grad_result, first):
-    g_own, g_oth, w_out, w_down, gains = full
-    _, back_last = jax.vjp(rms_norm, kept["down_out"], gains[3])
-    grad_down, gain_three = back_last(grad_result)
-    grad_down_low = grad_down.astype(BF)
-    grad_hidden = dot_t(grad_down_low, w_down)
-    _, back_gated = jax.vjp(gated, kept["gate"], kept["up"])
-    grad_gate, grad_up = back_gated(grad_hidden)
-    gu_own, gu_oth = pick(first, grad_gate.astype(BF), grad_up.astype(BF))
-    grad_normed_two = dot_t(gu_own, g_own) + dot_t(gu_oth, g_oth)
-    _, back_norm_two = jax.vjp(rms_norm, kept["middle"], gains[2])
-    grad_middle_part, gain_two = back_norm_two(grad_normed_two)
-    grad_middle = grad_result + grad_middle_part
-    _, back_norm_one = jax.vjp(rms_norm, kept["branch"], gains[1])
-    grad_branch, gain_one = back_norm_one(grad_middle)
-    grad_branch_low = grad_branch.astype(BF)
-    wg_g = (t_dot(kept["normed_two"], gu_own), t_dot(kept["normed_two"], gu_oth).astype(BF))
-    wg_out = t_dot(kept["mixed"], grad_branch_low).astype(BF)
-    wg_down = t_dot(kept["hidden"], grad_down_low).astype(BF)
-    return grad_middle, grad_branch_low, wg_g, wg_out, wg_down, [gain_one, gain_two, gain_three]
-
-
-def backward_attend(w_out, kept, grad_branch_low, places, all_places, window):
-    tokens = kept["x"].shape[0]
-    grad_mixed = dot_t(grad_branch_low, w_out).astype(BF).reshape(tokens * HEADS, HD)
-    flat_queries, all_keys, all_values = kept["flat_queries"], kept["all_keys"], kept["all_values"]
-    probabilities = attention_weights(flat_queries, all_keys, places, all_places, window)
-    prob_low = probabilities.astype(BF)
-    grad_probs = dot_t(grad_mixed, all_values)
-    inner_sum = jnp.sum(probabilities * grad_probs, axis=-1, keepdims=True)
-    grad_scores = (probabilities * (grad_probs - inner_sum)).astype(BF)
-    grad_keys_all = t_dot(grad_scores, flat_queries) * SCALE
-    grad_values_all = t_dot(prob_low, grad_mixed)
-    blocks = jnp.concatenate([grad_keys_all, grad_values_all], axis=1)
-    return grad_scores, blocks
-
-
-def backward_queries(kept, grad_scores):
-    grad_queries = dot(grad_scores, kept["all_keys"]) * SCALE
-    return grad_queries.reshape(-1, HEADS, HD)
-
-
-def backward_keys(full, kept, grad_middle, grad_queries, grad_kv, cosine, sine_table, first):
-    q_own, q_oth, gains, heads = full
-
-    def prepare(query_in, key_in, query_gain, key_gain):
-        return head_prepare(query_in, key_in, query_gain, key_gain, cosine, sine_table)
-
-    _, back_heads = jax.vjp(
-        prepare, kept["query_product"], kept["key_product"], heads[0], heads[1]
-    )
-    grad_qp, grad_kp, query_gain, key_gain = back_heads((grad_queries, grad_kv[:, :HD]))
-    lo = jnp.concatenate([grad_qp[:, :QH], grad_kp], axis=1).astype(BF)
-    hi = jnp.concatenate([grad_qp[:, QH:], grad_kv[:, HD:]], axis=1).astype(BF)
-    q_grad_own, q_grad_oth = pick(first, lo, hi)
-    grad_normed = dot_t(q_grad_own, q_own) + dot_t(q_grad_oth, q_oth)
-    _, back_norm_zero = jax.vjp(rms_norm, kept["x"], gains[0])
-    grad_part, gain_zero = back_norm_zero(grad_normed)
-    wg_q = (
-        t_dot(kept["normed"], q_grad_own).astype(BF),
-        t_dot(kept["normed"], q_grad_oth).astype(BF),
-    )
-    return grad_middle + grad_part, wg_q, gain_zero, [query_gain, key_gain]
 
 
 def local(
@@ -358,13 +479,14 @@
     moved = exchange(lax.dynamic_index_in_dim(boundary[0, :, 0], 1 - section, 0, False), "section", 1)
     kept_in = lax.dynamic_index_in_dim(boundary[0, :, 0], section, 0, False)
     x0, cotangent = pick(first, kept_in, moved)
-    x0, cotangent = x0.astype(F32), cotangent.astype(F32)
+    x0 = x0.astype(F32)
     seq_places = lax.dynamic_index_in_dim(positions[:, 0], section, 0, False)
     near = [
         lax.dynamic_slice_in_dim(seq_places, (ctx_index ^ j) * tokens, tokens)
         for j in range(lax.axis_size("ctx"))
     ]
-    places, all_places = near[0], jnp.concatenate(near)
+    pos = (near[0], jnp.concatenate(near))
+    flag = section.astype(jnp.int32).reshape(1)
 
     gain_cols = jnp.concatenate(
         [
@@ -408,7 +530,7 @@
         gain_part = q_own[:, QW:].astype(F32)
         gains = gain_part[:, :4].T
         heads = gain_part[:, 4:6].reshape(blocks, nr, 2)[:, :hr].reshape(blocks * hr, 2).T
-        return q_own[:, :QW], q_oth[:, :QW], gains, heads
+        return q_own, q_oth, gains, heads
 
     def feed_side(g_pair, b_pair, gains):
         g_own, g_oth = [v.reshape(blocks * nr, -1) for v in g_pair]
@@ -437,8 +559,8 @@
         return (part(section).astype(F32) + recv.astype(F32)).astype(BF)
 
     def reduce_query(wg_q, norm_grads, head_grads):
-        norm_part = jnp.stack(norm_grads).T
-        head_part = jnp.stack(head_grads).T.reshape(blocks, hr, 2)
+        norm_part = jnp.concatenate(norm_grads, axis=0).T
+        head_part = head_grads.T.reshape(blocks, hr, 2)
         head_part = jnp.pad(head_part, ((0, 0), (0, nr - hr), (0, 0))).reshape(blocks * nr, 2)
         fill = jnp.zeros((blocks * nr, 128 - 6), F32)
         cols = jnp.concatenate([norm_part, head_part, fill], axis=1).astype(BF)
@@ -446,68 +568,64 @@
         oth = jnp.concatenate([wg_q[1], cols], axis=1)
         return reduce_cols(own, oth)
 
-    tables = [rope_tables(places, base) for base in BASES]
+    tables = [rope_tables(pos[0], base) for base in BASES]
     windows = (WIN, seq_length)
 
     gather0 = Gather(layer_cols[0], layer_rows[0])
     gather0.along_z()
-    cols1, rows1, *gather0.parts = tie(layer_cols[1], layer_rows[1], *gather0.parts)
+    cols1, rows1 = tie(layer_cols[1], layer_rows[1], *gather0.parts)[:2]
     cols1 = lax.all_gather(cols1, GRID, axis=0)
     rows1 = lax.all_gather(rows1, GRID, axis=0)
     gather0.plane(0)
     gather0.plane(1)
     pairs0 = gather0.pairs()
     query0 = query_side(pairs0[0])
-    kept0 = forward_keys(query0, x0, *tables[0], first)
-    mixed = forward_attend(kept0, places, all_places, windows[0])
+    kept0 = forward_keys(query0, x0, *tables[0], flag)
     feed0 = feed_side(*pairs0[1:], query0[2])
-    y0 = forward_rest(feed0, kept0, mixed, first).astype(BF)
+    y0 = forward_rest(feed0, kept0, pos, windows[0], flag).astype(BF)
     cols1 = (cols1, exchange(cols1, "section", 1))
     rows1 = (rows1, exchange(rows1, "section", 1))
     query1 = query_side([v[..., :QP] for v in cols1])
-    kept1 = forward_keys(query1, y0.astype(F32), *tables[1], first)
-    mixed = forward_attend(kept1, places, all_places, windows[1])
+    kept1 = forward_keys(query1, y0.astype(F32), *tables[1], flag)
     feed1 = feed_side([v[..., QP:] for v in cols1], rows1, query1[2])
-    y1 = forward_rest(feed1, kept1, mixed, first)
+    y1 = forward_rest(feed1, kept1, pos, windows[1], flag)
 
     middle1, branch1, wg_g, wg_out, wg_down, norm_grads = backward_feed(
-        feed1, kept1, cotangent, first
+        feed1, kept1, cotangent, flag
     )
     sum_g1 = reduce_cols(*wg_g)
     sum_b1 = reduce_rows(wg_out, wg_down)
     red_b1 = lax.psum_scatter(sum_b1, GRID, scatter_dimension=0).astype(F32)
-    scores1, kv_blocks = backward_attend(feed1[2], kept1, branch1, places, all_places, windows[1])
-    scores1, kv_blocks, sum_g1 = tie(scores1, kv_blocks, sum_g1)
+    grad_q1, kv_blocks = backward_attend(feed1[2], kept1, branch1, pos, windows[1], flag)
+    grad_q1, kv_blocks, sum_g1 = tie(grad_q1, kv_blocks, sum_g1)
     grad_kv = key_return(kv_blocks)
-    grad_q = backward_queries(kept1, scores1)
     grad1, wg_q, gain_zero, head_grads = backward_keys(
-        query1, kept1, middle1, grad_q, grad_kv, *tables[1], first
-    )
-    sum_q1 = reduce_query(wg_q, [gain_zero] + norm_grads, head_grads)
+        query1, kept1, middle1, grad_q1, grad_kv, *tables[1], flag
+    )
+    sum_q1 = reduce_query(wg_q, [gain_zero, norm_grads], head_grads)
     sum_c1 = jnp.concatenate([sum_q1, sum_g1], axis=-1)
     red_c1 = lax.psum_scatter(sum_c1, GRID, scatter_dimension=0).astype(F32)
     grad1 = grad1.astype(BF)
 
     middle0, branch0, wg_g, wg_out, wg_down, norm_grads = backward_feed(
-        feed0, kept0, grad1.astype(F32), first
+        feed0, kept0, grad1, flag
     )
     scat_g0 = Scatter(reduce_cols(*wg_g), True)
     scat_b0 = Scatter(reduce_rows(wg_out, wg_down), False)
-    scores0, kv_blocks = backward_attend(feed0[2], kept0, branch0, places, all_places, windows[0])
-    scores0, kv_blocks, *held = tie(scores0, kv_blocks, *scat_g0.values(), *scat_b0.values())
+    grad_q0, kv_blocks = backward_attend(feed0[2], kept0, branch0, pos, windows[0], flag)
+    grad_q0, kv_blocks, *held = tie(grad_q0, kv_blocks, *scat_g0.values(), *scat_b0.values())
     scat_g0.after(*held)
     scat_b0.after(*held)
     grad_kv = key_return(kv_blocks)
     scat_g0.plane(0)
     scat_b0.plane(0)
-    grad_q = backward_queries(kept0, scores0)
     grad0, wg_q, gain_zero, head_grads = backward_keys(
-        query0, kept0, middle0, grad_q, grad_kv, *tables[0], first
+        query0, kept0, middle0, grad_q0, grad_kv, *tables[0], flag
     )
     wg_q0, wg_q1, *held = tie(wg_q[0], wg_q[1], *scat_g0.values(), *scat_b0.values())
     scat_g0.after(*held)
     scat_b0.after(*held)
-    scat_q0 = Scatter(reduce_query((wg_q0, wg_q1), [gain_zero] + norm_grads, head_grads), False)
+    scat_q0 = Scatter(reduce_query((wg_q0, wg_q1), [gain_zero, norm_grads], head_grads), False)
     scat_g0.plane(1)
     scat_b0.plane(1)
     scat_q0.plane(0)

time: 556 us -> 590 us (1.061)
  waiting for transfers between devices: 190 us -> 312 us
  Pallas kernels: 0 us -> 82.4 us
  matrix products: 83.7 us -> 23.8 us
  local copies, waits for them, and re-layouts: 80.4 us -> 33.5 us
  other arithmetic: 97.5 us -> 59.4 us
  starting transfers between devices: 79.2 us -> 60.1 us
    pallas_call x0 -> x10, Pallas kernels: none -> 82.4 us  [whole_call(): pl.pallas_call(body, out_shape=[jax.ShapeDtypeStruct(s, t) for s, t in ou...]
    unnamed x5, waiting for transfers between devices: 13.5 us -> 79.8 us
    dot_general x32 -> x0, matrix products: 57.4 us -> none  [the longest x16 29.2 us: dot_t(): return jnp.einsum('tc,dc->td', a, b, preferred_element_type=F32)]
    all_gather x1, waiting for transfers between devices: 0.02 us -> 45.4 us  [local(): rows1 = lax.all_gather(rows1, GRID, axis=0)]
    ppermute x54, starting transfers between devices: 69.2 us -> 50 us  [exchange(): return lax.ppermute(shard, axis, pairs)]
    ppermute x54, waiting for transfers between devices: 126 us -> 144 us  [exchange(): return lax.ppermute(shard, axis, pairs)]
    unnamed x417 -> x127, local copies, waits for them, and re-layouts: 22.7 us -> 6.76 us
    reshape x18 -> x0, local copies, waits for them, and re-layouts: 13.1 us -> none  [the longest x2 5.11 us: backward_queries(): return grad_queries.reshape(-1, HEADS, HD)]
  transfers between devices with their start and end apart: 67 -> 67, of which waited for: 31 -> 35; matrix products, arithmetic and copies ran while one was open for 37% -> 16% of each run, Pallas kernels for 0% -> 9%
where the time goes in v4:
time: 590 us; the launch traced here: 586 us
  waiting for transfers between devices  312 us (53%)
  Pallas kernels  82.4 us (14%)
  starting transfers between devices  60.1 us (10%)
  other arithmetic  59.4 us (10%)
  local copies, waits for them, and re-layouts  33.5 us (6%)
  matrix products  23.8 us (4%)
  between operations  15.2 us (3%)
    ppermute x54, waiting for transfers between devices, exchange(): return lax.ppermute(shard, axis, pairs)  144 us
    pallas_call x10, Pallas kernels, whole_call(): pl.pallas_call(body, out_shape=[jax.ShapeDtypeStruct(s, t) for s, t in ou...  82.4 us
    unnamed x5, waiting for transfers between devices  79.8 us
    ppermute x54, starting transfers between devices, exchange(): return lax.ppermute(shard, axis, pairs)  50 us
    all_gather x1, waiting for transfers between devices, local(): rows1 = lax.all_gather(rows1, GRID, axis=0)  45.4 us
    dot_general x12, matrix products, t_dot(): return jnp.einsum('ta,tb->ab', a, b, preferred_element_type=F32)  23.8 us
    ppermute x9, waiting for transfers between devices, z_gather(): pieces.append(lax.ppermute(pieces[-1], 'fsdp', pairs))  23.2 us
    all_gather x1, waiting for transfers between devices, local(): cols1 = lax.all_gather(cols1, GRID, axis=0)  19.6 us
  transfers between devices with their start and end apart: 67, of which 35 were waited for; matrix products, arithmetic and copies ran while one was open for 16% of the time, Pallas kernels for 9%

profile of v4, /device:TPU:0, one launch (start us, length us, event | category | flops | bytes accessed | tf_op | source)
XLA Modules:
  0.0 585.9 jit_solution(6235037937718492009)
XLA Ops:
  14.7 3.0 collective-permute-start.12
  21.7 3.7 collective-permute-done.2
  26.8 4.8 collective-permute-done.3
  34.6 4.0 collective-permute-done.4
  39.3 2.6 collective-permute-done.19
  42.1 6.9 %collective-permute-done.20 = bf16[40,2048]{1,0:T(8,128)(2,1)S(1)} collective-permute-done((bf16[40,2048]{1,0:T(8,128)(2,1)S(1)}, bf16[40,2048]{1,0:T(8,128)(2,1)S(1)}, u32[]{:S(2)}, u32[]{:S(2)}) %collective-permute-start.20) | collective-permute-done | bytes 163872 | tf_op jit(solution)/shard_map/ppermute | solution.py:57
  60.4 6.0 %collective-permute-done.15 = bf16[4,1,1,96,640]{4,3,2,1,0:T(8,128)(2,1)S(1)} collective-permute-done((bf16[4,1,1,96,640]{4,3,2,1,0:T(8,128)(2,1)S(1)}, bf16[4,1,1,96,640]{4,3,2,1,0:T(8,128)(2,1)S(1)}, u32[]{:S(2)}, u32[]{:S(2)}) %collective-permute-start.15) | collective-permute-done | bytes 491552 | tf_op jit(solution)/shard_map/ppermute | solution.py:35
  67.3 6.3 %collective-permute-done.21 = bf16[2,1,1,40,2048]{4,3,0,2,1:T(8,128)(2,1)} collective-permute-done((bf16[2,1,1,40,2048]{4,3,0,2,1:T(8,128)(2,1)}, bf16[2,1,1,40,2048]{4,3,0,2,1:T(8,128)(2,1)}, u32[]{:S(2)}, u32[]{:S(2)}) %collective-permute-start.21) | collective-permute-done | bytes 327712 | tf_op jit(solution)/shard_map/ppermute | solution.py:35
  76.4 2.6 collective-permute-start.24
  78.9 13.5 %collective-permute-done.6 = bf16[4,2,1,40,896]{4,3,2,1,0:T(8,128)(2,1)S(1)} collective-permute-done((bf16[4,2,1,40,896]{4,3,2,1,0:T(8,128)(2,1)S(1)}, bf16[4,2,1,40,896]{4,3,2,1,0:T(8,128)(2,1)S(1)}, u32[]{:S(2)}, u32[]{:S(2)}) %collective-permute-start.6) | collective-permute-done | bytes 573472 | tf_op jit(solution)/shard_map/ppermute | solution.py:35
  92.8 12.5 %collective-permute-done.22 = bf16[2,1,2,40,2048]{4,3,0,2,1:T(8,128)(2,1)S(1)} collective-permute-done((bf16[2,1,2,40,2048]{4,3,0,2,1:T(8,128)(2,1)S(1)}, bf16[2,1,2,40,2048]{4,3,0,2,1:T(8,128)(2,1)S(1)}, u32[]{:S(2)}, u32[]{:S(2)}) %collective-permute-start.22) | collective-permute-done | bytes 655392 | tf_op jit(solution)/shard_map/ppermute | solution.py:35
  110.0 19.6 %all-gather.5.cloned.1.call-done = bf16[640,2944]{1,0:T(8,128)(2,1)} async-done(((bf16[40,2944]{1,0:T(8,128)(2,1)}), bf16[640,2944]{1,0:T(8,128)(2,1)}) %all-gather.5.cloned.1.call-update) | async-done | bytes 3768336 | tf_op jit(solution)/shard_map/all_gather | solution.py:577
  132.9 3.7 shard_map.152
  138.6 7.6 %collective-permute-done.8 = bf16[256,512]{1,0:T(8,128)(2,1)S(1)} collective-permute-done((bf16[256,512]{1,0:T(8,128)(2,1)S(1)}, bf16[256,512]{1,0:T(8,128)(2,1)S(1)}, u32[]{:S(2)}, u32[]{:S(2)}) %collective-permute-start.8) | collective-permute-done | bytes 262176 | tf_op jit(solution)/shard_map/ppermute | solution.py:35
  146.2 45.4 %all-gather.7.cloned.1.call-done = bf16[1536,640]{1,0:T(8,128)(2,1)} async-done(((bf16[96,640]{1,0:T(8,128)(2,1)}), bf16[1536,640]{1,0:T(8,128)(2,1)}) %all-gather.7.cloned.1.call-update) | async-done | bytes 1966096 | tf_op jit(solution)/shard_map/all_gather | solution.py:578
  193.4 8.1 %collective-permute-done.10 = bf16[256,512]{1,0:T(8,128)(2,1)S(1)} collective-permute-done((bf16[256,512]{1,0:T(8,128)(2,1)S(1)}, bf16[256,512]{1,0:T(8,128)(2,1)S(1)}, u32[]{:S(2)}, u32[]{:S(2)}) %collective-permute-start.10) | collective-permute-done | bytes 262176 | tf_op jit(solution)/shard_map/ppermute | solution.py:35
  201.5 2.9 broadcast_select_fusion.3
  207.9 13.4 %shard_map.153 = (bf16[256,1024]{1,0:T(8,128)(2,1)S(1)}, f32[256,640]{1,0:T(8,128)}, f32[256,640]{1,0:T(8,128)}, bf16[256,640]{1,0:T(8,128)(2,1)S(1)}, f32[256,2...) custom-call(s32[1]{0:T(128)} %bitcast.flag, ...), custom_call_target="tpu_custom_call" | custom-call | flops 3422552064 | bytes 20134916 | tf_op jit(solution)/shard_map/pallas_call | solution.py:196
  231.0 2.4 slice.207
  233.4 3.9 shard_map.154
  243.9 3.6 slice.215
  247.5 4.5 collective-permute-done.28
  253.0 12.8 %shard_map.155 = (bf16[256,1024]{1,0:T(8,128)(2,1)S(1)}, f32[256,640]{1,0:T(8,128)}, f32[256,640]{1,0:T(8,128)}, bf16[256,640]{1,0:T(8,128)(2,1)S(1)}, f32[256,2...) custom-call(s32[1]{0:T(128)} %bitcast.flag, ...), custom_call_target="tpu_custom_call" | custom-call | flops 3422552064 | bytes 20134916 | tf_op jit(solution)/shard_map/pallas_call | solution.py:196
  265.9 10.7 %shard_map.156 = (f32[256,640]{1,0:T(8,128)S(1)}, bf16[256,640]{1,0:T(8,128)(2,1)S(1)}, bf16[256,2048]{1,0:T(8,128)(2,1)}, bf16[256,2048]{1,0:T(8,128)(2,1)}, bf...) custom-call(s32[1]{0:T(128)} %bitcast.flag, bf16[256,640]{1,0:T(8,128)(2,1)S(1)} %get-tuple-element.206.dy, ...), custom_call_target="tpu_custom_call" | custom-call | flops 2013265920 | bytes 17778180 | tf_op jit(solution)/shard_map/pallas_call | solution.py:196
  276.6 4.0 convolution_convert_fusion.3
  285.6 8.7 %shard_map.157 = (f32[256,1024]{1,0:T(8,128)}, bf16[1024,512]{1,0:T(8,128)(2,1)}) custom-call(s32[1]{0:T(128)} %bitcast.flag, bf16[256,640]{1,0:T(8,128)(2,1)S(1)} %get-tuple-element.95.da, bf16[1024,640]{1,0:T(8,128)(2,1)} %bitcast.312, bf16[256,1024]{1,0:T(8,128)(2,1)S(1)} %copy-done.27, bf16[1024,512]{1,0:T(8,128)(2,1)} %copy-done.54, ...), custom_call_target="tpu_custom_call" | custom-call | flops 3019898880 | bytes 5313540 | tf_op jit(solution)/shard_map/pallas_call | solution.py:196
  294.4 4.2 add_convert_fusion.1
  304.7 3.1 collective-permute-done.32
  307.8 5.5 collective-permute-done.33
  313.5 5.2 shard_map.158
  320.1 10.4 %shard_map.159 = (f32[256,640]{1,0:T(8,128)S(1)}, bf16[256,640]{1,0:T(8,128)(2,1)S(1)}, bf16[256,2048]{1,0:T(8,128)(2,1)}, bf16[256,2048]{1,0:T(8,128)(2,1)}, bf...) custom-call(s32[1]{0:T(128)} %bitcast.flag, bf16[256,640]{1,0:T(8,128)(2,1)S(1)} %convert_element_type.277.dy, ...), custom_call_target="tpu_custom_call" | custom-call | flops 2013265920 | bytes 17778180 | tf_op jit(solution)/shard_map/pallas_call | solution.py:196
  330.5 3.8 convolution_convert_fusion.2
  340.3 3.7 add_convert_fusion.2
  347.5 8.7 %shard_map.160 = (f32[256,1024]{1,0:T(8,128)}, bf16[1024,512]{1,0:T(8,128)(2,1)}) custom-call(s32[1]{0:T(128)} %bitcast.flag, bf16[256,640]{1,0:T(8,128)(2,1)S(1)} %get-tuple-element.112.da, bf16[1024,640]{1,0:T(8,128)(2,1)} %bitcast.310, bf16[256,1024]{1,0:T(8,128)(2,1)S(1)} %copy-done.25, bf16[1024,512]{1,0:T(8,128)(2,1)} %copy-done.55, ...), custom_call_target="tpu_custom_call" | custom-call | flops 3019898880 | bytes 5313540 | tf_op jit(solution)/shard_map/pallas_call | solution.py:196
  358.4 3.3 add_convert_fusion
  371.0 24.9 %collective-permute-done.37 = bf16[256,512]{1,0:T(8,128)(2,1)S(1)} collective-permute-done((bf16[256,512]{1,0:T(8,128)(2,1)S(1)}, bf16[256,512]{1,0:T(8,128)(2,1)S(1)}, u32[]{:S(2)}, u32[]{:S(2)}) %collective-permute-start.37) | collective-permute-done | bytes 262176 | tf_op jit(solution)/shard_map/ppermute | solution.py:35
  397.2 5.8 collective-permute-done.39
  403.2 5.0 shard_map.161
  412.8 3.9 collective-permute-done.41
  433.6 2.9 maximum_select_fusion
  438.1 4.0 collective-permute-done.51
  442.2 7.7 %collective-permute-done.50 = bf16[2,1,1,40,2048]{4,3,0,2,1:T(8,128)(2,1)S(1)} collective-permute-done((bf16[2,1,1,40,2048]{4,3,0,2,1:T(8,128)(2,1)S(1)}, bf16[2,1,1,40,2048]{4,3,0,2,1:T(8,128)(2,1)S(1)}, u32[]{:S(2)}, u32[]{:S(2)}) %collective-permute-start.50) | collective-permute-done | bytes 327712 | tf_op jit(solution)/shard_map/ppermute | solution.py:35
  456.9 3.4 collective-permute-done.52
  460.3 7.4 %collective-permute-done.53 = bf16[40,2048]{1,0:T(8,128)(2,1)S(1)} collective-permute-done((bf16[40,2048]{1,0:T(8,128)(2,1)S(1)}, bf16[40,2048]{1,0:T(8,128)(2,1)S(1)}, u32[]{:S(2)}, u32[]{:S(2)}) %collective-permute-start.53) | collective-permute-done | bytes 163872 | tf_op jit(solution)/shard_map/ppermute | solution.py:35
  473.6 2.3 collective-permute-start.60
  481.3 5.0 collective-permute-done.59
  487.4 5.4 collective-permute-done.48
  492.8 79.7 %reduce-scatter.8.cloned.1.call-done = bf16[1,40,2944]{2,1,0:T(8,128)(2,1)} async-done(((bf16[16,40,2944]{2,1,0:T(8,128)(2,1)}), bf16[1,40,2944]{2,1,0:T(8,128)(2,1)}) %reduce-scatter.8.cloned.1.call-update) | async-done | bytes 235536
  (398 shorter events, 148.4 us)
Async XLA Ops:
  7.2 122.5 %all-gather.5.cloned.1.call-start = ((), (), s32[]{:S(2)}) async-start(), calls=%async_computation.3 | async-start | bytes 4003840 | tf_op jit(solution)/shard_map/all_gather | solution.py:577
  14.7 10.7 %collective-permute-start.12 = (bf16[96,640]{1,0:T(8,128)(2,1)S(1)}, bf16[96,640]{1,0:T(8,128)(2,1)S(1)}, u32[]{:S(2)}, u32[]{:S(2)}) collective-permute-start(bf16[96,640]{1,0:T(8,128)(2,1)S(1)} %get-tuple-element.239), channel_id=1, source_target_pairs={{0,4},{4,8},{8,12},{12,0},{1,5},{5,9},{9,13},{13,1},{2,6},{6,10},{... | collective-permute-start | bytes 368648 | tf_op jit(solution)/shard_map/ppermute | solution.py:57
  20.1 12.8 %collective-permute-start.18 = (bf16[40,2048]{1,0:T(8,128)(2,1)S(1)}, bf16[40,2048]{1,0:T(8,128)(2,1)S(1)}, u32[]{:S(2)}, u32[]{:S(2)}) collective-permute-start(bf16[40,2048]{1,0:T(8,128)(2,1)S(1)} %slice.203), channel_id=1, source_target_pairs={{0,4},{4,8},{8,12},{12,0},{1,5},{5,9},{9,13},{13,1},{2,6},{6,10},{... | collective-permute-start | bytes 491528 | tf_op jit(solution)/shard_map/ppermute | solution.py:57
  50.7 141.0 %all-gather.7.cloned.1.call-start = ((), (), s32[]{:S(2)}) async-start(), calls=%async_computation.4 | async-start | bytes 2088960 | tf_op jit(solution)/shard_map/all_gather | solution.py:578
  52.3 14.1 %collective-permute-start.15 = (bf16[4,1,1,96,640]{4,3,2,1,0:T(8,128)(2,1)S(1)}, bf16[4,1,1,96,640]{4,3,2,1,0:T(8,128)(2,1)S(1)}, u32[]{:S(2)}, u32[]{:S(2)}) collective-permute-start(bf16[4,1,1,96,640]{4,3,2,1,0:T(8,128)(2,1)S(1)} %maximum_bitcast_fusion.1), channel_id=1, source_target_pairs={{0,1},{1,0},{2,3},{3,2},{4,5},{5,4},{6,7},{7,6},{8,9},{9,8},{10,11... | collective-permute-start | bytes 1474568 | tf_op jit(solution)/shard_map/ppermute | solution.py:35
  54.5 76.1 %collective-permute-start = (bf16[256,640]{1,0:T(8,128)(2,1)}, bf16[256,640]{1,0:T(8,128)(2,1)}, u32[]{:S(2)}, u32[]{:S(2)}) collective-permute-start(bf16[256,640]{1,0:T(8,128)(2,1)} %dynamic-slice_bitcast_fusion.8), channel_id=1, source_target_pairs={{0,16},{16,0},{1,17},{17,1},{2,18},{18,2},{3,19},{19,3},{4,20},{20... | collective-permute-start | bytes 983048 | tf_op jit(solution)/shard_map/ppermute | solution.py:35
  54.5 19.0 %collective-permute-start.21 = (bf16[2,1,1,40,2048]{4,3,0,2,1:T(8,128)(2,1)}, bf16[2,1,1,40,2048]{4,3,0,2,1:T(8,128)(2,1)}, u32[]{:S(2)}, u32[]{:S(2)}) collective-permute-start(bf16[2,1,1,40,2048]{4,3,0,2,1:T(8,128)(2,1)} %maximum_bitcast_fusion.2), channel_id=1, source_target_pairs={{0,1},{1,0},{2,3},{3,2},{4,5},{5,4},{6,7},{7,6},{8,9},{9,8},{10,11... | collective-permute-start | bytes 983048 | tf_op jit(solution)/shard_map/ppermute | solution.py:35
  55.1 20.2 %collective-permute-start.23 = (bf16[2,1,1,40,2048]{4,3,0,2,1:T(8,128)(2,1)}, bf16[2,1,1,40,2048]{4,3,0,2,1:T(8,128)(2,1)}, u32[]{:S(2)}, u32[]{:S(2)}) collective-permute-start(bf16[2,1,1,40,2048]{4,3,0,2,1:T(8,128)(2,1)} %maximum_bitcast_fusion.3), channel_id=1, source_target_pairs={{0,2},{1,3},{2,0},{3,1},{4,6},{5,7},{6,4},{7,5},{8,10},{9,11},{10,... | collective-permute-start | bytes 983048 | tf_op jit(solution)/shard_map/ppermute | solution.py:35
  55.6 425.7 %reduce-scatter.6.cloned.1.call-start = ((), (), s32[]{:S(2)}) async-start(), calls=%async_computation.2 | async-start | bytes 2088960 | tf_op jit(solution)/shard_map/reduce_scatter | solution.py:598
  58.8 33.6 %collective-permute-start.6 = (bf16[4,2,1,40,896]{4,3,2,1,0:T(8,128)(2,1)S(1)}, bf16[4,2,1,40,896]{4,3,2,1,0:T(8,128)(2,1)S(1)}, u32[]{:S(2)}, u32[]{:S(2)}) collective-permute-start(bf16[4,2,1,40,896]{4,3,2,1,0:T(8,128)(2,1)S(1)} %pad_maximum_fusion.23), channel_id=1, source_target_pairs={{0,1},{1,0},{2,3},{3,2},{4,5},{5,4},{6,7},{7,6},{8,9},{9,8},{10,11... | collective-permute-start | bytes 1720328 | tf_op jit(solution)/shard_map/ppermute | solution.py:35
  66.7 39.3 %collective-permute-start.16 = (bf16[4,1,2,96,640]{4,3,2,1,0:T(8,128)(2,1)S(1)}, bf16[4,1,2,96,640]{4,3,2,1,0:T(8,128)(2,1)S(1)}, u32[]{:S(2)}, u32[]{:S(2)}) collective-permute-start(bf16[4,1,2,96,640]{4,3,2,1,0:T(8,128)(2,1)S(1)} %pad_maximum_fusion.20), channel_id=1, source_target_pairs={{0,2},{1,3},{2,0},{3,1},{4,6},{5,7},{6,4},{7,5},{8,10},{9,11},{10,... | collective-permute-start | bytes 2949128 | tf_op jit(solution)/shard_map/ppermute | solution.py:35
  74.6 30.7 %collective-permute-start.22 = (bf16[2,1,2,40,2048]{4,3,0,2,1:T(8,128)(2,1)S(1)}, bf16[2,1,2,40,2048]{4,3,0,2,1:T(8,128)(2,1)S(1)}, u32[]{:S(2)}, u32[]{:S(2)}) collective-permute-start(bf16[2,1,2,40,2048]{4,3,0,2,1:T(8,128)(2,1)S(1)} %pad_maximum_fusion.21), channel_id=1, source_target_pairs={{0,2},{1,3},{2,0},{3,1},{4,6},{5,7},{6,4},{7,5},{8,10},{9,11},{10,... | collective-permute-start | bytes 1966088 | tf_op jit(solution)/shard_map/ppermute | solution.py:35
  76.4 29.3 %collective-permute-start.24 = (bf16[2,2,1,40,2048]{4,3,0,2,1:T(8,128)(2,1)S(1)}, bf16[2,2,1,40,2048]{4,3,0,2,1:T(8,128)(2,1)S(1)}, u32[]{:S(2)}, u32[]{:S(2)}) collective-permute-start(bf16[2,2,1,40,2048]{4,3,0,2,1:T(8,128)(2,1)S(1)} %pad_maximum_fusion.22), channel_id=1, source_target_pairs={{0,1},{1,0},{2,3},{3,2},{4,5},{5,4},{6,7},{7,6},{8,9},{9,8},{10,11... | collective-permute-start | bytes 1966088 | tf_op jit(solution)/shard_map/ppermute | solution.py:35
  92.7 40.3 %collective-permute-start.7 = (bf16[16,40,896]{2,1,0:T(8,128)(2,1)S(1)}, bf16[16,40,896]{2,1,0:T(8,128)(2,1)}, u32[]{:S(2)}, u32[]{:S(2)}) collective-permute-start(bf16[16,40,896]{2,1,0:T(8,128)(2,1)S(1)} %bitcast.265), channel_id=1, source_target_pairs={{0,16},{16,0},{1,17},{17,1},{2,18},{18,2},{3,19},{19,3},{4,20},{20... | collective-permute-start | bytes 3440648 | tf_op jit(solution)/shard_map/ppermute | solution.py:35
  107.6 93.9 %collective-permute-start.17 = (bf16[16,96,640]{2,1,0:T(8,128)(2,1)}, bf16[16,96,640]{2,1,0:T(8,128)(2,1)}, u32[]{:S(2)}, u32[]{:S(2)}) collective-permute-start(bf16[16,96,640]{2,1,0:T(8,128)(2,1)} %bitcast.39), channel_id=1, source_target_pairs={{0,16},{16,0},{1,17},{17,1},{2,18},{18,2},{3,19},{19,3},{4,20},{20... | collective-permute-start | bytes 5898248 | tf_op jit(solution)/shard_map/ppermute | solution.py:35
  109.4 98.5 %collective-permute-start.25 = (bf16[16,40,2048]{2,1,0:T(8,128)(2,1)}, bf16[16,40,2048]{2,1,0:T(8,128)(2,1)}, u32[]{:S(2)}, u32[]{:S(2)}) collective-permute-start(bf16[16,40,2048]{2,1,0:T(8,128)(2,1)} %pad_maximum_fusion.1), channel_id=1, source_target_pairs={{0,16},{16,0},{1,17},{17,1},{2,18},{18,2},{3,19},{19,3},{4,20},{20... | collective-permute-start | bytes 7864328 | tf_op jit(solution)/shard_map/ppermute | solution.py:35
  129.6 101.4 %collective-permute-start.26 = (bf16[16,40,2944]{2,1,0:T(8,128)(2,1)}, bf16[16,40,2944]{2,1,0:T(8,128)(2,1)}, u32[]{:S(2)}, u32[]{:S(2)}) collective-permute-start(bf16[16,40,2944]{2,1,0:T(8,128)(2,1)} %bitcast.298), channel_id=1, source_target_pairs={{0,16},{16,0},{1,17},{17,1},{2,18},{18,2},{3,19},{19,3},{4,20},{20... | collective-permute-start | bytes 11304968 | tf_op jit(solution)/shard_map/ppermute | solution.py:35
  137.9 53.9 %collective-permute-start.9 = (bf16[256,512]{1,0:T(8,128)(2,1)S(1)}, bf16[256,512]{1,0:T(8,128)(2,1)S(1)}, u32[]{:S(2)}, u32[]{:S(2)}) collective-permute-start(bf16[256,512]{1,0:T(8,128)(2,1)S(1)} %get-tuple-element.84), channel_id=1, source_target_pairs={{0,2},{1,3},{2,0},{3,1},{4,6},{5,7},{6,4},{7,5},{8,10},{9,11},{10,... | collective-permute-start | bytes 786440 | tf_op jit(solution)/shard_map/ppermute | solution.py:35
  191.6 31.6 %collective-permute-start.30 = (bf16[16,96,640]{2,1,0:T(8,128)(2,1)}, bf16[16,96,640]{2,1,0:T(8,128)(2,1)}, u32[]{:S(2)}, u32[]{:S(2)}) collective-permute-start(bf16[16,96,640]{2,1,0:T(8,128)(2,1)} %bitcast.303), channel_id=1, source_target_pairs={{0,16},{16,0},{1,17},{17,1},{2,18},{18,2},{3,19},{19,3},{4,20},{20... | collective-permute-start | bytes 5898248 | tf_op jit(solution)/shard_map/ppermute | solution.py:35
  191.8 9.7 %collective-permute-start.10 = (bf16[256,512]{1,0:T(8,128)(2,1)S(1)}, bf16[256,512]{1,0:T(8,128)(2,1)S(1)}, u32[]{:S(2)}, u32[]{:S(2)}) collective-permute-start(bf16[256,512]{1,0:T(8,128)(2,1)S(1)} %get-tuple-element.84), channel_id=1, source_target_pairs={{0,3},{1,2},{2,1},{3,0},{4,7},{5,6},{6,5},{7,4},{8,11},{9,10},{10,... | collective-permute-start | bytes 786440 | tf_op jit(solution)/shard_map/ppermute | solution.py:35
  237.2 10.3 %collective-permute-start.27 = (bf16[256,512]{1,0:T(8,128)(2,1)S(1)}, bf16[256,512]{1,0:T(8,128)(2,1)S(1)}, u32[]{:S(2)}, u32[]{:S(2)}) collective-permute-start(bf16[256,512]{1,0:T(8,128)(2,1)S(1)} %get-tuple-element.88), channel_id=1, source_target_pairs={{0,1},{1,0},{2,3},{3,2},{4,5},{5,4},{6,7},{7,6},{8,9},{9,8},{10,11... | collective-permute-start | bytes 786440 | tf_op jit(solution)/shard_map/ppermute | solution.py:35
  238.7 13.3 %collective-permute-start.28 = (bf16[256,512]{1,0:T(8,128)(2,1)S(1)}, bf16[256,512]{1,0:T(8,128)(2,1)S(1)}, u32[]{:S(2)}, u32[]{:S(2)}) collective-permute-start(bf16[256,512]{1,0:T(8,128)(2,1)S(1)} %get-tuple-element.88), channel_id=1, source_target_pairs={{0,2},{1,3},{2,0},{3,1},{4,6},{5,7},{6,4},{7,5},{8,10},{9,11},{10,... | collective-permute-start | bytes 786440 | tf_op jit(solution)/shard_map/ppermute | solution.py:35
  280.6 13.8 %collective-permute-start.31 = (bf16[640,2048]{1,0:T(8,128)(2,1)}, bf16[640,2048]{1,0:T(8,128)(2,1)}, u32[]{:S(2)}, u32[]{:S(2)}) collective-permute-start(bf16[640,2048]{1,0:T(8,128)(2,1)} %convolution_convert_fusion.3), channel_id=1, source_target_pairs={{0,16},{16,0},{1,17},{17,1},{2,18},{18,2},{3,19},{19,3},{4,20},{20... | collective-permute-start | bytes 7864328 | tf_op jit(solution)/shard_map/ppermute | solution.py:35
  299.3 14.0 %collective-permute-start.33 = (bf16[256,512]{1,0:T(8,128)(2,1)S(1)}, bf16[256,512]{1,0:T(8,128)(2,1)S(1)}, u32[]{:S(2)}, u32[]{:S(2)}) collective-permute-start(bf16[256,512]{1,0:T(8,128)(2,1)S(1)} %get-tuple-element.205), channel_id=1, source_target_pairs={{0,2},{1,3},{2,0},{3,1},{4,6},{5,7},{6,4},{7,5},{8,10},{9,11},{10,... | collective-permute-start | bytes 786440 | tf_op jit(solution)/shard_map/ppermute | solution.py:35
  300.8 12.6 %collective-permute-start.34 = (bf16[256,512]{1,0:T(8,128)(2,1)S(1)}, bf16[256,512]{1,0:T(8,128)(2,1)S(1)}, u32[]{:S(2)}, u32[]{:S(2)}) collective-permute-start(bf16[256,512]{1,0:T(8,128)(2,1)S(1)} %get-tuple-element.204), channel_id=1, source_target_pairs={{0,3},{1,2},{2,1},{3,0},{4,7},{5,6},{6,5},{7,4},{8,11},{9,10},{10,... | collective-permute-start | bytes 786440 | tf_op jit(solution)/shard_map/ppermute | solution.py:35
  304.7 35.6 %collective-permute-start.61 = (bf16[16,96,640]{2,1,0:T(8,128)(2,1)}, bf16[16,96,640]{2,1,0:T(8,128)(2,1)}, u32[]{:S(2)}, u32[]{:S(2)}) collective-permute-start(bf16[16,96,640]{2,1,0:T(8,128)(2,1)} %pad_maximum_fusion.6), channel_id=1, source_target_pairs={{0,16},{16,0},{1,17},{17,1},{2,18},{18,2},{3,19},{19,3},{4,20},{20... | collective-permute-start | bytes 5898248 | tf_op jit(solution)/shard_map/ppermute | solution.py:35
  334.3 24.2 %collective-permute-start.35 = (bf16[640,2048]{1,0:T(8,128)(2,1)}, bf16[640,2048]{1,0:T(8,128)(2,1)}, u32[]{:S(2)}, u32[]{:S(2)}) collective-permute-start(bf16[640,2048]{1,0:T(8,128)(2,1)} %convolution_convert_fusion.2), channel_id=1, source_target_pairs={{0,16},{16,0},{1,17},{17,1},{2,18},{18,2},{3,19},{19,3},{4,20},{20... | collective-permute-start | bytes 7864328 | tf_op jit(solution)/shard_map/ppermute | solution.py:35
  339.7 16.6 %collective-permute-start.36 = (bf16[16,96,640]{2,1,0:T(8,128)(2,1)}, bf16[16,96,640]{2,1,0:T(8,128)(2,1)}, u32[]{:S(2)}, u32[]{:S(2)}) collective-permute-start(bf16[16,96,640]{2,1,0:T(8,128)(2,1)} %pad_maximum_fusion.5), channel_id=1, source_target_pairs={{0,16},{16,0},{1,17},{17,1},{2,18},{18,2},{3,19},{19,3},{4,20},{20... | collective-permute-start | bytes 5898248 | tf_op jit(solution)/shard_map/ppermute | solution.py:35
  344.0 228.5 %reduce-scatter.8.cloned.1.call-start = ((), (), s32[]{:S(2)}) async-start(), calls=%async_computation.5 | async-start | bytes 4003840
  363.1 55.7 %collective-permute-start.43 = (bf16[4,2,1,96,640]{4,3,2,1,0:T(8,128)(2,1)}, bf16[4,2,1,96,640]{4,3,2,1,0:T(8,128)(2,1)}, u32[]{:S(2)}, u32[]{:S(2)}) collective-permute-start(bf16[4,2,1,96,640]{4,3,2,1,0:T(8,128)(2,1)} %constant_dynamic-slice_fusion.5), channel_id=1, source_target_pairs={{0,1},{1,0},{2,3},{3,2},{4,5},{5,4},{6,7},{7,6},{8,9},{9,8},{10,11... | collective-permute-start | bytes 2949128 | tf_op jit(solution)/shard_map/ppermute | solution.py:35
  364.7 31.2 %collective-permute-start.37 = (bf16[256,512]{1,0:T(8,128)(2,1)S(1)}, bf16[256,512]{1,0:T(8,128)(2,1)S(1)}, u32[]{:S(2)}, u32[]{:S(2)}) collective-permute-start(bf16[256,512]{1,0:T(8,128)(2,1)S(1)} %get-tuple-element.200), channel_id=1, source_target_pairs={{0,1},{1,0},{2,3},{3,2},{4,5},{5,4},{6,7},{7,6},{8,9},{9,8},{10,11... | collective-permute-start | bytes 786440 | tf_op jit(solution)/shard_map/ppermute | solution.py:35
  365.7 31.6 %collective-permute-start.38 = (bf16[256,512]{1,0:T(8,128)(2,1)S(1)}, bf16[256,512]{1,0:T(8,128)(2,1)S(1)}, u32[]{:S(2)}, u32[]{:S(2)}) collective-permute-start(bf16[256,512]{1,0:T(8,128)(2,1)S(1)} %get-tuple-element.202), channel_id=1, source_target_pairs={{0,2},{1,3},{2,0},{3,1},{4,6},{5,7},{6,4},{7,5},{8,10},{9,11},{10,... | collective-permute-start | bytes 786440 | tf_op jit(solution)/shard_map/ppermute | solution.py:35
  366.8 36.3 %collective-permute-start.39 = (bf16[256,512]{1,0:T(8,128)(2,1)S(1)}, bf16[256,512]{1,0:T(8,128)(2,1)S(1)}, u32[]{:S(2)}, u32[]{:S(2)}) collective-permute-start(bf16[256,512]{1,0:T(8,128)(2,1)S(1)} %get-tuple-element.201), channel_id=1, source_target_pairs={{0,3},{1,2},{2,1},{3,0},{4,7},{5,6},{6,5},{7,4},{8,11},{9,10},{10,... | collective-permute-start | bytes 786440 | tf_op jit(solution)/shard_map/ppermute | solution.py:35
  369.1 41.4 %collective-permute-start.42 = (bf16[2,1,2,40,2048]{4,3,0,2,1:T(8,128)(2,1)}, bf16[2,1,2,40,2048]{4,3,0,2,1:T(8,128)(2,1)}, u32[]{:S(2)}, u32[]{:S(2)}) collective-permute-start(bf16[2,1,2,40,2048]{4,3,0,2,1:T(8,128)(2,1)} %constant_dynamic-slice_fusion.6), channel_id=1, source_target_pairs={{0,2},{1,3},{2,0},{3,1},{4,6},{5,7},{6,4},{7,5},{8,10},{9,11},{10,... | collective-permute-start | bytes 1966088 | tf_op jit(solution)/shard_map/ppermute | solution.py:35
  395.9 20.8 %collective-permute-start.41 = (bf16[2,2,1,40,2048]{4,3,0,2,1:T(8,128)(2,1)}, bf16[2,2,1,40,2048]{4,3,0,2,1:T(8,128)(2,1)}, u32[]{:S(2)}, u32[]{:S(2)}) collective-permute-start(bf16[2,2,1,40,2048]{4,3,0,2,1:T(8,128)(2,1)} %constant_dynamic-slice_fusion.7), channel_id=1, source_target_pairs={{0,1},{1,0},{2,3},{3,2},{4,5},{5,4},{6,7},{7,6},{8,9},{9,8},{10,11... | collective-permute-start | bytes 1966088 | tf_op jit(solution)/shard_map/ppermute | solution.py:35
  431.3 10.8 %collective-permute-start.51 = (bf16[2,1,1,40,2048]{4,3,0,2,1:T(8,128)(2,1)S(1)}, bf16[2,1,1,40,2048]{4,3,0,2,1:T(8,128)(2,1)S(1)}, u32[]{:S(2)}, u32[]{:S(2)}) collective-permute-start(bf16[2,1,1,40,2048]{4,3,0,2,1:T(8,128)(2,1)S(1)} %constant_dynamic-slice_fusion.1), channel_id=1, source_target_pairs={{0,1},{1,0},{2,3},{3,2},{4,5},{5,4},{6,7},{7,6},{8,9},{9,8},{10,11... | collective-permute-start | bytes 983048 | tf_op jit(solution)/shard_map/ppermute | solution.py:35
  436.5 13.3 %collective-permute-start.50 = (bf16[2,1,1,40,2048]{4,3,0,2,1:T(8,128)(2,1)S(1)}, bf16[2,1,1,40,2048]{4,3,0,2,1:T(8,128)(2,1)S(1)}, u32[]{:S(2)}, u32[]{:S(2)}) collective-permute-start(bf16[2,1,1,40,2048]{4,3,0,2,1:T(8,128)(2,1)S(1)} %constant_dynamic-slice_fusion.2), channel_id=1, source_target_pairs={{0,2},{1,3},{2,0},{3,1},{4,6},{5,7},{6,4},{7,5},{8,10},{9,11},{10,... | collective-permute-start | bytes 983048 | tf_op jit(solution)/shard_map/ppermute | solution.py:35
  450.2 10.1 %collective-permute-start.52 = (bf16[40,2048]{1,0:T(8,128)(2,1)S(1)}, bf16[40,2048]{1,0:T(8,128)(2,1)S(1)}, u32[]{:S(2)}, u32[]{:S(2)}) collective-permute-start(bf16[40,2048]{1,0:T(8,128)(2,1)S(1)} %get-tuple-element.216), channel_id=1, source_target_pairs={{0,4},{4,0},{8,12},{12,8},{1,5},{5,1},{9,13},{13,9},{2,6},{6,2},{1... | collective-permute-start | bytes 491528 | tf_op jit(solution)/shard_map/ppermute | solution.py:35
  451.5 16.2 %collective-permute-start.53 = (bf16[40,2048]{1,0:T(8,128)(2,1)S(1)}, bf16[40,2048]{1,0:T(8,128)(2,1)S(1)}, u32[]{:S(2)}, u32[]{:S(2)}) collective-permute-start(bf16[40,2048]{1,0:T(8,128)(2,1)S(1)} %get-tuple-element.217), channel_id=1, source_target_pairs={{0,8},{4,12},{8,0},{12,4},{1,9},{5,13},{9,1},{13,5},{2,10},{6,14},... | collective-permute-start | bytes 491528 | tf_op jit(solution)/shard_map/ppermute | solution.py:35
  452.7 15.0 %collective-permute-start.54 = (bf16[40,2048]{1,0:T(8,128)(2,1)S(1)}, bf16[40,2048]{1,0:T(8,128)(2,1)S(1)}, u32[]{:S(2)}, u32[]{:S(2)}) collective-permute-start(bf16[40,2048]{1,0:T(8,128)(2,1)S(1)} %get-tuple-element.218), channel_id=1, source_target_pairs={{0,12},{4,8},{8,4},{12,0},{1,13},{5,9},{9,5},{13,1},{2,14},{6,10},... | collective-permute-start | bytes 491528 | tf_op jit(solution)/shard_map/ppermute | solution.py:35
  454.7 14.4 %collective-permute-start.45 = (bf16[4,2,1,40,896]{4,3,2,1,0:T(8,128)(2,1)S(1)}, bf16[4,2,1,40,896]{4,3,2,1,0:T(8,128)(2,1)S(1)}, u32[]{:S(2)}, u32[]{:S(2)}) collective-permute-start(bf16[4,2,1,40,896]{4,3,2,1,0:T(8,128)(2,1)S(1)} %constant_dynamic-slice_fusion.4), channel_id=1, source_target_pairs={{0,1},{1,0},{2,3},{3,2},{4,5},{5,4},{6,7},{7,6},{8,9},{9,8},{10,11... | collective-permute-start | bytes 1720328 | tf_op jit(solution)/shard_map/ppermute | solution.py:35
  456.2 15.1 %collective-permute-start.57 = (bf16[4,1,1,96,640]{4,3,2,1,0:T(8,128)(2,1)S(1)}, bf16[4,1,1,96,640]{4,3,2,1,0:T(8,128)(2,1)S(1)}, u32[]{:S(2)}, u32[]{:S(2)}) collective-permute-start(bf16[4,1,1,96,640]{4,3,2,1,0:T(8,128)(2,1)S(1)} %constant_dynamic-slice_fusion), channel_id=1, source_target_pairs={{0,2},{1,3},{2,0},{3,1},{4,6},{5,7},{6,4},{7,5},{8,10},{9,11},{10,... | collective-permute-start | bytes 1474568 | tf_op jit(solution)/shard_map/ppermute | solution.py:35
  472.5 13.7 %collective-permute-start.59 = (bf16[96,640]{1,0:T(8,128)(2,1)S(1)}, bf16[96,640]{1,0:T(8,128)(2,1)S(1)}, u32[]{:S(2)}, u32[]{:S(2)}) collective-permute-start(bf16[96,640]{1,0:T(8,128)(2,1)S(1)} %get-tuple-element.229), channel_id=1, source_target_pairs={{0,8},{4,12},{8,0},{12,4},{1,9},{5,13},{9,1},{13,5},{2,10},{6,14},... | collective-permute-start | bytes 368648 | tf_op jit(solution)/shard_map/ppermute | solution.py:35
  473.6 12.7 %collective-permute-start.60 = (bf16[96,640]{1,0:T(8,128)(2,1)S(1)}, bf16[96,640]{1,0:T(8,128)(2,1)S(1)}, u32[]{:S(2)}, u32[]{:S(2)}) collective-permute-start(bf16[96,640]{1,0:T(8,128)(2,1)S(1)} %get-tuple-element.228), channel_id=1, source_target_pairs={{0,12},{4,8},{8,4},{12,0},{1,13},{5,9},{9,5},{13,1},{2,14},{6,10},... | collective-permute-start | bytes 368648 | tf_op jit(solution)/shard_map/ppermute | solution.py:35
  476.5 10.8 %collective-permute-start.47 = (bf16[40,896]{1,0:T(8,128)(2,1)S(1)}, bf16[40,896]{1,0:T(8,128)(2,1)S(1)}, u32[]{:S(2)}, u32[]{:S(2)}) collective-permute-start(bf16[40,896]{1,0:T(8,128)(2,1)S(1)} %get-tuple-element.242), channel_id=1, source_target_pairs={{0,4},{4,0},{8,12},{12,8},{1,5},{5,1},{9,13},{13,9},{2,6},{6,2},{1... | collective-permute-start | bytes 215048 | tf_op jit(solution)/shard_map/ppermute | solution.py:35
  478.8 13.9 %collective-permute-start.48 = (bf16[40,896]{1,0:T(8,128)(2,1)S(1)}, bf16[40,896]{1,0:T(8,128)(2,1)S(1)}, u32[]{:S(2)}, u32[]{:S(2)}) collective-permute-start(bf16[40,896]{1,0:T(8,128)(2,1)S(1)} %get-tuple-element.244), channel_id=1, source_target_pairs={{0,8},{4,12},{8,0},{12,4},{1,9},{5,13},{9,1},{13,5},{2,10},{6,14},... | collective-permute-start | bytes 215048 | tf_op jit(solution)/shard_map/ppermute | solution.py:35
  479.8 12.9 %collective-permute-start.49 = (bf16[40,896]{1,0:T(8,128)(2,1)S(1)}, bf16[40,896]{1,0:T(8,128)(2,1)S(1)}, u32[]{:S(2)}, u32[]{:S(2)}) collective-permute-start(bf16[40,896]{1,0:T(8,128)(2,1)S(1)} %get-tuple-element.243), channel_id=1, source_target_pairs={{0,12},{4,8},{8,4},{12,0},{1,13},{5,9},{9,5},{13,1},{2,14},{6,10},... | collective-permute-start | bytes 215048 | tf_op jit(solution)/shard_map/ppermute | solution.py:35
  487.3 86.4 %collective-permute-start.62 = (f32[96,640]{1,0:T(8,128)S(1)}, f32[96,640]{1,0:T(8,128)S(1)}, u32[]{:S(2)}, u32[]{:S(2)}) collective-permute-start(f32[96,640]{1,0:T(8,128)S(1)} %get-tuple-element.174), channel_id=1, source_target_pairs={{0,16},{16,0},{1,17},{17,1},{2,18},{18,2},{3,19},{19,3},{4,20},{20... | collective-permute-start | bytes 737288 | tf_op jit(solution)/shard_map/ppermute | solution.py:35
  (76 other events, 864.5 us)
Sparse Core Ops, SparseCore 0:
  50.8 78.8 all-gather.4
  133.0 58.5 all-gather.6
  344.1 132.3 reduce-scatter.5
  478.8 93.6 reduce-scatter.7

commit v5 on v4

--- a/solution.py
+++ b/solution.py
@@ -22,7 +22,6 @@
 BASES = (math.log(10000.0), math.log(1000000.0))
 SCALE = 1.0 / math.sqrt(HD)
 BF = jnp.bfloat16
-GRID = ("fsdp", "ctx")
 F32 = jnp.float32
 
 
@@ -94,22 +93,32 @@
     return total
 
 
+def z_ring_scatter(buf):
+    count = lax.axis_size("fsdp")
+    pairs = [(i, (i + 1) % count) for i in range(count)]
+    me = lax.axis_index("fsdp")
+
+    def block(back):
+        return lax.dynamic_index_in_dim(buf, (me - back) % count, 0, False)
+
+    total = block(1)
+    for step in range(count - 1):
+        recv = lax.ppermute(total, "fsdp", pairs)
+        total = (recv.astype(F32) + block(step + 2).astype(F32)).astype(BF)
+    return total
+
+
 class Gather:
-    ORDERS = ("yx", "xy", "yx", "xy")
+    ORDERS = ("yx", "xy", "yx")
 
     def __init__(self, cols, rows):
         self.q, self.g, self.b = cols[:, :QP], cols[:, QP:], rows
 
-    def after(self, *others):
-        self.q, self.g, self.b = tie(self.q, self.g, self.b, *others)[:3]
-
-    def along_z(self):
-        q, g, b = z_gather(self.q), z_gather(self.g), z_gather(self.b)
+    def begin(self):
+        q, g = z_gather(self.q), z_gather(self.g)
         half = g.shape[0] // 2
-        self.parts = [ctx_open(v) for v in (q, g[:half], g[half:], b)]
-
-    def parts_after(self, *others):
-        self.parts = list(tie(*self.parts, *others)[:4])
+        self.parts = [ctx_open(v) for v in (q, g[:half], g[half:])]
+        self.rows = ctx_gather(ctx_open(self.b[None]), ctx_steps("xy"))
 
     def plane(self, stage):
         done = []
@@ -118,10 +127,13 @@
             done.append(ctx_gather(v, steps[:1] if stage == 0 else steps[1:]))
         self.parts = done
 
+    def rows_z(self):
+        self.rows = z_gather(self.rows[0])
+
     def pairs(self):
-        q, g1, g2, b = self.parts
+        q, g1, g2 = self.parts
         q = ctx_close(q, self.q.shape)
-        b = ctx_close(b, self.b.shape)
+        b = ctx_close(self.rows, self.b.shape)
         g = jnp.concatenate([ctx_close(g1, self.g.shape), ctx_close(g2, self.g.shape)], axis=0)
         return [(v, exchange(v, "section", 1)) for v in (q, g, b)]
 
@@ -133,23 +145,31 @@
         buf = blocks.reshape((fs,) + (2,) * cb + self.tail)
         self.parts = [(buf[: fs // 2], "xy"), (buf[fs // 2 :], "yx")] if split else [(buf, "xy")]
 
-    def after(self, *others):
-        values = tie(*[p[0] for p in self.parts], *others)
-        self.parts = [(v, p[1]) for v, p in zip(values, self.parts)]
-
     def values(self):
         return [p[0] for p in self.parts]
+
+    def put(self, values):
+        self.parts = [(v, p[1]) for v, p in zip(values, self.parts)]
 
     def plane(self, stage):
         done = []
         for v, order in self.parts:
             steps = ctx_steps(order)
-            done.append((ctx_scatter(v, steps[:1] if stage == 0 else steps[1:]), order))
-        self.parts = done
+            done.append(ctx_scatter(v, steps[:1] if stage == 0 else steps[1:]))
+        self.put(done)
 
     def along_z(self):
         buf = jnp.concatenate([v.reshape((-1,) + self.tail) for v in self.values()], axis=0)
         return z_scatter(buf)
+
+
+def rows_z(blocks):
+    fs, cb = lax.axis_size("fsdp"), bits_of("ctx")
+    return z_ring_scatter(blocks.reshape((fs,) + (2,) * cb + blocks.shape[1:]))
+
+
+def rows_plane(buf):
+    return ctx_scatter(buf[None], ctx_steps("yx")).reshape(buf.shape[-2:]).astype(F32)
 
 
 def rope_tables(places, log_base):
@@ -272,11 +292,7 @@
 GELU_B = 0.044715
 
 
-def rest_body(
-    window, flag, x, q, kv, pos_q, pos_k, w_out, g_own, g_oth, w_down, gains,
-    mixed, branch, middle, normed, gate_out, up_out, hidden, down, result,
-):
-    first = flag[0] == 0
+def mix_body(window, flag, q, kv, pos_q, pos_k, mixed):
     reach = pos_q[...] - pos_k[...]
     allowed = (reach >= 0) & (reach < window)
     k, v = kv[:, :HD], kv[:, HD:]
@@ -286,6 +302,23 @@
         e = jnp.exp(s - jnp.max(s, axis=-1, keepdims=True))
         total = jnp.sum(e, axis=-1, keepdims=True)
         mixed[:, cols] = (dot(e.astype(BF), v) * (1.0 / total)).astype(BF)
+
+
+def forward_attend(kept, pos, window, flag):
+    t, keys = kept["x"].shape[0], kept["kv"].shape[0]
+    return whole_call(
+        functools.partial(mix_body, window),
+        [((t, HEADS * HD), BF)],
+        (flag, kept["q"], kept["kv"], pos[0][:, None], pos[1][None, :]),
+        4 * t * HEADS * HD * keys,
+    )[0]
+
+
+def rest_body(
+    flag, x, mixed, w_out, g_own, g_oth, w_down, gains,
+    branch, middle, normed, gate_out, up_out, hidden, down, result,
+):
+    first = flag[0] == 0
     b = dot(mixed[...], w_out[...])
     branch[...] = b
     m = x[...] + b * inverse_rms(b) * gains[1:2, :]
@@ -306,22 +339,19 @@
     result[...] = m + total * inverse_rms(total) * gains[3:4, :]
 
 
-def forward_rest(full, kept, pos, window, flag):
+def forward_rest(full, kept, mixed, flag):
     g_own, g_oth, w_out, w_down, gains = full
     t = kept["x"].shape[0]
-    keys = kept["kv"].shape[0]
-    names = ("mixed", "branch", "middle", "normed_two", "gate", "up", "hidden", "down", "result")
+    kept["mixed"] = mixed
+    names = ("branch", "middle", "normed_two", "gate", "up", "hidden", "down", "result")
     outs = whole_call(
-        functools.partial(rest_body, window),
+        rest_body,
         [
-            ((t, HEADS * HD), BF), ((t, D), F32), ((t, D), F32), ((t, D), BF), ((t, FF), F32),
+            ((t, D), F32), ((t, D), F32), ((t, D), BF), ((t, FF), F32),
             ((t, FF), F32), ((t, FF), BF), ((t, D), F32), ((t, D), F32),
         ],
-        (
-            flag, kept["x"], kept["q"], kept["kv"], pos[0][:, None], pos[1][None, :], w_out,
-            g_own, g_oth, w_down, gains,
-        ),
-        2 * t * HEADS * HD * (2 * keys + D) + 6 * t * D * FF,
+        (flag, kept["x"], mixed, w_out, g_own, g_oth, w_down, gains),
+        2 * t * HEADS * HD * D + 6 * t * D * FF,
     )
     kept.update(zip(names, outs))
     return kept["result"]
@@ -572,67 +602,94 @@
     windows = (WIN, seq_length)
 
     gather0 = Gather(layer_cols[0], layer_rows[0])
-    gather0.along_z()
-    cols1, rows1 = tie(layer_cols[1], layer_rows[1], *gather0.parts)[:2]
-    cols1 = lax.all_gather(cols1, GRID, axis=0)
-    rows1 = lax.all_gather(rows1, GRID, axis=0)
+    gather0.begin()
+    gather0.rows_z()
     gather0.plane(0)
     gather0.plane(1)
+    cols1, rows1 = tie(layer_cols[1], layer_rows[1], *gather0.parts, gather0.rows)[:2]
+    gather1 = Gather(cols1, rows1)
     pairs0 = gather0.pairs()
     query0 = query_side(pairs0[0])
     kept0 = forward_keys(query0, x0, *tables[0], flag)
+    gather1.begin()
+    swapped = [v for pair in pairs0[1:] for v in pair]
+    kept0["kv"], *held = tie(kept0["kv"], *swapped, *gather1.parts)
+    pairs0[1:] = [held[:2], held[2:4]]
+    gather1.parts = held[4:]
+    gather1.rows_z()
+    gather1.plane(0)
+    mixed = forward_attend(kept0, pos, windows[0], flag)
+    mixed, *gather1.parts = tie(mixed, *gather1.parts)
+    gather1.plane(1)
     feed0 = feed_side(*pairs0[1:], query0[2])
-    y0 = forward_rest(feed0, kept0, pos, windows[0], flag).astype(BF)
-    cols1 = (cols1, exchange(cols1, "section", 1))
-    rows1 = (rows1, exchange(rows1, "section", 1))
-    query1 = query_side([v[..., :QP] for v in cols1])
+    y0 = forward_rest(feed0, kept0, mixed, flag).astype(BF)
+    pairs1 = gather1.pairs()
+    query1 = query_side(pairs1[0])
     kept1 = forward_keys(query1, y0.astype(F32), *tables[1], flag)
-    feed1 = feed_side([v[..., QP:] for v in cols1], rows1, query1[2])
-    y1 = forward_rest(feed1, kept1, pos, windows[1], flag)
+    feed1 = feed_side(*pairs1[1:], query1[2])
+    mixed = forward_attend(kept1, pos, windows[1], flag)
+    y1 = forward_rest(feed1, kept1, mixed, flag)
 
     middle1, branch1, wg_g, wg_out, wg_down, norm_grads = backward_feed(
         feed1, kept1, cotangent, flag
     )
     sum_g1 = reduce_cols(*wg_g)
     sum_b1 = reduce_rows(wg_out, wg_down)
-    red_b1 = lax.psum_scatter(sum_b1, GRID, scatter_dimension=0).astype(F32)
     grad_q1, kv_blocks = backward_attend(feed1[2], kept1, branch1, pos, windows[1], flag)
-    grad_q1, kv_blocks, sum_g1 = tie(grad_q1, kv_blocks, sum_g1)
+    grad_q1, kv_blocks, sum_g1, sum_b1 = tie(grad_q1, kv_blocks, sum_g1, sum_b1)
     grad_kv = key_return(kv_blocks)
+    rows1 = rows_z(sum_b1)
+    grad_kv, sum_g1 = tie(grad_kv, sum_g1)
+    scat_g1 = Scatter(sum_g1, True)
+    scat_g1.plane(0)
     grad1, wg_q, gain_zero, head_grads = backward_keys(
         query1, kept1, middle1, grad_q1, grad_kv, *tables[1], flag
     )
+    grad1 = grad1.astype(BF)
     sum_q1 = reduce_query(wg_q, [gain_zero, norm_grads], head_grads)
-    sum_c1 = jnp.concatenate([sum_q1, sum_g1], axis=-1)
-    red_c1 = lax.psum_scatter(sum_c1, GRID, scatter_dimension=0).astype(F32)
-    grad1 = grad1.astype(BF)
+    grad1, rows1, sum_q1, *held = tie(grad1, rows1, sum_q1, *scat_g1.values())
+    scat_g1.put(held)
+    scat_g1.plane(1)
+    scat_q1 = Scatter(sum_q1, False)
+    scat_q1.plane(0)
 
     middle0, branch0, wg_g, wg_out, wg_down, norm_grads = backward_feed(
         feed0, kept0, grad1, flag
     )
-    scat_g0 = Scatter(reduce_cols(*wg_g), True)
-    scat_b0 = Scatter(reduce_rows(wg_out, wg_down), False)
+    branch0, rows1, *held = tie(branch0, rows1, *scat_q1.values(), *scat_g1.values())
+    scat_q1.put(held[:1])
+    scat_g1.put(held[1:])
+    red_g1 = scat_g1.along_z()
+    red_b1 = rows_plane(rows1)
+    scat_q1.plane(1)
+    sum_g0 = reduce_cols(*wg_g)
+    sum_b0 = reduce_rows(wg_out, wg_down)
     grad_q0, kv_blocks = backward_attend(feed0[2], kept0, branch0, pos, windows[0], flag)
-    grad_q0, kv_blocks, *held = tie(grad_q0, kv_blocks, *scat_g0.values(), *scat_b0.values())
-    scat_g0.after(*held)
-    scat_b0.after(*held)
+    grad_q0, kv_blocks, sum_g0, sum_b0, red_g1, red_b1, *held = tie(
+        grad_q0, kv_blocks, sum_g0, sum_b0, red_g1, red_b1, *scat_q1.values()
+    )
+    scat_q1.put(held)
     grad_kv = key_return(kv_blocks)
+    red_q1 = scat_q1.along_z()
+    rows0 = rows_z(sum_b0)
+    grad_kv, red_q1, sum_g0 = tie(grad_kv, red_q1, sum_g0)
+    scat_g0 = Scatter(sum_g0, True)
     scat_g0.plane(0)
-    scat_b0.plane(0)
     grad0, wg_q, gain_zero, head_grads = backward_keys(
         query0, kept0, middle0, grad_q0, grad_kv, *tables[0], flag
     )
-    wg_q0, wg_q1, *held = tie(wg_q[0], wg_q[1], *scat_g0.values(), *scat_b0.values())
-    scat_g0.after(*held)
-    scat_b0.after(*held)
-    scat_q0 = Scatter(reduce_query((wg_q0, wg_q1), [gain_zero, norm_grads], head_grads), False)
+    sum_q0 = reduce_query(wg_q, [gain_zero, norm_grads], head_grads)
+    sum_q0, rows0, *held = tie(sum_q0, rows0, *scat_g0.values())
+    scat_g0.put(held)
+    scat_q0 = Scatter(sum_q0, False)
+    scat_q0.plane(0)
     scat_g0.plane(1)
-    scat_b0.plane(1)
-    scat_q0.plane(0)
     scat_q0.plane(1)
-    red_g0, red_b0 = scat_g0.along_z(), scat_b0.along_z()
     red_q0 = scat_q0.along_z()
+    red_g0 = scat_g0.along_z()
+    red_b0 = rows_plane(rows0)
     red_c0 = jnp.concatenate([red_q0, red_g0], axis=1)
+    red_c1 = jnp.concatenate([red_q1, red_g1], axis=1)
 
     out_moved = exchange(jnp.where(first, y1, grad0), "section", 1)
     c_keep, c_send = pick(first, red_c0, red_c1)

time: 590 us -> 539 us (0.914)
  waiting for transfers between devices: 312 us -> 245 us
  starting transfers between devices: 60.1 us -> 76.4 us
  between operations: 15.2 us -> 2.65 us
  matrix products: 23.8 us -> 16.1 us
  local copies, waits for them, and re-layouts: 33.5 us -> 40.7 us
  other arithmetic: 59.4 us -> 65.4 us
    unnamed x5 -> x0, waiting for transfers between devices: 79.8 us -> none
    all_gather x2 -> x0, waiting for transfers between devices: 65 us -> none  [the longest x1 45.4 us: local(): rows1 = lax.all_gather(rows1, GRID, axis=0)]
    ppermute x0 -> x6, waiting for transfers between devices: none -> 47.8 us  [z_ring_scatter(): recv = lax.ppermute(total, 'fsdp', pairs)]
    ppermute x9 -> x18, waiting for transfers between devices: 23.2 us -> 64.6 us  [z_gather(): pieces.append(lax.ppermute(pieces[-1], 'fsdp', pairs))]
    ppermute x54 -> x74, starting transfers between devices: 50 us -> 66.3 us  [exchange(): return lax.ppermute(shard, axis, pairs)]
    ppermute x54 -> x74, waiting for transfers between devices: 144 us -> 133 us  [exchange(): return lax.ppermute(shard, axis, pairs)]
    slice x4 -> x0, local copies, waits for them, and re-layouts: 9.19 us -> none  [the longest x2 5.46 us: local(): feed1 = feed_side([v[..., QP:] for v in cols1], rows1, query1[2])]
    unnamed x127 -> x123, local copies, waits for them, and re-layouts: 6.76 us -> 15.6 us
  transfers between devices with their start and end apart: 67 -> 98, of which waited for: 35 -> 49; matrix products, arithmetic and copies ran while one was open for 16% -> 18% of each run, Pallas kernels for 9% -> 12%
where the time goes in v5:
time: 539 us; the launch traced here: 530 us
  waiting for transfers between devices  245 us (45%)
  Pallas kernels  84.1 us (16%)
  starting transfers between devices  76.4 us (14%)
  other arithmetic  65.4 us (12%)
  local copies, waits for them, and re-layouts  40.7 us (8%)
  matrix products  16.1 us (3%)
    ppermute x74, waiting for transfers between devices, exchange(): return lax.ppermute(shard, axis, pairs)  133 us
    pallas_call x12, Pallas kernels, whole_call(): pl.pallas_call(body, out_shape=[jax.ShapeDtypeStruct(s, t) for s, t in ou...  84.1 us
    ppermute x74, starting transfers between devices, exchange(): return lax.ppermute(shard, axis, pairs)  66.3 us
    ppermute x18, waiting for transfers between devices, z_gather(): pieces.append(lax.ppermute(pieces[-1], 'fsdp', pairs))  64.6 us
    ppermute x6, waiting for transfers between devices, z_ring_scatter(): recv = lax.ppermute(total, 'fsdp', pairs)  47.8 us
    dot_general x12, matrix products, t_dot(): return jnp.einsum('ta,tb->ab', a, b, preferred_element_type=F32)  16.1 us
    unnamed x123, local copies, waits for them, and re-layouts  15.6 us
  transfers between devices with their start and end apart: 98, of which 49 were waited for; matrix products, arithmetic and copies ran while one was open for 18% of the time, Pallas kernels for 12%

profile of v5, /device:TPU:0, one launch (start us, length us, event | category | flops | bytes accessed | tf_op | source)
XLA Modules:
  0.0 530.3 jit_solution(3313624628600725840)
XLA Ops:
  16.1 3.2 collective-permute-done.2
  19.4 6.1 %collective-permute-done.3 = bf16[40,896]{1,0:T(8,128)(2,1)S(1)} collective-permute-done((bf16[40,896]{1,0:T(8,128)(2,1)S(1)}, bf16[40,896]{1,0:T(8,128)(2,1)S(1)}, u32[]{:S(2)}, u32[]{:S(2)}) %collective-permute-start.3) | collective-permute-done | bytes 71712 | tf_op jit(solution)/shard_map/ppermute | solution.py:56
  27.1 4.6 collective-permute-done.4
  36.2 6.9 %collective-permute-done.13 = bf16[40,2048]{1,0:T(8,128)(2,1)S(1)} collective-permute-done((bf16[40,2048]{1,0:T(8,128)(2,1)S(1)}, bf16[40,2048]{1,0:T(8,128)(2,1)S(1)}, u32[]{:S(2)}, u32[]{:S(2)}) %collective-permute-start.13) | collective-permute-done | bytes 163872 | tf_op jit(solution)/shard_map/ppermute | solution.py:56
  46.4 3.2 collective-permute-done.22
  56.3 10.3 %collective-permute-done.6 = bf16[4,2,1,40,896]{4,3,2,1,0:T(8,128)(2,1)S(1)} collective-permute-done((bf16[4,2,1,40,896]{4,3,2,1,0:T(8,128)(2,1)S(1)}, bf16[4,2,1,40,896]{4,3,2,1,0:T(8,128)(2,1)S(1)}, u32[]{:S(2)}, u32[]{:S(2)}) %collective-permute-start.6) | collective-permute-done | bytes 573472 | tf_op jit(solution)/shard_map/ppermute | solution.py:34
  67.0 6.6 %collective-permute-done.17 = bf16[2,2,1,40,2048]{4,3,0,2,1:T(8,128)(2,1)S(1)} collective-permute-done((bf16[2,2,1,40,2048]{4,3,0,2,1:T(8,128)(2,1)S(1)}, bf16[2,2,1,40,2048]{4,3,0,2,1:T(8,128)(2,1)S(1)}, u32[]{:S(2)}, u32[]{:S(2)}) %collective-permute-start.17) | collective-permute-done | bytes 655392 | tf_op jit(solution)/shard_map/ppermute | solution.py:34
  74.3 8.1 %collective-permute-done.24 = bf16[2,2,96,640]{3,2,1,0:T(8,128)(2,1)S(1)} collective-permute-done((bf16[2,2,96,640]{3,2,1,0:T(8,128)(2,1)S(1)}, bf16[2,2,96,640]{3,2,1,0:T(8,128)(2,1)S(1)}, u32[]{:S(2)}, u32[]{:S(2)}) %collective-permute-start.24) | collective-permute-done | bytes 491552 | tf_op jit(solution)/shard_map/ppermute | solution.py:56
  86.7 4.4 collective-permute-done.26
  107.0 12.3 %collective-permute-done.30 = bf16[40,2048]{1,0:T(8,128)(2,1)S(1)} collective-permute-done((bf16[40,2048]{1,0:T(8,128)(2,1)}, bf16[40,2048]{1,0:T(8,128)(2,1)S(1)}, u32[]{:S(2)}, u32[]{:S(2)}) %collective-permute-start.30) | collective-permute-done | bytes 163872 | tf_op jit(solution)/shard_map/ppermute | solution.py:56
  120.5 3.7 shard_map.152
  129.8 4.5 collective-permute-done.10
  141.8 6.6 %collective-permute-done.44 = bf16[2,2,96,640]{3,2,1,0:T(8,128)(2,1)S(1)} collective-permute-done((bf16[2,2,96,640]{3,2,1,0:T(8,128)(2,1)S(1)}, bf16[2,2,96,640]{3,2,1,0:T(8,128)(2,1)S(1)}, u32[]{:S(2)}, u32[]{:S(2)}) %collective-permute-start.44) | collective-permute-done | bytes 491552 | tf_op jit(solution)/shard_map/ppermute | solution.py:56
  154.4 3.5 shard_map.153.mixed
  158.5 4.9 collective-permute-done.34
  176.1 11.5 %collective-permute-done.47 = bf16[2,2,1,40,2048]{4,3,0,2,1:T(8,128)(2,1)S(1)} collective-permute-done((bf16[2,2,1,40,2048]{4,3,0,2,1:T(8,128)(2,1)S(1)}, bf16[2,2,1,40,2048]{4,3,0,2,1:T(8,128)(2,1)S(1)}, u32[]{:S(2)}, u32[]{:S(2)}) %collective-permute-start.47) | collective-permute-done | bytes 655392 | tf_op jit(solution)/shard_map/ppermute | solution.py:34
  191.4 7.4 %collective-permute-done.35 = bf16[4,2,1,40,896]{4,3,2,1,0:T(8,128)(2,1)S(1)} collective-permute-done((bf16[4,2,1,40,896]{4,3,2,1,0:T(8,128)(2,1)S(1)}, bf16[4,2,1,40,896]{4,3,2,1,0:T(8,128)(2,1)S(1)}, u32[]{:S(2)}, u32[]{:S(2)}) %collective-permute-start.35) | collective-permute-done | bytes 573472 | tf_op jit(solution)/shard_map/ppermute | solution.py:34
  200.1 10.6 %shard_map.154 = (f32[256,640]{1,0:T(8,128)S(1)}, f32[256,640]{1,0:T(8,128)}, bf16[256,640]{1,0:T(8,128)(2,1)S(1)}, f32[256,2048]{1,0:T(8,128)}, f32[256,2048]{1...) custom-call(s32[1]{0:T(128)} %bitcast.flag, f32[256,640]{1,0:T(8,128)} %get-tuple-element.261.x, ...), custom_call_target="tpu_custom_call" | custom-call | flops 2348810240 | bytes 18556932 | tf_op jit(solution)/shard_map/pallas_call | solution.py:216
  219.5 3.7 shard_map.155
  227.9 4.3 collective-permute-done.37
  232.3 6.3 %collective-permute-done.38 = bf16[256,512]{1,0:T(8,128)(2,1)S(1)} collective-permute-done((bf16[256,512]{1,0:T(8,128)(2,1)S(1)}, bf16[256,512]{1,0:T(8,128)(2,1)S(1)}, u32[]{:S(2)}, u32[]{:S(2)}) %collective-permute-start.38) | collective-permute-done | bytes 262176 | tf_op jit(solution)/shard_map/ppermute | solution.py:34
  239.6 3.5 shard_map.156.mixed
  243.1 10.7 %shard_map.157 = (f32[256,640]{1,0:T(8,128)S(1)}, f32[256,640]{1,0:T(8,128)}, bf16[256,640]{1,0:T(8,128)(2,1)S(1)}, f32[256,2048]{1,0:T(8,128)}, f32[256,2048]{1...) custom-call(s32[1]{0:T(128)} %bitcast.flag, f32[256,640]{1,0:T(8,128)} %convert_convert_fusion.x, ...), custom_call_target="tpu_custom_call" | custom-call | flops 2348810240 | bytes 18556932 | tf_op jit(solution)/shard_map/pallas_call | solution.py:216
  254.7 10.3 %shard_map.158 = (f32[256,640]{1,0:T(8,128)S(1)}, bf16[256,640]{1,0:T(8,128)(2,1)S(1)}, bf16[256,2048]{1,0:T(8,128)(2,1)}, bf16[256,2048]{1,0:T(8,128)(2,1)}, bf...) custom-call(s32[1]{0:T(128)} %bitcast.flag, bf16[256,640]{1,0:T(8,128)(2,1)S(1)} %get-tuple-element.260.dy, ...), custom_call_target="tpu_custom_call" | custom-call | flops 2013265920 | bytes 17778180 | tf_op jit(solution)/shard_map/pallas_call | solution.py:216
  274.8 8.7 %shard_map.159 = (f32[256,1024]{1,0:T(8,128)}, bf16[1024,512]{1,0:T(8,128)(2,1)}) custom-call(s32[1]{0:T(128)} %bitcast.flag, bf16[256,640]{1,0:T(8,128)(2,1)S(1)} %get-tuple-element.128.da, bf16[1024,640]{1,0:T(8,128)(2,1)} %bitcast.389, bf16[256,1024]{1,0:T(8,128)(2,1)S(1)} %copy-done.11, bf16[1024,512]{1,0:T(8,128)(2,1)} %copy-done.52, ...), custom_call_target="tpu_custom_call" | custom-call | flops 3019898880 | bytes 5313540 | tf_op jit(solution)/shard_map/pallas_call | solution.py:216
  283.6 3.5 add_convert_fusion.3
  287.0 4.2 add_convert_fusion.1
  297.5 4.0 collective-permute-done.51
  301.4 5.2 collective-permute-done.52
  315.5 5.0 shard_map.160
  328.8 10.9 %collective-permute-done.55 = bf16[2,2,96,640]{3,2,1,0:T(8,128)(2,1)S(1)} collective-permute-done((bf16[2,2,96,640]{3,2,1,0:T(8,128)(2,1)S(1)}, bf16[2,2,96,640]{3,2,1,0:T(8,128)(2,1)S(1)}, u32[]{:S(2)}, u32[]{:S(2)}) %collective-permute-start.55) | collective-permute-done | bytes 491552 | tf_op jit(solution)/shard_map/ppermute | solution.py:106
  341.9 12.0 %collective-permute-done.56 = bf16[2,2,96,640]{3,2,1,0:T(8,128)(2,1)S(1)} collective-permute-done((bf16[2,2,96,640]{3,2,1,0:T(8,128)(2,1)S(1)}, bf16[2,2,96,640]{3,2,1,0:T(8,128)(2,1)S(1)}, u32[]{:S(2)}, u32[]{:S(2)}) %collective-permute-start.56) | collective-permute-done | bytes 491552 | tf_op jit(solution)/shard_map/ppermute | solution.py:106
  360.0 10.5 %shard_map.161 = (f32[256,640]{1,0:T(8,128)S(1)}, bf16[256,640]{1,0:T(8,128)(2,1)S(1)}, bf16[256,2048]{1,0:T(8,128)(2,1)}, bf16[256,2048]{1,0:T(8,128)(2,1)}, bf...) custom-call(s32[1]{0:T(128)} %bitcast.flag, bf16[256,640]{1,0:T(8,128)(2,1)S(1)} %convert_element_type.463.dy, ...), custom_call_target="tpu_custom_call" | custom-call | flops 2013265920 | bytes 17778180 | tf_op jit(solution)/shard_map/pallas_call | solution.py:216
  380.1 4.3 collective-permute-start.67
  384.4 9.0 %shard_map.162 = (f32[256,1024]{1,0:T(8,128)}, bf16[1024,512]{1,0:T(8,128)(2,1)}) custom-call(s32[1]{0:T(128)} %bitcast.flag, bf16[256,640]{1,0:T(8,128)(2,1)S(1)} %get-tuple-element.163.da, bf16[1024,640]{1,0:T(8,128)(2,1)} %bitcast.387, bf16[256,1024]{1,0:T(8,128)(2,1)S(1)} %copy-done.9, bf16[1024,512]{1,0:T(8,128)(2,1)} %pad_maximum_fusion.24.kv, ...), custom_call_target="tpu_custom_call" | custom-call | flops 3019898880 | bytes 5313540 | tf_op jit(solution)/shard_map/pallas_call | solution.py:216
  397.5 9.3 %collective-permute-done.68 = bf16[1,1,2,96,640]{4,3,2,1,0:T(8,128)(2,1)S(1)} collective-permute-done((bf16[1,1,2,96,640]{4,3,2,1,0:T(8,128)(2,1)S(1)}, bf16[1,1,2,96,640]{4,3,2,1,0:T(8,128)(2,1)S(1)}, u32[]{:S(2)}, u32[]{:S(2)}) %collective-permute-start.68) | collective-permute-done | bytes 245792 | tf_op jit(solution)/shard_map/ppermute | solution.py:34
  407.8 4.1 collective-permute-done.69
  415.3 3.3 add_convert_fusion
  419.7 3.5 collective-permute-start.76
  430.6 3.4 collective-permute-done.72
  439.9 4.9 shard_map.163
  450.7 13.6 %collective-permute-done.80 = bf16[2,2,96,640]{3,2,1,0:T(8,128)(2,1)S(1)} collective-permute-done((bf16[2,2,96,640]{3,2,1,0:T(8,128)(2,1)S(1)}, bf16[2,2,96,640]{3,2,1,0:T(8,128)(2,1)S(1)}, u32[]{:S(2)}, u32[]{:S(2)}) %collective-permute-start.80) | collective-permute-done | bytes 491552 | tf_op jit(solution)/shard_map/ppermute | solution.py:106
  467.7 11.2 %collective-permute-done.81 = bf16[2,2,96,640]{3,2,1,0:T(8,128)(2,1)S(1)} collective-permute-done((bf16[2,2,96,640]{3,2,1,0:T(8,128)(2,1)S(1)}, bf16[2,2,96,640]{3,2,1,0:T(8,128)(2,1)S(1)}, u32[]{:S(2)}, u32[]{:S(2)}) %collective-permute-start.81) | collective-permute-done | bytes 491552 | tf_op jit(solution)/shard_map/ppermute | solution.py:106
  483.5 4.1 collective-permute-done.95
  489.4 12.7 %collective-permute-done.90 = bf16[2,1,1,40,2048]{4,3,0,2,1:T(8,128)(2,1)S(1)} collective-permute-done((bf16[2,1,1,40,2048]{4,3,0,2,1:T(8,128)(2,1)S(1)}, bf16[2,1,1,40,2048]{4,3,0,2,1:T(8,128)(2,1)S(1)}, u32[]{:S(2)}, u32[]{:S(2)}) %collective-permute-start.90) | collective-permute-done | bytes 327712 | tf_op jit(solution)/shard_map/ppermute | solution.py:34
  503.4 4.3 collective-permute-start.93
  510.5 7.7 %collective-permute-done.92 = bf16[40,2048]{1,0:T(8,128)(2,1)S(1)} collective-permute-done((bf16[40,2048]{1,0:T(8,128)(2,1)S(1)}, bf16[40,2048]{1,0:T(8,128)(2,1)S(1)}, u32[]{:S(2)}, u32[]{:S(2)}) %collective-permute-start.92) | collective-permute-done | bytes 163872 | tf_op jit(solution)/shard_map/ppermute | solution.py:34
  521.2 3.2 collective-permute-done.88
  (508 shorter events, 207.8 us)
Async XLA Ops:
  8.3 85.1 %collective-permute-start = (bf16[256,640]{1,0:T(8,128)(2,1)}, bf16[256,640]{1,0:T(8,128)(2,1)}, u32[]{:S(2)}, u32[]{:S(2)}) collective-permute-start(bf16[256,640]{1,0:T(8,128)(2,1)} %dynamic-slice_bitcast_fusion.10), channel_id=1, source_target_pairs={{0,16},{16,0},{1,17},{17,1},{2,18},{18,2},{3,19},{19,3},{4,20},{20... | collective-permute-start | bytes 983048 | tf_op jit(solution)/shard_map/ppermute | solution.py:34
  34.3 15.2 %collective-permute-start.22 = (bf16[2,2,96,640]{3,2,1,0:T(8,128)(2,1)S(1)}, bf16[2,2,96,640]{3,2,1,0:T(8,128)(2,1)S(1)}, u32[]{:S(2)}, u32[]{:S(2)}) collective-permute-start(bf16[2,2,96,640]{3,2,1,0:T(8,128)(2,1)S(1)} %maximum_bitcast_fusion.1), channel_id=1, source_target_pairs={{0,4},{4,8},{8,12},{12,0},{1,5},{5,9},{9,13},{13,1},{2,6},{6,10},{... | collective-permute-start | bytes 1474568 | tf_op jit(solution)/shard_map/ppermute | solution.py:56
  44.8 21.8 %collective-permute-start.6 = (bf16[4,2,1,40,896]{4,3,2,1,0:T(8,128)(2,1)S(1)}, bf16[4,2,1,40,896]{4,3,2,1,0:T(8,128)(2,1)S(1)}, u32[]{:S(2)}, u32[]{:S(2)}) collective-permute-start(bf16[4,2,1,40,896]{4,3,2,1,0:T(8,128)(2,1)S(1)} %pad_maximum_fusion.29), channel_id=1, source_target_pairs={{0,1},{1,0},{2,3},{3,2},{4,5},{5,4},{6,7},{7,6},{8,9},{9,8},{10,11... | collective-permute-start | bytes 1720328 | tf_op jit(solution)/shard_map/ppermute | solution.py:34
  49.5 17.4 %collective-permute-start.23 = (bf16[2,2,96,640]{3,2,1,0:T(8,128)(2,1)S(1)}, bf16[2,2,96,640]{3,2,1,0:T(8,128)(2,1)S(1)}, u32[]{:S(2)}, u32[]{:S(2)}) collective-permute-start(bf16[2,2,96,640]{3,2,1,0:T(8,128)(2,1)S(1)} %collective-permute-done.22), channel_id=1, source_target_pairs={{0,4},{4,8},{8,12},{12,0},{1,5},{5,9},{9,13},{13,1},{2,6},{6,10},{... | collective-permute-start | bytes 1474568 | tf_op jit(solution)/shard_map/ppermute | solution.py:56
  52.1 21.6 %collective-permute-start.17 = (bf16[2,2,1,40,2048]{4,3,0,2,1:T(8,128)(2,1)S(1)}, bf16[2,2,1,40,2048]{4,3,0,2,1:T(8,128)(2,1)S(1)}, u32[]{:S(2)}, u32[]{:S(2)}) collective-permute-start(bf16[2,2,1,40,2048]{4,3,0,2,1:T(8,128)(2,1)S(1)} %pad_maximum_fusion.26), channel_id=1, source_target_pairs={{0,1},{1,0},{2,3},{3,2},{4,5},{5,4},{6,7},{7,6},{8,9},{9,8},{10,11... | collective-permute-start | bytes 1966088 | tf_op jit(solution)/shard_map/ppermute | solution.py:34
  54.9 18.9 %collective-permute-start.15 = (bf16[2,1,2,40,2048]{4,3,0,2,1:T(8,128)(2,1)S(1)}, bf16[2,1,2,40,2048]{4,3,0,2,1:T(8,128)(2,1)S(1)}, u32[]{:S(2)}, u32[]{:S(2)}) collective-permute-start(bf16[2,1,2,40,2048]{4,3,0,2,1:T(8,128)(2,1)S(1)} %pad_maximum_fusion.25), channel_id=1, source_target_pairs={{0,2},{1,3},{2,0},{3,1},{4,6},{5,7},{6,4},{7,5},{8,10},{9,11},{10,... | collective-permute-start | bytes 1966088 | tf_op jit(solution)/shard_map/ppermute | solution.py:34
  66.9 53.6 %collective-permute-start.7 = (bf16[16,40,896]{2,1,0:T(8,128)(2,1)S(1)}, bf16[16,40,896]{2,1,0:T(8,128)(2,1)}, u32[]{:S(2)}, u32[]{:S(2)}) collective-permute-start(bf16[16,40,896]{2,1,0:T(8,128)(2,1)S(1)} %bitcast.368), channel_id=1, source_target_pairs={{0,16},{16,0},{1,17},{17,1},{2,18},{18,2},{3,19},{19,3},{4,20},{20... | collective-permute-start | bytes 3440648 | tf_op jit(solution)/shard_map/ppermute | solution.py:34
  67.0 15.4 %collective-permute-start.24 = (bf16[2,2,96,640]{3,2,1,0:T(8,128)(2,1)S(1)}, bf16[2,2,96,640]{3,2,1,0:T(8,128)(2,1)S(1)}, u32[]{:S(2)}, u32[]{:S(2)}) collective-permute-start(bf16[2,2,96,640]{3,2,1,0:T(8,128)(2,1)S(1)} %collective-permute-done.23), channel_id=1, source_target_pairs={{0,4},{4,8},{8,12},{12,0},{1,5},{5,9},{9,13},{13,1},{2,6},{6,10},{... | collective-permute-start | bytes 1474568 | tf_op jit(solution)/shard_map/ppermute | solution.py:56
  86.7 63.0 %collective-permute-start.18 = (bf16[16,40,2048]{2,1,0:T(8,128)(2,1)}, bf16[16,40,2048]{2,1,0:T(8,128)(2,1)}, u32[]{:S(2)}, u32[]{:S(2)}) collective-permute-start(bf16[16,40,2048]{2,1,0:T(8,128)(2,1)} %pad_maximum_fusion), channel_id=1, source_target_pairs={{0,16},{16,0},{1,17},{17,1},{2,18},{18,2},{3,19},{19,3},{4,20},{20... | collective-permute-start | bytes 7864328 | tf_op jit(solution)/shard_map/ppermute | solution.py:34
  97.3 52.3 %collective-permute-start.25 = (bf16[16,96,640]{2,1,0:T(8,128)(2,1)}, bf16[16,96,640]{2,1,0:T(8,128)(2,1)}, u32[]{:S(2)}, u32[]{:S(2)}) collective-permute-start(bf16[16,96,640]{2,1,0:T(8,128)(2,1)} %bitcast.384), channel_id=1, source_target_pairs={{0,16},{16,0},{1,17},{17,1},{2,18},{18,2},{3,19},{19,3},{4,20},{20... | collective-permute-start | bytes 5898248 | tf_op jit(solution)/shard_map/ppermute | solution.py:34
  102.6 17.5 %collective-permute-start.42 = (bf16[2,2,96,640]{3,2,1,0:T(8,128)(2,1)}, bf16[2,2,96,640]{3,2,1,0:T(8,128)(2,1)}, u32[]{:S(2)}, u32[]{:S(2)}) collective-permute-start(bf16[2,2,96,640]{3,2,1,0:T(8,128)(2,1)} %maximum_bitcast_fusion.2), channel_id=1, source_target_pairs={{0,4},{4,8},{8,12},{12,0},{1,5},{5,9},{9,13},{13,1},{2,6},{6,10},{... | collective-permute-start | bytes 1474568 | tf_op jit(solution)/shard_map/ppermute | solution.py:56
  120.2 15.8 %collective-permute-start.43 = (bf16[2,2,96,640]{3,2,1,0:T(8,128)(2,1)}, bf16[2,2,96,640]{3,2,1,0:T(8,128)(2,1)S(1)}, u32[]{:S(2)}, u32[]{:S(2)}) collective-permute-start(bf16[2,2,96,640]{3,2,1,0:T(8,128)(2,1)} %collective-permute-done.42), channel_id=1, source_target_pairs={{0,4},{4,8},{8,12},{12,0},{1,5},{5,9},{9,13},{13,1},{2,6},{6,10},{... | collective-permute-start | bytes 1474568 | tf_op jit(solution)/shard_map/ppermute | solution.py:56
  166.9 47.8 %collective-permute-start.45 = (bf16[16,96,640]{2,1,0:T(8,128)(2,1)}, bf16[16,96,640]{2,1,0:T(8,128)(2,1)}, u32[]{:S(2)}, u32[]{:S(2)}) collective-permute-start(bf16[16,96,640]{2,1,0:T(8,128)(2,1)} %bitcast.75), channel_id=1, source_target_pairs={{0,16},{16,0},{1,17},{17,1},{2,18},{18,2},{3,19},{19,3},{4,20},{20... | collective-permute-start | bytes 5898248 | tf_op jit(solution)/shard_map/ppermute | solution.py:34
  169.9 17.7 %collective-permute-start.47 = (bf16[2,2,1,40,2048]{4,3,0,2,1:T(8,128)(2,1)S(1)}, bf16[2,2,1,40,2048]{4,3,0,2,1:T(8,128)(2,1)S(1)}, u32[]{:S(2)}, u32[]{:S(2)}) collective-permute-start(bf16[2,2,1,40,2048]{4,3,0,2,1:T(8,128)(2,1)S(1)} %pad_maximum_fusion.28), channel_id=1, source_target_pairs={{0,1},{1,0},{2,3},{3,2},{4,5},{5,4},{6,7},{7,6},{8,9},{9,8},{10,11... | collective-permute-start | bytes 1966088 | tf_op jit(solution)/shard_map/ppermute | solution.py:34
  173.2 25.6 %collective-permute-start.35 = (bf16[4,2,1,40,896]{4,3,2,1,0:T(8,128)(2,1)S(1)}, bf16[4,2,1,40,896]{4,3,2,1,0:T(8,128)(2,1)S(1)}, u32[]{:S(2)}, u32[]{:S(2)}) collective-permute-start(bf16[4,2,1,40,896]{4,3,2,1,0:T(8,128)(2,1)S(1)} %pad_maximum_fusion.30), channel_id=1, source_target_pairs={{0,1},{1,0},{2,3},{3,2},{4,5},{5,4},{6,7},{7,6},{8,9},{9,8},{10,11... | collective-permute-start | bytes 1720328 | tf_op jit(solution)/shard_map/ppermute | solution.py:34
  190.2 53.0 %collective-permute-start.48 = (bf16[16,40,2048]{2,1,0:T(8,128)(2,1)}, bf16[16,40,2048]{2,1,0:T(8,128)(2,1)}, u32[]{:S(2)}, u32[]{:S(2)}) collective-permute-start(bf16[16,40,2048]{2,1,0:T(8,128)(2,1)} %pad_maximum_fusion.2), channel_id=1, source_target_pairs={{0,16},{16,0},{1,17},{17,1},{2,18},{18,2},{3,19},{19,3},{4,20},{20... | collective-permute-start | bytes 7864328 | tf_op jit(solution)/shard_map/ppermute | solution.py:34
  200.1 19.4 %collective-permute-start.36 = (bf16[16,40,896]{2,1,0:T(8,128)(2,1)}, bf16[16,40,896]{2,1,0:T(8,128)(2,1)}, u32[]{:S(2)}, u32[]{:S(2)}) collective-permute-start(bf16[16,40,896]{2,1,0:T(8,128)(2,1)} %bitcast.65), channel_id=1, source_target_pairs={{0,16},{16,0},{1,17},{17,1},{2,18},{18,2},{3,19},{19,3},{4,20},{20... | collective-permute-start | bytes 3440648 | tf_op jit(solution)/shard_map/ppermute | solution.py:34
  224.5 14.1 %collective-permute-start.38 = (bf16[256,512]{1,0:T(8,128)(2,1)S(1)}, bf16[256,512]{1,0:T(8,128)(2,1)S(1)}, u32[]{:S(2)}, u32[]{:S(2)}) collective-permute-start(bf16[256,512]{1,0:T(8,128)(2,1)S(1)} %get-tuple-element.119), channel_id=1, source_target_pairs={{0,2},{1,3},{2,0},{3,1},{4,6},{5,7},{6,4},{7,5},{8,10},{9,11},{10,... | collective-permute-start | bytes 786440 | tf_op jit(solution)/shard_map/ppermute | solution.py:34
  268.9 18.1 %collective-permute-start.49 = (bf16[640,2048]{1,0:T(8,128)(2,1)}, bf16[640,2048]{1,0:T(8,128)(2,1)}, u32[]{:S(2)}, u32[]{:S(2)}) collective-permute-start(bf16[640,2048]{1,0:T(8,128)(2,1)} %convolution_convert_fusion.3), channel_id=1, source_target_pairs={{0,16},{16,0},{1,17},{17,1},{2,18},{18,2},{3,19},{19,3},{4,20},{20... | collective-permute-start | bytes 7864328 | tf_op jit(solution)/shard_map/ppermute | solution.py:34
  292.8 13.9 %collective-permute-start.52 = (bf16[256,512]{1,0:T(8,128)(2,1)}, bf16[256,512]{1,0:T(8,128)(2,1)}, u32[]{:S(2)}, u32[]{:S(2)}) collective-permute-start(bf16[256,512]{1,0:T(8,128)(2,1)} %get-tuple-element.259), channel_id=1, source_target_pairs={{0,2},{1,3},{2,0},{3,1},{4,6},{5,7},{6,4},{7,5},{8,10},{9,11},{10,... | collective-permute-start | bytes 786440 | tf_op jit(solution)/shard_map/ppermute | solution.py:34
  297.5 26.2 %collective-permute-start.54 = (bf16[2,2,96,640]{3,2,1,0:T(8,128)(2,1)}, bf16[2,2,96,640]{3,2,1,0:T(8,128)(2,1)}, u32[]{:S(2)}, u32[]{:S(2)}) collective-permute-start(bf16[2,2,96,640]{3,2,1,0:T(8,128)(2,1)} %dynamic-slice_bitcast_fusion.9), channel_id=1, source_target_pairs={{0,4},{4,8},{8,12},{12,0},{1,5},{5,9},{9,13},{13,1},{2,6},{6,10},{... | collective-permute-start | bytes 1474568 | tf_op jit(solution)/shard_map/ppermute | solution.py:106
  311.8 15.7 %collective-permute-start.59 = (bf16[2,1,2,40,2048]{4,3,0,2,1:T(8,128)(2,1)}, bf16[2,1,2,40,2048]{4,3,0,2,1:T(8,128)(2,1)}, u32[]{:S(2)}, u32[]{:S(2)}) collective-permute-start(bf16[2,1,2,40,2048]{4,3,0,2,1:T(8,128)(2,1)} %copy.71), channel_id=1, source_target_pairs={{0,2},{1,3},{2,0},{3,1},{4,6},{5,7},{6,4},{7,5},{8,10},{9,11},{10,... | collective-permute-start | bytes 1966088 | tf_op jit(solution)/shard_map/ppermute | solution.py:34
  314.7 25.5 %collective-permute-start.58 = (bf16[2,2,1,40,2048]{4,3,0,2,1:T(8,128)(2,1)}, bf16[2,2,1,40,2048]{4,3,0,2,1:T(8,128)(2,1)}, u32[]{:S(2)}, u32[]{:S(2)}) collective-permute-start(bf16[2,2,1,40,2048]{4,3,0,2,1:T(8,128)(2,1)} %copy.69), channel_id=1, source_target_pairs={{0,1},{1,0},{2,3},{3,2},{4,5},{5,4},{6,7},{7,6},{8,9},{9,8},{10,11... | collective-permute-start | bytes 1966088 | tf_op jit(solution)/shard_map/ppermute | solution.py:34
  322.5 19.0 %collective-permute-start.57 = (bf16[640,896]{1,0:T(8,128)(2,1)S(1)}, bf16[640,896]{1,0:T(8,128)(2,1)S(1)}, u32[]{:S(2)}, u32[]{:S(2)}) collective-permute-start(bf16[640,896]{1,0:T(8,128)(2,1)S(1)} %fusion.3), channel_id=1, source_target_pairs={{0,16},{16,0},{1,17},{17,1},{2,18},{18,2},{3,19},{19,3},{4,20},{20... | collective-permute-start | bytes 3440648 | tf_op jit(solution)/shard_map/ppermute | solution.py:34
  325.0 14.7 %collective-permute-start.55 = (bf16[2,2,96,640]{3,2,1,0:T(8,128)(2,1)S(1)}, bf16[2,2,96,640]{3,2,1,0:T(8,128)(2,1)S(1)}, u32[]{:S(2)}, u32[]{:S(2)}) collective-permute-start(bf16[2,2,96,640]{3,2,1,0:T(8,128)(2,1)S(1)} %fusion.9), channel_id=1, source_target_pairs={{0,4},{4,8},{8,12},{12,0},{1,5},{5,9},{9,13},{13,1},{2,6},{6,10},{... | collective-permute-start | bytes 1474568 | tf_op jit(solution)/shard_map/ppermute | solution.py:106
  339.9 14.0 %collective-permute-start.56 = (bf16[2,2,96,640]{3,2,1,0:T(8,128)(2,1)S(1)}, bf16[2,2,96,640]{3,2,1,0:T(8,128)(2,1)S(1)}, u32[]{:S(2)}, u32[]{:S(2)}) collective-permute-start(bf16[2,2,96,640]{3,2,1,0:T(8,128)(2,1)S(1)} %fusion.8), channel_id=1, source_target_pairs={{0,4},{4,8},{8,12},{12,0},{1,5},{5,9},{9,13},{13,1},{2,6},{6,10},{... | collective-permute-start | bytes 1474568 | tf_op jit(solution)/shard_map/ppermute | solution.py:106
  354.9 21.5 %collective-permute-start.62 = (bf16[2,1,1,40,2048]{4,3,0,2,1:T(8,128)(2,1)S(1)}, bf16[2,1,1,40,2048]{4,3,0,2,1:T(8,128)(2,1)}, u32[]{:S(2)}, u32[]{:S(2)}) collective-permute-start(bf16[2,1,1,40,2048]{4,3,0,2,1:T(8,128)(2,1)S(1)} %constant_dynamic-slice_fusion.11), channel_id=1, source_target_pairs={{0,1},{1,0},{2,3},{3,2},{4,5},{5,4},{6,7},{7,6},{8,9},{9,8},{10,11... | collective-permute-start | bytes 983048 | tf_op jit(solution)/shard_map/ppermute | solution.py:34
  356.8 20.6 %collective-permute-start.61 = (bf16[2,1,1,40,2048]{4,3,0,2,1:T(8,128)(2,1)}, bf16[2,1,1,40,2048]{4,3,0,2,1:T(8,128)(2,1)}, u32[]{:S(2)}, u32[]{:S(2)}) collective-permute-start(bf16[2,1,1,40,2048]{4,3,0,2,1:T(8,128)(2,1)} %constant_dynamic-slice_fusion.12), channel_id=1, source_target_pairs={{0,2},{1,3},{2,0},{3,1},{4,6},{5,7},{6,4},{7,5},{8,10},{9,11},{10,... | collective-permute-start | bytes 983048 | tf_op jit(solution)/shard_map/ppermute | solution.py:34
  358.7 19.8 %collective-permute-start.60 = (bf16[4,2,1,40,896]{4,3,2,1,0:T(8,128)(2,1)}, bf16[4,2,1,40,896]{4,3,2,1,0:T(8,128)(2,1)}, u32[]{:S(2)}, u32[]{:S(2)}) collective-permute-start(bf16[4,2,1,40,896]{4,3,2,1,0:T(8,128)(2,1)} %constant_dynamic-slice_fusion.13), channel_id=1, source_target_pairs={{0,1},{1,0},{2,3},{3,2},{4,5},{5,4},{6,7},{7,6},{8,9},{9,8},{10,11... | collective-permute-start | bytes 1720328 | tf_op jit(solution)/shard_map/ppermute | solution.py:34
  374.9 37.1 %collective-permute-start.64 = (bf16[16,96,640]{2,1,0:T(8,128)(2,1)}, bf16[16,96,640]{2,1,0:T(8,128)(2,1)S(1)}, u32[]{:S(2)}, u32[]{:S(2)}) collective-permute-start(bf16[16,96,640]{2,1,0:T(8,128)(2,1)} %pad_maximum_fusion.7), channel_id=1, source_target_pairs={{0,16},{16,0},{1,17},{17,1},{2,18},{18,2},{3,19},{19,3},{4,20},{20... | collective-permute-start | bytes 5898248 | tf_op jit(solution)/shard_map/ppermute | solution.py:34
  375.8 39.5 %collective-permute-start.63 = (bf16[640,2048]{1,0:T(8,128)(2,1)S(1)}, bf16[640,2048]{1,0:T(8,128)(2,1)}, u32[]{:S(2)}, u32[]{:S(2)}) collective-permute-start(bf16[640,2048]{1,0:T(8,128)(2,1)S(1)} %convolution_convert_fusion.1), channel_id=1, source_target_pairs={{0,16},{16,0},{1,17},{17,1},{2,18},{18,2},{3,19},{19,3},{4,20},{20... | collective-permute-start | bytes 7864328 | tf_op jit(solution)/shard_map/ppermute | solution.py:34
  380.0 13.6 %collective-permute-start.65 = (bf16[40,2048]{1,0:T(8,128)(2,1)S(1)}, bf16[40,2048]{1,0:T(8,128)(2,1)S(1)}, u32[]{:S(2)}, u32[]{:S(2)}) collective-permute-start(bf16[40,2048]{1,0:T(8,128)(2,1)S(1)} %get-tuple-element.275), channel_id=1, source_target_pairs={{0,4},{4,0},{8,12},{12,8},{1,5},{5,1},{9,13},{13,9},{2,6},{6,2},{1... | collective-permute-start | bytes 491528 | tf_op jit(solution)/shard_map/ppermute | solution.py:34
  380.0 15.1 %collective-permute-start.66 = (bf16[40,2048]{1,0:T(8,128)(2,1)S(1)}, bf16[40,2048]{1,0:T(8,128)(2,1)S(1)}, u32[]{:S(2)}, u32[]{:S(2)}) collective-permute-start(bf16[40,2048]{1,0:T(8,128)(2,1)S(1)} %get-tuple-element.276), channel_id=1, source_target_pairs={{0,8},{4,12},{8,0},{12,4},{1,9},{5,13},{9,1},{13,5},{2,10},{6,14},... | collective-permute-start | bytes 491528 | tf_op jit(solution)/shard_map/ppermute | solution.py:34
  380.1 15.6 %collective-permute-start.67 = (bf16[40,2048]{1,0:T(8,128)(2,1)S(1)}, bf16[40,2048]{1,0:T(8,128)(2,1)}, u32[]{:S(2)}, u32[]{:S(2)}) collective-permute-start(bf16[40,2048]{1,0:T(8,128)(2,1)S(1)} %get-tuple-element.277), channel_id=1, source_target_pairs={{0,12},{4,8},{8,4},{12,0},{1,13},{5,9},{9,5},{13,1},{2,14},{6,10},... | collective-permute-start | bytes 491528 | tf_op jit(solution)/shard_map/ppermute | solution.py:34
  393.6 14.2 %collective-permute-start.70 = (bf16[4,1,1,40,896]{4,3,2,1,0:T(8,128)(2,1)S(1)}, bf16[4,1,1,40,896]{4,3,2,1,0:T(8,128)(2,1)S(1)}, u32[]{:S(2)}, u32[]{:S(2)}) collective-permute-start(bf16[4,1,1,40,896]{4,3,2,1,0:T(8,128)(2,1)S(1)} %constant_dynamic-slice_fusion.9), channel_id=1, source_target_pairs={{0,2},{1,3},{2,0},{3,1},{4,6},{5,7},{6,4},{7,5},{8,10},{9,11},{10,... | collective-permute-start | bytes 860168 | tf_op jit(solution)/shard_map/ppermute | solution.py:34
  427.6 19.7 %collective-permute-start.79 = (bf16[2,2,96,640]{3,2,1,0:T(8,128)(2,1)}, bf16[2,2,96,640]{3,2,1,0:T(8,128)(2,1)}, u32[]{:S(2)}, u32[]{:S(2)}) collective-permute-start(bf16[2,2,96,640]{3,2,1,0:T(8,128)(2,1)} %dynamic-slice_bitcast_fusion.8), channel_id=1, source_target_pairs={{0,4},{4,8},{8,12},{12,0},{1,5},{5,9},{9,13},{13,1},{2,6},{6,10},{... | collective-permute-start | bytes 1474568 | tf_op jit(solution)/shard_map/ppermute | solution.py:106
  439.1 25.6 %collective-permute-start.82 = (bf16[2,2,1,40,2048]{4,3,0,2,1:T(8,128)(2,1)}, bf16[2,2,1,40,2048]{4,3,0,2,1:T(8,128)(2,1)}, u32[]{:S(2)}, u32[]{:S(2)}) collective-permute-start(bf16[2,2,1,40,2048]{4,3,0,2,1:T(8,128)(2,1)} %copy.73), channel_id=1, source_target_pairs={{0,1},{1,0},{2,3},{3,2},{4,5},{5,4},{6,7},{7,6},{8,9},{9,8},{10,11... | collective-permute-start | bytes 1966088 | tf_op jit(solution)/shard_map/ppermute | solution.py:34
  446.1 21.2 %collective-permute-start.78 = (bf16[640,896]{1,0:T(8,128)(2,1)S(1)}, bf16[640,896]{1,0:T(8,128)(2,1)S(1)}, u32[]{:S(2)}, u32[]{:S(2)}) collective-permute-start(bf16[640,896]{1,0:T(8,128)(2,1)S(1)} %fusion.1), channel_id=1, source_target_pairs={{0,16},{16,0},{1,17},{17,1},{2,18},{18,2},{3,19},{19,3},{4,20},{20... | collective-permute-start | bytes 3440648 | tf_op jit(solution)/shard_map/ppermute | solution.py:34
  446.7 19.4 %collective-permute-start.77 = (f32[256,640]{1,0:T(8,128)S(1)}, f32[256,640]{1,0:T(8,128)S(1)}, u32[]{:S(2)}, u32[]{:S(2)}) collective-permute-start(f32[256,640]{1,0:T(8,128)S(1)} %broadcast_select_fusion.24), channel_id=1, source_target_pairs={{0,16},{16,0},{1,17},{17,1},{2,18},{18,2},{3,19},{19,3},{4,20},{20... | collective-permute-start | bytes 1966088 | tf_op jit(solution)/shard_map/ppermute | solution.py:34
  449.3 15.1 %collective-permute-start.80 = (bf16[2,2,96,640]{3,2,1,0:T(8,128)(2,1)S(1)}, bf16[2,2,96,640]{3,2,1,0:T(8,128)(2,1)S(1)}, u32[]{:S(2)}, u32[]{:S(2)}) collective-permute-start(bf16[2,2,96,640]{3,2,1,0:T(8,128)(2,1)S(1)} %fusion.6), channel_id=1, source_target_pairs={{0,4},{4,8},{8,12},{12,0},{1,5},{5,9},{9,13},{13,1},{2,6},{6,10},{... | collective-permute-start | bytes 1474568 | tf_op jit(solution)/shard_map/ppermute | solution.py:106
  464.5 14.4 %collective-permute-start.81 = (bf16[2,2,96,640]{3,2,1,0:T(8,128)(2,1)S(1)}, bf16[2,2,96,640]{3,2,1,0:T(8,128)(2,1)S(1)}, u32[]{:S(2)}, u32[]{:S(2)}) collective-permute-start(bf16[2,2,96,640]{3,2,1,0:T(8,128)(2,1)S(1)} %fusion.5), channel_id=1, source_target_pairs={{0,4},{4,8},{8,12},{12,0},{1,5},{5,9},{9,13},{13,1},{2,6},{6,10},{... | collective-permute-start | bytes 1474568 | tf_op jit(solution)/shard_map/ppermute | solution.py:106
  480.8 21.5 %collective-permute-start.84 = (bf16[4,2,1,40,896]{4,3,2,1,0:T(8,128)(2,1)S(1)}, bf16[4,2,1,40,896]{4,3,2,1,0:T(8,128)(2,1)S(1)}, u32[]{:S(2)}, u32[]{:S(2)}) collective-permute-start(bf16[4,2,1,40,896]{4,3,2,1,0:T(8,128)(2,1)S(1)} %constant_dynamic-slice_fusion.4), channel_id=1, source_target_pairs={{0,1},{1,0},{2,3},{3,2},{4,5},{5,4},{6,7},{7,6},{8,9},{9,8},{10,11... | collective-permute-start | bytes 1720328 | tf_op jit(solution)/shard_map/ppermute | solution.py:34
  481.5 20.6 %collective-permute-start.90 = (bf16[2,1,1,40,2048]{4,3,0,2,1:T(8,128)(2,1)S(1)}, bf16[2,1,1,40,2048]{4,3,0,2,1:T(8,128)(2,1)S(1)}, u32[]{:S(2)}, u32[]{:S(2)}) collective-permute-start(bf16[2,1,1,40,2048]{4,3,0,2,1:T(8,128)(2,1)S(1)} %constant_dynamic-slice_fusion.1), channel_id=1, source_target_pairs={{0,1},{1,0},{2,3},{3,2},{4,5},{5,4},{6,7},{7,6},{8,9},{9,8},{10,11... | collective-permute-start | bytes 983048 | tf_op jit(solution)/shard_map/ppermute | solution.py:34
  483.0 19.2 %collective-permute-start.89 = (bf16[2,1,1,40,2048]{4,3,0,2,1:T(8,128)(2,1)S(1)}, bf16[2,1,1,40,2048]{4,3,0,2,1:T(8,128)(2,1)S(1)}, u32[]{:S(2)}, u32[]{:S(2)}) collective-permute-start(bf16[2,1,1,40,2048]{4,3,0,2,1:T(8,128)(2,1)S(1)} %constant_dynamic-slice_fusion.2), channel_id=1, source_target_pairs={{0,2},{1,3},{2,0},{3,1},{4,6},{5,7},{6,4},{7,5},{8,10},{9,11},{10,... | collective-permute-start | bytes 983048 | tf_op jit(solution)/shard_map/ppermute | solution.py:34
  487.7 20.0 %collective-permute-start.96 = (bf16[1,1,1,96,640]{4,3,2,1,0:T(8,128)(2,1)S(1)}, bf16[1,1,1,96,640]{4,3,2,1,0:T(8,128)(2,1)S(1)}, u32[]{:S(2)}, u32[]{:S(2)}) collective-permute-start(bf16[1,1,1,96,640]{4,3,2,1,0:T(8,128)(2,1)S(1)} %constant_dynamic-slice_fusion), channel_id=1, source_target_pairs={{0,1},{1,0},{2,3},{3,2},{4,5},{5,4},{6,7},{7,6},{8,9},{9,8},{10,11... | collective-permute-start | bytes 368648 | tf_op jit(solution)/shard_map/ppermute | solution.py:34
  503.3 14.9 %collective-permute-start.92 = (bf16[40,2048]{1,0:T(8,128)(2,1)S(1)}, bf16[40,2048]{1,0:T(8,128)(2,1)S(1)}, u32[]{:S(2)}, u32[]{:S(2)}) collective-permute-start(bf16[40,2048]{1,0:T(8,128)(2,1)S(1)} %get-tuple-element.273), channel_id=1, source_target_pairs={{0,8},{4,12},{8,0},{12,4},{1,9},{5,13},{9,1},{13,5},{2,10},{6,14},... | collective-permute-start | bytes 491528 | tf_op jit(solution)/shard_map/ppermute | solution.py:34
  503.4 14.8 %collective-permute-start.93 = (bf16[40,2048]{1,0:T(8,128)(2,1)S(1)}, bf16[40,2048]{1,0:T(8,128)(2,1)S(1)}, u32[]{:S(2)}, u32[]{:S(2)}) collective-permute-start(bf16[40,2048]{1,0:T(8,128)(2,1)S(1)} %get-tuple-element.274), channel_id=1, source_target_pairs={{0,12},{4,8},{8,4},{12,0},{1,13},{5,9},{9,5},{13,1},{2,14},{6,10},... | collective-permute-start | bytes 491528 | tf_op jit(solution)/shard_map/ppermute | solution.py:34
  507.8 16.8 %collective-permute-start.97 = (f32[96,640]{1,0:T(8,128)S(1)}, f32[96,640]{1,0:T(8,128)S(1)}, u32[]{:S(2)}, u32[]{:S(2)}) collective-permute-start(f32[96,640]{1,0:T(8,128)S(1)} %get-tuple-element.208), channel_id=1, source_target_pairs={{0,16},{16,0},{1,17},{17,1},{2,18},{18,2},{3,19},{19,3},{4,20},{20... | collective-permute-start | bytes 737288 | tf_op jit(solution)/shard_map/ppermute | solution.py:34
  (104 other events, 873.4 us)

commit v6 on v5

--- a/solution.py
+++ b/solution.py
@@ -50,12 +50,9 @@
 
 def z_gather(block):
     count = lax.axis_size("fsdp")
-    pairs = [(i, (i + 1) % count) for i in range(count)]
-    pieces = [block]
-    for _ in range(count - 1):
-        pieces.append(lax.ppermute(pieces[-1], "fsdp", pairs))
+    pieces = [block] + [exchange(block, "fsdp", j) for j in range(1, count)]
     me = lax.axis_index("fsdp")
-    return jnp.stack([lax.select_n((me - at) % count, *pieces) for at in range(count)])
+    return jnp.stack([lax.select_n(me ^ at, *pieces) for at in range(count)])
 
 
 def ctx_open(buf):
@@ -93,21 +90,6 @@
     return total
 
 
-def z_ring_scatter(buf):
-    count = lax.axis_size("fsdp")
-    pairs = [(i, (i + 1) % count) for i in range(count)]
-    me = lax.axis_index("fsdp")
-
-    def block(back):
-        return lax.dynamic_index_in_dim(buf, (me - back) % count, 0, False)
-
-    total = block(1)
-    for step in range(count - 1):
-        recv = lax.ppermute(total, "fsdp", pairs)
-        total = (recv.astype(F32) + block(step + 2).astype(F32)).astype(BF)
-    return total
-
-
 class Gather:
     ORDERS = ("yx", "xy", "yx")
 
@@ -139,11 +121,12 @@
 
 
 class Scatter:
-    def __init__(self, blocks, split):
+    def __init__(self, blocks, order):
         fs, cb = lax.axis_size("fsdp"), bits_of("ctx")
         self.tail = blocks.shape[1:]
         buf = blocks.reshape((fs,) + (2,) * cb + self.tail)
-        self.parts = [(buf[: fs // 2], "xy"), (buf[fs // 2 :], "yx")] if split else [(buf, "xy")]
+        split = order == "both"
+        self.parts = [(buf[: fs // 2], "xy"), (buf[fs // 2 :], "yx")] if split else [(buf, order)]
 
     def values(self):
         return [p[0] for p in self.parts]
@@ -161,15 +144,6 @@
     def along_z(self):
         buf = jnp.concatenate([v.reshape((-1,) + self.tail) for v in self.values()], axis=0)
         return z_scatter(buf)
-
-
-def rows_z(blocks):
-    fs, cb = lax.axis_size("fsdp"), bits_of("ctx")
-    return z_ring_scatter(blocks.reshape((fs,) + (2,) * cb + blocks.shape[1:]))
-
-
-def rows_plane(buf):
-    return ctx_scatter(buf[None], ctx_steps("yx")).reshape(buf.shape[-2:]).astype(F32)
 
 
 def rope_tables(places, log_base):
@@ -606,20 +580,20 @@
     gather0.rows_z()
     gather0.plane(0)
     gather0.plane(1)
-    cols1, rows1 = tie(layer_cols[1], layer_rows[1], *gather0.parts, gather0.rows)[:2]
-    gather1 = Gather(cols1, rows1)
     pairs0 = gather0.pairs()
     query0 = query_side(pairs0[0])
     kept0 = forward_keys(query0, x0, *tables[0], flag)
+    cols1, rows1 = tie(layer_cols[1], layer_rows[1], kept0["q"], *gather0.parts)[:2]
+    gather1 = Gather(cols1, rows1)
     gather1.begin()
     swapped = [v for pair in pairs0[1:] for v in pair]
     kept0["kv"], *held = tie(kept0["kv"], *swapped, *gather1.parts)
     pairs0[1:] = [held[:2], held[2:4]]
     gather1.parts = held[4:]
-    gather1.rows_z()
     gather1.plane(0)
     mixed = forward_attend(kept0, pos, windows[0], flag)
-    mixed, *gather1.parts = tie(mixed, *gather1.parts)
+    mixed, gather1.rows, *gather1.parts = tie(mixed, gather1.rows, *gather1.parts)
+    gather1.rows_z()
     gather1.plane(1)
     feed0 = feed_side(*pairs0[1:], query0[2])
     y0 = forward_rest(feed0, kept0, mixed, flag).astype(BF)
@@ -638,56 +612,61 @@
     grad_q1, kv_blocks = backward_attend(feed1[2], kept1, branch1, pos, windows[1], flag)
     grad_q1, kv_blocks, sum_g1, sum_b1 = tie(grad_q1, kv_blocks, sum_g1, sum_b1)
     grad_kv = key_return(kv_blocks)
-    rows1 = rows_z(sum_b1)
-    grad_kv, sum_g1 = tie(grad_kv, sum_g1)
-    scat_g1 = Scatter(sum_g1, True)
+    grad_kv, sum_g1, sum_b1 = tie(grad_kv, sum_g1, sum_b1)
+    scat_g1, scat_b1 = Scatter(sum_g1, "both"), Scatter(sum_b1, "yx")
     scat_g1.plane(0)
     grad1, wg_q, gain_zero, head_grads = backward_keys(
         query1, kept1, middle1, grad_q1, grad_kv, *tables[1], flag
     )
     grad1 = grad1.astype(BF)
     sum_q1 = reduce_query(wg_q, [gain_zero, norm_grads], head_grads)
-    grad1, rows1, sum_q1, *held = tie(grad1, rows1, sum_q1, *scat_g1.values())
-    scat_g1.put(held)
-    scat_g1.plane(1)
-    scat_q1 = Scatter(sum_q1, False)
-    scat_q1.plane(0)
 
     middle0, branch0, wg_g, wg_out, wg_down, norm_grads = backward_feed(
         feed0, kept0, grad1, flag
     )
-    branch0, rows1, *held = tie(branch0, rows1, *scat_q1.values(), *scat_g1.values())
-    scat_q1.put(held[:1])
-    scat_g1.put(held[1:])
+    branch0, sum_q1, held0, *held = tie(branch0, sum_q1, *scat_b1.values(), *scat_g1.values())
+    scat_g1.put(held)
+    scat_b1.put([held0])
+    scat_q1 = Scatter(sum_q1, "xy")
+    scat_g1.plane(1)
+    scat_q1.plane(0)
+    scat_b1.plane(0)
     red_g1 = scat_g1.along_z()
-    red_b1 = rows_plane(rows1)
-    scat_q1.plane(1)
     sum_g0 = reduce_cols(*wg_g)
     sum_b0 = reduce_rows(wg_out, wg_down)
     grad_q0, kv_blocks = backward_attend(feed0[2], kept0, branch0, pos, windows[0], flag)
-    grad_q0, kv_blocks, sum_g0, sum_b0, red_g1, red_b1, *held = tie(
-        grad_q0, kv_blocks, sum_g0, sum_b0, red_g1, red_b1, *scat_q1.values()
-    )
-    scat_q1.put(held)
+    grad_q0, kv_blocks, sum_g0, sum_b0, red_g1, held0 = tie(
+        grad_q0, kv_blocks, sum_g0, sum_b0, red_g1, *scat_q1.values()
+    )
+    scat_q1.put([held0])
     grad_kv = key_return(kv_blocks)
-    red_q1 = scat_q1.along_z()
-    rows0 = rows_z(sum_b0)
-    grad_kv, red_q1, sum_g0 = tie(grad_kv, red_q1, sum_g0)
-    scat_g0 = Scatter(sum_g0, True)
+    scat_b0 = Scatter(sum_b0, "yx")
+    scat_b0.plane(0)
+    grad_kv, sum_g0, *held = tie(grad_kv, sum_g0, *scat_q1.values(), *scat_b1.values())
+    scat_q1.put(held[:1])
+    scat_b1.put(held[1:])
+    scat_g0 = Scatter(sum_g0, "both")
     scat_g0.plane(0)
     grad0, wg_q, gain_zero, head_grads = backward_keys(
         query0, kept0, middle0, grad_q0, grad_kv, *tables[0], flag
     )
     sum_q0 = reduce_query(wg_q, [gain_zero, norm_grads], head_grads)
-    sum_q0, rows0, *held = tie(sum_q0, rows0, *scat_g0.values())
+    sum_q0, held1, held2, *held = tie(
+        sum_q0, *scat_q1.values(), *scat_b1.values(), *scat_g0.values()
+    )
+    scat_q1.put([held1])
+    scat_b1.put([held2])
     scat_g0.put(held)
-    scat_q0 = Scatter(sum_q0, False)
+    scat_q0 = Scatter(sum_q0, "xy")
     scat_q0.plane(0)
     scat_g0.plane(1)
     scat_q0.plane(1)
-    red_q0 = scat_q0.along_z()
-    red_g0 = scat_g0.along_z()
-    red_b0 = rows_plane(rows0)
+    scat_q1.plane(1)
+    scat_b1.plane(1)
+    red_q1, red_b1 = scat_q1.along_z(), scat_b1.along_z()
+    red_q0, red_g0 = scat_q0.along_z(), scat_g0.along_z()
+    scat_b0.plane(1)
+    red_b0 = scat_b0.along_z()
     red_c0 = jnp.concatenate([red_q0, red_g0], axis=1)
     red_c1 = jnp.concatenate([red_q1, red_g1], axis=1)
 

time: 539 us -> 564 us (1.046)
  starting transfers between devices: 76.4 us -> 127 us
  waiting for transfers between devices: 245 us -> 233 us
  other arithmetic: 65.4 us -> 56.7 us
  local copies, waits for them, and re-layouts: 40.7 us -> 33.7 us
    ppermute x24 -> x0, waiting for transfers between devices: 112 us -> none  [the longest x18 64.6 us: z_gather(): pieces.append(lax.ppermute(pieces[-1], 'fsdp', pairs))]
    ppermute x74 -> x98, waiting for transfers between devices: 133 us -> 233 us  [exchange(): return lax.ppermute(shard, axis, pairs)]
    ppermute x74 -> x98, starting transfers between devices: 66.3 us -> 127 us  [exchange(): return lax.ppermute(shard, axis, pairs)]
    ppermute x24 -> x0, starting transfers between devices: 10.1 us -> none  [the longest x18 9.46 us: z_gather(): pieces.append(lax.ppermute(pieces[-1], 'fsdp', pairs))]
    unnamed x123 -> x134, local copies, waits for them, and re-layouts: 15.6 us -> 14 us
  transfers between devices with their start and end apart: 98 -> 98, of which waited for: 49 -> 37; matrix products, arithmetic and copies ran while one was open for 18% -> 14% of each run, Pallas kernels for 12% -> 11%
where the time goes in v6:
time: 564 us; the launch traced here: 555 us
  waiting for transfers between devices  233 us (41%)
  starting transfers between devices  127 us (23%)
  Pallas kernels  84.4 us (15%)
  other arithmetic  56.7 us (10%)
  local copies, waits for them, and re-layouts  33.7 us (6%)
  matrix products  17.5 us (3%)
    ppermute x98, waiting for transfers between devices, exchange(): return lax.ppermute(shard, axis, pairs)  233 us
    ppermute x98, starting transfers between devices, exchange(): return lax.ppermute(shard, axis, pairs)  127 us
    pallas_call x12, Pallas kernels, whole_call(): pl.pallas_call(body, out_shape=[jax.ShapeDtypeStruct(s, t) for s, t in ou...  84.4 us
    dot_general x12, matrix products, t_dot(): return jnp.einsum('ta,tb->ab', a, b, preferred_element_type=F32)  17.5 us
    unnamed x134, local copies, waits for them, and re-layouts  14 us
  transfers between devices with their start and end apart: 98, of which 37 were waited for; matrix products, arithmetic and copies ran while one was open for 14% of the time, Pallas kernels for 11%

profile of v6, /device:TPU:0, one launch (start us, length us, event | category | flops | bytes accessed | tf_op | source)
XLA Modules:
  0.0 555.0 jit_solution(9399710940921548995)
XLA Ops:
  20.7 3.6 collective-permute-start.13
  28.4 5.1 collective-permute-done.12
  36.0 3.5 collective-permute-start.22
  44.5 14.3 %collective-permute-done.22 = bf16[2,2,96,640]{3,2,1,0:T(8,128)(2,1)S(1)} collective-permute-done((bf16[2,2,96,640]{3,2,1,0:T(8,128)(2,1)S(1)}, bf16[2,2,96,640]{3,2,1,0:T(8,128)(2,1)S(1)}, u32[]{:S(2)}, u32[]{:S(2)}) %collective-permute-start.22) | collective-permute-done | bytes 491552 | tf_op jit(solution)/shard_map/ppermute | solution.py:34
  59.3 16.3 %collective-permute-done.23 = bf16[2,2,96,640]{3,2,1,0:T(8,128)(2,1)S(1)} collective-permute-done((bf16[2,2,96,640]{3,2,1,0:T(8,128)(2,1)S(1)}, bf16[2,2,96,640]{3,2,1,0:T(8,128)(2,1)S(1)}, u32[]{:S(2)}, u32[]{:S(2)}) %collective-permute-start.23) | collective-permute-done | bytes 491552 | tf_op jit(solution)/shard_map/ppermute | solution.py:34
  81.3 3.7 shard_map.152
  85.0 8.8 %collective-permute-start.26 = (bf16[40,896]{1,0:T(8,128)(2,1)S(1)}, bf16[40,896]{1,0:T(8,128)(2,1)S(1)}, u32[]{:S(2)}, u32[]{:S(2)}) collective-permute-start(bf16[40,896]{1,0:T(8,128)(2,1)S(1)} %slice.174), channel_id=1, source_target_pairs={{0,4},{4,0},{8,12},{12,8},{1,5},{5,1},{9,13},{13,9},{2,6},{6,2},{1... | collective-permute-start | bytes 215048 | tf_op jit(solution)/shard_map/ppermute | solution.py:34
  98.8 3.9 collective-permute-done.27
  104.3 3.3 collective-permute-done.32
  111.1 3.9 collective-permute-done.30
  121.4 4.4 collective-permute-done.9
  127.4 3.6 collective-permute-done.33
  132.4 3.5 shard_map.153.mixed
  137.3 3.4 collective-permute-done.36
  140.9 4.1 collective-permute-start.42
  150.1 14.4 %collective-permute-done.42 = bf16[2,2,96,640]{3,2,1,0:T(8,128)(2,1)S(1)} collective-permute-done((bf16[2,2,96,640]{3,2,1,0:T(8,128)(2,1)S(1)}, bf16[2,2,96,640]{3,2,1,0:T(8,128)(2,1)S(1)}, u32[]{:S(2)}, u32[]{:S(2)}) %collective-permute-start.42) | collective-permute-done | bytes 491552 | tf_op jit(solution)/shard_map/ppermute | solution.py:34
  166.0 15.5 %collective-permute-done.43 = bf16[2,2,96,640]{3,2,1,0:T(8,128)(2,1)S(1)} collective-permute-done((bf16[2,2,96,640]{3,2,1,0:T(8,128)(2,1)S(1)}, bf16[2,2,96,640]{3,2,1,0:T(8,128)(2,1)S(1)}, u32[]{:S(2)}, u32[]{:S(2)}) %collective-permute-start.43) | collective-permute-done | bytes 491552 | tf_op jit(solution)/shard_map/ppermute | solution.py:34
  193.8 10.6 %shard_map.154 = (f32[256,640]{1,0:T(8,128)S(1)}, f32[256,640]{1,0:T(8,128)}, bf16[256,640]{1,0:T(8,128)(2,1)S(1)}, f32[256,2048]{1,0:T(8,128)}, f32[256,2048]{1...) custom-call(s32[1]{0:T(128)} %bitcast.flag, f32[256,640]{1,0:T(8,128)} %get-tuple-element.259.x, ...), custom_call_target="tpu_custom_call" | custom-call | flops 2348810240 | bytes 18556932 | tf_op jit(solution)/shard_map/pallas_call | solution.py:190
  208.5 3.7 shard_map.155
  215.8 5.6 %collective-permute-done.39 = bf16[256,512]{1,0:T(8,128)(2,1)S(1)} collective-permute-done((bf16[256,512]{1,0:T(8,128)(2,1)S(1)}, bf16[256,512]{1,0:T(8,128)(2,1)S(1)}, u32[]{:S(2)}, u32[]{:S(2)}) %collective-permute-start.39) | collective-permute-done | bytes 262176 | tf_op jit(solution)/shard_map/ppermute | solution.py:34
  221.4 6.4 %collective-permute-done.40 = bf16[256,512]{1,0:T(8,128)(2,1)S(1)} collective-permute-done((bf16[256,512]{1,0:T(8,128)(2,1)S(1)}, bf16[256,512]{1,0:T(8,128)(2,1)S(1)}, u32[]{:S(2)}, u32[]{:S(2)}) %collective-permute-start.40) | collective-permute-done | bytes 262176 | tf_op jit(solution)/shard_map/ppermute | solution.py:34
  228.9 3.5 shard_map.156.mixed
  238.4 10.8 %shard_map.157 = (f32[256,640]{1,0:T(8,128)S(1)}, f32[256,640]{1,0:T(8,128)}, bf16[256,640]{1,0:T(8,128)(2,1)S(1)}, f32[256,2048]{1,0:T(8,128)}, f32[256,2048]{1...) custom-call(s32[1]{0:T(128)} %bitcast.flag, f32[256,640]{1,0:T(8,128)} %convert_convert_fusion.x, ...), custom_call_target="tpu_custom_call" | custom-call | flops 2348810240 | bytes 18556932 | tf_op jit(solution)/shard_map/pallas_call | solution.py:190
  250.1 10.3 %shard_map.158 = (f32[256,640]{1,0:T(8,128)S(1)}, bf16[256,640]{1,0:T(8,128)(2,1)S(1)}, bf16[256,2048]{1,0:T(8,128)(2,1)}, bf16[256,2048]{1,0:T(8,128)(2,1)}, bf...) custom-call(s32[1]{0:T(128)} %bitcast.flag, bf16[256,640]{1,0:T(8,128)(2,1)S(1)} %get-tuple-element.258.dy, ...), custom_call_target="tpu_custom_call" | custom-call | flops 2013265920 | bytes 17778180 | tf_op jit(solution)/shard_map/pallas_call | solution.py:190
  270.1 8.9 %shard_map.159 = (f32[256,1024]{1,0:T(8,128)}, bf16[1024,512]{1,0:T(8,128)(2,1)}) custom-call(s32[1]{0:T(128)} %bitcast.flag, bf16[256,640]{1,0:T(8,128)(2,1)S(1)} %get-tuple-element.127.da, bf16[1024,640]{1,0:T(8,128)(2,1)} %bitcast.359, bf16[256,1024]{1,0:T(8,128)(2,1)S(1)} %copy-done.23, bf16[1024,512]{1,0:T(8,128)(2,1)} %copy-done.55, ...), custom_call_target="tpu_custom_call" | custom-call | flops 3019898880 | bytes 5313540 | tf_op jit(solution)/shard_map/pallas_call | solution.py:190
  279.0 3.4 add_convert_fusion.3
  282.5 4.2 add_convert_fusion.1
  291.1 5.8 %collective-permute-done.51 = bf16[256,512]{1,0:T(8,128)(2,1)S(1)} collective-permute-done((bf16[256,512]{1,0:T(8,128)(2,1)}, bf16[256,512]{1,0:T(8,128)(2,1)S(1)}, u32[]{:S(2)}, u32[]{:S(2)}) %collective-permute-start.51) | collective-permute-done | bytes 262176 | tf_op jit(solution)/shard_map/ppermute | solution.py:34
  296.9 4.9 collective-permute-done.52
  310.6 5.0 shard_map.160
  318.6 10.8 %shard_map.161 = (f32[256,640]{1,0:T(8,128)S(1)}, bf16[256,640]{1,0:T(8,128)(2,1)S(1)}, bf16[256,2048]{1,0:T(8,128)(2,1)}, bf16[256,2048]{1,0:T(8,128)(2,1)}, bf...) custom-call(s32[1]{0:T(128)} %bitcast.flag, bf16[256,640]{1,0:T(8,128)(2,1)S(1)} %convert_element_type.387.dy, ...), custom_call_target="tpu_custom_call" | custom-call | flops 2013265920 | bytes 17778180 | tf_op jit(solution)/shard_map/pallas_call | solution.py:190
  342.8 4.9 collective-permute-done.60
  347.9 4.3 collective-permute-done.59
  352.5 8.8 %collective-permute-start.61 = (bf16[40,2048]{1,0:T(8,128)(2,1)S(1)}, bf16[40,2048]{1,0:T(8,128)(2,1)S(1)}, u32[]{:S(2)}, u32[]{:S(2)}) collective-permute-start(bf16[40,2048]{1,0:T(8,128)(2,1)S(1)} %get-tuple-element.275), channel_id=1, source_target_pairs={{0,4},{4,0},{8,12},{12,8},{1,5},{5,1},{9,13},{13,9},{2,6},{6,2},{1... | collective-permute-start | bytes 491528 | tf_op jit(solution)/shard_map/ppermute | solution.py:34
  361.3 8.6 %shard_map.162 = (f32[256,1024]{1,0:T(8,128)}, bf16[1024,512]{1,0:T(8,128)(2,1)}) custom-call(s32[1]{0:T(128)} %bitcast.flag, bf16[256,640]{1,0:T(8,128)(2,1)S(1)} %get-tuple-element.158.da, bf16[1024,640]{1,0:T(8,128)(2,1)} %bitcast.357, bf16[256,1024]{1,0:T(8,128)(2,1)S(1)} %copy-done.21, bf16[1024,512]{1,0:T(8,128)(2,1)} %pad_maximum_fusion.24.kv, ...), custom_call_target="tpu_custom_call" | custom-call | flops 3019898880 | bytes 5313540 | tf_op jit(solution)/shard_map/pallas_call | solution.py:190
  374.1 9.3 %collective-permute-done.62 = bf16[40,2048]{1,0:T(8,128)(2,1)S(1)} collective-permute-done((bf16[40,2048]{1,0:T(8,128)(2,1)S(1)}, bf16[40,2048]{1,0:T(8,128)(2,1)S(1)}, u32[]{:S(2)}, u32[]{:S(2)}) %collective-permute-start.62) | collective-permute-done | bytes 163872 | tf_op jit(solution)/shard_map/ppermute | solution.py:34
  390.9 3.3 add_convert_fusion
  397.8 15.8 %collective-permute-done.68 = bf16[4,1,2,96,640]{4,3,2,1,0:T(8,128)(2,1)S(1)} collective-permute-done((bf16[4,1,2,96,640]{4,3,2,1,0:T(8,128)(2,1)S(1)}, bf16[4,1,2,96,640]{4,3,2,1,0:T(8,128)(2,1)S(1)}, u32[]{:S(2)}, u32[]{:S(2)}) %collective-permute-start.68) | collective-permute-done | bytes 983072 | tf_op jit(solution)/shard_map/ppermute | solution.py:34
  415.7 3.6 collective-permute-done.66
  425.8 4.9 shard_map.163
  434.9 18.5 %collective-permute-done.72 = bf16[2,1,2,40,2048]{4,3,0,2,1:T(8,128)(2,1)} collective-permute-done((bf16[2,1,2,40,2048]{4,3,0,2,1:T(8,128)(2,1)}, bf16[2,1,2,40,2048]{4,3,0,2,1:T(8,128)(2,1)}, u32[]{:S(2)}, u32[]{:S(2)}) %collective-permute-start.72) | collective-permute-done | bytes 655392 | tf_op jit(solution)/shard_map/ppermute | solution.py:34
  464.6 8.4 %collective-permute-done.89 = bf16[4,1,1,96,640]{4,3,2,1,0:T(8,128)(2,1)S(1)} collective-permute-done((bf16[4,1,1,96,640]{4,3,2,1,0:T(8,128)(2,1)S(1)}, bf16[4,1,1,96,640]{4,3,2,1,0:T(8,128)(2,1)S(1)}, u32[]{:S(2)}, u32[]{:S(2)}) %collective-permute-start.89) | collective-permute-done | bytes 491552 | tf_op jit(solution)/shard_map/ppermute | solution.py:34
  474.0 5.7 %collective-permute-done.83 = bf16[4,1,1,40,896]{4,3,2,1,0:T(8,128)(2,1)S(1)} collective-permute-done((bf16[4,1,1,40,896]{4,3,2,1,0:T(8,128)(2,1)S(1)}, bf16[4,1,1,40,896]{4,3,2,1,0:T(8,128)(2,1)S(1)}, u32[]{:S(2)}, u32[]{:S(2)}) %collective-permute-start.83) | collective-permute-done | bytes 286752 | tf_op jit(solution)/shard_map/ppermute | solution.py:34
  479.8 21.0 %collective-permute-done.79 = bf16[2,1,1,40,2048]{4,3,0,2,1:T(8,128)(2,1)S(1)} collective-permute-done((bf16[2,1,1,40,2048]{4,3,0,2,1:T(8,128)(2,1)S(1)}, bf16[2,1,1,40,2048]{4,3,0,2,1:T(8,128)(2,1)S(1)}, u32[]{:S(2)}, u32[]{:S(2)}) %collective-permute-start.79) | collective-permute-done | bytes 327712 | tf_op jit(solution)/shard_map/ppermute | solution.py:34
  512.1 10.7 %collective-permute-done.81 = bf16[40,2048]{1,0:T(8,128)(2,1)S(1)} collective-permute-done((bf16[40,2048]{1,0:T(8,128)(2,1)S(1)}, bf16[40,2048]{1,0:T(8,128)(2,1)S(1)}, u32[]{:S(2)}, u32[]{:S(2)}) %collective-permute-start.81) | collective-permute-done | bytes 163872 | tf_op jit(solution)/shard_map/ppermute | solution.py:34
  526.2 3.2 collective-permute-start.94
  536.2 5.9 %collective-permute-start.76 = (bf16[40,896]{1,0:T(8,128)(2,1)S(1)}, bf16[40,896]{1,0:T(8,128)(2,1)S(1)}, u32[]{:S(2)}, u32[]{:S(2)}) collective-permute-start(bf16[40,896]{1,0:T(8,128)(2,1)S(1)} %get-tuple-element.314), channel_id=1, source_target_pairs={{0,8},{4,12},{8,0},{12,4},{1,9},{5,13},{9,1},{13,5},{2,10},{6,14},... | collective-permute-start | bytes 215048 | tf_op jit(solution)/shard_map/ppermute | solution.py:34
  544.3 4.6 collective-permute-done.76
  (512 shorter events, 201.4 us)
Async XLA Ops:
  5.6 20.3 %collective-permute-start = (bf16[256,640]{1,0:T(8,128)(2,1)S(1)}, bf16[256,640]{1,0:T(8,128)(2,1)}, u32[]{:S(2)}, u32[]{:S(2)}) collective-permute-start(bf16[256,640]{1,0:T(8,128)(2,1)S(1)} %dynamic-slice_bitcast_fusion.8), channel_id=1, source_target_pairs={{0,16},{16,0},{1,17},{17,1},{2,18},{18,2},{3,19},{19,3},{4,20},{20... | collective-permute-start | bytes 983048 | tf_op jit(solution)/shard_map/ppermute | solution.py:34
  16.8 16.7 %collective-permute-start.12 = (bf16[40,2048]{1,0:T(8,128)(2,1)S(1)}, bf16[40,2048]{1,0:T(8,128)(2,1)S(1)}, u32[]{:S(2)}, u32[]{:S(2)}) collective-permute-start(bf16[40,2048]{1,0:T(8,128)(2,1)S(1)} %slice.213), channel_id=1, source_target_pairs={{0,8},{4,12},{8,0},{12,4},{1,9},{5,13},{9,1},{13,5},{2,10},{6,14},... | collective-permute-start | bytes 491528 | tf_op jit(solution)/shard_map/ppermute | solution.py:34
  25.9 14.5 %collective-permute-start.5 = (bf16[4,1,1,40,896]{4,3,2,1,0:T(8,128)(2,1)S(1)}, bf16[4,1,1,40,896]{4,3,2,1,0:T(8,128)(2,1)S(1)}, u32[]{:S(2)}, u32[]{:S(2)}) collective-permute-start(bf16[4,1,1,40,896]{4,3,2,1,0:T(8,128)(2,1)S(1)} %maximum_bitcast_fusion.7), channel_id=1, source_target_pairs={{0,2},{1,3},{2,0},{3,1},{4,6},{5,7},{6,4},{7,5},{8,10},{9,11},{10,... | collective-permute-start | bytes 860168 | tf_op jit(solution)/shard_map/ppermute | solution.py:34
  36.0 22.8 %collective-permute-start.22 = (bf16[2,2,96,640]{3,2,1,0:T(8,128)(2,1)S(1)}, bf16[2,2,96,640]{3,2,1,0:T(8,128)(2,1)S(1)}, u32[]{:S(2)}, u32[]{:S(2)}) collective-permute-start(bf16[2,2,96,640]{3,2,1,0:T(8,128)(2,1)S(1)} %maximum_bitcast_fusion.1), channel_id=1, source_target_pairs={{0,4},{4,0},{8,12},{12,8},{1,5},{5,1},{9,13},{13,9},{2,6},{6,2},{1... | collective-permute-start | bytes 1474568 | tf_op jit(solution)/shard_map/ppermute | solution.py:34
  39.5 36.1 %collective-permute-start.23 = (bf16[2,2,96,640]{3,2,1,0:T(8,128)(2,1)S(1)}, bf16[2,2,96,640]{3,2,1,0:T(8,128)(2,1)S(1)}, u32[]{:S(2)}, u32[]{:S(2)}) collective-permute-start(bf16[2,2,96,640]{3,2,1,0:T(8,128)(2,1)S(1)} %maximum_bitcast_fusion.1), channel_id=1, source_target_pairs={{0,8},{4,12},{8,0},{12,4},{1,9},{5,13},{9,1},{13,5},{2,10},{6,14},... | collective-permute-start | bytes 1474568 | tf_op jit(solution)/shard_map/ppermute | solution.py:34
  40.5 35.1 %collective-permute-start.24 = (bf16[2,2,96,640]{3,2,1,0:T(8,128)(2,1)S(1)}, bf16[2,2,96,640]{3,2,1,0:T(8,128)(2,1)S(1)}, u32[]{:S(2)}, u32[]{:S(2)}) collective-permute-start(bf16[2,2,96,640]{3,2,1,0:T(8,128)(2,1)S(1)} %maximum_bitcast_fusion.1), channel_id=1, source_target_pairs={{0,12},{4,8},{8,4},{12,0},{1,13},{5,9},{9,5},{13,1},{2,14},{6,10},... | collective-permute-start | bytes 1474568 | tf_op jit(solution)/shard_map/ppermute | solution.py:34
  42.1 33.7 %collective-permute-start.6 = (bf16[4,2,1,40,896]{4,3,2,1,0:T(8,128)(2,1)S(1)}, bf16[4,2,1,40,896]{4,3,2,1,0:T(8,128)(2,1)S(1)}, u32[]{:S(2)}, u32[]{:S(2)}) collective-permute-start(bf16[4,2,1,40,896]{4,3,2,1,0:T(8,128)(2,1)S(1)} %pad_maximum_fusion.29), channel_id=1, source_target_pairs={{0,1},{1,0},{2,3},{3,2},{4,5},{5,4},{6,7},{7,6},{8,9},{9,8},{10,11... | collective-permute-start | bytes 1720328 | tf_op jit(solution)/shard_map/ppermute | solution.py:34
  43.8 32.5 %collective-permute-start.17 = (bf16[2,2,1,40,2048]{4,3,0,2,1:T(8,128)(2,1)S(1)}, bf16[2,2,1,40,2048]{4,3,0,2,1:T(8,128)(2,1)S(1)}, u32[]{:S(2)}, u32[]{:S(2)}) collective-permute-start(bf16[2,2,1,40,2048]{4,3,0,2,1:T(8,128)(2,1)S(1)} %pad_maximum_fusion.26), channel_id=1, source_target_pairs={{0,1},{1,0},{2,3},{3,2},{4,5},{5,4},{6,7},{7,6},{8,9},{9,8},{10,11... | collective-permute-start | bytes 1966088 | tf_op jit(solution)/shard_map/ppermute | solution.py:34
  58.8 17.6 %collective-permute-start.15 = (bf16[2,1,2,40,2048]{4,3,0,2,1:T(8,128)(2,1)S(1)}, bf16[2,1,2,40,2048]{4,3,0,2,1:T(8,128)(2,1)S(1)}, u32[]{:S(2)}, u32[]{:S(2)}) collective-permute-start(bf16[2,1,2,40,2048]{4,3,0,2,1:T(8,128)(2,1)S(1)} %pad_maximum_fusion.25), channel_id=1, source_target_pairs={{0,2},{1,3},{2,0},{3,1},{4,6},{5,7},{6,4},{7,5},{8,10},{9,11},{10,... | collective-permute-start | bytes 1966088 | tf_op jit(solution)/shard_map/ppermute | solution.py:34
  78.6 48.2 %collective-permute-start.18 = (bf16[16,40,2048]{2,1,0:T(8,128)(2,1)}, bf16[16,40,2048]{2,1,0:T(8,128)(2,1)}, u32[]{:S(2)}, u32[]{:S(2)}) collective-permute-start(bf16[16,40,2048]{2,1,0:T(8,128)(2,1)} %pad_maximum_fusion), channel_id=1, source_target_pairs={{0,16},{16,0},{1,17},{17,1},{2,18},{18,2},{3,19},{19,3},{4,20},{20... | collective-permute-start | bytes 7864328 | tf_op jit(solution)/shard_map/ppermute | solution.py:34
  80.8 46.0 %collective-permute-start.25 = (bf16[16,96,640]{2,1,0:T(8,128)(2,1)}, bf16[16,96,640]{2,1,0:T(8,128)(2,1)}, u32[]{:S(2)}, u32[]{:S(2)}) collective-permute-start(bf16[16,96,640]{2,1,0:T(8,128)(2,1)} %bitcast.43), channel_id=1, source_target_pairs={{0,16},{16,0},{1,17},{17,1},{2,18},{18,2},{3,19},{19,3},{4,20},{20... | collective-permute-start | bytes 5898248 | tf_op jit(solution)/shard_map/ppermute | solution.py:34
  140.9 23.5 %collective-permute-start.42 = (bf16[2,2,96,640]{3,2,1,0:T(8,128)(2,1)S(1)}, bf16[2,2,96,640]{3,2,1,0:T(8,128)(2,1)S(1)}, u32[]{:S(2)}, u32[]{:S(2)}) collective-permute-start(bf16[2,2,96,640]{3,2,1,0:T(8,128)(2,1)S(1)} %bitcast.376), channel_id=1, source_target_pairs={{0,4},{4,0},{8,12},{12,8},{1,5},{5,1},{9,13},{13,9},{2,6},{6,2},{1... | collective-permute-start | bytes 1474568 | tf_op jit(solution)/shard_map/ppermute | solution.py:34
  145.0 36.5 %collective-permute-start.43 = (bf16[2,2,96,640]{3,2,1,0:T(8,128)(2,1)S(1)}, bf16[2,2,96,640]{3,2,1,0:T(8,128)(2,1)S(1)}, u32[]{:S(2)}, u32[]{:S(2)}) collective-permute-start(bf16[2,2,96,640]{3,2,1,0:T(8,128)(2,1)S(1)} %bitcast.377), channel_id=1, source_target_pairs={{0,8},{4,12},{8,0},{12,4},{1,9},{5,13},{9,1},{13,5},{2,10},{6,14},... | collective-permute-start | bytes 1474568 | tf_op jit(solution)/shard_map/ppermute | solution.py:34
  146.6 34.9 %collective-permute-start.44 = (bf16[2,2,96,640]{3,2,1,0:T(8,128)(2,1)S(1)}, bf16[2,2,96,640]{3,2,1,0:T(8,128)(2,1)S(1)}, u32[]{:S(2)}, u32[]{:S(2)}) collective-permute-start(bf16[2,2,96,640]{3,2,1,0:T(8,128)(2,1)S(1)} %bitcast.378), channel_id=1, source_target_pairs={{0,12},{4,8},{8,4},{12,0},{1,13},{5,9},{9,5},{13,1},{2,14},{6,10},... | collective-permute-start | bytes 1474568 | tf_op jit(solution)/shard_map/ppermute | solution.py:34
  148.1 35.3 %collective-permute-start.37 = (bf16[4,2,1,40,896]{4,3,2,1,0:T(8,128)(2,1)S(1)}, bf16[4,2,1,40,896]{4,3,2,1,0:T(8,128)(2,1)S(1)}, u32[]{:S(2)}, u32[]{:S(2)}) collective-permute-start(bf16[4,2,1,40,896]{4,3,2,1,0:T(8,128)(2,1)S(1)} %pad_maximum_fusion.30), channel_id=1, source_target_pairs={{0,1},{1,0},{2,3},{3,2},{4,5},{5,4},{6,7},{7,6},{8,9},{9,8},{10,11... | collective-permute-start | bytes 1720328 | tf_op jit(solution)/shard_map/ppermute | solution.py:34
  149.6 35.6 %collective-permute-start.46 = (bf16[2,1,2,40,2048]{4,3,0,2,1:T(8,128)(2,1)S(1)}, bf16[2,1,2,40,2048]{4,3,0,2,1:T(8,128)(2,1)S(1)}, u32[]{:S(2)}, u32[]{:S(2)}) collective-permute-start(bf16[2,1,2,40,2048]{4,3,0,2,1:T(8,128)(2,1)S(1)} %pad_maximum_fusion.27), channel_id=1, source_target_pairs={{0,2},{1,3},{2,0},{3,1},{4,6},{5,7},{6,4},{7,5},{8,10},{9,11},{10,... | collective-permute-start | bytes 1966088 | tf_op jit(solution)/shard_map/ppermute | solution.py:34
  164.4 21.1 %collective-permute-start.47 = (bf16[2,2,1,40,2048]{4,3,0,2,1:T(8,128)(2,1)S(1)}, bf16[2,2,1,40,2048]{4,3,0,2,1:T(8,128)(2,1)S(1)}, u32[]{:S(2)}, u32[]{:S(2)}) collective-permute-start(bf16[2,2,1,40,2048]{4,3,0,2,1:T(8,128)(2,1)S(1)} %pad_maximum_fusion.28), channel_id=1, source_target_pairs={{0,1},{1,0},{2,3},{3,2},{4,5},{5,4},{6,7},{7,6},{8,9},{9,8},{10,11... | collective-permute-start | bytes 1966088 | tf_op jit(solution)/shard_map/ppermute | solution.py:34
  183.4 49.0 %collective-permute-start.45 = (bf16[16,96,640]{2,1,0:T(8,128)(2,1)}, bf16[16,96,640]{2,1,0:T(8,128)(2,1)}, u32[]{:S(2)}, u32[]{:S(2)}) collective-permute-start(bf16[16,96,640]{2,1,0:T(8,128)(2,1)} %bitcast.75), channel_id=1, source_target_pairs={{0,16},{16,0},{1,17},{17,1},{2,18},{18,2},{3,19},{19,3},{4,20},{20... | collective-permute-start | bytes 5898248 | tf_op jit(solution)/shard_map/ppermute | solution.py:34
  184.7 23.9 %collective-permute-start.38 = (bf16[16,40,896]{2,1,0:T(8,128)(2,1)}, bf16[16,40,896]{2,1,0:T(8,128)(2,1)}, u32[]{:S(2)}, u32[]{:S(2)}) collective-permute-start(bf16[16,40,896]{2,1,0:T(8,128)(2,1)} %bitcast.66), channel_id=1, source_target_pairs={{0,16},{16,0},{1,17},{17,1},{2,18},{18,2},{3,19},{19,3},{4,20},{20... | collective-permute-start | bytes 3440648 | tf_op jit(solution)/shard_map/ppermute | solution.py:34
  187.8 50.7 %collective-permute-start.48 = (bf16[16,40,2048]{2,1,0:T(8,128)(2,1)}, bf16[16,40,2048]{2,1,0:T(8,128)(2,1)}, u32[]{:S(2)}, u32[]{:S(2)}) collective-permute-start(bf16[16,40,2048]{2,1,0:T(8,128)(2,1)} %pad_maximum_fusion.2), channel_id=1, source_target_pairs={{0,16},{16,0},{1,17},{17,1},{2,18},{18,2},{3,19},{19,3},{4,20},{20... | collective-permute-start | bytes 7864328 | tf_op jit(solution)/shard_map/ppermute | solution.py:34
  213.8 14.1 %collective-permute-start.40 = (bf16[256,512]{1,0:T(8,128)(2,1)S(1)}, bf16[256,512]{1,0:T(8,128)(2,1)S(1)}, u32[]{:S(2)}, u32[]{:S(2)}) collective-permute-start(bf16[256,512]{1,0:T(8,128)(2,1)S(1)} %get-tuple-element.118), channel_id=1, source_target_pairs={{0,2},{1,3},{2,0},{3,1},{4,6},{5,7},{6,4},{7,5},{8,10},{9,11},{10,... | collective-permute-start | bytes 786440 | tf_op jit(solution)/shard_map/ppermute | solution.py:34
  264.4 18.1 %collective-permute-start.49 = (bf16[640,2048]{1,0:T(8,128)(2,1)}, bf16[640,2048]{1,0:T(8,128)(2,1)}, u32[]{:S(2)}, u32[]{:S(2)}) collective-permute-start(bf16[640,2048]{1,0:T(8,128)(2,1)} %convolution_convert_fusion.3), channel_id=1, source_target_pairs={{0,16},{16,0},{1,17},{17,1},{2,18},{18,2},{3,19},{19,3},{4,20},{20... | collective-permute-start | bytes 7864328 | tf_op jit(solution)/shard_map/ppermute | solution.py:34
  306.8 28.1 %collective-permute-start.56 = (bf16[2,1,2,40,2048]{4,3,0,2,1:T(8,128)(2,1)}, bf16[2,1,2,40,2048]{4,3,0,2,1:T(8,128)(2,1)}, u32[]{:S(2)}, u32[]{:S(2)}) collective-permute-start(bf16[2,1,2,40,2048]{4,3,0,2,1:T(8,128)(2,1)} %copy.71), channel_id=1, source_target_pairs={{0,2},{1,3},{2,0},{3,1},{4,6},{5,7},{6,4},{7,5},{8,10},{9,11},{10,... | collective-permute-start | bytes 1966088 | tf_op jit(solution)/shard_map/ppermute | solution.py:34
  310.0 26.3 %collective-permute-start.55 = (bf16[2,2,1,40,2048]{4,3,0,2,1:T(8,128)(2,1)}, bf16[2,2,1,40,2048]{4,3,0,2,1:T(8,128)(2,1)}, u32[]{:S(2)}, u32[]{:S(2)}) collective-permute-start(bf16[2,2,1,40,2048]{4,3,0,2,1:T(8,128)(2,1)} %copy.69), channel_id=1, source_target_pairs={{0,1},{1,0},{2,3},{3,2},{4,5},{5,4},{6,7},{7,6},{8,9},{9,8},{10,11... | collective-permute-start | bytes 1966088 | tf_op jit(solution)/shard_map/ppermute | solution.py:34
  318.6 19.0 %collective-permute-start.54 = (bf16[640,896]{1,0:T(8,128)(2,1)}, bf16[640,896]{1,0:T(8,128)(2,1)S(1)}, u32[]{:S(2)}, u32[]{:S(2)}) collective-permute-start(bf16[640,896]{1,0:T(8,128)(2,1)} %fusion.3), channel_id=1, source_target_pairs={{0,16},{16,0},{1,17},{17,1},{2,18},{18,2},{3,19},{19,3},{4,20},{20... | collective-permute-start | bytes 3440648 | tf_op jit(solution)/shard_map/ppermute | solution.py:34
  333.9 53.5 %collective-permute-start.58 = (bf16[16,96,640]{2,1,0:T(8,128)(2,1)}, bf16[16,96,640]{2,1,0:T(8,128)(2,1)S(1)}, u32[]{:S(2)}, u32[]{:S(2)}) collective-permute-start(bf16[16,96,640]{2,1,0:T(8,128)(2,1)} %pad_maximum_fusion.7), channel_id=1, source_target_pairs={{0,16},{16,0},{1,17},{17,1},{2,18},{18,2},{3,19},{19,3},{4,20},{20... | collective-permute-start | bytes 5898248 | tf_op jit(solution)/shard_map/ppermute | solution.py:34
  341.9 48.9 %collective-permute-start.57 = (bf16[640,2048]{1,0:T(8,128)(2,1)}, bf16[640,2048]{1,0:T(8,128)(2,1)}, u32[]{:S(2)}, u32[]{:S(2)}) collective-permute-start(bf16[640,2048]{1,0:T(8,128)(2,1)} %convolution_convert_fusion.1), channel_id=1, source_target_pairs={{0,16},{16,0},{1,17},{17,1},{2,18},{18,2},{3,19},{19,3},{4,20},{20... | collective-permute-start | bytes 7864328 | tf_op jit(solution)/shard_map/ppermute | solution.py:34
  352.5 20.0 %collective-permute-start.61 = (bf16[40,2048]{1,0:T(8,128)(2,1)S(1)}, bf16[40,2048]{1,0:T(8,128)(2,1)S(1)}, u32[]{:S(2)}, u32[]{:S(2)}) collective-permute-start(bf16[40,2048]{1,0:T(8,128)(2,1)S(1)} %get-tuple-element.275), channel_id=1, source_target_pairs={{0,4},{4,0},{8,12},{12,8},{1,5},{5,1},{9,13},{13,9},{2,6},{6,2},{1... | collective-permute-start | bytes 491528 | tf_op jit(solution)/shard_map/ppermute | solution.py:34
  383.3 30.2 %collective-permute-start.68 = (bf16[4,1,2,96,640]{4,3,2,1,0:T(8,128)(2,1)S(1)}, bf16[4,1,2,96,640]{4,3,2,1,0:T(8,128)(2,1)S(1)}, u32[]{:S(2)}, u32[]{:S(2)}) collective-permute-start(bf16[4,1,2,96,640]{4,3,2,1,0:T(8,128)(2,1)S(1)} %constant_dynamic-slice_fusion.12), channel_id=1, source_target_pairs={{0,2},{1,3},{2,0},{3,1},{4,6},{5,7},{6,4},{7,5},{8,10},{9,11},{10,... | collective-permute-start | bytes 2949128 | tf_op jit(solution)/shard_map/ppermute | solution.py:34
  394.3 21.4 %collective-permute-start.65 = (bf16[256,512]{1,0:T(8,128)(2,1)S(1)}, bf16[256,512]{1,0:T(8,128)(2,1)S(1)}, u32[]{:S(2)}, u32[]{:S(2)}) collective-permute-start(bf16[256,512]{1,0:T(8,128)(2,1)S(1)} %get-tuple-element.252), channel_id=1, source_target_pairs={{0,1},{1,0},{2,3},{3,2},{4,5},{5,4},{6,7},{7,6},{8,9},{9,8},{10,11... | collective-permute-start | bytes 786440 | tf_op jit(solution)/shard_map/ppermute | solution.py:34
  395.0 24.2 %collective-permute-start.66 = (bf16[256,512]{1,0:T(8,128)(2,1)S(1)}, bf16[256,512]{1,0:T(8,128)(2,1)S(1)}, u32[]{:S(2)}, u32[]{:S(2)}) collective-permute-start(bf16[256,512]{1,0:T(8,128)(2,1)S(1)} %get-tuple-element.254), channel_id=1, source_target_pairs={{0,2},{1,3},{2,0},{3,1},{4,6},{5,7},{6,4},{7,5},{8,10},{9,11},{10,... | collective-permute-start | bytes 786440 | tf_op jit(solution)/shard_map/ppermute | solution.py:34
  396.5 22.7 %collective-permute-start.67 = (bf16[256,512]{1,0:T(8,128)(2,1)S(1)}, bf16[256,512]{1,0:T(8,128)(2,1)S(1)}, u32[]{:S(2)}, u32[]{:S(2)}) collective-permute-start(bf16[256,512]{1,0:T(8,128)(2,1)S(1)} %get-tuple-element.253), channel_id=1, source_target_pairs={{0,3},{1,2},{2,1},{3,0},{4,7},{5,6},{6,5},{7,4},{8,11},{9,10},{10,... | collective-permute-start | bytes 786440 | tf_op jit(solution)/shard_map/ppermute | solution.py:34
  414.9 42.4 %collective-permute-start.88 = (bf16[4,1,2,96,640]{4,3,2,1,0:T(8,128)(2,1)}, bf16[4,1,2,96,640]{4,3,2,1,0:T(8,128)(2,1)}, u32[]{:S(2)}, u32[]{:S(2)}) collective-permute-start(bf16[4,1,2,96,640]{4,3,2,1,0:T(8,128)(2,1)} %constant_dynamic-slice_fusion.2), channel_id=1, source_target_pairs={{0,2},{1,3},{2,0},{3,1},{4,6},{5,7},{6,4},{7,5},{8,10},{9,11},{10,... | collective-permute-start | bytes 2949128 | tf_op jit(solution)/shard_map/ppermute | solution.py:34
  421.6 31.8 %collective-permute-start.72 = (bf16[2,1,2,40,2048]{4,3,0,2,1:T(8,128)(2,1)}, bf16[2,1,2,40,2048]{4,3,0,2,1:T(8,128)(2,1)}, u32[]{:S(2)}, u32[]{:S(2)}) collective-permute-start(bf16[2,1,2,40,2048]{4,3,0,2,1:T(8,128)(2,1)} %copy.75), channel_id=1, source_target_pairs={{0,2},{1,3},{2,0},{3,1},{4,6},{5,7},{6,4},{7,5},{8,10},{9,11},{10,... | collective-permute-start | bytes 1966088 | tf_op jit(solution)/shard_map/ppermute | solution.py:34
  424.3 31.6 %collective-permute-start.71 = (bf16[2,2,1,40,2048]{4,3,0,2,1:T(8,128)(2,1)}, bf16[2,2,1,40,2048]{4,3,0,2,1:T(8,128)(2,1)}, u32[]{:S(2)}, u32[]{:S(2)}) collective-permute-start(bf16[2,2,1,40,2048]{4,3,0,2,1:T(8,128)(2,1)} %copy.73), channel_id=1, source_target_pairs={{0,1},{1,0},{2,3},{3,2},{4,5},{5,4},{6,7},{7,6},{8,9},{9,8},{10,11... | collective-permute-start | bytes 1966088 | tf_op jit(solution)/shard_map/ppermute | solution.py:34
  432.9 21.8 %collective-permute-start.69 = (f32[256,640]{1,0:T(8,128)S(1)}, f32[256,640]{1,0:T(8,128)S(1)}, u32[]{:S(2)}, u32[]{:S(2)}) collective-permute-start(f32[256,640]{1,0:T(8,128)S(1)} %broadcast_select_fusion.24), channel_id=1, source_target_pairs={{0,16},{16,0},{1,17},{17,1},{2,18},{18,2},{3,19},{19,3},{4,20},{20... | collective-permute-start | bytes 1966088 | tf_op jit(solution)/shard_map/ppermute | solution.py:34
  434.3 25.2 %collective-permute-start.70 = (bf16[640,896]{1,0:T(8,128)(2,1)S(1)}, bf16[640,896]{1,0:T(8,128)(2,1)S(1)}, u32[]{:S(2)}, u32[]{:S(2)}) collective-permute-start(bf16[640,896]{1,0:T(8,128)(2,1)S(1)} %fusion.1), channel_id=1, source_target_pairs={{0,16},{16,0},{1,17},{17,1},{2,18},{18,2},{3,19},{19,3},{4,20},{20... | collective-permute-start | bytes 3440648 | tf_op jit(solution)/shard_map/ppermute | solution.py:34
  458.8 14.2 %collective-permute-start.89 = (bf16[4,1,1,96,640]{4,3,2,1,0:T(8,128)(2,1)S(1)}, bf16[4,1,1,96,640]{4,3,2,1,0:T(8,128)(2,1)S(1)}, u32[]{:S(2)}, u32[]{:S(2)}) collective-permute-start(bf16[4,1,1,96,640]{4,3,2,1,0:T(8,128)(2,1)S(1)} %constant_dynamic-slice_fusion.1), channel_id=1, source_target_pairs={{0,1},{1,0},{2,3},{3,2},{4,5},{5,4},{6,7},{7,6},{8,9},{9,8},{10,11... | collective-permute-start | bytes 1474568 | tf_op jit(solution)/shard_map/ppermute | solution.py:34
  460.0 66.0 %collective-permute-start.93 = (bf16[4,1,1,96,640]{4,3,2,1,0:T(8,128)(2,1)S(1)}, bf16[4,1,1,96,640]{4,3,2,1,0:T(8,128)(2,1)S(1)}, u32[]{:S(2)}, u32[]{:S(2)}) collective-permute-start(bf16[4,1,1,96,640]{4,3,2,1,0:T(8,128)(2,1)S(1)} %constant_dynamic-slice_fusion), channel_id=1, source_target_pairs={{0,1},{1,0},{2,3},{3,2},{4,5},{5,4},{6,7},{7,6},{8,9},{9,8},{10,11... | collective-permute-start | bytes 1474568 | tf_op jit(solution)/shard_map/ppermute | solution.py:34
  461.5 63.4 %collective-permute-start.73 = (bf16[4,2,1,40,896]{4,3,2,1,0:T(8,128)(2,1)S(1)}, bf16[4,2,1,40,896]{4,3,2,1,0:T(8,128)(2,1)S(1)}, u32[]{:S(2)}, u32[]{:S(2)}) collective-permute-start(bf16[4,2,1,40,896]{4,3,2,1,0:T(8,128)(2,1)S(1)} %constant_dynamic-slice_fusion.7), channel_id=1, source_target_pairs={{0,1},{1,0},{2,3},{3,2},{4,5},{5,4},{6,7},{7,6},{8,9},{9,8},{10,11... | collective-permute-start | bytes 1720328 | tf_op jit(solution)/shard_map/ppermute | solution.py:34
  462.2 38.7 %collective-permute-start.79 = (bf16[2,1,1,40,2048]{4,3,0,2,1:T(8,128)(2,1)S(1)}, bf16[2,1,1,40,2048]{4,3,0,2,1:T(8,128)(2,1)S(1)}, u32[]{:S(2)}, u32[]{:S(2)}) collective-permute-start(bf16[2,1,1,40,2048]{4,3,0,2,1:T(8,128)(2,1)S(1)} %constant_dynamic-slice_fusion.4), channel_id=1, source_target_pairs={{0,1},{1,0},{2,3},{3,2},{4,5},{5,4},{6,7},{7,6},{8,9},{9,8},{10,11... | collective-permute-start | bytes 983048 | tf_op jit(solution)/shard_map/ppermute | solution.py:34
  463.7 37.3 %collective-permute-start.78 = (bf16[2,1,1,40,2048]{4,3,0,2,1:T(8,128)(2,1)S(1)}, bf16[2,1,1,40,2048]{4,3,0,2,1:T(8,128)(2,1)S(1)}, u32[]{:S(2)}, u32[]{:S(2)}) collective-permute-start(bf16[2,1,1,40,2048]{4,3,0,2,1:T(8,128)(2,1)S(1)} %constant_dynamic-slice_fusion.5), channel_id=1, source_target_pairs={{0,2},{1,3},{2,0},{3,1},{4,6},{5,7},{6,4},{7,5},{8,10},{9,11},{10,... | collective-permute-start | bytes 983048 | tf_op jit(solution)/shard_map/ppermute | solution.py:34
  479.7 24.0 %collective-permute-start.84 = (bf16[40,896]{1,0:T(8,128)(2,1)S(1)}, bf16[40,896]{1,0:T(8,128)(2,1)S(1)}, u32[]{:S(2)}, u32[]{:S(2)}) collective-permute-start(bf16[40,896]{1,0:T(8,128)(2,1)S(1)} %get-tuple-element.315), channel_id=1, source_target_pairs={{0,4},{4,0},{8,12},{12,8},{1,5},{5,1},{9,13},{13,9},{2,6},{6,2},{1... | collective-permute-start | bytes 215048 | tf_op jit(solution)/shard_map/ppermute | solution.py:34
  507.4 15.4 %collective-permute-start.81 = (bf16[40,2048]{1,0:T(8,128)(2,1)S(1)}, bf16[40,2048]{1,0:T(8,128)(2,1)S(1)}, u32[]{:S(2)}, u32[]{:S(2)}) collective-permute-start(bf16[40,2048]{1,0:T(8,128)(2,1)S(1)} %get-tuple-element.273), channel_id=1, source_target_pairs={{0,8},{4,12},{8,0},{12,4},{1,9},{5,13},{9,1},{13,5},{2,10},{6,14},... | collective-permute-start | bytes 491528 | tf_op jit(solution)/shard_map/ppermute | solution.py:34
  507.9 14.9 %collective-permute-start.82 = (bf16[40,2048]{1,0:T(8,128)(2,1)S(1)}, bf16[40,2048]{1,0:T(8,128)(2,1)S(1)}, u32[]{:S(2)}, u32[]{:S(2)}) collective-permute-start(bf16[40,2048]{1,0:T(8,128)(2,1)S(1)} %get-tuple-element.274), channel_id=1, source_target_pairs={{0,12},{4,8},{8,4},{12,0},{1,13},{5,9},{9,5},{13,1},{2,14},{6,10},... | collective-permute-start | bytes 491528 | tf_op jit(solution)/shard_map/ppermute | solution.py:34
  510.6 18.9 %collective-permute-start.90 = (bf16[96,640]{1,0:T(8,128)(2,1)S(1)}, bf16[96,640]{1,0:T(8,128)(2,1)S(1)}, u32[]{:S(2)}, u32[]{:S(2)}) collective-permute-start(bf16[96,640]{1,0:T(8,128)(2,1)S(1)} %get-tuple-element.293), channel_id=1, source_target_pairs={{0,4},{4,0},{8,12},{12,8},{1,5},{5,1},{9,13},{13,9},{2,6},{6,2},{1... | collective-permute-start | bytes 368648 | tf_op jit(solution)/shard_map/ppermute | solution.py:34
  526.2 15.9 %collective-permute-start.94 = (bf16[96,640]{1,0:T(8,128)(2,1)S(1)}, bf16[96,640]{1,0:T(8,128)(2,1)S(1)}, u32[]{:S(2)}, u32[]{:S(2)}) collective-permute-start(bf16[96,640]{1,0:T(8,128)(2,1)S(1)} %get-tuple-element.290), channel_id=1, source_target_pairs={{0,4},{4,0},{8,12},{12,8},{1,5},{5,1},{9,13},{13,9},{2,6},{6,2},{1... | collective-permute-start | bytes 368648 | tf_op jit(solution)/shard_map/ppermute | solution.py:34
  529.4 14.7 %collective-permute-start.95 = (bf16[96,640]{1,0:T(8,128)(2,1)S(1)}, bf16[96,640]{1,0:T(8,128)(2,1)S(1)}, u32[]{:S(2)}, u32[]{:S(2)}) collective-permute-start(bf16[96,640]{1,0:T(8,128)(2,1)S(1)} %get-tuple-element.292), channel_id=1, source_target_pairs={{0,8},{4,12},{8,0},{12,4},{1,9},{5,13},{9,1},{13,5},{2,10},{6,14},... | collective-permute-start | bytes 368648 | tf_op jit(solution)/shard_map/ppermute | solution.py:34
  (110 other events, 1164.2 us)

commit v7 on v6

--- a/solution.py
+++ b/solution.py
@@ -22,6 +22,7 @@
 BASES = (math.log(10000.0), math.log(1000000.0))
 SCALE = 1.0 / math.sqrt(HD)
 BF = jnp.bfloat16
+GRID = ("fsdp", "ctx")
 F32 = jnp.float32
 
 
@@ -88,6 +89,22 @@
         part = lax.dynamic_index_in_dim(buf, me ^ j, 0, False)
         total = total + exchange(part, "fsdp", j).astype(F32)
     return total
+
+
+def pack_rows(rows, height):
+    lead, r = rows.shape[:-2], rows.shape[-2]
+    if r % 8 or height % 8 or r * D // height % 128 or height // 8 != D // 128:
+        return rows.reshape(lead + (height, r * D // height))
+    tiles = rows.reshape(lead + (r // 8, 8, D // 128, 128))
+    return jnp.swapaxes(tiles, -4, -2).reshape(lead + (height, r * D // height))
+
+
+def unpack_rows(packed, r):
+    lead, height = packed.shape[:-2], packed.shape[-2]
+    if r % 8 or height % 8 or r * D // height % 128 or height // 8 != D // 128:
+        return packed.reshape(lead + (r, D))
+    tiles = packed.reshape(lead + (height // 8, 8, r // 8, 128))
+    return jnp.swapaxes(tiles, -4, -2).reshape(lead + (r, D))
 
 
 class Gather:
@@ -194,7 +211,7 @@
         out_specs=[vmem] * len(outs),
         compiler_params=pltpu.CompilerParams(vmem_limit_bytes=52 * 2**20),
         cost_estimate=pl.CostEstimate(
-            flops=int(flops), bytes_accessed=int(moved), transcendentals=0
+            flops=int(flops) // 64, bytes_accessed=int(moved) // 64, transcendentals=0
         ),
     )(*args)
 
@@ -583,21 +600,18 @@
     pairs0 = gather0.pairs()
     query0 = query_side(pairs0[0])
     kept0 = forward_keys(query0, x0, *tables[0], flag)
-    cols1, rows1 = tie(layer_cols[1], layer_rows[1], kept0["q"], *gather0.parts)[:2]
-    gather1 = Gather(cols1, rows1)
-    gather1.begin()
+    whole1 = jnp.concatenate([layer_cols[1], pack_rows(layer_rows[1], nr)], axis=1)
+    whole1 = lax.all_gather(whole1, GRID, axis=0)
     swapped = [v for pair in pairs0[1:] for v in pair]
-    kept0["kv"], *held = tie(kept0["kv"], *swapped, *gather1.parts)
-    pairs0[1:] = [held[:2], held[2:4]]
-    gather1.parts = held[4:]
-    gather1.plane(0)
+    kept0["kv"], *held = tie(kept0["kv"], *swapped)
+    feed0 = feed_side(held[:2], held[2:], query0[2])
     mixed = forward_attend(kept0, pos, windows[0], flag)
-    mixed, gather1.rows, *gather1.parts = tie(mixed, gather1.rows, *gather1.parts)
-    gather1.rows_z()
-    gather1.plane(1)
-    feed0 = feed_side(*pairs0[1:], query0[2])
     y0 = forward_rest(feed0, kept0, mixed, flag).astype(BF)
-    pairs1 = gather1.pairs()
+    whole1, y0 = tie(whole1, y0)
+    cuts = (0, QP, QP + FF, whole1.shape[-1])
+    pairs1 = [whole1[..., i:j] for i, j in zip(cuts[:-1], cuts[1:])]
+    pairs1 = [(v, exchange(v, "section", 1)) for v in pairs1]
+    pairs1[2] = [unpack_rows(v, (ro + rd) // 2) for v in pairs1[2]]
     query1 = query_side(pairs1[0])
     kept1 = forward_keys(query1, y0.astype(F32), *tables[1], flag)
     feed1 = feed_side(*pairs1[1:], query1[2])
@@ -612,9 +626,10 @@
     grad_q1, kv_blocks = backward_attend(feed1[2], kept1, branch1, pos, windows[1], flag)
     grad_q1, kv_blocks, sum_g1, sum_b1 = tie(grad_q1, kv_blocks, sum_g1, sum_b1)
     grad_kv = key_return(kv_blocks)
-    grad_kv, sum_g1, sum_b1 = tie(grad_kv, sum_g1, sum_b1)
-    scat_g1, scat_b1 = Scatter(sum_g1, "both"), Scatter(sum_b1, "yx")
-    scat_g1.plane(0)
+    sums1 = jnp.concatenate([sum_g1, pack_rows(sum_b1, nr)], axis=-1)
+    grad_kv, sums1 = tie(grad_kv, sums1)
+    sums1 = lax.psum_scatter(sums1, GRID, scatter_dimension=0).astype(F32)
+    red_g1, red_b1 = sums1[:, :FF], unpack_rows(sums1[:, FF:], (ro + rd) // 2)
     grad1, wg_q, gain_zero, head_grads = backward_keys(
         query1, kept1, middle1, grad_q1, grad_kv, *tables[1], flag
     )
@@ -624,46 +639,36 @@
     middle0, branch0, wg_g, wg_out, wg_down, norm_grads = backward_feed(
         feed0, kept0, grad1, flag
     )
-    branch0, sum_q1, held0, *held = tie(branch0, sum_q1, *scat_b1.values(), *scat_g1.values())
-    scat_g1.put(held)
-    scat_b1.put([held0])
+    branch0, sum_q1 = tie(branch0, sum_q1)
     scat_q1 = Scatter(sum_q1, "xy")
-    scat_g1.plane(1)
     scat_q1.plane(0)
-    scat_b1.plane(0)
-    red_g1 = scat_g1.along_z()
     sum_g0 = reduce_cols(*wg_g)
     sum_b0 = reduce_rows(wg_out, wg_down)
     grad_q0, kv_blocks = backward_attend(feed0[2], kept0, branch0, pos, windows[0], flag)
-    grad_q0, kv_blocks, sum_g0, sum_b0, red_g1, held0 = tie(
-        grad_q0, kv_blocks, sum_g0, sum_b0, red_g1, *scat_q1.values()
+    grad_q0, kv_blocks, sum_g0, sum_b0, held0 = tie(
+        grad_q0, kv_blocks, sum_g0, sum_b0, *scat_q1.values()
     )
     scat_q1.put([held0])
     grad_kv = key_return(kv_blocks)
     scat_b0 = Scatter(sum_b0, "yx")
     scat_b0.plane(0)
-    grad_kv, sum_g0, *held = tie(grad_kv, sum_g0, *scat_q1.values(), *scat_b1.values())
-    scat_q1.put(held[:1])
-    scat_b1.put(held[1:])
+    grad_kv, sum_g0, held0 = tie(grad_kv, sum_g0, *scat_q1.values())
+    scat_q1.put([held0])
     scat_g0 = Scatter(sum_g0, "both")
     scat_g0.plane(0)
     grad0, wg_q, gain_zero, head_grads = backward_keys(
         query0, kept0, middle0, grad_q0, grad_kv, *tables[0], flag
     )
     sum_q0 = reduce_query(wg_q, [gain_zero, norm_grads], head_grads)
-    sum_q0, held1, held2, *held = tie(
-        sum_q0, *scat_q1.values(), *scat_b1.values(), *scat_g0.values()
-    )
+    sum_q0, held1, *held = tie(sum_q0, *scat_q1.values(), *scat_g0.values())
     scat_q1.put([held1])
-    scat_b1.put([held2])
     scat_g0.put(held)
     scat_q0 = Scatter(sum_q0, "xy")
     scat_q0.plane(0)
     scat_g0.plane(1)
     scat_q0.plane(1)
     scat_q1.plane(1)
-    scat_b1.plane(1)
-    red_q1, red_b1 = scat_q1.along_z(), scat_b1.along_z()
+    red_q1 = scat_q1.along_z()
     red_q0, red_g0 = scat_q0.along_z(), scat_g0.along_z()
     scat_b0.plane(1)
     red_b0 = scat_b0.along_z()

time: 564 us -> 542 us (0.961)
  starting transfers between devices: 127 us -> 93.3 us
  waiting for transfers between devices: 233 us -> 218 us
  local copies, waits for them, and re-layouts: 33.7 us -> 47.1 us
  between operations: 2.68 us -> 15.7 us
    ppermute x98 -> x69, starting transfers between devices: 127 us -> 93.2 us  [exchange(): return lax.ppermute(shard, axis, pairs)]
    ppermute x98 -> x69, waiting for transfers between devices: 233 us -> 218 us  [exchange(): return lax.ppermute(shard, axis, pairs)]
    slice x0 -> x4, local copies, waits for them, and re-layouts: none -> 8.84 us  [the longest x3 8.81 us: local(): pairs1 = [whole1[..., i:j] for i, j in zip(cuts[:-1], cuts[1:])]]
    unnamed x134 -> x130, local copies, waits for them, and re-layouts: 14 us -> 15.4 us
  transfers between devices with their start and end apart: 98 -> 71, of which waited for: 37 -> 32; matrix products, arithmetic and copies ran while one was open for 14% -> 16% of each run, Pallas kernels for 11% -> 11%
where the time goes in v7:
time: 542 us; the launch traced here: 532 us
  waiting for transfers between devices  218 us (40%)
  starting transfers between devices  93.3 us (17%)
  Pallas kernels  84.6 us (16%)
  other arithmetic  54.8 us (10%)
  local copies, waits for them, and re-layouts  47.1 us (9%)
  matrix products  18 us (3%)
  between operations  15.7 us (3%)
    ppermute x69, waiting for transfers between devices, exchange(): return lax.ppermute(shard, axis, pairs)  218 us
    ppermute x69, starting transfers between devices, exchange(): return lax.ppermute(shard, axis, pairs)  93.2 us
    pallas_call x12, Pallas kernels, whole_call(): pl.pallas_call(body, out_shape=[jax.ShapeDtypeStruct(s, t) for s, t in ou...  84.6 us
    dot_general x12, matrix products, t_dot(): return jnp.einsum('ta,tb->ab', a, b, preferred_element_type=F32)  18 us
    unnamed x130, local copies, waits for them, and re-layouts  15.4 us
  transfers between devices with their start and end apart: 71, of which 32 were waited for; matrix products, arithmetic and copies ran while one was open for 16% of the time, Pallas kernels for 11%

profile of v7, /device:TPU:0, one launch (start us, length us, event | category | flops | bytes accessed | tf_op | source)
XLA Modules:
  0.0 531.6 jit_solution(11151721562507271115)
XLA Ops:
  24.1 3.6 collective-permute-start.5
  27.8 4.6 collective-permute-done.3
  32.4 3.1 collective-permute-start.14
  35.6 9.5 %collective-permute-done.4 = bf16[40,896]{1,0:T(8,128)(2,1)S(1)} collective-permute-done((bf16[40,896]{1,0:T(8,128)(2,1)S(1)}, bf16[40,896]{1,0:T(8,128)(2,1)S(1)}, u32[]{:S(2)}, u32[]{:S(2)}) %collective-permute-start.4) | collective-permute-done | bytes 71712 | tf_op jit(solution)/shard_map/ppermute | solution.py:35
  49.1 3.6 collective-permute-done.21
  59.3 7.3 %collective-permute-done.17 = bf16[2,1,1,40,2048]{4,3,0,2,1:T(8,128)(2,1)S(1)} collective-permute-done((bf16[2,1,1,40,2048]{4,3,0,2,1:T(8,128)(2,1)S(1)}, bf16[2,1,1,40,2048]{4,3,0,2,1:T(8,128)(2,1)S(1)}, u32[]{:S(2)}, u32[]{:S(2)}) %collective-permute-start.17) | collective-permute-done | bytes 327712 | tf_op jit(solution)/shard_map/ppermute | solution.py:35
  69.2 9.3 %collective-permute-done.16 = bf16[2,1,2,40,2048]{4,3,0,2,1:T(8,128)(2,1)S(1)} collective-permute-done((bf16[2,1,2,40,2048]{4,3,0,2,1:T(8,128)(2,1)S(1)}, bf16[2,1,2,40,2048]{4,3,0,2,1:T(8,128)(2,1)S(1)}, u32[]{:S(2)}, u32[]{:S(2)}) %collective-permute-start.16) | collective-permute-done | bytes 655392 | tf_op jit(solution)/shard_map/ppermute | solution.py:35
  80.6 12.1 %collective-permute-done.18 = bf16[2,2,1,40,2048]{4,3,0,2,1:T(8,128)(2,1)S(1)} collective-permute-done((bf16[2,2,1,40,2048]{4,3,0,2,1:T(8,128)(2,1)S(1)}, bf16[2,2,1,40,2048]{4,3,0,2,1:T(8,128)(2,1)S(1)}, u32[]{:S(2)}, u32[]{:S(2)}) %collective-permute-start.18) | collective-permute-done | bytes 655392 | tf_op jit(solution)/shard_map/ppermute | solution.py:35
  94.8 9.6 %collective-permute-done.23 = bf16[2,2,96,640]{3,2,1,0:T(8,128)(2,1)S(1)} collective-permute-done((bf16[2,2,96,640]{3,2,1,0:T(8,128)(2,1)S(1)}, bf16[2,2,96,640]{3,2,1,0:T(8,128)(2,1)S(1)}, u32[]{:S(2)}, u32[]{:S(2)}) %collective-permute-start.23) | collective-permute-done | bytes 491552 | tf_op jit(solution)/shard_map/ppermute | solution.py:35
  113.6 3.7 shard_map.152
  121.6 16.4 %collective-permute-done.10 = bf16[256,512]{1,0:T(8,128)(2,1)S(1)} collective-permute-done((bf16[256,512]{1,0:T(8,128)(2,1)S(1)}, bf16[256,512]{1,0:T(8,128)(2,1)S(1)}, u32[]{:S(2)}, u32[]{:S(2)}) %collective-permute-start.10) | collective-permute-done | bytes 262176 | tf_op jit(solution)/shard_map/ppermute | solution.py:35
  138.1 5.4 %collective-permute-done.9 = bf16[256,512]{1,0:T(8,128)(2,1)S(1)} collective-permute-done((bf16[256,512]{1,0:T(8,128)(2,1)S(1)}, bf16[256,512]{1,0:T(8,128)(2,1)S(1)}, u32[]{:S(2)}, u32[]{:S(2)}) %collective-permute-start.9) | collective-permute-done | bytes 262176 | tf_op jit(solution)/shard_map/ppermute | solution.py:35
  147.6 3.5 shard_map.153.mixed
  154.1 11.0 %shard_map.154 = (f32[256,640]{1,0:T(8,128)S(1)}, f32[256,640]{1,0:T(8,128)}, bf16[256,640]{1,0:T(8,128)(2,1)S(1)}, f32[256,2048]{1,0:T(8,128)}, f32[256,2048]{1...) custom-call(s32[1]{0:T(128)} %bitcast.flag, f32[256,640]{1,0:T(8,128)} %get-tuple-element.220.x, ...), custom_call_target="tpu_custom_call" | custom-call | flops 36700160 | bytes 289952 | tf_op jit(solution)/shard_map/pallas_call | solution.py:207
  167.1 2.9 slice.176
  170.0 3.5 slice.179
  180.6 3.7 shard_map.155
  187.8 5.6 %collective-permute-done.27 = bf16[256,512]{1,0:T(8,128)(2,1)S(1)} collective-permute-done((bf16[256,512]{1,0:T(8,128)(2,1)S(1)}, bf16[256,512]{1,0:T(8,128)(2,1)S(1)}, u32[]{:S(2)}, u32[]{:S(2)}) %collective-permute-start.27) | collective-permute-done | bytes 262176 | tf_op jit(solution)/shard_map/ppermute | solution.py:35
  193.4 4.3 collective-permute-done.28
  200.4 3.5 shard_map.156.mixed
  210.4 10.6 %shard_map.157 = (f32[256,640]{1,0:T(8,128)S(1)}, f32[256,640]{1,0:T(8,128)}, bf16[256,640]{1,0:T(8,128)(2,1)S(1)}, f32[256,2048]{1,0:T(8,128)}, f32[256,2048]{1...) custom-call(s32[1]{0:T(128)} %bitcast.flag, f32[256,640]{1,0:T(8,128)} %convert_element_type.295.x, ...), custom_call_target="tpu_custom_call" | custom-call | flops 36700160 | bytes 289952 | tf_op jit(solution)/shard_map/pallas_call | solution.py:207
  221.9 10.5 %shard_map.158 = (f32[256,640]{1,0:T(8,128)S(1)}, bf16[256,640]{1,0:T(8,128)(2,1)S(1)}, bf16[256,2048]{1,0:T(8,128)(2,1)}, bf16[256,2048]{1,0:T(8,128)(2,1)}, bf...) custom-call(s32[1]{0:T(128)} %bitcast.flag, bf16[256,640]{1,0:T(8,128)(2,1)S(1)} %get-tuple-element.219.dy, ...), custom_call_target="tpu_custom_call" | custom-call | flops 31457280 | bytes 277784 | tf_op jit(solution)/shard_map/pallas_call | solution.py:207
  244.0 9.0 %shard_map.159 = (f32[256,1024]{1,0:T(8,128)}, bf16[1024,512]{1,0:T(8,128)(2,1)}) custom-call(s32[1]{0:T(128)} %bitcast.flag, bf16[256,640]{1,0:T(8,128)(2,1)S(1)} %copy-done.1, bf16[1024,640]{1,0:T(8,128)(2,1)} %bitcast.320, bf16[256,1024]{1,0:T(8,128)(2,1)S(1)} %get-tuple-element.97.q, bf16[1024,512]{1,0:T(8,128)(2,1)} %copy-done.30, ...), custom_call_target="tpu_custom_call" | custom-call | flops 47185920 | bytes 83024 | tf_op jit(solution)/shard_map/pallas_call | solution.py:207
  265.8 3.4 collective-permute-done.34
  269.2 5.4 %collective-permute-done.35 = bf16[256,512]{1,0:T(8,128)(2,1)} collective-permute-done((bf16[256,512]{1,0:T(8,128)(2,1)}, bf16[256,512]{1,0:T(8,128)(2,1)}, u32[]{:S(2)}, u32[]{:S(2)}) %collective-permute-start.35) | collective-permute-done | bytes 262176 | tf_op jit(solution)/shard_map/ppermute | solution.py:35
  276.9 5.0 shard_map.160
  286.7 10.3 %shard_map.161 = (f32[256,640]{1,0:T(8,128)S(1)}, bf16[256,640]{1,0:T(8,128)(2,1)S(1)}, bf16[256,2048]{1,0:T(8,128)(2,1)}, bf16[256,2048]{1,0:T(8,128)(2,1)}, bf...) custom-call(s32[1]{0:T(128)} %bitcast.flag, bf16[256,640]{1,0:T(8,128)(2,1)S(1)} %convert_element_type.309.dy, ...), custom_call_target="tpu_custom_call" | custom-call | flops 31457280 | bytes 277784 | tf_op jit(solution)/shard_map/pallas_call | solution.py:207
  312.5 8.8 %shard_map.162 = (f32[256,1024]{1,0:T(8,128)}, bf16[1024,512]{1,0:T(8,128)(2,1)}) custom-call(s32[1]{0:T(128)} %bitcast.flag, bf16[256,640]{1,0:T(8,128)(2,1)S(1)} %get-tuple-element.133.da, bf16[1024,640]{1,0:T(8,128)(2,1)} %bitcast.318, bf16[256,1024]{1,0:T(8,128)(2,1)S(1)} %get-tuple-element.87.q, bf16[1024,512]{1,0:T(8,128)(2,1)} %pad_maximum_fusion.20.kv, ...), custom_call_target="tpu_custom_call" | custom-call | flops 47185920 | bytes 83024 | tf_op jit(solution)/shard_map/pallas_call | solution.py:207
  321.3 9.8 %collective-permute-done.40 = bf16[4,2,1,40,896]{4,3,2,1,0:T(8,128)(2,1)} collective-permute-done((bf16[4,2,1,40,896]{4,3,2,1,0:T(8,128)(2,1)}, bf16[4,2,1,40,896]{4,3,2,1,0:T(8,128)(2,1)}, u32[]{:S(2)}, u32[]{:S(2)}) %collective-permute-start.40) | collective-permute-done | bytes 573472 | tf_op jit(solution)/shard_map/ppermute | solution.py:35
  333.2 3.4 add_convert_fusion.2
  336.6 4.2 add_convert_fusion
  341.8 2.8 collective-permute-start.41
  349.3 16.2 %collective-permute-done.41 = bf16[256,512]{1,0:T(8,128)(2,1)S(1)} collective-permute-done((bf16[256,512]{1,0:T(8,128)(2,1)}, bf16[256,512]{1,0:T(8,128)(2,1)S(1)}, u32[]{:S(2)}, u32[]{:S(2)}) %collective-permute-start.41) | collective-permute-done | bytes 262176 | tf_op jit(solution)/shard_map/ppermute | solution.py:35
  365.5 13.7 %collective-permute-done.43 = bf16[256,512]{1,0:T(8,128)(2,1)} collective-permute-done((bf16[256,512]{1,0:T(8,128)(2,1)}, bf16[256,512]{1,0:T(8,128)(2,1)}, u32[]{:S(2)}, u32[]{:S(2)}) %collective-permute-start.43) | collective-permute-done | bytes 262176 | tf_op jit(solution)/shard_map/ppermute | solution.py:35
  384.5 3.9 collective-permute-start.46
  388.4 5.1 shard_map.163
  396.1 20.1 %collective-permute-done.47 = bf16[2,1,2,40,2048]{4,3,0,2,1:T(8,128)(2,1)} collective-permute-done((bf16[2,1,2,40,2048]{4,3,0,2,1:T(8,128)(2,1)}, bf16[2,1,2,40,2048]{4,3,0,2,1:T(8,128)(2,1)}, u32[]{:S(2)}, u32[]{:S(2)}) %collective-permute-start.47) | collective-permute-done | bytes 655392 | tf_op jit(solution)/shard_map/ppermute | solution.py:35
  418.7 11.7 %collective-permute-done.46 = bf16[2,2,1,40,2048]{4,3,0,2,1:T(8,128)(2,1)} collective-permute-done((bf16[2,2,1,40,2048]{4,3,0,2,1:T(8,128)(2,1)}, bf16[2,2,1,40,2048]{4,3,0,2,1:T(8,128)(2,1)}, u32[]{:S(2)}, u32[]{:S(2)}) %collective-permute-start.46) | collective-permute-done | bytes 655392 | tf_op jit(solution)/shard_map/ppermute | solution.py:35
  433.2 3.2 collective-permute-start.64
  441.4 14.0 %collective-permute-done.64 = bf16[4,1,1,96,640]{4,3,2,1,0:T(8,128)(2,1)S(1)} collective-permute-done((bf16[4,1,1,96,640]{4,3,2,1,0:T(8,128)(2,1)S(1)}, bf16[4,1,1,96,640]{4,3,2,1,0:T(8,128)(2,1)S(1)}, u32[]{:S(2)}, u32[]{:S(2)}) %collective-permute-start.64) | collective-permute-done | bytes 491552 | tf_op jit(solution)/shard_map/ppermute | solution.py:35
  455.6 7.4 %collective-permute-start.65 = (bf16[96,640]{1,0:T(8,128)(2,1)S(1)}, bf16[96,640]{1,0:T(8,128)(2,1)S(1)}, u32[]{:S(2)}, u32[]{:S(2)}) collective-permute-start(bf16[96,640]{1,0:T(8,128)(2,1)S(1)} %get-tuple-element.238), channel_id=1, source_target_pairs={{0,4},{4,0},{8,12},{12,8},{1,5},{5,1},{9,13},{13,9},{2,6},{6,2},{1... | collective-permute-start | bytes 368648 | tf_op jit(solution)/shard_map/ppermute | solution.py:35
  464.2 9.3 %collective-permute-done.54 = bf16[2,1,1,40,2048]{4,3,0,2,1:T(8,128)(2,1)S(1)} collective-permute-done((bf16[2,1,1,40,2048]{4,3,0,2,1:T(8,128)(2,1)S(1)}, bf16[2,1,1,40,2048]{4,3,0,2,1:T(8,128)(2,1)S(1)}, u32[]{:S(2)}, u32[]{:S(2)}) %collective-permute-start.54) | collective-permute-done | bytes 327712 | tf_op jit(solution)/shard_map/ppermute | solution.py:35
  473.5 10.7 %collective-permute-start.60 = (bf16[40,896]{1,0:T(8,128)(2,1)S(1)}, bf16[40,896]{1,0:T(8,128)(2,1)S(1)}, u32[]{:S(2)}, u32[]{:S(2)}) collective-permute-start(bf16[40,896]{1,0:T(8,128)(2,1)S(1)} %get-tuple-element.256), channel_id=1, source_target_pairs={{0,8},{4,12},{8,0},{12,4},{1,9},{5,13},{9,1},{13,5},{2,10},{6,14},... | collective-permute-start | bytes 215048 | tf_op jit(solution)/shard_map/ppermute | solution.py:35
  485.4 3.7 collective-permute-done.60
  491.4 4.1 collective-permute-start.56
  495.6 3.6 collective-permute-start.57
  501.1 7.6 %collective-permute-done.56 = bf16[40,2048]{1,0:T(8,128)(2,1)S(1)} collective-permute-done((bf16[40,2048]{1,0:T(8,128)(2,1)S(1)}, bf16[40,2048]{1,0:T(8,128)(2,1)S(1)}, u32[]{:S(2)}, u32[]{:S(2)}) %collective-permute-start.56) | collective-permute-done | bytes 163872 | tf_op jit(solution)/shard_map/ppermute | solution.py:35
  512.7 2.7 collective-permute-done.51
  (426 shorter events, 169.3 us)
Async XLA Ops:
  7.2 159.9 %all-gather.3.cloned.1.call-start = ((), (), s32[]{:S(2)}) async-start(), calls=%async_computation.2 | async-start | bytes 6092800 | tf_op jit(solution)/shard_map/all_gather | solution.py:604
  16.3 499.3 %reduce-scatter.2.cloned.1.call-start = ((), (), s32[]{:S(2)}) async-start(), calls=%async_computation.1 | async-start | bytes 4874240 | tf_op jit(solution)/shard_map/reduce_scatter | solution.py:631
  19.1 28.2 %collective-permute-start.12 = (bf16[40,2048]{1,0:T(8,128)(2,1)S(1)}, bf16[40,2048]{1,0:T(8,128)(2,1)S(1)}, u32[]{:S(2)}, u32[]{:S(2)}) collective-permute-start(bf16[40,2048]{1,0:T(8,128)(2,1)S(1)} %slice.205), channel_id=1, source_target_pairs={{0,4},{4,0},{8,12},{12,8},{1,5},{5,1},{9,13},{13,9},{2,6},{6,2},{1... | collective-permute-start | bytes 491528 | tf_op jit(solution)/shard_map/ppermute | solution.py:35
  20.7 26.5 %collective-permute-start.13 = (bf16[40,2048]{1,0:T(8,128)(2,1)S(1)}, bf16[40,2048]{1,0:T(8,128)(2,1)S(1)}, u32[]{:S(2)}, u32[]{:S(2)}) collective-permute-start(bf16[40,2048]{1,0:T(8,128)(2,1)S(1)} %slice.205), channel_id=1, source_target_pairs={{0,8},{4,12},{8,0},{12,4},{1,9},{5,13},{9,1},{13,5},{2,10},{6,14},... | collective-permute-start | bytes 491528 | tf_op jit(solution)/shard_map/ppermute | solution.py:35
  23.8 21.3 %collective-permute-start.4 = (bf16[40,896]{1,0:T(8,128)(2,1)S(1)}, bf16[40,896]{1,0:T(8,128)(2,1)S(1)}, u32[]{:S(2)}, u32[]{:S(2)}) collective-permute-start(bf16[40,896]{1,0:T(8,128)(2,1)S(1)} %slice.200), channel_id=1, source_target_pairs={{0,8},{4,12},{8,0},{12,4},{1,9},{5,13},{9,1},{13,5},{2,10},{6,14},... | collective-permute-start | bytes 215048 | tf_op jit(solution)/shard_map/ppermute | solution.py:35
  24.1 22.5 %collective-permute-start.5 = (bf16[40,896]{1,0:T(8,128)(2,1)S(1)}, bf16[40,896]{1,0:T(8,128)(2,1)S(1)}, u32[]{:S(2)}, u32[]{:S(2)}) collective-permute-start(bf16[40,896]{1,0:T(8,128)(2,1)S(1)} %slice.200), channel_id=1, source_target_pairs={{0,12},{4,8},{8,4},{12,0},{1,13},{5,9},{9,5},{13,1},{2,14},{6,10},... | collective-permute-start | bytes 215048 | tf_op jit(solution)/shard_map/ppermute | solution.py:35
  32.4 14.8 %collective-permute-start.14 = (bf16[40,2048]{1,0:T(8,128)(2,1)S(1)}, bf16[40,2048]{1,0:T(8,128)(2,1)S(1)}, u32[]{:S(2)}, u32[]{:S(2)}) collective-permute-start(bf16[40,2048]{1,0:T(8,128)(2,1)S(1)} %slice.205), channel_id=1, source_target_pairs={{0,12},{4,8},{8,4},{12,0},{1,13},{5,9},{9,5},{13,1},{2,14},{6,10},... | collective-permute-start | bytes 491528 | tf_op jit(solution)/shard_map/ppermute | solution.py:35
  47.5 19.1 %collective-permute-start.17 = (bf16[2,1,1,40,2048]{4,3,0,2,1:T(8,128)(2,1)S(1)}, bf16[2,1,1,40,2048]{4,3,0,2,1:T(8,128)(2,1)S(1)}, u32[]{:S(2)}, u32[]{:S(2)}) collective-permute-start(bf16[2,1,1,40,2048]{4,3,0,2,1:T(8,128)(2,1)S(1)} %maximum_bitcast_fusion.3), channel_id=1, source_target_pairs={{0,2},{1,3},{2,0},{3,1},{4,6},{5,7},{6,4},{7,5},{8,10},{9,11},{10,... | collective-permute-start | bytes 983048 | tf_op jit(solution)/shard_map/ppermute | solution.py:35
  52.9 42.0 %collective-permute-start.22 = (bf16[2,2,96,640]{3,2,1,0:T(8,128)(2,1)S(1)}, bf16[2,2,96,640]{3,2,1,0:T(8,128)(2,1)S(1)}, u32[]{:S(2)}, u32[]{:S(2)}) collective-permute-start(bf16[2,2,96,640]{3,2,1,0:T(8,128)(2,1)S(1)} %maximum_bitcast_fusion.1), channel_id=1, source_target_pairs={{0,4},{4,0},{8,12},{12,8},{1,5},{5,1},{9,13},{13,9},{2,6},{6,2},{1... | collective-permute-start | bytes 1474568 | tf_op jit(solution)/shard_map/ppermute | solution.py:35
  55.0 49.4 %collective-permute-start.23 = (bf16[2,2,96,640]{3,2,1,0:T(8,128)(2,1)S(1)}, bf16[2,2,96,640]{3,2,1,0:T(8,128)(2,1)S(1)}, u32[]{:S(2)}, u32[]{:S(2)}) collective-permute-start(bf16[2,2,96,640]{3,2,1,0:T(8,128)(2,1)S(1)} %maximum_bitcast_fusion.1), channel_id=1, source_target_pairs={{0,8},{4,12},{8,0},{12,4},{1,9},{5,13},{9,1},{13,5},{2,10},{6,14},... | collective-permute-start | bytes 1474568 | tf_op jit(solution)/shard_map/ppermute | solution.py:35
  56.4 48.0 %collective-permute-start.24 = (bf16[2,2,96,640]{3,2,1,0:T(8,128)(2,1)S(1)}, bf16[2,2,96,640]{3,2,1,0:T(8,128)(2,1)S(1)}, u32[]{:S(2)}, u32[]{:S(2)}) collective-permute-start(bf16[2,2,96,640]{3,2,1,0:T(8,128)(2,1)S(1)} %maximum_bitcast_fusion.1), channel_id=1, source_target_pairs={{0,12},{4,8},{8,4},{12,0},{1,13},{5,9},{9,5},{13,1},{2,14},{6,10},... | collective-permute-start | bytes 1474568 | tf_op jit(solution)/shard_map/ppermute | solution.py:35
  58.6 47.7 %collective-permute-start.7 = (bf16[4,2,1,40,896]{4,3,0,2,1:T(8,128)(2,1)S(1)}, bf16[4,2,1,40,896]{4,3,0,2,1:T(8,128)(2,1)S(1)}, u32[]{:S(2)}, u32[]{:S(2)}) collective-permute-start(bf16[4,2,1,40,896]{4,3,0,2,1:T(8,128)(2,1)S(1)} %pad_maximum_fusion.23), channel_id=1, source_target_pairs={{0,1},{1,0},{2,3},{3,2},{4,5},{5,4},{6,7},{7,6},{8,9},{9,8},{10,11... | collective-permute-start | bytes 1720328 | tf_op jit(solution)/shard_map/ppermute | solution.py:35
  78.5 14.2 %collective-permute-start.18 = (bf16[2,2,1,40,2048]{4,3,0,2,1:T(8,128)(2,1)S(1)}, bf16[2,2,1,40,2048]{4,3,0,2,1:T(8,128)(2,1)S(1)}, u32[]{:S(2)}, u32[]{:S(2)}) collective-permute-start(bf16[2,2,1,40,2048]{4,3,0,2,1:T(8,128)(2,1)S(1)} %pad_maximum_fusion.22), channel_id=1, source_target_pairs={{0,1},{1,0},{2,3},{3,2},{4,5},{5,4},{6,7},{7,6},{8,9},{9,8},{10,11... | collective-permute-start | bytes 1966088 | tf_op jit(solution)/shard_map/ppermute | solution.py:35
  94.8 49.7 %collective-permute-start.19 = (bf16[16,40,2048]{2,1,0:T(8,128)(2,1)}, bf16[16,40,2048]{2,1,0:T(8,128)(2,1)}, u32[]{:S(2)}, u32[]{:S(2)}) collective-permute-start(bf16[16,40,2048]{2,1,0:T(8,128)(2,1)} %pad_maximum_fusion.1), channel_id=1, source_target_pairs={{0,16},{16,0},{1,17},{17,1},{2,18},{18,2},{3,19},{19,3},{4,20},{20... | collective-permute-start | bytes 7864328 | tf_op jit(solution)/shard_map/ppermute | solution.py:35
  106.3 38.2 %collective-permute-start.25 = (bf16[16,96,640]{2,1,0:T(8,128)(2,1)}, bf16[16,96,640]{2,1,0:T(8,128)(2,1)}, u32[]{:S(2)}, u32[]{:S(2)}) collective-permute-start(bf16[16,96,640]{2,1,0:T(8,128)(2,1)} %bitcast.47), channel_id=1, source_target_pairs={{0,16},{16,0},{1,17},{17,1},{2,18},{18,2},{3,19},{19,3},{4,20},{20... | collective-permute-start | bytes 5898248 | tf_op jit(solution)/shard_map/ppermute | solution.py:35
  118.0 20.1 %collective-permute-start.10 = (bf16[256,512]{1,0:T(8,128)(2,1)S(1)}, bf16[256,512]{1,0:T(8,128)(2,1)S(1)}, u32[]{:S(2)}, u32[]{:S(2)}) collective-permute-start(bf16[256,512]{1,0:T(8,128)(2,1)S(1)} %get-tuple-element.88), channel_id=1, source_target_pairs={{0,2},{1,3},{2,0},{3,1},{4,6},{5,7},{6,4},{7,5},{8,10},{9,11},{10,... | collective-permute-start | bytes 786440 | tf_op jit(solution)/shard_map/ppermute | solution.py:35
  119.4 18.7 %collective-permute-start.11 = (bf16[256,512]{1,0:T(8,128)(2,1)S(1)}, bf16[256,512]{1,0:T(8,128)(2,1)S(1)}, u32[]{:S(2)}, u32[]{:S(2)}) collective-permute-start(bf16[256,512]{1,0:T(8,128)(2,1)S(1)} %get-tuple-element.88), channel_id=1, source_target_pairs={{0,3},{1,2},{2,1},{3,0},{4,7},{5,6},{6,5},{7,4},{8,11},{9,10},{10,... | collective-permute-start | bytes 786440 | tf_op jit(solution)/shard_map/ppermute | solution.py:35
  120.9 22.6 %collective-permute-start.9 = (bf16[256,512]{1,0:T(8,128)(2,1)S(1)}, bf16[256,512]{1,0:T(8,128)(2,1)S(1)}, u32[]{:S(2)}, u32[]{:S(2)}) collective-permute-start(bf16[256,512]{1,0:T(8,128)(2,1)S(1)} %get-tuple-element.88), channel_id=1, source_target_pairs={{0,1},{1,0},{2,3},{3,2},{4,5},{5,4},{6,7},{7,6},{8,9},{9,8},{10,11... | collective-permute-start | bytes 786440 | tf_op jit(solution)/shard_map/ppermute | solution.py:35
  170.0 33.9 %collective-permute-start.30 = (bf16[16,40,1536]{2,1,0:T(8,128)(2,1)}, bf16[16,40,1536]{2,1,0:T(8,128)(2,1)}, u32[]{:S(2)}, u32[]{:S(2)}) collective-permute-start(bf16[16,40,1536]{2,1,0:T(8,128)(2,1)} %slice.176), channel_id=1, source_target_pairs={{0,16},{16,0},{1,17},{17,1},{2,18},{18,2},{3,19},{19,3},{4,20},{20... | collective-permute-start | bytes 5898248 | tf_op jit(solution)/shard_map/ppermute | solution.py:35
  173.6 36.9 %collective-permute-start.31 = (bf16[16,40,2048]{2,1,0:T(8,128)(2,1)}, bf16[16,40,2048]{2,1,0:T(8,128)(2,1)}, u32[]{:S(2)}, u32[]{:S(2)}) collective-permute-start(bf16[16,40,2048]{2,1,0:T(8,128)(2,1)} %slice.179), channel_id=1, source_target_pairs={{0,16},{16,0},{1,17},{17,1},{2,18},{18,2},{3,19},{19,3},{4,20},{20... | collective-permute-start | bytes 7864328 | tf_op jit(solution)/shard_map/ppermute | solution.py:35
  184.7 13.0 %collective-permute-start.28 = (bf16[256,512]{1,0:T(8,128)(2,1)S(1)}, bf16[256,512]{1,0:T(8,128)(2,1)S(1)}, u32[]{:S(2)}, u32[]{:S(2)}) collective-permute-start(bf16[256,512]{1,0:T(8,128)(2,1)S(1)} %get-tuple-element.98), channel_id=1, source_target_pairs={{0,2},{1,3},{2,0},{3,1},{4,6},{5,7},{6,4},{7,5},{8,10},{9,11},{10,... | collective-permute-start | bytes 786440 | tf_op jit(solution)/shard_map/ppermute | solution.py:35
  186.3 13.0 %collective-permute-start.29 = (bf16[256,512]{1,0:T(8,128)(2,1)S(1)}, bf16[256,512]{1,0:T(8,128)(2,1)S(1)}, u32[]{:S(2)}, u32[]{:S(2)}) collective-permute-start(bf16[256,512]{1,0:T(8,128)(2,1)S(1)} %get-tuple-element.98), channel_id=1, source_target_pairs={{0,3},{1,2},{2,1},{3,0},{4,7},{5,6},{6,5},{7,4},{8,11},{9,10},{10,... | collective-permute-start | bytes 786440 | tf_op jit(solution)/shard_map/ppermute | solution.py:35
  236.3 18.8 %collective-permute-start.32 = (bf16[640,2048]{1,0:T(8,128)(2,1)}, bf16[640,2048]{1,0:T(8,128)(2,1)}, u32[]{:S(2)}, u32[]{:S(2)}) collective-permute-start(bf16[640,2048]{1,0:T(8,128)(2,1)} %convolution_convert_fusion.3), channel_id=1, source_target_pairs={{0,16},{16,0},{1,17},{17,1},{2,18},{18,2},{3,19},{19,3},{4,20},{20... | collective-permute-start | bytes 7864328 | tf_op jit(solution)/shard_map/ppermute | solution.py:35
  240.2 12.7 %collective-permute-start.33 = (bf16[16,96,640]{2,1,0:T(8,128)(2,1)}, bf16[16,96,640]{2,1,0:T(8,128)(2,1)}, u32[]{:S(2)}, u32[]{:S(2)}) collective-permute-start(bf16[16,96,640]{2,1,0:T(8,128)(2,1)} %pad_maximum_fusion.5), channel_id=1, source_target_pairs={{0,16},{16,0},{1,17},{17,1},{2,18},{18,2},{3,19},{19,3},{4,20},{20... | collective-permute-start | bytes 5898248 | tf_op jit(solution)/shard_map/ppermute | solution.py:35
  260.8 13.9 %collective-permute-start.35 = (bf16[256,512]{1,0:T(8,128)(2,1)}, bf16[256,512]{1,0:T(8,128)(2,1)}, u32[]{:S(2)}, u32[]{:S(2)}) collective-permute-start(bf16[256,512]{1,0:T(8,128)(2,1)} %get-tuple-element.218), channel_id=1, source_target_pairs={{0,2},{1,3},{2,0},{3,1},{4,6},{5,7},{6,4},{7,5},{8,10},{9,11},{10,... | collective-permute-start | bytes 786440 | tf_op jit(solution)/shard_map/ppermute | solution.py:35
  286.6 20.3 %collective-permute-start.37 = (bf16[640,896]{1,0:T(8,128)(2,1)}, bf16[640,896]{1,0:T(8,128)(2,1)}, u32[]{:S(2)}, u32[]{:S(2)}) collective-permute-start(bf16[640,896]{1,0:T(8,128)(2,1)} %fusion.3), channel_id=1, source_target_pairs={{0,16},{16,0},{1,17},{17,1},{2,18},{18,2},{3,19},{19,3},{4,20},{20... | collective-permute-start | bytes 3440648 | tf_op jit(solution)/shard_map/ppermute | solution.py:35
  300.8 35.8 %collective-permute-start.38 = (bf16[640,2048]{1,0:T(8,128)(2,1)}, bf16[640,2048]{1,0:T(8,128)(2,1)}, u32[]{:S(2)}, u32[]{:S(2)}) collective-permute-start(bf16[640,2048]{1,0:T(8,128)(2,1)} %convolution_convert_fusion.1), channel_id=1, source_target_pairs={{0,16},{16,0},{1,17},{17,1},{2,18},{18,2},{3,19},{19,3},{4,20},{20... | collective-permute-start | bytes 7864328 | tf_op jit(solution)/shard_map/ppermute | solution.py:35
  306.5 26.7 %collective-permute-start.39 = (bf16[16,96,640]{2,1,0:T(8,128)(2,1)}, bf16[16,96,640]{2,1,0:T(8,128)(2,1)}, u32[]{:S(2)}, u32[]{:S(2)}) collective-permute-start(bf16[16,96,640]{2,1,0:T(8,128)(2,1)} %pad_maximum_fusion.6), channel_id=1, source_target_pairs={{0,16},{16,0},{1,17},{17,1},{2,18},{18,2},{3,19},{19,3},{4,20},{20... | collective-permute-start | bytes 5898248 | tf_op jit(solution)/shard_map/ppermute | solution.py:35
  310.6 20.5 %collective-permute-start.40 = (bf16[4,2,1,40,896]{4,3,2,1,0:T(8,128)(2,1)}, bf16[4,2,1,40,896]{4,3,2,1,0:T(8,128)(2,1)}, u32[]{:S(2)}, u32[]{:S(2)}) collective-permute-start(bf16[4,2,1,40,896]{4,3,2,1,0:T(8,128)(2,1)} %constant_dynamic-slice_fusion.11), channel_id=1, source_target_pairs={{0,1},{1,0},{2,3},{3,2},{4,5},{5,4},{6,7},{7,6},{8,9},{9,8},{10,11... | collective-permute-start | bytes 1720328 | tf_op jit(solution)/shard_map/ppermute | solution.py:35
  341.8 23.7 %collective-permute-start.41 = (bf16[256,512]{1,0:T(8,128)(2,1)}, bf16[256,512]{1,0:T(8,128)(2,1)S(1)}, u32[]{:S(2)}, u32[]{:S(2)}) collective-permute-start(bf16[256,512]{1,0:T(8,128)(2,1)} %get-tuple-element.213), channel_id=1, source_target_pairs={{0,1},{1,0},{2,3},{3,2},{4,5},{5,4},{6,7},{7,6},{8,9},{9,8},{10,11... | collective-permute-start | bytes 786440 | tf_op jit(solution)/shard_map/ppermute | solution.py:35
  344.6 20.9 %collective-permute-start.42 = (bf16[256,512]{1,0:T(8,128)(2,1)}, bf16[256,512]{1,0:T(8,128)(2,1)}, u32[]{:S(2)}, u32[]{:S(2)}) collective-permute-start(bf16[256,512]{1,0:T(8,128)(2,1)} %get-tuple-element.215), channel_id=1, source_target_pairs={{0,2},{1,3},{2,0},{3,1},{4,6},{5,7},{6,4},{7,5},{8,10},{9,11},{10,... | collective-permute-start | bytes 786440 | tf_op jit(solution)/shard_map/ppermute | solution.py:35
  344.6 34.6 %collective-permute-start.43 = (bf16[256,512]{1,0:T(8,128)(2,1)}, bf16[256,512]{1,0:T(8,128)(2,1)}, u32[]{:S(2)}, u32[]{:S(2)}) collective-permute-start(bf16[256,512]{1,0:T(8,128)(2,1)} %get-tuple-element.214), channel_id=1, source_target_pairs={{0,3},{1,2},{2,1},{3,0},{4,7},{5,6},{6,5},{7,4},{8,11},{9,10},{10,... | collective-permute-start | bytes 786440 | tf_op jit(solution)/shard_map/ppermute | solution.py:35
  348.3 83.4 %collective-permute-start.63 = (bf16[4,1,2,96,640]{4,3,2,1,0:T(8,128)(2,1)}, bf16[4,1,2,96,640]{4,3,2,1,0:T(8,128)(2,1)}, u32[]{:S(2)}, u32[]{:S(2)}) collective-permute-start(bf16[4,1,2,96,640]{4,3,2,1,0:T(8,128)(2,1)} %constant_dynamic-slice_fusion.1), channel_id=1, source_target_pairs={{0,2},{1,3},{2,0},{3,1},{4,6},{5,7},{6,4},{7,5},{8,10},{9,11},{10,... | collective-permute-start | bytes 2949128 | tf_op jit(solution)/shard_map/ppermute | solution.py:35
  382.6 33.6 %collective-permute-start.47 = (bf16[2,1,2,40,2048]{4,3,0,2,1:T(8,128)(2,1)}, bf16[2,1,2,40,2048]{4,3,0,2,1:T(8,128)(2,1)}, u32[]{:S(2)}, u32[]{:S(2)}) collective-permute-start(bf16[2,1,2,40,2048]{4,3,0,2,1:T(8,128)(2,1)} %copy.105), channel_id=1, source_target_pairs={{0,2},{1,3},{2,0},{3,1},{4,6},{5,7},{6,4},{7,5},{8,10},{9,11},{10,... | collective-permute-start | bytes 1966088 | tf_op jit(solution)/shard_map/ppermute | solution.py:35
  384.5 45.9 %collective-permute-start.46 = (bf16[2,2,1,40,2048]{4,3,0,2,1:T(8,128)(2,1)}, bf16[2,2,1,40,2048]{4,3,0,2,1:T(8,128)(2,1)}, u32[]{:S(2)}, u32[]{:S(2)}) collective-permute-start(bf16[2,2,1,40,2048]{4,3,0,2,1:T(8,128)(2,1)} %copy.103), channel_id=1, source_target_pairs={{0,1},{1,0},{2,3},{3,2},{4,5},{5,4},{6,7},{7,6},{8,9},{9,8},{10,11... | collective-permute-start | bytes 1966088 | tf_op jit(solution)/shard_map/ppermute | solution.py:35
  394.0 23.5 %collective-permute-start.44 = (f32[256,640]{1,0:T(8,128)S(1)}, f32[256,640]{1,0:T(8,128)S(1)}, u32[]{:S(2)}, u32[]{:S(2)}) collective-permute-start(f32[256,640]{1,0:T(8,128)S(1)} %broadcast_select_fusion.12), channel_id=1, source_target_pairs={{0,16},{16,0},{1,17},{17,1},{2,18},{18,2},{3,19},{19,3},{4,20},{20... | collective-permute-start | bytes 1966088 | tf_op jit(solution)/shard_map/ppermute | solution.py:35
  395.5 40.9 %collective-permute-start.45 = (bf16[640,896]{1,0:T(8,128)(2,1)S(1)}, bf16[640,896]{1,0:T(8,128)(2,1)S(1)}, u32[]{:S(2)}, u32[]{:S(2)}) collective-permute-start(bf16[640,896]{1,0:T(8,128)(2,1)S(1)} %fusion.1), channel_id=1, source_target_pairs={{0,16},{16,0},{1,17},{17,1},{2,18},{18,2},{3,19},{19,3},{4,20},{20... | collective-permute-start | bytes 3440648 | tf_op jit(solution)/shard_map/ppermute | solution.py:35
  433.2 22.2 %collective-permute-start.64 = (bf16[4,1,1,96,640]{4,3,2,1,0:T(8,128)(2,1)S(1)}, bf16[4,1,1,96,640]{4,3,2,1,0:T(8,128)(2,1)S(1)}, u32[]{:S(2)}, u32[]{:S(2)}) collective-permute-start(bf16[4,1,1,96,640]{4,3,2,1,0:T(8,128)(2,1)S(1)} %constant_dynamic-slice_fusion), channel_id=1, source_target_pairs={{0,1},{1,0},{2,3},{3,2},{4,5},{5,4},{6,7},{7,6},{8,9},{9,8},{10,11... | collective-permute-start | bytes 1474568 | tf_op jit(solution)/shard_map/ppermute | solution.py:35
  437.0 47.5 %collective-permute-start.48 = (bf16[4,2,1,40,896]{4,3,2,1,0:T(8,128)(2,1)S(1)}, bf16[4,2,1,40,896]{4,3,2,1,0:T(8,128)(2,1)S(1)}, u32[]{:S(2)}, u32[]{:S(2)}) collective-permute-start(bf16[4,2,1,40,896]{4,3,2,1,0:T(8,128)(2,1)S(1)} %constant_dynamic-slice_fusion.6), channel_id=1, source_target_pairs={{0,1},{1,0},{2,3},{3,2},{4,5},{5,4},{6,7},{7,6},{8,9},{9,8},{10,11... | collective-permute-start | bytes 1720328 | tf_op jit(solution)/shard_map/ppermute | solution.py:35
  437.1 36.4 %collective-permute-start.54 = (bf16[2,1,1,40,2048]{4,3,0,2,1:T(8,128)(2,1)S(1)}, bf16[2,1,1,40,2048]{4,3,0,2,1:T(8,128)(2,1)S(1)}, u32[]{:S(2)}, u32[]{:S(2)}) collective-permute-start(bf16[2,1,1,40,2048]{4,3,0,2,1:T(8,128)(2,1)S(1)} %constant_dynamic-slice_fusion.3), channel_id=1, source_target_pairs={{0,1},{1,0},{2,3},{3,2},{4,5},{5,4},{6,7},{7,6},{8,9},{9,8},{10,11... | collective-permute-start | bytes 983048 | tf_op jit(solution)/shard_map/ppermute | solution.py:35
  439.2 45.1 %collective-permute-start.53 = (bf16[2,1,1,40,2048]{4,3,0,2,1:T(8,128)(2,1)S(1)}, bf16[2,1,1,40,2048]{4,3,0,2,1:T(8,128)(2,1)S(1)}, u32[]{:S(2)}, u32[]{:S(2)}) collective-permute-start(bf16[2,1,1,40,2048]{4,3,0,2,1:T(8,128)(2,1)S(1)} %constant_dynamic-slice_fusion.4), channel_id=1, source_target_pairs={{0,2},{1,3},{2,0},{3,1},{4,6},{5,7},{6,4},{7,5},{8,10},{9,11},{10,... | collective-permute-start | bytes 983048 | tf_op jit(solution)/shard_map/ppermute | solution.py:35
  439.3 23.7 %collective-permute-start.58 = (bf16[4,1,1,40,896]{4,3,2,1,0:T(8,128)(2,1)S(1)}, bf16[4,1,1,40,896]{4,3,2,1,0:T(8,128)(2,1)S(1)}, u32[]{:S(2)}, u32[]{:S(2)}) collective-permute-start(bf16[4,1,1,40,896]{4,3,2,1,0:T(8,128)(2,1)S(1)} %constant_dynamic-slice_fusion.2), channel_id=1, source_target_pairs={{0,2},{1,3},{2,0},{3,1},{4,6},{5,7},{6,4},{7,5},{8,10},{9,11},{10,... | collective-permute-start | bytes 860168 | tf_op jit(solution)/shard_map/ppermute | solution.py:35
  455.6 61.0 %collective-permute-start.65 = (bf16[96,640]{1,0:T(8,128)(2,1)S(1)}, bf16[96,640]{1,0:T(8,128)(2,1)S(1)}, u32[]{:S(2)}, u32[]{:S(2)}) collective-permute-start(bf16[96,640]{1,0:T(8,128)(2,1)S(1)} %get-tuple-element.238), channel_id=1, source_target_pairs={{0,4},{4,0},{8,12},{12,8},{1,5},{5,1},{9,13},{13,9},{2,6},{6,2},{1... | collective-permute-start | bytes 368648 | tf_op jit(solution)/shard_map/ppermute | solution.py:35
  463.1 22.2 %collective-permute-start.59 = (bf16[40,896]{1,0:T(8,128)(2,1)S(1)}, bf16[40,896]{1,0:T(8,128)(2,1)S(1)}, u32[]{:S(2)}, u32[]{:S(2)}) collective-permute-start(bf16[40,896]{1,0:T(8,128)(2,1)S(1)} %get-tuple-element.254), channel_id=1, source_target_pairs={{0,4},{4,0},{8,12},{12,8},{1,5},{5,1},{9,13},{13,9},{2,6},{6,2},{1... | collective-permute-start | bytes 215048 | tf_op jit(solution)/shard_map/ppermute | solution.py:35
  473.5 15.6 %collective-permute-start.60 = (bf16[40,896]{1,0:T(8,128)(2,1)S(1)}, bf16[40,896]{1,0:T(8,128)(2,1)S(1)}, u32[]{:S(2)}, u32[]{:S(2)}) collective-permute-start(bf16[40,896]{1,0:T(8,128)(2,1)S(1)} %get-tuple-element.256), channel_id=1, source_target_pairs={{0,8},{4,12},{8,0},{12,4},{1,9},{5,13},{9,1},{13,5},{2,10},{6,14},... | collective-permute-start | bytes 215048 | tf_op jit(solution)/shard_map/ppermute | solution.py:35
  485.3 31.3 %collective-permute-start.66 = (bf16[96,640]{1,0:T(8,128)(2,1)S(1)}, bf16[96,640]{1,0:T(8,128)(2,1)S(1)}, u32[]{:S(2)}, u32[]{:S(2)}) collective-permute-start(bf16[96,640]{1,0:T(8,128)(2,1)S(1)} %get-tuple-element.240), channel_id=1, source_target_pairs={{0,8},{4,12},{8,0},{12,4},{1,9},{5,13},{9,1},{13,5},{2,10},{6,14},... | collective-permute-start | bytes 368648 | tf_op jit(solution)/shard_map/ppermute | solution.py:35
  491.4 17.2 %collective-permute-start.56 = (bf16[40,2048]{1,0:T(8,128)(2,1)S(1)}, bf16[40,2048]{1,0:T(8,128)(2,1)S(1)}, u32[]{:S(2)}, u32[]{:S(2)}) collective-permute-start(bf16[40,2048]{1,0:T(8,128)(2,1)S(1)} %get-tuple-element.230), channel_id=1, source_target_pairs={{0,8},{4,12},{8,0},{12,4},{1,9},{5,13},{9,1},{13,5},{2,10},{6,14},... | collective-permute-start | bytes 491528 | tf_op jit(solution)/shard_map/ppermute | solution.py:35
  495.6 13.1 %collective-permute-start.57 = (bf16[40,2048]{1,0:T(8,128)(2,1)S(1)}, bf16[40,2048]{1,0:T(8,128)(2,1)S(1)}, u32[]{:S(2)}, u32[]{:S(2)}) collective-permute-start(bf16[40,2048]{1,0:T(8,128)(2,1)S(1)} %get-tuple-element.231), channel_id=1, source_target_pairs={{0,12},{4,8},{8,4},{12,0},{1,13},{5,9},{9,5},{13,1},{2,14},{6,10},... | collective-permute-start | bytes 491528 | tf_op jit(solution)/shard_map/ppermute | solution.py:35
  (82 other events, 790.4 us)
Sparse Core Ops, SparseCore 0:
  16.4 137.9 all-gather.2
  311.9 140.4 reduce-scatter.1

commit v8 on v7

--- a/solution.py
+++ b/solution.py
@@ -158,9 +158,32 @@
             done.append(ctx_scatter(v, steps[:1] if stage == 0 else steps[1:]))
         self.put(done)
 
+    def ready_for_z(self):
+        return jnp.concatenate([v.reshape((-1,) + self.tail) for v in self.values()], axis=0)
+
     def along_z(self):
         buf = jnp.concatenate([v.reshape((-1,) + self.tail) for v in self.values()], axis=0)
         return z_scatter(buf)
+
+
+def rows_ring(blocks):
+    count = lax.axis_size("fsdp")
+    pairs = [(i, (i + 1) % count) for i in range(count)]
+    me = lax.axis_index("fsdp")
+    buf = blocks.reshape((count,) + (2,) * bits_of("ctx") + blocks.shape[1:])
+
+    def block(back):
+        return lax.dynamic_index_in_dim(buf, (me - back) % count, 0, False)
+
+    total = block(1)
+    for step in range(count - 1):
+        recv = lax.ppermute(total, "fsdp", pairs)
+        total = (recv.astype(F32) + block(step + 2).astype(F32)).astype(BF)
+    return total
+
+
+def rows_plane(buf):
+    return ctx_scatter(buf[None], ctx_steps("yx")).reshape(buf.shape[-2:]).astype(F32)
 
 
 def rope_tables(places, log_base):
@@ -626,10 +649,10 @@
     grad_q1, kv_blocks = backward_attend(feed1[2], kept1, branch1, pos, windows[1], flag)
     grad_q1, kv_blocks, sum_g1, sum_b1 = tie(grad_q1, kv_blocks, sum_g1, sum_b1)
     grad_kv = key_return(kv_blocks)
-    sums1 = jnp.concatenate([sum_g1, pack_rows(sum_b1, nr)], axis=-1)
-    grad_kv, sums1 = tie(grad_kv, sums1)
-    sums1 = lax.psum_scatter(sums1, GRID, scatter_dimension=0).astype(F32)
-    red_g1, red_b1 = sums1[:, :FF], unpack_rows(sums1[:, FF:], (ro + rd) // 2)
+    rows1 = rows_ring(sum_b1)
+    grad_kv, sum_g1 = tie(grad_kv, sum_g1)
+    scat_g1 = Scatter(sum_g1, "both")
+    scat_g1.plane(0)
     grad1, wg_q, gain_zero, head_grads = backward_keys(
         query1, kept1, middle1, grad_q1, grad_kv, *tables[1], flag
     )
@@ -639,41 +662,44 @@
     middle0, branch0, wg_g, wg_out, wg_down, norm_grads = backward_feed(
         feed0, kept0, grad1, flag
     )
-    branch0, sum_q1 = tie(branch0, sum_q1)
+    branch0, sum_q1, *held = tie(branch0, sum_q1, *scat_g1.values())
+    scat_g1.put(held)
     scat_q1 = Scatter(sum_q1, "xy")
+    scat_g1.plane(1)
     scat_q1.plane(0)
     sum_g0 = reduce_cols(*wg_g)
     sum_b0 = reduce_rows(wg_out, wg_down)
     grad_q0, kv_blocks = backward_attend(feed0[2], kept0, branch0, pos, windows[0], flag)
-    grad_q0, kv_blocks, sum_g0, sum_b0, held0 = tie(
-        grad_q0, kv_blocks, sum_g0, sum_b0, *scat_q1.values()
-    )
-    scat_q1.put([held0])
+    grad_q0, kv_blocks, sum_g0, sum_b0, rows1, held0, *held = tie(
+        grad_q0, kv_blocks, sum_g0, sum_b0, rows1, *scat_q1.values(), *scat_g1.values()
+    )
     grad_kv = key_return(kv_blocks)
-    scat_b0 = Scatter(sum_b0, "yx")
-    scat_b0.plane(0)
-    grad_kv, sum_g0, held0 = tie(grad_kv, sum_g0, *scat_q1.values())
-    scat_q1.put([held0])
+    rows0 = rows_ring(sum_b0)
+    grad_kv, sum_g0, rows1, held0, *held = tie(grad_kv, sum_g0, rows1, held0, *held)
     scat_g0 = Scatter(sum_g0, "both")
     scat_g0.plane(0)
     grad0, wg_q, gain_zero, head_grads = backward_keys(
         query0, kept0, middle0, grad_q0, grad_kv, *tables[0], flag
     )
     sum_q0 = reduce_query(wg_q, [gain_zero, norm_grads], head_grads)
-    sum_q0, held1, *held = tie(sum_q0, *scat_q1.values(), *scat_g0.values())
-    scat_q1.put([held1])
-    scat_g0.put(held)
+    sum_q0, rows1, held0, first_part, second_part, *held = tie(
+        sum_q0, rows1, held0, *scat_g0.values(), *held
+    )
+    scat_g0.put([first_part, second_part])
+    scat_q1.put([held0])
+    scat_g1.put(held)
     scat_q0 = Scatter(sum_q0, "xy")
     scat_q0.plane(0)
     scat_g0.plane(1)
+    scat_q1.plane(1)
+    red_b1 = rows_plane(rows1)
     scat_q0.plane(1)
-    scat_q1.plane(1)
-    red_q1 = scat_q1.along_z()
+    red_c1 = z_scatter(
+        jnp.concatenate([scat_q1.ready_for_z(), scat_g1.ready_for_z()], axis=-1)
+    )
     red_q0, red_g0 = scat_q0.along_z(), scat_g0.along_z()
-    scat_b0.plane(1)
-    red_b0 = scat_b0.along_z()
+    red_b0 = rows_plane(rows0)
     red_c0 = jnp.concatenate([red_q0, red_g0], axis=1)
-    red_c1 = jnp.concatenate([red_q1, red_g1], axis=1)
 
     out_moved = exchange(jnp.where(first, y1, grad0), "section", 1)
     c_keep, c_send = pick(first, red_c0, red_c1)

time: 542 us -> 516 us (0.952)
  waiting for transfers between devices: 218 us -> 176 us
  starting transfers between devices: 93.3 us -> 102 us
    ppermute x69 -> x72, waiting for transfers between devices: 218 us -> 150 us  [exchange(): return lax.ppermute(shard, axis, pairs)]
    ppermute x0 -> x6, waiting for transfers between devices: none -> 26.7 us  [rows_ring(): recv = lax.ppermute(total, 'fsdp', pairs)]
    ppermute x0 -> x6, starting transfers between devices: none -> 21.3 us  [rows_ring(): recv = lax.ppermute(total, 'fsdp', pairs)]
    ppermute x69 -> x72, starting transfers between devices: 93.2 us -> 80.3 us  [exchange(): return lax.ppermute(shard, axis, pairs)]
    unnamed x130 -> x131, local copies, waits for them, and re-layouts: 15.4 us -> 13.7 us
  transfers between devices with their start and end apart: 71 -> 79, of which waited for: 32 -> 28; matrix products, arithmetic and copies ran while one was open for 16% -> 19% of each run, Pallas kernels for 11% -> 13%
where the time goes in v8:
time: 516 us; the launch traced here: 506 us
  waiting for transfers between devices  176 us (34%)
  starting transfers between devices  102 us (20%)
  Pallas kernels  84.5 us (16%)
  other arithmetic  59.8 us (12%)
  local copies, waits for them, and re-layouts  49.4 us (10%)
  matrix products  18.7 us (4%)
  between operations  15.6 us (3%)
    ppermute x72, waiting for transfers between devices, exchange(): return lax.ppermute(shard, axis, pairs)  150 us
    pallas_call x12, Pallas kernels, whole_call(): pl.pallas_call(body, out_shape=[jax.ShapeDtypeStruct(s, t) for s, t in ou...  84.5 us
    ppermute x72, starting transfers between devices, exchange(): return lax.ppermute(shard, axis, pairs)  80.3 us
    ppermute x6, waiting for transfers between devices, rows_ring(): recv = lax.ppermute(total, 'fsdp', pairs)  26.7 us
    ppermute x6, starting transfers between devices, rows_ring(): recv = lax.ppermute(total, 'fsdp', pairs)  21.3 us
    dot_general x12, matrix products, t_dot(): return jnp.einsum('ta,tb->ab', a, b, preferred_element_type=F32)  18.7 us
    unnamed x131, local copies, waits for them, and re-layouts  13.7 us
  transfers between devices with their start and end apart: 79, of which 28 were waited for; matrix products, arithmetic and copies ran while one was open for 19% of the time, Pallas kernels for 13%

profile of v8, /device:TPU:0, one launch (start us, length us, event | category | flops | bytes accessed | tf_op | source)
XLA Modules:
  0.0 506.0 jit_solution(16806808476162316353)
XLA Ops:
  16.3 2.7 collective-permute-start.20
  20.6 2.6 collective-permute-start.13
  24.0 3.6 collective-permute-start.5
  27.7 4.6 collective-permute-done.3
  32.3 3.1 collective-permute-start.14
  35.4 9.5 %collective-permute-done.4 = bf16[40,896]{1,0:T(8,128)(2,1)S(1)} collective-permute-done((bf16[40,896]{1,0:T(8,128)(2,1)S(1)}, bf16[40,896]{1,0:T(8,128)(2,1)S(1)}, u32[]{:S(2)}, u32[]{:S(2)}) %collective-permute-start.4) | collective-permute-done | bytes 71712 | tf_op jit(solution)/shard_map/ppermute | solution.py:35
  49.0 3.6 collective-permute-done.21
  59.3 7.3 %collective-permute-done.17 = bf16[2,1,1,40,2048]{4,3,0,2,1:T(8,128)(2,1)S(1)} collective-permute-done((bf16[2,1,1,40,2048]{4,3,0,2,1:T(8,128)(2,1)S(1)}, bf16[2,1,1,40,2048]{4,3,0,2,1:T(8,128)(2,1)S(1)}, u32[]{:S(2)}, u32[]{:S(2)}) %collective-permute-start.17) | collective-permute-done | bytes 327712 | tf_op jit(solution)/shard_map/ppermute | solution.py:35
  69.1 9.3 %collective-permute-done.16 = bf16[2,1,2,40,2048]{4,3,0,2,1:T(8,128)(2,1)S(1)} collective-permute-done((bf16[2,1,2,40,2048]{4,3,0,2,1:T(8,128)(2,1)S(1)}, bf16[2,1,2,40,2048]{4,3,0,2,1:T(8,128)(2,1)S(1)}, u32[]{:S(2)}, u32[]{:S(2)}) %collective-permute-start.16) | collective-permute-done | bytes 655392 | tf_op jit(solution)/shard_map/ppermute | solution.py:35
  80.5 12.2 %collective-permute-done.18 = bf16[2,2,1,40,2048]{4,3,0,2,1:T(8,128)(2,1)S(1)} collective-permute-done((bf16[2,2,1,40,2048]{4,3,0,2,1:T(8,128)(2,1)S(1)}, bf16[2,2,1,40,2048]{4,3,0,2,1:T(8,128)(2,1)S(1)}, u32[]{:S(2)}, u32[]{:S(2)}) %collective-permute-start.18) | collective-permute-done | bytes 655392 | tf_op jit(solution)/shard_map/ppermute | solution.py:35
  94.8 9.5 %collective-permute-done.23 = bf16[2,2,96,640]{3,2,1,0:T(8,128)(2,1)S(1)} collective-permute-done((bf16[2,2,96,640]{3,2,1,0:T(8,128)(2,1)S(1)}, bf16[2,2,96,640]{3,2,1,0:T(8,128)(2,1)S(1)}, u32[]{:S(2)}, u32[]{:S(2)}) %collective-permute-start.23) | collective-permute-done | bytes 491552 | tf_op jit(solution)/shard_map/ppermute | solution.py:35
  113.5 3.7 shard_map.152
  121.6 16.4 %collective-permute-done.10 = bf16[256,512]{1,0:T(8,128)(2,1)S(1)} collective-permute-done((bf16[256,512]{1,0:T(8,128)(2,1)S(1)}, bf16[256,512]{1,0:T(8,128)(2,1)S(1)}, u32[]{:S(2)}, u32[]{:S(2)}) %collective-permute-start.10) | collective-permute-done | bytes 262176 | tf_op jit(solution)/shard_map/ppermute | solution.py:35
  138.1 5.4 %collective-permute-done.9 = bf16[256,512]{1,0:T(8,128)(2,1)S(1)} collective-permute-done((bf16[256,512]{1,0:T(8,128)(2,1)S(1)}, bf16[256,512]{1,0:T(8,128)(2,1)S(1)}, u32[]{:S(2)}, u32[]{:S(2)}) %collective-permute-start.9) | collective-permute-done | bytes 262176 | tf_op jit(solution)/shard_map/ppermute | solution.py:35
  147.5 3.5 shard_map.153.mixed
  154.0 11.0 %shard_map.154 = (f32[256,640]{1,0:T(8,128)S(1)}, f32[256,640]{1,0:T(8,128)}, bf16[256,640]{1,0:T(8,128)(2,1)S(1)}, f32[256,2048]{1,0:T(8,128)}, f32[256,2048]{1...) custom-call(s32[1]{0:T(128)} %bitcast.flag, f32[256,640]{1,0:T(8,128)} %get-tuple-element.253.x, ...), custom_call_target="tpu_custom_call" | custom-call | flops 36700160 | bytes 289952 | tf_op jit(solution)/shard_map/pallas_call | solution.py:230
  167.1 3.0 slice.182
  170.0 3.6 slice.185
  180.6 3.7 shard_map.155
  187.8 5.6 %collective-permute-done.27 = bf16[256,512]{1,0:T(8,128)(2,1)S(1)} collective-permute-done((bf16[256,512]{1,0:T(8,128)(2,1)S(1)}, bf16[256,512]{1,0:T(8,128)(2,1)S(1)}, u32[]{:S(2)}, u32[]{:S(2)}) %collective-permute-start.27) | collective-permute-done | bytes 262176 | tf_op jit(solution)/shard_map/ppermute | solution.py:35
  193.5 4.3 collective-permute-done.28
  200.4 3.5 shard_map.156.mixed
  210.5 10.7 %shard_map.157 = (f32[256,640]{1,0:T(8,128)S(1)}, f32[256,640]{1,0:T(8,128)}, bf16[256,640]{1,0:T(8,128)(2,1)S(1)}, f32[256,2048]{1,0:T(8,128)}, f32[256,2048]{1...) custom-call(s32[1]{0:T(128)} %bitcast.flag, f32[256,640]{1,0:T(8,128)} %convert_element_type.430.x, ...), custom_call_target="tpu_custom_call" | custom-call | flops 36700160 | bytes 289952 | tf_op jit(solution)/shard_map/pallas_call | solution.py:230
  222.1 10.3 %shard_map.158 = (f32[256,640]{1,0:T(8,128)S(1)}, bf16[256,640]{1,0:T(8,128)(2,1)S(1)}, bf16[256,2048]{1,0:T(8,128)(2,1)}, bf16[256,2048]{1,0:T(8,128)(2,1)}, bf...) custom-call(s32[1]{0:T(128)} %bitcast.flag, bf16[256,640]{1,0:T(8,128)(2,1)S(1)} %get-tuple-element.252.dy, ...), custom_call_target="tpu_custom_call" | custom-call | flops 31457280 | bytes 277784 | tf_op jit(solution)/shard_map/pallas_call | solution.py:230
  242.7 9.0 %shard_map.159 = (f32[256,1024]{1,0:T(8,128)}, bf16[1024,512]{1,0:T(8,128)(2,1)}) custom-call(s32[1]{0:T(128)} %bitcast.flag, bf16[256,640]{1,0:T(8,128)(2,1)S(1)} %copy-done.1, bf16[1024,640]{1,0:T(8,128)(2,1)} %bitcast.335, bf16[256,1024]{1,0:T(8,128)(2,1)S(1)} %get-tuple-element.108.q, bf16[1024,512]{1,0:T(8,128)(2,1)} %copy-done.30, ...), custom_call_target="tpu_custom_call" | custom-call | flops 47185920 | bytes 83024 | tf_op jit(solution)/shard_map/pallas_call | solution.py:230
  251.6 3.5 add_convert_fusion.3
  255.1 4.2 add_convert_fusion.1
  265.6 6.8 %collective-permute-start.42 = (bf16[2,2,96,640]{3,2,1,0:T(8,128)(2,1)}, bf16[2,2,96,640]{3,2,1,0:T(8,128)(2,1)}, u32[]{:S(2)}, u32[]{:S(2)}) collective-permute-start(bf16[2,2,96,640]{3,2,1,0:T(8,128)(2,1)} %dynamic-slice_bitcast_fusion.9), channel_id=1, source_target_pairs={{0,4},{4,8},{8,12},{12,0},{1,5},{5,9},{9,13},{13,1},{2,6},{6,10},{... | collective-permute-start | bytes 1474568 | tf_op jit(solution)/shard_map/ppermute | solution.py:180
  272.4 2.5 collective-permute-done.35
  283.9 5.0 shard_map.160
  295.9 10.3 %shard_map.161 = (f32[256,640]{1,0:T(8,128)S(1)}, bf16[256,640]{1,0:T(8,128)(2,1)S(1)}, bf16[256,2048]{1,0:T(8,128)(2,1)}, bf16[256,2048]{1,0:T(8,128)(2,1)}, bf...) custom-call(s32[1]{0:T(128)} %bitcast.flag, bf16[256,640]{1,0:T(8,128)(2,1)S(1)} %convert_element_type.444.dy, ...), custom_call_target="tpu_custom_call" | custom-call | flops 31457280 | bytes 277784 | tf_op jit(solution)/shard_map/pallas_call | solution.py:230
  314.6 6.2 %collective-permute-start.43 = (bf16[2,2,96,640]{3,2,1,0:T(8,128)(2,1)S(1)}, bf16[2,2,96,640]{3,2,1,0:T(8,128)(2,1)S(1)}, u32[]{:S(2)}, u32[]{:S(2)}) collective-permute-start(bf16[2,2,96,640]{3,2,1,0:T(8,128)(2,1)S(1)} %fusion.9), channel_id=1, source_target_pairs={{0,4},{4,8},{8,12},{12,0},{1,5},{5,9},{9,13},{13,1},{2,6},{6,10},{... | collective-permute-start | bytes 1474568 | tf_op jit(solution)/shard_map/ppermute | solution.py:180
  323.6 8.0 %collective-permute-done.43 = bf16[2,2,96,640]{3,2,1,0:T(8,128)(2,1)S(1)} collective-permute-done((bf16[2,2,96,640]{3,2,1,0:T(8,128)(2,1)S(1)}, bf16[2,2,96,640]{3,2,1,0:T(8,128)(2,1)S(1)}, u32[]{:S(2)}, u32[]{:S(2)}) %collective-permute-start.43) | collective-permute-done | bytes 491552 | tf_op jit(solution)/shard_map/ppermute | solution.py:180
  332.5 3.2 collective-permute-start.44
  340.4 8.7 %shard_map.162 = (f32[256,1024]{1,0:T(8,128)}, bf16[1024,512]{1,0:T(8,128)(2,1)}) custom-call(s32[1]{0:T(128)} %bitcast.flag, bf16[256,640]{1,0:T(8,128)(2,1)S(1)} %get-tuple-element.144.da, bf16[1024,640]{1,0:T(8,128)(2,1)} %bitcast.333, bf16[256,1024]{1,0:T(8,128)(2,1)S(1)} %get-tuple-element.98.q, bf16[1024,512]{1,0:T(8,128)(2,1)} %pad_maximum_fusion.19.kv, ...), custom_call_target="tpu_custom_call" | custom-call | flops 47185920 | bytes 83024 | tf_op jit(solution)/shard_map/pallas_call | solution.py:230
  354.2 8.3 %collective-permute-done.45 = bf16[4,2,1,40,896]{4,3,0,2,1:T(8,128)(2,1)S(1)} collective-permute-done((bf16[4,2,1,40,896]{4,3,0,2,1:T(8,128)(2,1)S(1)}, bf16[4,2,1,40,896]{4,3,0,2,1:T(8,128)(2,1)S(1)}, u32[]{:S(2)}, u32[]{:S(2)}) %collective-permute-start.45) | collective-permute-done | bytes 573472 | tf_op jit(solution)/shard_map/ppermute | solution.py:35
  363.5 3.4 add_convert_fusion.2
  366.9 4.2 add_convert_fusion
  379.8 3.7 collective-permute-done.49
  391.3 5.0 shard_map.163
  406.1 9.4 %collective-permute-done.71 = bf16[2,2,96,640]{3,2,1,0:T(8,128)(2,1)S(1)} collective-permute-done((bf16[2,2,96,640]{3,2,1,0:T(8,128)(2,1)S(1)}, bf16[2,2,96,640]{3,2,1,0:T(8,128)(2,1)S(1)}, u32[]{:S(2)}, u32[]{:S(2)}) %collective-permute-start.71) | collective-permute-done | bytes 491552 | tf_op jit(solution)/shard_map/ppermute | solution.py:180
  421.2 9.2 %collective-permute-done.72 = bf16[2,2,96,640]{3,2,1,0:T(8,128)(2,1)S(1)} collective-permute-done((bf16[2,2,96,640]{3,2,1,0:T(8,128)(2,1)S(1)}, bf16[2,2,96,640]{3,2,1,0:T(8,128)(2,1)S(1)}, u32[]{:S(2)}, u32[]{:S(2)}) %collective-permute-start.72) | collective-permute-done | bytes 491552 | tf_op jit(solution)/shard_map/ppermute | solution.py:180
  434.0 10.1 %collective-permute-done.73 = bf16[1,1,2,96,640]{4,3,2,1,0:T(8,128)(2,1)S(1)} collective-permute-done((bf16[1,1,2,96,640]{4,3,2,1,0:T(8,128)(2,1)S(1)}, bf16[1,1,2,96,640]{4,3,2,1,0:T(8,128)(2,1)S(1)}, u32[]{:S(2)}, u32[]{:S(2)}) %collective-permute-start.73) | collective-permute-done | bytes 245792 | tf_op jit(solution)/shard_map/ppermute | solution.py:35
  449.1 3.0 collective-permute-done.56
  459.3 13.2 %collective-permute-done.63 = bf16[40,2048]{1,0:T(8,128)(2,1)S(1)} collective-permute-done((bf16[40,2048]{1,0:T(8,128)(2,1)S(1)}, bf16[40,2048]{1,0:T(8,128)(2,1)S(1)}, u32[]{:S(2)}, u32[]{:S(2)}) %collective-permute-start.63) | collective-permute-done | bytes 163872 | tf_op jit(solution)/shard_map/ppermute | solution.py:35
  474.5 2.6 collective-permute-start.58
  477.1 2.6 collective-permute-start.59
  479.8 12.3 %collective-permute-done.58 = bf16[40,896]{1,0:T(8,128)(2,1)S(1)} collective-permute-done((bf16[40,896]{1,0:T(8,128)(2,1)S(1)}, bf16[40,896]{1,0:T(8,128)(2,1)S(1)}, u32[]{:S(2)}, u32[]{:S(2)}) %collective-permute-start.58) | collective-permute-done | bytes 71712 | tf_op jit(solution)/shard_map/ppermute | solution.py:35
  (456 shorter events, 183.1 us)
Async XLA Ops:
  7.2 159.9 %all-gather.3.cloned.1.call-start = ((), (), s32[]{:S(2)}) async-start(), calls=%async_computation | async-start | bytes 6092800 | tf_op jit(solution)/shard_map/all_gather | solution.py:627
  19.0 28.2 %collective-permute-start.12 = (bf16[40,2048]{1,0:T(8,128)(2,1)S(1)}, bf16[40,2048]{1,0:T(8,128)(2,1)S(1)}, u32[]{:S(2)}, u32[]{:S(2)}) collective-permute-start(bf16[40,2048]{1,0:T(8,128)(2,1)S(1)} %slice.213), channel_id=1, source_target_pairs={{0,4},{4,0},{8,12},{12,8},{1,5},{5,1},{9,13},{13,9},{2,6},{6,2},{1... | collective-permute-start | bytes 491528 | tf_op jit(solution)/shard_map/ppermute | solution.py:35
  20.6 26.5 %collective-permute-start.13 = (bf16[40,2048]{1,0:T(8,128)(2,1)S(1)}, bf16[40,2048]{1,0:T(8,128)(2,1)S(1)}, u32[]{:S(2)}, u32[]{:S(2)}) collective-permute-start(bf16[40,2048]{1,0:T(8,128)(2,1)S(1)} %slice.213), channel_id=1, source_target_pairs={{0,8},{4,12},{8,0},{12,4},{1,9},{5,13},{9,1},{13,5},{2,10},{6,14},... | collective-permute-start | bytes 491528 | tf_op jit(solution)/shard_map/ppermute | solution.py:35
  23.7 21.3 %collective-permute-start.4 = (bf16[40,896]{1,0:T(8,128)(2,1)S(1)}, bf16[40,896]{1,0:T(8,128)(2,1)S(1)}, u32[]{:S(2)}, u32[]{:S(2)}) collective-permute-start(bf16[40,896]{1,0:T(8,128)(2,1)S(1)} %slice.208), channel_id=1, source_target_pairs={{0,8},{4,12},{8,0},{12,4},{1,9},{5,13},{9,1},{13,5},{2,10},{6,14},... | collective-permute-start | bytes 215048 | tf_op jit(solution)/shard_map/ppermute | solution.py:35
  24.0 22.5 %collective-permute-start.5 = (bf16[40,896]{1,0:T(8,128)(2,1)S(1)}, bf16[40,896]{1,0:T(8,128)(2,1)S(1)}, u32[]{:S(2)}, u32[]{:S(2)}) collective-permute-start(bf16[40,896]{1,0:T(8,128)(2,1)S(1)} %slice.208), channel_id=1, source_target_pairs={{0,12},{4,8},{8,4},{12,0},{1,13},{5,9},{9,5},{13,1},{2,14},{6,10},... | collective-permute-start | bytes 215048 | tf_op jit(solution)/shard_map/ppermute | solution.py:35
  32.3 14.9 %collective-permute-start.14 = (bf16[40,2048]{1,0:T(8,128)(2,1)S(1)}, bf16[40,2048]{1,0:T(8,128)(2,1)S(1)}, u32[]{:S(2)}, u32[]{:S(2)}) collective-permute-start(bf16[40,2048]{1,0:T(8,128)(2,1)S(1)} %slice.213), channel_id=1, source_target_pairs={{0,12},{4,8},{8,4},{12,0},{1,13},{5,9},{9,5},{13,1},{2,14},{6,10},... | collective-permute-start | bytes 491528 | tf_op jit(solution)/shard_map/ppermute | solution.py:35
  47.4 19.1 %collective-permute-start.17 = (bf16[2,1,1,40,2048]{4,3,0,2,1:T(8,128)(2,1)S(1)}, bf16[2,1,1,40,2048]{4,3,0,2,1:T(8,128)(2,1)S(1)}, u32[]{:S(2)}, u32[]{:S(2)}) collective-permute-start(bf16[2,1,1,40,2048]{4,3,0,2,1:T(8,128)(2,1)S(1)} %maximum_bitcast_fusion.3), channel_id=1, source_target_pairs={{0,2},{1,3},{2,0},{3,1},{4,6},{5,7},{6,4},{7,5},{8,10},{9,11},{10,... | collective-permute-start | bytes 983048 | tf_op jit(solution)/shard_map/ppermute | solution.py:35
  52.8 42.0 %collective-permute-start.22 = (bf16[2,2,96,640]{3,2,1,0:T(8,128)(2,1)S(1)}, bf16[2,2,96,640]{3,2,1,0:T(8,128)(2,1)S(1)}, u32[]{:S(2)}, u32[]{:S(2)}) collective-permute-start(bf16[2,2,96,640]{3,2,1,0:T(8,128)(2,1)S(1)} %maximum_bitcast_fusion.1), channel_id=1, source_target_pairs={{0,4},{4,0},{8,12},{12,8},{1,5},{5,1},{9,13},{13,9},{2,6},{6,2},{1... | collective-permute-start | bytes 1474568 | tf_op jit(solution)/shard_map/ppermute | solution.py:35
  54.9 49.4 %collective-permute-start.23 = (bf16[2,2,96,640]{3,2,1,0:T(8,128)(2,1)S(1)}, bf16[2,2,96,640]{3,2,1,0:T(8,128)(2,1)S(1)}, u32[]{:S(2)}, u32[]{:S(2)}) collective-permute-start(bf16[2,2,96,640]{3,2,1,0:T(8,128)(2,1)S(1)} %maximum_bitcast_fusion.1), channel_id=1, source_target_pairs={{0,8},{4,12},{8,0},{12,4},{1,9},{5,13},{9,1},{13,5},{2,10},{6,14},... | collective-permute-start | bytes 1474568 | tf_op jit(solution)/shard_map/ppermute | solution.py:35
  56.3 48.1 %collective-permute-start.24 = (bf16[2,2,96,640]{3,2,1,0:T(8,128)(2,1)S(1)}, bf16[2,2,96,640]{3,2,1,0:T(8,128)(2,1)S(1)}, u32[]{:S(2)}, u32[]{:S(2)}) collective-permute-start(bf16[2,2,96,640]{3,2,1,0:T(8,128)(2,1)S(1)} %maximum_bitcast_fusion.1), channel_id=1, source_target_pairs={{0,12},{4,8},{8,4},{12,0},{1,13},{5,9},{9,5},{13,1},{2,14},{6,10},... | collective-permute-start | bytes 1474568 | tf_op jit(solution)/shard_map/ppermute | solution.py:35
  58.5 47.8 %collective-permute-start.7 = (bf16[4,2,1,40,896]{4,3,0,2,1:T(8,128)(2,1)S(1)}, bf16[4,2,1,40,896]{4,3,0,2,1:T(8,128)(2,1)S(1)}, u32[]{:S(2)}, u32[]{:S(2)}) collective-permute-start(bf16[4,2,1,40,896]{4,3,0,2,1:T(8,128)(2,1)S(1)} %pad_maximum_fusion.22), channel_id=1, source_target_pairs={{0,1},{1,0},{2,3},{3,2},{4,5},{5,4},{6,7},{7,6},{8,9},{9,8},{10,11... | collective-permute-start | bytes 1720328 | tf_op jit(solution)/shard_map/ppermute | solution.py:35
  94.8 49.7 %collective-permute-start.19 = (bf16[16,40,2048]{2,1,0:T(8,128)(2,1)}, bf16[16,40,2048]{2,1,0:T(8,128)(2,1)}, u32[]{:S(2)}, u32[]{:S(2)}) collective-permute-start(bf16[16,40,2048]{2,1,0:T(8,128)(2,1)} %pad_maximum_fusion), channel_id=1, source_target_pairs={{0,16},{16,0},{1,17},{17,1},{2,18},{18,2},{3,19},{19,3},{4,20},{20... | collective-permute-start | bytes 7864328 | tf_op jit(solution)/shard_map/ppermute | solution.py:35
  106.3 38.2 %collective-permute-start.25 = (bf16[16,96,640]{2,1,0:T(8,128)(2,1)}, bf16[16,96,640]{2,1,0:T(8,128)(2,1)}, u32[]{:S(2)}, u32[]{:S(2)}) collective-permute-start(bf16[16,96,640]{2,1,0:T(8,128)(2,1)} %bitcast.47), channel_id=1, source_target_pairs={{0,16},{16,0},{1,17},{17,1},{2,18},{18,2},{3,19},{19,3},{4,20},{20... | collective-permute-start | bytes 5898248 | tf_op jit(solution)/shard_map/ppermute | solution.py:35
  118.0 20.1 %collective-permute-start.10 = (bf16[256,512]{1,0:T(8,128)(2,1)S(1)}, bf16[256,512]{1,0:T(8,128)(2,1)S(1)}, u32[]{:S(2)}, u32[]{:S(2)}) collective-permute-start(bf16[256,512]{1,0:T(8,128)(2,1)S(1)} %get-tuple-element.99), channel_id=1, source_target_pairs={{0,2},{1,3},{2,0},{3,1},{4,6},{5,7},{6,4},{7,5},{8,10},{9,11},{10,... | collective-permute-start | bytes 786440 | tf_op jit(solution)/shard_map/ppermute | solution.py:35
  119.4 18.6 %collective-permute-start.11 = (bf16[256,512]{1,0:T(8,128)(2,1)S(1)}, bf16[256,512]{1,0:T(8,128)(2,1)S(1)}, u32[]{:S(2)}, u32[]{:S(2)}) collective-permute-start(bf16[256,512]{1,0:T(8,128)(2,1)S(1)} %get-tuple-element.99), channel_id=1, source_target_pairs={{0,3},{1,2},{2,1},{3,0},{4,7},{5,6},{6,5},{7,4},{8,11},{9,10},{10,... | collective-permute-start | bytes 786440 | tf_op jit(solution)/shard_map/ppermute | solution.py:35
  121.0 22.5 %collective-permute-start.9 = (bf16[256,512]{1,0:T(8,128)(2,1)S(1)}, bf16[256,512]{1,0:T(8,128)(2,1)S(1)}, u32[]{:S(2)}, u32[]{:S(2)}) collective-permute-start(bf16[256,512]{1,0:T(8,128)(2,1)S(1)} %get-tuple-element.99), channel_id=1, source_target_pairs={{0,1},{1,0},{2,3},{3,2},{4,5},{5,4},{6,7},{7,6},{8,9},{9,8},{10,11... | collective-permute-start | bytes 786440 | tf_op jit(solution)/shard_map/ppermute | solution.py:35
  170.0 33.9 %collective-permute-start.30 = (bf16[16,40,1536]{2,1,0:T(8,128)(2,1)}, bf16[16,40,1536]{2,1,0:T(8,128)(2,1)}, u32[]{:S(2)}, u32[]{:S(2)}) collective-permute-start(bf16[16,40,1536]{2,1,0:T(8,128)(2,1)} %slice.182), channel_id=1, source_target_pairs={{0,16},{16,0},{1,17},{17,1},{2,18},{18,2},{3,19},{19,3},{4,20},{20... | collective-permute-start | bytes 5898248 | tf_op jit(solution)/shard_map/ppermute | solution.py:35
  173.6 36.9 %collective-permute-start.31 = (bf16[16,40,2048]{2,1,0:T(8,128)(2,1)}, bf16[16,40,2048]{2,1,0:T(8,128)(2,1)}, u32[]{:S(2)}, u32[]{:S(2)}) collective-permute-start(bf16[16,40,2048]{2,1,0:T(8,128)(2,1)} %slice.185), channel_id=1, source_target_pairs={{0,16},{16,0},{1,17},{17,1},{2,18},{18,2},{3,19},{19,3},{4,20},{20... | collective-permute-start | bytes 7864328 | tf_op jit(solution)/shard_map/ppermute | solution.py:35
  236.4 18.7 %collective-permute-start.32 = (bf16[640,2048]{1,0:T(8,128)(2,1)}, bf16[640,2048]{1,0:T(8,128)(2,1)}, u32[]{:S(2)}, u32[]{:S(2)}) collective-permute-start(bf16[640,2048]{1,0:T(8,128)(2,1)} %convolution_convert_fusion.3), channel_id=1, source_target_pairs={{0,16},{16,0},{1,17},{17,1},{2,18},{18,2},{3,19},{19,3},{4,20},{20... | collective-permute-start | bytes 7864328 | tf_op jit(solution)/shard_map/ppermute | solution.py:35
  265.6 47.3 %collective-permute-start.42 = (bf16[2,2,96,640]{3,2,1,0:T(8,128)(2,1)}, bf16[2,2,96,640]{3,2,1,0:T(8,128)(2,1)}, u32[]{:S(2)}, u32[]{:S(2)}) collective-permute-start(bf16[2,2,96,640]{3,2,1,0:T(8,128)(2,1)} %dynamic-slice_bitcast_fusion.9), channel_id=1, source_target_pairs={{0,4},{4,8},{8,12},{12,0},{1,5},{5,9},{9,13},{13,1},{2,6},{6,10},{... | collective-permute-start | bytes 1474568 | tf_op jit(solution)/shard_map/ppermute | solution.py:180
  279.9 34.7 %collective-permute-start.39 = (bf16[2,1,2,40,2048]{4,3,0,2,1:T(8,128)(2,1)}, bf16[2,1,2,40,2048]{4,3,0,2,1:T(8,128)(2,1)}, u32[]{:S(2)}, u32[]{:S(2)}) collective-permute-start(bf16[2,1,2,40,2048]{4,3,0,2,1:T(8,128)(2,1)} %copy.111), channel_id=1, source_target_pairs={{0,2},{1,3},{2,0},{3,1},{4,6},{5,7},{6,4},{7,5},{8,10},{9,11},{10,... | collective-permute-start | bytes 1966088 | tf_op jit(solution)/shard_map/ppermute | solution.py:35
  283.3 38.9 %collective-permute-start.38 = (bf16[2,2,1,40,2048]{4,3,0,2,1:T(8,128)(2,1)}, bf16[2,2,1,40,2048]{4,3,0,2,1:T(8,128)(2,1)}, u32[]{:S(2)}, u32[]{:S(2)}) collective-permute-start(bf16[2,2,1,40,2048]{4,3,0,2,1:T(8,128)(2,1)} %copy.109), channel_id=1, source_target_pairs={{0,1},{1,0},{2,3},{3,2},{4,5},{5,4},{6,7},{7,6},{8,9},{9,8},{10,11... | collective-permute-start | bytes 1966088 | tf_op jit(solution)/shard_map/ppermute | solution.py:35
  294.8 41.0 %collective-permute-start.37 = (bf16[640,896]{1,0:T(8,128)(2,1)}, bf16[640,896]{1,0:T(8,128)(2,1)}, u32[]{:S(2)}, u32[]{:S(2)}) collective-permute-start(bf16[640,896]{1,0:T(8,128)(2,1)} %fusion.3), channel_id=1, source_target_pairs={{0,16},{16,0},{1,17},{17,1},{2,18},{18,2},{3,19},{19,3},{4,20},{20... | collective-permute-start | bytes 3440648 | tf_op jit(solution)/shard_map/ppermute | solution.py:35
  311.4 52.1 %collective-permute-start.41 = (bf16[16,96,640]{2,1,0:T(8,128)(2,1)}, bf16[16,96,640]{2,1,0:T(8,128)(2,1)}, u32[]{:S(2)}, u32[]{:S(2)}) collective-permute-start(bf16[16,96,640]{2,1,0:T(8,128)(2,1)} %pad_maximum_fusion.5), channel_id=1, source_target_pairs={{0,16},{16,0},{1,17},{17,1},{2,18},{18,2},{3,19},{19,3},{4,20},{20... | collective-permute-start | bytes 5898248 | tf_op jit(solution)/shard_map/ppermute | solution.py:35
  312.8 54.0 %collective-permute-start.40 = (bf16[640,2048]{1,0:T(8,128)(2,1)S(1)}, bf16[640,2048]{1,0:T(8,128)(2,1)}, u32[]{:S(2)}, u32[]{:S(2)}) collective-permute-start(bf16[640,2048]{1,0:T(8,128)(2,1)S(1)} %convolution_convert_fusion.1), channel_id=1, source_target_pairs={{0,16},{16,0},{1,17},{17,1},{2,18},{18,2},{3,19},{19,3},{4,20},{20... | collective-permute-start | bytes 7864328 | tf_op jit(solution)/shard_map/ppermute | solution.py:35
  314.6 17.0 %collective-permute-start.43 = (bf16[2,2,96,640]{3,2,1,0:T(8,128)(2,1)S(1)}, bf16[2,2,96,640]{3,2,1,0:T(8,128)(2,1)S(1)}, u32[]{:S(2)}, u32[]{:S(2)}) collective-permute-start(bf16[2,2,96,640]{3,2,1,0:T(8,128)(2,1)S(1)} %fusion.9), channel_id=1, source_target_pairs={{0,4},{4,8},{8,12},{12,0},{1,5},{5,9},{9,13},{13,1},{2,6},{6,10},{... | collective-permute-start | bytes 1474568 | tf_op jit(solution)/shard_map/ppermute | solution.py:180
  332.5 16.6 %collective-permute-start.44 = (bf16[2,2,96,640]{3,2,1,0:T(8,128)(2,1)}, bf16[2,2,96,640]{3,2,1,0:T(8,128)(2,1)}, u32[]{:S(2)}, u32[]{:S(2)}) collective-permute-start(bf16[2,2,96,640]{3,2,1,0:T(8,128)(2,1)} %fusion.8), channel_id=1, source_target_pairs={{0,4},{4,8},{8,12},{12,0},{1,5},{5,9},{9,13},{13,1},{2,6},{6,10},{... | collective-permute-start | bytes 1474568 | tf_op jit(solution)/shard_map/ppermute | solution.py:180
  338.2 14.3 %collective-permute-start.47 = (bf16[2,1,1,40,2048]{4,3,0,2,1:T(8,128)(2,1)}, bf16[2,1,1,40,2048]{4,3,0,2,1:T(8,128)(2,1)S(1)}, u32[]{:S(2)}, u32[]{:S(2)}) collective-permute-start(bf16[2,1,1,40,2048]{4,3,0,2,1:T(8,128)(2,1)} %constant_dynamic-slice_fusion.11), channel_id=1, source_target_pairs={{0,1},{1,0},{2,3},{3,2},{4,5},{5,4},{6,7},{7,6},{8,9},{9,8},{10,11... | collective-permute-start | bytes 983048 | tf_op jit(solution)/shard_map/ppermute | solution.py:35
  376.5 22.2 %collective-permute-start.70 = (bf16[2,2,96,640]{3,2,1,0:T(8,128)(2,1)}, bf16[2,2,96,640]{3,2,1,0:T(8,128)(2,1)}, u32[]{:S(2)}, u32[]{:S(2)}) collective-permute-start(bf16[2,2,96,640]{3,2,1,0:T(8,128)(2,1)} %dynamic-slice_bitcast_fusion.8), channel_id=1, source_target_pairs={{0,4},{4,8},{8,12},{12,0},{1,5},{5,9},{9,13},{13,1},{2,6},{6,10},{... | collective-permute-start | bytes 1474568 | tf_op jit(solution)/shard_map/ppermute | solution.py:180
  387.4 16.0 %collective-permute-start.54 = (bf16[2,1,2,40,2048]{4,3,0,2,1:T(8,128)(2,1)}, bf16[2,1,2,40,2048]{4,3,0,2,1:T(8,128)(2,1)}, u32[]{:S(2)}, u32[]{:S(2)}) collective-permute-start(bf16[2,1,2,40,2048]{4,3,0,2,1:T(8,128)(2,1)} %copy.117), channel_id=1, source_target_pairs={{0,2},{1,3},{2,0},{3,1},{4,6},{5,7},{6,4},{7,5},{8,10},{9,11},{10,... | collective-permute-start | bytes 1966088 | tf_op jit(solution)/shard_map/ppermute | solution.py:35
  390.1 14.7 %collective-permute-start.53 = (bf16[2,2,1,40,2048]{4,3,0,2,1:T(8,128)(2,1)}, bf16[2,2,1,40,2048]{4,3,0,2,1:T(8,128)(2,1)}, u32[]{:S(2)}, u32[]{:S(2)}) collective-permute-start(bf16[2,2,1,40,2048]{4,3,0,2,1:T(8,128)(2,1)} %copy.115), channel_id=1, source_target_pairs={{0,1},{1,0},{2,3},{3,2},{4,5},{5,4},{6,7},{7,6},{8,9},{9,8},{10,11... | collective-permute-start | bytes 1966088 | tf_op jit(solution)/shard_map/ppermute | solution.py:35
  397.7 18.5 %collective-permute-start.52 = (bf16[640,896]{1,0:T(8,128)(2,1)S(1)}, bf16[640,896]{1,0:T(8,128)(2,1)S(1)}, u32[]{:S(2)}, u32[]{:S(2)}) collective-permute-start(bf16[640,896]{1,0:T(8,128)(2,1)S(1)} %fusion.1), channel_id=1, source_target_pairs={{0,16},{16,0},{1,17},{17,1},{2,18},{18,2},{3,19},{19,3},{4,20},{20... | collective-permute-start | bytes 3440648 | tf_op jit(solution)/shard_map/ppermute | solution.py:35
  400.1 15.5 %collective-permute-start.71 = (bf16[2,2,96,640]{3,2,1,0:T(8,128)(2,1)S(1)}, bf16[2,2,96,640]{3,2,1,0:T(8,128)(2,1)S(1)}, u32[]{:S(2)}, u32[]{:S(2)}) collective-permute-start(bf16[2,2,96,640]{3,2,1,0:T(8,128)(2,1)S(1)} %fusion.6), channel_id=1, source_target_pairs={{0,4},{4,8},{8,12},{12,0},{1,5},{5,9},{9,13},{13,1},{2,6},{6,10},{... | collective-permute-start | bytes 1474568 | tf_op jit(solution)/shard_map/ppermute | solution.py:180
  415.7 14.7 %collective-permute-start.72 = (bf16[2,2,96,640]{3,2,1,0:T(8,128)(2,1)S(1)}, bf16[2,2,96,640]{3,2,1,0:T(8,128)(2,1)S(1)}, u32[]{:S(2)}, u32[]{:S(2)}) collective-permute-start(bf16[2,2,96,640]{3,2,1,0:T(8,128)(2,1)S(1)} %fusion.5), channel_id=1, source_target_pairs={{0,4},{4,8},{8,12},{12,0},{1,5},{5,9},{9,13},{13,1},{2,6},{6,10},{... | collective-permute-start | bytes 1474568 | tf_op jit(solution)/shard_map/ppermute | solution.py:180
  416.7 14.7 %collective-permute-start.75 = (bf16[1,1,2,96,640]{4,3,2,1,0:T(8,128)(2,1)S(1)}, bf16[1,1,2,96,640]{4,3,2,1,0:T(8,128)(2,1)S(1)}, u32[]{:S(2)}, u32[]{:S(2)}) collective-permute-start(bf16[1,1,2,96,640]{4,3,2,1,0:T(8,128)(2,1)S(1)} %dynamic-slice_bitcast_fusion.11), channel_id=1, source_target_pairs={{0,2},{1,3},{2,0},{3,1},{4,6},{5,7},{6,4},{7,5},{8,10},{9,11},{10,... | collective-permute-start | bytes 737288 | tf_op jit(solution)/shard_map/ppermute | solution.py:35
  417.7 15.1 %collective-permute-start.65 = (bf16[4,1,1,40,896]{4,3,0,2,1:T(8,128)(2,1)S(1)}, bf16[4,1,1,40,896]{4,3,0,2,1:T(8,128)(2,1)S(1)}, u32[]{:S(2)}, u32[]{:S(2)}) collective-permute-start(bf16[4,1,1,40,896]{4,3,0,2,1:T(8,128)(2,1)S(1)} %constant_dynamic-slice_fusion.2), channel_id=1, source_target_pairs={{0,2},{1,3},{2,0},{3,1},{4,6},{5,7},{6,4},{7,5},{8,10},{9,11},{10,... | collective-permute-start | bytes 860168 | tf_op jit(solution)/shard_map/ppermute | solution.py:35
  419.0 26.3 %collective-permute-start.55 = (bf16[4,2,1,40,896]{4,3,2,1,0:T(8,128)(2,1)S(1)}, bf16[4,2,1,40,896]{4,3,2,1,0:T(8,128)(2,1)S(1)}, u32[]{:S(2)}, u32[]{:S(2)}) collective-permute-start(bf16[4,2,1,40,896]{4,3,2,1,0:T(8,128)(2,1)S(1)} %constant_dynamic-slice_fusion.6), channel_id=1, source_target_pairs={{0,1},{1,0},{2,3},{3,2},{4,5},{5,4},{6,7},{7,6},{8,9},{9,8},{10,11... | collective-permute-start | bytes 1720328 | tf_op jit(solution)/shard_map/ppermute | solution.py:35
  420.0 24.2 %collective-permute-start.61 = (bf16[2,1,1,40,2048]{4,3,0,2,1:T(8,128)(2,1)S(1)}, bf16[2,1,1,40,2048]{4,3,0,2,1:T(8,128)(2,1)S(1)}, u32[]{:S(2)}, u32[]{:S(2)}) collective-permute-start(bf16[2,1,1,40,2048]{4,3,0,2,1:T(8,128)(2,1)S(1)} %constant_dynamic-slice_fusion.3), channel_id=1, source_target_pairs={{0,1},{1,0},{2,3},{3,2},{4,5},{5,4},{6,7},{7,6},{8,9},{9,8},{10,11... | collective-permute-start | bytes 983048 | tf_op jit(solution)/shard_map/ppermute | solution.py:35
  430.4 16.4 %collective-permute-start.60 = (bf16[2,1,1,40,2048]{4,3,0,2,1:T(8,128)(2,1)S(1)}, bf16[2,1,1,40,2048]{4,3,0,2,1:T(8,128)(2,1)S(1)}, u32[]{:S(2)}, u32[]{:S(2)}) collective-permute-start(bf16[2,1,1,40,2048]{4,3,0,2,1:T(8,128)(2,1)S(1)} %constant_dynamic-slice_fusion.4), channel_id=1, source_target_pairs={{0,2},{1,3},{2,0},{3,1},{4,6},{5,7},{6,4},{7,5},{8,10},{9,11},{10,... | collective-permute-start | bytes 983048 | tf_op jit(solution)/shard_map/ppermute | solution.py:35
  432.8 21.9 %collective-permute-start.76 = (bf16[1,1,1,96,640]{4,3,2,1,0:T(8,128)(2,1)S(1)}, bf16[1,1,1,96,640]{4,3,2,1,0:T(8,128)(2,1)S(1)}, u32[]{:S(2)}, u32[]{:S(2)}) collective-permute-start(bf16[1,1,1,96,640]{4,3,2,1,0:T(8,128)(2,1)S(1)} %constant_dynamic-slice_fusion), channel_id=1, source_target_pairs={{0,1},{1,0},{2,3},{3,2},{4,5},{5,4},{6,7},{7,6},{8,9},{9,8},{10,11... | collective-permute-start | bytes 368648 | tf_op jit(solution)/shard_map/ppermute | solution.py:35
  444.1 48.1 %collective-permute-start.66 = (bf16[40,2944]{1,0:T(8,128)(2,1)S(1)}, bf16[40,2944]{1,0:T(8,128)(2,1)S(1)}, u32[]{:S(2)}, u32[]{:S(2)}) collective-permute-start(bf16[40,2944]{1,0:T(8,128)(2,1)S(1)} %get-tuple-element.254), channel_id=1, source_target_pairs={{0,4},{4,0},{8,12},{12,8},{1,5},{5,1},{9,13},{13,9},{2,6},{6,2},{1... | collective-permute-start | bytes 706568 | tf_op jit(solution)/shard_map/ppermute | solution.py:35
  452.2 20.3 %collective-permute-start.63 = (bf16[40,2048]{1,0:T(8,128)(2,1)S(1)}, bf16[40,2048]{1,0:T(8,128)(2,1)S(1)}, u32[]{:S(2)}, u32[]{:S(2)}) collective-permute-start(bf16[40,2048]{1,0:T(8,128)(2,1)S(1)} %get-tuple-element.264), channel_id=1, source_target_pairs={{0,8},{4,12},{8,0},{12,4},{1,9},{5,13},{9,1},{13,5},{2,10},{6,14},... | collective-permute-start | bytes 491528 | tf_op jit(solution)/shard_map/ppermute | solution.py:35
  454.7 19.8 %collective-permute-start.64 = (bf16[40,2048]{1,0:T(8,128)(2,1)S(1)}, bf16[40,2048]{1,0:T(8,128)(2,1)S(1)}, u32[]{:S(2)}, u32[]{:S(2)}) collective-permute-start(bf16[40,2048]{1,0:T(8,128)(2,1)S(1)} %get-tuple-element.265), channel_id=1, source_target_pairs={{0,12},{4,8},{8,4},{12,0},{1,13},{5,9},{9,5},{13,1},{2,14},{6,10},... | collective-permute-start | bytes 491528 | tf_op jit(solution)/shard_map/ppermute | solution.py:35
  456.7 20.3 %collective-permute-start.57 = (bf16[40,896]{1,0:T(8,128)(2,1)S(1)}, bf16[40,896]{1,0:T(8,128)(2,1)S(1)}, u32[]{:S(2)}, u32[]{:S(2)}) collective-permute-start(bf16[40,896]{1,0:T(8,128)(2,1)S(1)} %get-tuple-element.284), channel_id=1, source_target_pairs={{0,4},{4,0},{8,12},{12,8},{1,5},{5,1},{9,13},{13,9},{2,6},{6,2},{1... | collective-permute-start | bytes 215048 | tf_op jit(solution)/shard_map/ppermute | solution.py:35
  456.8 35.3 %collective-permute-start.67 = (bf16[40,2944]{1,0:T(8,128)(2,1)S(1)}, bf16[40,2944]{1,0:T(8,128)(2,1)S(1)}, u32[]{:S(2)}, u32[]{:S(2)}) collective-permute-start(bf16[40,2944]{1,0:T(8,128)(2,1)S(1)} %get-tuple-element.256), channel_id=1, source_target_pairs={{0,8},{4,12},{8,0},{12,4},{1,9},{5,13},{9,1},{13,5},{2,10},{6,14},... | collective-permute-start | bytes 706568 | tf_op jit(solution)/shard_map/ppermute | solution.py:35
  472.5 19.7 %collective-permute-start.68 = (bf16[40,2944]{1,0:T(8,128)(2,1)S(1)}, bf16[40,2944]{1,0:T(8,128)(2,1)S(1)}, u32[]{:S(2)}, u32[]{:S(2)}) collective-permute-start(bf16[40,2944]{1,0:T(8,128)(2,1)S(1)} %get-tuple-element.255), channel_id=1, source_target_pairs={{0,12},{4,8},{8,4},{12,0},{1,13},{5,9},{9,5},{13,1},{2,14},{6,10},... | collective-permute-start | bytes 706568 | tf_op jit(solution)/shard_map/ppermute | solution.py:35
  474.5 17.6 %collective-permute-start.58 = (bf16[40,896]{1,0:T(8,128)(2,1)S(1)}, bf16[40,896]{1,0:T(8,128)(2,1)S(1)}, u32[]{:S(2)}, u32[]{:S(2)}) collective-permute-start(bf16[40,896]{1,0:T(8,128)(2,1)S(1)} %get-tuple-element.286), channel_id=1, source_target_pairs={{0,8},{4,12},{8,0},{12,4},{1,9},{5,13},{9,1},{13,5},{2,10},{6,14},... | collective-permute-start | bytes 215048 | tf_op jit(solution)/shard_map/ppermute | solution.py:35
  477.1 15.0 %collective-permute-start.59 = (bf16[40,896]{1,0:T(8,128)(2,1)S(1)}, bf16[40,896]{1,0:T(8,128)(2,1)S(1)}, u32[]{:S(2)}, u32[]{:S(2)}) collective-permute-start(bf16[40,896]{1,0:T(8,128)(2,1)S(1)} %get-tuple-element.285), channel_id=1, source_target_pairs={{0,12},{4,8},{8,4},{12,0},{1,13},{5,9},{9,5},{13,1},{2,14},{6,10},... | collective-permute-start | bytes 215048 | tf_op jit(solution)/shard_map/ppermute | solution.py:35
  (89 other events, 756.6 us)
Sparse Core Ops, SparseCore 0:
  16.4 137.9 all-gather.2
